TPU v7x, 32 devices: a whole 2x2x4 slice. The times are simulated.
32 devices in a mesh: dp: 8 (over z, x), head: 4 (over y, core).
Axes of the slice: x: 2, y: 2, z: 4, core: 2. Of those that a mesh axis runs over, the one named last changes fastest.
Arguments:
- frames: bfloat16 [6144, 1024], P(('dp', 'head')), may hold values from -6 to 6
- cotangent: bfloat16 [6144, 1024], P(('dp', 'head')), may hold values from -6 to 6
- lengths: int32 [8, 2], P('dp'), may hold values from 145 to 432, as said below
- norm_gains: bfloat16 [6, 1024], P(None, ('dp', 'head')), may hold values from 0.099609375 to 1.8984375
- position_bias: bfloat16 [1024], P(('dp', 'head')), may hold values from -4 to 4
- attend_weight: bfloat16 [1024, 3072], P(('dp', 'head')), may hold values from -0.1875 to 0.1875
- merge_weight: bfloat16 [1024, 1024], P(('dp', 'head')), may hold values from -1.5 to 1.5
- glu_weight: bfloat16 [1024, 2048], P(('dp', 'head')), may hold values from -0.1875 to 0.1875
- depth_weight: bfloat16 [31, 1024], P(None, ('dp', 'head')), may hold values from -1 to 1
- point_weight: bfloat16 [1024, 1024], P(('dp', 'head')), may hold values from -0.1875 to 0.1875
- inner_weight: bfloat16 [2, 1024, 4096], P(None, None, ('dp', 'head')), may hold values from -0.1875 to 0.1875
- outer_weight: bfloat16 [2, 4096, 1024], P(None, ('dp', 'head')), may hold values from -0.09375 to 0.09375
Outputs:
- layer_out: bfloat16 [6144, 1024], P(('dp', 'head'))
- frames_grad: float32 [6144, 1024], P(('dp', 'head'))
- gains_grad: float32 [6, 1024], P(None, ('dp', 'head'))
- position_grad: float32 [1024], P(('dp', 'head'))
- attend_grad: float32 [1024, 3072], P(('dp', 'head'))
- merge_grad: float32 [1024, 1024], P(('dp', 'head'))
- glu_grad: float32 [1024, 2048], P(('dp', 'head'))
- depth_grad: float32 [31, 1024], P(None, ('dp', 'head'))
- point_grad: float32 [1024, 1024], P(('dp', 'head'))
- inner_grad: float32 [2, 1024, 4096], P(None, None, ('dp', 'head'))
- outer_grad: float32 [2, 4096, 1024], P(None, ('dp', 'head'))
Inputs may be any that keep to these rules, and one draw needn't show every extreme that they name: `lengths`: in every row the second utterance has exactly 432 frames; the first has fewer than 192 frames, and so has the third, which holds the rest of the group's frames. In some row the first utterance has the least number of frames.
All inputs are finite; a program needn't handle non-finite values.
Results may differ from a plain program's by a relative error of at most 0.017.
Values may be sent and summed in bfloat16 or wider, within the bound.
No kernel may reach another device: no remote copies, remote signals or barrier semaphores. Data moves between devices by JAX's collectives and lax.ppermute only.
A program may use at most 384 MiB of HBM per device.

v0:
```python
import jax
import jax.numpy as jnp
from jax import lax
from jax.sharding import PartitionSpec as P

HEADS = 16
HD = 64
NB = 64


EPS = 1e-05
SCALE = 0.125


def with_halo(block, sides, width):
    for axis, dim in sides:
        count = lax.axis_size(axis)
        forward = [(i, i + 1) for i in range(count - 1)]
        backward = [(target, source) for source, target in forward]
        low = lax.ppermute(
            lax.slice_in_dim(block, block.shape[dim] - width, None, axis=dim), axis, forward
        )
        high = lax.ppermute(lax.slice_in_dim(block, 0, width, axis=dim), axis, backward)
        block = jnp.concatenate([low, block, high], axis=dim)
    return block


def product(left_in, right_in):
    return jnp.dot(left_in, right_in, preferred_element_type=jnp.float32)


def left_product(left_in, right_in):
    return jnp.einsum("nd,nf->df", left_in, right_in, preferred_element_type=jnp.float32)


def right_product(left_in, right_in):
    return jnp.einsum("nf,df->nd", left_in, right_in, preferred_element_type=jnp.float32)


def normalize(values):
    average = jnp.mean(values, axis=-1, keepdims=True)
    centred = values - average
    inverse = lax.rsqrt(jnp.mean(centred * centred, axis=-1, keepdims=True) + EPS)
    return (centred * inverse, inverse)


def norm_back(upstream, normed, inverse, gain):
    gain_grad = jnp.sum(upstream * normed, axis=0)
    scaled = upstream * gain
    back = inverse * (
        scaled
        - jnp.mean(scaled, axis=-1, keepdims=True)
        - normed * jnp.mean(scaled * normed, axis=-1, keepdims=True)
    )
    return (back, gain_grad)


def silu_slope(values):
    sigma = jax.nn.sigmoid(values)
    return sigma * (1.0 + values * (1.0 - sigma))


def segments_of(lengths_row, positions):
    first_end = lengths_row[0]
    second_end = first_end + lengths_row[1]
    return (positions >= first_end).astype(jnp.int32) + (positions >= second_end).astype(jnp.int32)


def buckets_of(query_pos, key_pos):
    offset = query_pos[:, None] - key_pos[None, :]
    distance = jnp.abs(offset)
    level = jnp.zeros_like(distance)
    for power in range(1, 14):
        level = level + (distance >= 2**power).astype(jnp.int32)
    plain = jnp.where(distance < 16, distance, jnp.minimum(12 + level, 31))
    return plain + 32 * (offset < 0).astype(jnp.int32)


def bias_of(table, bucket):

    def add_one(number, total):
        column = lax.dynamic_index_in_dim(table, number, 1, keepdims=False)
        return total + jnp.where((bucket == number)[None], column[:, None, None], 0.0)

    return lax.fori_loop(
        0, table.shape[1], add_one, jnp.zeros((table.shape[0],) + bucket.shape, jnp.float32)
    )


def bias_back(score_grad, bucket, table):

    def add_one(number, total):
        summed = jnp.sum(jnp.where((bucket == number)[None], score_grad, 0.0), axis=(1, 2))
        return lax.dynamic_update_index_in_dim(total, summed, number, 1)

    return lax.fori_loop(0, table.shape[1], add_one, jnp.zeros(table.shape, jnp.float32))


def block_scores(query_block, key_rows, table, segment, positions, start, block_rows):
    raw = jnp.einsum("qhd,khd->hqk", query_block, key_rows, preferred_element_type=jnp.float32)
    query_pos = lax.dynamic_slice_in_dim(positions, start, block_rows)
    bucket = buckets_of(query_pos, positions)
    bias = bias_of(table, bucket)
    query_seg = lax.dynamic_slice_in_dim(segment, start, block_rows)
    same = (query_seg[:, None] == segment[None, :])[None]
    return (jnp.where(same, raw * SCALE + bias, -1e30), bucket)


def attend_forward(queries, key_rows, value_rows, table, segment, positions, block_rows):
    block_count = queries.shape[0] // block_rows

    def one_block(start):
        query_block = lax.dynamic_slice_in_dim(queries, start, block_rows, 0)
        scores, bucket = block_scores(
            query_block, key_rows, table, segment, positions, start, block_rows
        )
        highest = jnp.max(scores, axis=-1, keepdims=True)
        raised = jnp.exp(scores - highest)
        totals = jnp.sum(raised, axis=-1, keepdims=True)
        weights = (raised / totals).astype(jnp.bfloat16)
        outputs = jnp.einsum(
            "hqk,khd->qhd", weights, value_rows, preferred_element_type=jnp.float32
        ).astype(jnp.bfloat16)
        return (outputs, (highest + jnp.log(totals))[..., 0])

    outputs, log_total = lax.map(one_block, jnp.arange(block_count, dtype=jnp.int32) * block_rows)
    return (outputs.reshape(queries.shape), log_total)


def attend_back(
    queries, key_rows, value_rows, table, segment, positions, block_rows, log_total, out_grad
):
    block_count = queries.shape[0] // block_rows

    def one_step(carry, number):
        key_grad, value_grad, table_grad = carry
        start = number * block_rows
        query_block = lax.dynamic_slice_in_dim(queries, start, block_rows, 0)
        grad_block = lax.dynamic_slice_in_dim(out_grad, start, block_rows, 0)
        scores, bucket = block_scores(
            query_block, key_rows, table, segment, positions, start, block_rows
        )
        weights = jnp.exp(scores - log_total[number][..., None])
        value_grad = value_grad + jnp.einsum(
            "hqk,qhd->khd",
            weights.astype(jnp.bfloat16),
            grad_block,
            preferred_element_type=jnp.float32,
        )
        weight_grad = jnp.einsum(
            "qhd,khd->hqk", grad_block, value_rows, preferred_element_type=jnp.float32
        )
        inner = jnp.sum(weights * weight_grad, axis=-1, keepdims=True)
        score_grad = weights * (weight_grad - inner)
        table_grad = table_grad + bias_back(score_grad, bucket, table)
        raw_grad = (score_grad * SCALE).astype(jnp.bfloat16)
        query_grad = jnp.einsum(
            "hqk,khd->qhd", raw_grad, key_rows, preferred_element_type=jnp.float32
        )
        key_grad = key_grad + jnp.einsum(
            "hqk,qhd->khd", raw_grad, query_block, preferred_element_type=jnp.float32
        )
        return ((key_grad, value_grad, table_grad), query_grad)

    empty = jnp.zeros(key_rows.shape, jnp.float32)
    (key_grad, value_grad, table_grad), query_grad = lax.scan(
        one_step,
        (empty, empty, jnp.zeros(table.shape, jnp.float32)),
        jnp.arange(block_count, dtype=jnp.int32),
    )
    return (query_grad.reshape(queries.shape), key_grad, value_grad, table_grad)


def feed_forward(hidden, gain, inner, outer):
    normed, inverse = normalize(hidden)
    entry = (normed * gain).astype(jnp.bfloat16)
    middle = product(entry, inner)
    activated = jax.nn.silu(middle).astype(jnp.bfloat16)
    return (hidden + 0.5 * product(activated, outer), (normed, inverse, entry, middle, activated))


def feed_back(upstream, gain, inner, outer, kept):
    normed, inverse, entry, middle, activated = kept
    half_grad = (0.5 * upstream).astype(jnp.bfloat16)
    outer_grad = left_product(activated, half_grad)
    active_grad = right_product(half_grad, outer)
    middle_grad = (active_grad * silu_slope(middle)).astype(jnp.bfloat16)
    inner_grad = left_product(entry, middle_grad)
    entry_grad = right_product(middle_grad, inner)
    back, gain_grad = norm_back(entry_grad, normed, inverse, gain)
    return (upstream + back, gain_grad, inner_grad, outer_grad)


def forward(params, hidden_in, layout):
    (
        gain_full,
        bias_full,
        attend_full,
        merge_full,
        glu_full,
        depth_full,
        point_full,
        inner_full,
        outer_full,
    ) = params
    (
        head_count,
        place,
        frame_rows,
        group_rows,
        segment,
        positions,
        segment_pad,
        segment_mid,
        margin,
        block_rows,
    ) = layout
    gain_table = gain_full.astype(jnp.float32)
    width = hidden_in.shape[1]
    channels = width // head_count
    local_heads = channels // HD
    first, first_kept = feed_forward(hidden_in, gain_table[0], inner_full[0], outer_full[0])
    normed_att, inverse_att = normalize(first)
    att_entry = (normed_att * gain_table[1]).astype(jnp.bfloat16)
    triple = (
        product(att_entry, attend_full)
        .astype(jnp.bfloat16)
        .reshape(frame_rows, 3, head_count, channels)
    )
    headed = lax.all_to_all(triple, "head", split_axis=2, concat_axis=0, tiled=True)
    queries = headed[:, 0, 0].reshape(group_rows, local_heads, HD)
    key_rows = headed[:, 1, 0].reshape(group_rows, local_heads, HD)
    value_rows = headed[:, 2, 0].reshape(group_rows, local_heads, HD)
    table = lax.dynamic_slice_in_dim(
        bias_full.astype(jnp.float32).reshape(NB, HEADS), place * local_heads, local_heads, 1
    ).T
    attended, log_total = attend_forward(
        queries, key_rows, value_rows, table, segment, positions, block_rows
    )
    att_rows = lax.all_to_all(
        attended.reshape(group_rows, 1, channels), "head", split_axis=0, concat_axis=1, tiled=True
    ).reshape(frame_rows, width)
    second = first + product(att_rows, merge_full)
    normed_conv, inverse_conv = normalize(second)
    conv_entry = (normed_conv * gain_table[2]).astype(jnp.bfloat16)
    gate_up = product(conv_entry, glu_full)
    gate_sig = jax.nn.sigmoid(gate_up[:, width:])
    glu_rows = (gate_up[:, :width] * gate_sig).astype(jnp.bfloat16)
    padded = with_halo(glu_rows, (("head", 0),), margin)
    depth_table = depth_full.astype(jnp.float32)
    mixed = jnp.zeros((frame_rows, width), jnp.float32)
    for tap in range(2 * margin + 1):
        match = (segment_pad[tap : tap + frame_rows] == segment_mid).astype(jnp.float32)[:, None]
        mixed = (
            mixed + depth_table[tap] * padded[tap : tap + frame_rows].astype(jnp.float32) * match
        )
    normed_mid, inverse_mid = normalize(mixed)
    activated = normed_mid * gain_table[3]
    swish = jax.nn.silu(activated).astype(jnp.bfloat16)
    third = second + product(swish, point_full)
    fourth, fourth_kept = feed_forward(third, gain_table[4], inner_full[1], outer_full[1])
    normed_last, inverse_last = normalize(fourth)
    result = (normed_last * gain_table[5]).astype(jnp.bfloat16)
    saved = (
        first_kept,
        normed_att,
        inverse_att,
        att_entry,
        queries,
        key_rows,
        value_rows,
        table,
        log_total,
        att_rows,
        normed_conv,
        inverse_conv,
        conv_entry,
        gate_up,
        gate_sig,
        padded,
        normed_mid,
        inverse_mid,
        activated,
        swish,
        fourth_kept,
        normed_last,
        inverse_last,
    )
    return (saved, result)


def backward(params, saved, upstream, layout):
    (
        gain_full,
        bias_full,
        attend_full,
        merge_full,
        glu_full,
        depth_full,
        point_full,
        inner_full,
        outer_full,
    ) = params
    (
        head_count,
        place,
        frame_rows,
        group_rows,
        segment,
        positions,
        segment_pad,
        segment_mid,
        margin,
        block_rows,
    ) = layout
    (
        first_kept,
        normed_att,
        inverse_att,
        att_entry,
        queries,
        key_rows,
        value_rows,
        table,
        log_total,
        att_rows,
        normed_conv,
        inverse_conv,
        conv_entry,
        gate_up,
        gate_sig,
        padded,
        normed_mid,
        inverse_mid,
        activated,
        swish,
        fourth_kept,
        normed_last,
        inverse_last,
    ) = saved
    gain_table = gain_full.astype(jnp.float32)
    width = upstream.shape[1]
    channels = width // head_count
    local_heads = channels // HD
    grad_fourth, gain_five = norm_back(upstream, normed_last, inverse_last, gain_table[5])
    grad_third, gain_four, inner_two, outer_two = feed_back(
        grad_fourth, gain_table[4], inner_full[1], outer_full[1], fourth_kept
    )
    conv_out_grad = grad_third.astype(jnp.bfloat16)
    point_grad = left_product(swish, conv_out_grad)
    swish_grad = right_product(conv_out_grad, point_full)
    act_grad = swish_grad * silu_slope(activated)
    mixed_grad, gain_three = norm_back(act_grad, normed_mid, inverse_mid, gain_table[3])
    mixed_low = mixed_grad.astype(jnp.bfloat16)
    depth_table = depth_full.astype(jnp.float32)
    grad_pad = with_halo(mixed_low, (("head", 0),), margin)
    depth_rows = []
    glu_back = jnp.zeros((frame_rows, width), jnp.float32)
    for tap in range(2 * margin + 1):
        match = (segment_pad[tap : tap + frame_rows] == segment_mid).astype(jnp.float32)[:, None]
        depth_rows.append(
            jnp.sum(
                mixed_low.astype(jnp.float32)
                * padded[tap : tap + frame_rows].astype(jnp.float32)
                * match,
                axis=0,
            )
        )
        mirror = 2 * margin - tap
        back_match = (segment_pad[mirror : mirror + frame_rows] == segment_mid).astype(jnp.float32)[
            :, None
        ]
        glu_back = (
            glu_back
            + depth_table[tap]
            * grad_pad[mirror : mirror + frame_rows].astype(jnp.float32)
            * back_match
        )
    value_part = gate_up[:, :width]
    gate_grad = jnp.concatenate(
        [glu_back * gate_sig, glu_back * value_part * gate_sig * (1.0 - gate_sig)], axis=1
    ).astype(jnp.bfloat16)
    glu_grad = left_product(conv_entry, gate_grad)
    conv_entry_grad = right_product(gate_grad, glu_full)
    depth_grad = jnp.stack(depth_rows)
    back_conv, gain_two = norm_back(conv_entry_grad, normed_conv, inverse_conv, gain_table[2])
    grad_second = grad_third + back_conv
    att_out_grad = grad_second.astype(jnp.bfloat16)
    merge_grad = left_product(att_rows, att_out_grad)
    att_rows_grad = right_product(att_out_grad, merge_full).astype(jnp.bfloat16)
    headed_grad = lax.all_to_all(
        att_rows_grad.reshape(frame_rows, head_count, channels),
        "head",
        split_axis=1,
        concat_axis=0,
        tiled=True,
    )
    attended_grad = headed_grad.reshape(group_rows, local_heads, HD)
    query_grad, key_grad, value_grad, table_grad = attend_back(
        queries,
        key_rows,
        value_rows,
        table,
        segment,
        positions,
        block_rows,
        log_total,
        attended_grad,
    )
    stacked = (
        jnp.stack([query_grad, key_grad, value_grad], axis=1)
        .reshape(group_rows, 3, 1, channels)
        .astype(jnp.bfloat16)
    )
    triple_grad = lax.all_to_all(stacked, "head", split_axis=0, concat_axis=2, tiled=True).reshape(
        frame_rows, 3 * width
    )
    attend_grad = left_product(att_entry, triple_grad)
    att_entry_grad = right_product(triple_grad, attend_full)
    bias_grid = lax.dynamic_update_slice(
        jnp.zeros((NB, HEADS), jnp.float32), table_grad.T, (jnp.int32(0), place * local_heads)
    ).reshape(NB * HEADS)
    back_att, gain_one = norm_back(att_entry_grad, normed_att, inverse_att, gain_table[1])
    grad_first = grad_second + back_att
    input_grad, gain_zero, inner_one, outer_one = feed_back(
        grad_first, gain_table[0], inner_full[0], outer_full[0], first_kept
    )
    gain_grads = jnp.stack([gain_zero, gain_one, gain_two, gain_three, gain_four, gain_five])
    gradients = (
        gain_grads,
        bias_grid,
        attend_grad,
        merge_grad,
        glu_grad,
        depth_grad,
        point_grad,
        jnp.stack([inner_one, inner_two]),
        jnp.stack([outer_one, outer_two]),
    )
    return (input_grad, gradients)


def on_device(
    frames,
    cotangent,
    lengths,
    norm_gains,
    position_bias,
    attend_weight,
    merge_weight,
    glu_weight,
    depth_weight,
    point_weight,
    inner_weight,
    outer_weight,
):

    def collect():
        return (
            lax.all_gather(norm_gains, ("dp", "head"), axis=1, tiled=True),
            lax.all_gather(position_bias, ("dp", "head"), axis=0, tiled=True),
            lax.all_gather(attend_weight, ("dp", "head"), axis=0, tiled=True),
            lax.all_gather(merge_weight, ("dp", "head"), axis=0, tiled=True),
            lax.all_gather(glu_weight, ("dp", "head"), axis=0, tiled=True),
            lax.all_gather(depth_weight, ("dp", "head"), axis=1, tiled=True),
            lax.all_gather(point_weight, ("dp", "head"), axis=0, tiled=True),
            lax.all_gather(inner_weight, ("dp", "head"), axis=2, tiled=True),
            lax.all_gather(outer_weight, ("dp", "head"), axis=1, tiled=True),
        )

    params = collect()
    head_count = lax.axis_size("head")
    place = lax.axis_index("head")
    frame_rows = frames.shape[0]
    group_rows = frame_rows * head_count
    block_rows = group_rows // ((group_rows + 511) // 512)
    margin = (depth_weight.shape[0] - 1) // 2
    lengths_row = lengths[0]
    positions = jnp.arange(group_rows, dtype=jnp.int32)
    segment = segments_of(lengths_row, positions)
    local_pos = place * frame_rows + jnp.arange(-margin, frame_rows + margin, dtype=jnp.int32)
    inside = (local_pos >= 0) & (local_pos < group_rows)
    segment_pad = jnp.where(inside, segments_of(lengths_row, local_pos), -1)
    segment_mid = segment_pad[margin : margin + frame_rows]
    layout = (
        head_count,
        place,
        frame_rows,
        group_rows,
        segment,
        positions,
        segment_pad,
        segment_mid,
        margin,
        block_rows,
    )
    hidden_in = frames.astype(jnp.float32)
    saved, result = forward(params, hidden_in, layout)
    back_params = collect()
    saved, unused_out = forward(back_params, hidden_in, layout)
    input_grad, gradients = backward(back_params, saved, cotangent.astype(jnp.float32), layout)
    summed = (
        lax.psum_scatter(gradients[0], ("dp", "head"), scatter_dimension=1, tiled=True),
        lax.psum_scatter(gradients[1], ("dp", "head"), scatter_dimension=0, tiled=True),
        lax.psum_scatter(gradients[2], ("dp", "head"), scatter_dimension=0, tiled=True),
        lax.psum_scatter(gradients[3], ("dp", "head"), scatter_dimension=0, tiled=True),
        lax.psum_scatter(gradients[4], ("dp", "head"), scatter_dimension=0, tiled=True),
        lax.psum_scatter(gradients[5], ("dp", "head"), scatter_dimension=1, tiled=True),
        lax.psum_scatter(gradients[6], ("dp", "head"), scatter_dimension=0, tiled=True),
        lax.psum_scatter(gradients[7], ("dp", "head"), scatter_dimension=2, tiled=True),
        lax.psum_scatter(gradients[8], ("dp", "head"), scatter_dimension=1, tiled=True),
    )
    return (
        result,
        input_grad,
        summed[0],
        summed[1],
        summed[2],
        summed[3],
        summed[4],
        summed[5],
        summed[6],
        summed[7],
        summed[8],
    )


def solution(mesh):
    in_specs = (
        P(("dp", "head"), None),
        P(("dp", "head"), None),
        P("dp", None),
        P(None, ("dp", "head")),
        P(("dp", "head")),
        P(("dp", "head"), None),
        P(("dp", "head"), None),
        P(("dp", "head"), None),
        P(None, ("dp", "head")),
        P(("dp", "head"), None),
        P(None, None, ("dp", "head")),
        P(None, ("dp", "head"), None),
    )
    out_specs = (
        P(("dp", "head"), None),
        P(("dp", "head"), None),
        P(None, ("dp", "head")),
        P(("dp", "head")),
        P(("dp", "head"), None),
        P(("dp", "head"), None),
        P(("dp", "head"), None),
        P(None, ("dp", "head")),
        P(("dp", "head"), None),
        P(None, None, ("dp", "head")),
        P(None, ("dp", "head"), None),
    )
    return jax.shard_map(
        on_device, mesh=mesh, in_specs=in_specs, out_specs=out_specs, check_vma=False
    )
```

profile of v0, /device:TPU:0, one launch (start us, length us, event | category | flops | bytes accessed | tf_op | source)
XLA Modules:
  0.0 5714.4 jit_solution(7370140544379846601)
XLA Ops:
  18.2 43.2 all-reduce
  61.6 43.3 all-gather
  105.7 38.8 all_gather.42
  144.6 18.2 all-gather.8.cloned.1.call-done
  162.8 6.9 fusion.127
  169.7 109.1 %all-gather.10.cloned.1.call-done = bf16[2,4096,1024]{2,1,0:T(8,128)(2,1)} async-done(((bf16[2,128,1024]{2,1,0:T(8,128)(2,1)}), bf16[2,4096,1024]{2,1,0:T(8,128)(2,1)}) %all-gather.10.cloned.1.call-update) | async-done | bytes 16777232 | tf_op jit(solution)/shard_map/all_gather | solution.py:468
  278.9 6.3 fusion.444
  285.4 64.1 %all-gather.12.cloned.1.call-done = bf16[1024,3072]{1,0:T(8,128)(2,1)} async-done(((bf16[32,3072]{1,0:T(8,128)(2,1)}), bf16[1024,3072]{1,0:T(8,128)(2,1)}) %all-gather.12.cloned.1.call-update) | async-done | bytes 6291472 | tf_op jit(solution)/shard_map/all_gather | solution.py:462
  380.0 957.0 %while.116 = (s32[]{:T(128)}, bf16[2,384,4,64]{1,3,2,0:T(8,128)(2,1)S(1)}, s32[2]{0:T(128)S(1)}, s32[768]{0:T(1024)S(1)}, bf16[768,4,64]{0,2,1:T(8,128)(2,1)S(1)...) while((s32[]{:T(128)}, ...), condition=%wide.region_9.10_spmd.clone.clone, body=%wide.region_4.9_spmd.clone.sunk.clone | while | flops 329518080 | bytes 54291884 | solution.py:126
  383.3 461.9 %while.115 = (s32[]{:T(128)}, f32[4,384,768]{2,1,0:T(8,128)}, f32[4,64]{0,1:T(8,128)S(1)}, s32[768]{0:T(1024)S(1)}, s32[384]{0:T(512)S(1)}, /*index=5*/s32[]{:T(128)}, s32[]{:T(128)}) while((s32[]{:T(128)}, f32[4,384,768]{2,1,0:T(8,128)}, f32[4,64]{0,1:T(8,128)S(1)}, s32[768]{0:T(1024)S(1)}, s32[384]{0:T(512)S(1)}, ...), condition=%wide.region_6.6_spmd.clone, body=%wide.region_5.5_spmd.clone.sunk | while | flops 17694724 | bytes 10031767 | solution.py:85
  852.2 6.7 fusion.560
  861.9 461.4 %while.115 = (s32[]{:T(128)}, f32[4,384,768]{2,1,0:T(8,128)}, f32[4,64]{0,1:T(8,128)S(1)}, s32[768]{0:T(1024)S(1)}, s32[384]{0:T(512)S(1)}, /*index=5*/s32[]{:T(128)}, s32[]{:T(128)}) while((s32[]{:T(128)}, f32[4,384,768]{2,1,0:T(8,128)}, f32[4,64]{0,1:T(8,128)S(1)}, s32[768]{0:T(1024)S(1)}, s32[384]{0:T(512)S(1)}, ...), condition=%wide.region_6.6_spmd.clone, body=%wide.region_5.5_spmd.clone.sunk | while | flops 17694724 | bytes 10031767 | solution.py:85
  1330.3 6.7 fusion.560
  1346.8 942.0 %while.118 = (s32[]{:T(128)}, bf16[2,384,4,64]{1,3,2,0:T(8,128)(2,1)S(1)}, f32[2,4,384]{2,1,0:T(4,128)S(1)}, s32[2]{0:T(128)S(1)}, s32[768]{0:T(1024)S(1)}, /*in...) while((s32[]{:T(128)}, ...), condition=%wide.region_23.24_spmd.clone.clone, body=%wide.region_18.23_spmd.clone.sunk.clone | while | flops 330693120 | bytes 30735772 | solution.py:126
  1349.8 461.4 %while.117 = (s32[]{:T(128)}, f32[4,384,768]{2,1,0:T(8,128)}, f32[4,64]{0,1:T(8,128)S(1)}, s32[768]{0:T(1024)S(1)}, s32[384]{0:T(512)S(1)}, /*index=5*/s32[]{:T(128)}, s32[]{:T(128)}) while((s32[]{:T(128)}, f32[4,384,768]{2,1,0:T(8,128)}, f32[4,64]{0,1:T(8,128)S(1)}, s32[768]{0:T(1024)S(1)}, s32[384]{0:T(512)S(1)}, ...), condition=%wide.region_20.20_spmd.clone, body=%wide.region_19.19_spmd.clone.sunk | while | flops 17694724 | bytes 10031767 | solution.py:85
  1820.8 461.4 %while.117 = (s32[]{:T(128)}, f32[4,384,768]{2,1,0:T(8,128)}, f32[4,64]{0,1:T(8,128)S(1)}, s32[768]{0:T(1024)S(1)}, s32[384]{0:T(512)S(1)}, /*index=5*/s32[]{:T(128)}, s32[]{:T(128)}) while((s32[]{:T(128)}, f32[4,384,768]{2,1,0:T(8,128)}, f32[4,64]{0,1:T(8,128)S(1)}, s32[768]{0:T(1024)S(1)}, s32[384]{0:T(512)S(1)}, ...), condition=%wide.region_20.20_spmd.clone, body=%wide.region_19.19_spmd.clone.sunk | while | flops 17694724 | bytes 10031767 | solution.py:85
  2337.5 10.4 fusion.450
  2361.5 6.6 fusion.447
  2369.3 6.8 fusion.139
  2376.1 7.0 multiply_reduce_fusion.1
  2396.2 18.4 multiply_convert_fusion.8
  2438.3 1687.5 %while.121 = (s32[]{:T(128)}, f32[768,4,64]{0,2,1:T(8,128)}, f32[768,4,64]{0,2,1:T(8,128)S(1)}, f32[4,64]{0,1:T(8,128)S(1)}, bf16[2,384,4,64]{1,3,2,0:T(8,128)(2...) while((s32[]{:T(128)}, f32[768,4,64]{0,2,1:T(8,128)}, ...), condition=%wide.region_47.48_spmd.clone.clone.clone, body=%wide.region_40.47_spmd.clone.clone.sunk.clone | while | flops 1113496832 | bytes 96577824 | solution.py:166
  2445.6 459.4 %while.119 = (s32[]{:T(128)}, f32[4,384,768]{2,1,0:T(8,128)}, f32[4,64]{0,1:T(8,128)S(1)}, s32[768]{0:T(1024)S(1)}, s32[384]{0:T(512)S(1)}, /*index=5*/s32[]{:T(128)}, s32[]{:T(128)}) while((s32[]{:T(128)}, f32[4,384,768]{2,1,0:T(8,128)}, f32[4,64]{0,1:T(8,128)S(1)}, s32[768]{0:T(1024)S(1)}, s32[384]{0:T(512)S(1)}, ...), condition=%wide.region_42.42_spmd.clone, body=%wide.region_41.41_spmd.clone.sunk | while | flops 17694724 | bytes 10031767 | solution.py:85
  2905.1 6.1 subtract_exponential_fusion.5
  2911.2 7.6 fusion.585
  2918.8 8.7 fusion.583
  2930.4 7.5 subtract_multiply_fusion.8
  2937.9 344.1 %while.120 = (s32[]{:T(128)}, f32[4,64]{0,1:T(8,128)S(1)}, f32[4,384,768]{2,1,0:T(8,128)}, s32[768]{0:T(1024)S(1)}, s32[384]{0:T(512)S(1)}, /*index=5*/s32[]{:T(128)}, s32[]{:T(128)}) while((s32[]{:T(128)}, f32[4,64]{0,1:T(8,128)S(1)}, f32[4,384,768]{2,1,0:T(8,128)}, s32[768]{0:T(1024)S(1)}, s32[384]{0:T(512)S(1)}, ...), condition=%wide.region_46.46_spmd.clone, body=%wide.region_44.45_spmd.clone.sunk | while | flops 16515070 | bytes 5313165 | solution.py:96
  3288.9 459.4 %while.119 = (s32[]{:T(128)}, f32[4,384,768]{2,1,0:T(8,128)}, f32[4,64]{0,1:T(8,128)S(1)}, s32[768]{0:T(1024)S(1)}, s32[384]{0:T(512)S(1)}, /*index=5*/s32[]{:T(128)}, s32[]{:T(128)}) while((s32[]{:T(128)}, f32[4,384,768]{2,1,0:T(8,128)}, f32[4,64]{0,1:T(8,128)S(1)}, s32[768]{0:T(1024)S(1)}, s32[384]{0:T(512)S(1)}, ...), condition=%wide.region_42.42_spmd.clone, body=%wide.region_41.41_spmd.clone.sunk | while | flops 17694724 | bytes 10031767 | solution.py:85
  3748.4 6.1 subtract_exponential_fusion.5
  3754.5 7.6 fusion.585
  3762.1 8.9 fusion.583
  3773.9 7.5 subtract_multiply_fusion.8
  3781.4 344.1 %while.120 = (s32[]{:T(128)}, f32[4,64]{0,1:T(8,128)S(1)}, f32[4,384,768]{2,1,0:T(8,128)}, s32[768]{0:T(1024)S(1)}, s32[384]{0:T(512)S(1)}, /*index=5*/s32[]{:T(128)}, s32[]{:T(128)}) while((s32[]{:T(128)}, f32[4,64]{0,1:T(8,128)S(1)}, f32[4,384,768]{2,1,0:T(8,128)}, s32[768]{0:T(1024)S(1)}, s32[384]{0:T(512)S(1)}, ...), condition=%wide.region_46.46_spmd.clone, body=%wide.region_44.45_spmd.clone.sunk | while | flops 16515070 | bytes 5313165 | solution.py:96
  4138.9 15.4 all-to-all-done.4
  4163.4 7.8 fusion.138
  4191.0 6.4 fusion.428
  4207.8 11.3 pad_maximum_fusion.1
  4227.1 11.2 pad_maximum_fusion
  4238.3 33.8 reduce-scatter.27.cloned.1.call-done
  4273.9 37.0 all-reduce.1
  4312.7 91.9 %reduce-scatter.25.cloned.1.call-done = f32[32,6]{1,0:T(8,128)} async-done(((f32[1024,6]{1,0:T(8,128)}), f32[32,6]{1,0:T(8,128)}) %reduce-scatter.25.cloned.1.call-update) | async-done | bytes 784
  4405.9 138.7 %reduce-scatter.19.cloned.1.call-done = f32[32,1024]{1,0:T(8,128)} async-done(((f32[1024,1024]{1,0:T(8,128)}), f32[32,1024]{1,0:T(8,128)}) %reduce-scatter.19.cloned.1.call-update) | async-done | bytes 131088 | tf_op jit(solution)/shard_map/reduce_scatter | solution.py:509
  4544.6 140.1 %reduce-scatter.15.cloned.1.call-done = f32[32,1024]{1,0:T(8,128)} async-done(((f32[1024,1024]{1,0:T(8,128)}), f32[32,1024]{1,0:T(8,128)}) %reduce-scatter.15.cloned.1.call-update) | async-done | bytes 131088 | tf_op jit(solution)/shard_map/reduce_scatter | solution.py:506
  4684.8 147.9 %reduce-scatter.17.cloned.1.call-done = f32[32,2048]{1,0:T(8,128)} async-done(((f32[1024,2048]{1,0:T(8,128)}), f32[32,2048]{1,0:T(8,128)}) %reduce-scatter.17.cloned.1.call-update) | async-done | bytes 262160 | tf_op jit(solution)/shard_map/reduce_scatter | solution.py:507
  4832.6 158.2 %reduce-scatter.13.cloned.1.call-done = f32[32,3072]{1,0:T(8,128)} async-done(((f32[1024,3072]{1,0:T(8,128)}), f32[32,3072]{1,0:T(8,128)}) %reduce-scatter.13.cloned.1.call-update) | async-done | bytes 393232 | tf_op jit(solution)/shard_map/reduce_scatter | solution.py:505
  4990.8 356.1 %reduce-scatter.23.cloned.1.call-done = f32[2,128,1024]{2,1,0:T(8,128)} async-done(((f32[2,4096,1024]{2,1,0:T(8,128)}), f32[2,128,1024]{2,1,0:T(8,128)}) %reduce-scatter.23.cloned.1.call-update) | async-done | bytes 1048592 | tf_op jit(solution)/shard_map/reduce_scatter | solution.py:511
  5347.0 360.4 %reduce-scatter.21.cloned.1.call-done = f32[2,1024,128]{2,1,0:T(8,128)} async-done(((f32[2,1024,4096]{2,1,0:T(8,128)}), f32[2,1024,128]{2,1,0:T(8,128)}) %reduce-scatter.21.cloned.1.call-update) | async-done | bytes 1048592 | tf_op jit(solution)/shard_map/reduce_scatter | solution.py:510
  (2240 shorter events, 3708.3 us)
Async XLA Ops:
  7.2 54.2 copy-start.201
  7.2 54.4 copy-start.210
  7.2 155.6 %all-gather.8.cloned.1.call-start = ((), (), s32[]{:S(2)}) async-start(), calls=%async_computation.13 | async-start | bytes 17301504 | tf_op jit(solution)/shard_map/all_gather | solution.py:467
  8.0 270.9 %all-gather.10.cloned.1.call-start = ((), (), s32[]{:S(2)}) async-start(), calls=%async_computation.14 | async-start | bytes 17301504 | tf_op jit(solution)/shard_map/all_gather | solution.py:468
  8.7 340.9 %all-gather.12.cloned.1.call-start = ((), (), s32[]{:S(2)}) async-start(), calls=%async_computation.15 | async-start | bytes 6488064 | tf_op jit(solution)/shard_map/all_gather | solution.py:462
  9.4 2291.1 %all-gather.14.cloned.1.call-start = ((), (), s32[]{:S(2)}) async-start(), calls=%async_computation.16 | async-start | bytes 2162688 | tf_op jit(solution)/shard_map/all_gather | solution.py:463
  10.0 2293.1 %all-gather.16.cloned.1.call-start = ((), (), s32[]{:S(2)}) async-start(), calls=%async_computation.17 | async-start | bytes 4325376 | tf_op jit(solution)/shard_map/all_gather | solution.py:464
  10.6 2323.1 %all-gather.18.cloned.1.call-start = ((), (), s32[]{:S(2)}) async-start(), calls=%async_computation.18 | async-start | bytes 2162688 | tf_op jit(solution)/shard_map/all_gather | solution.py:466
  17.6 152.1 %copy-start.100 = (f32[192]{0:T(256)}, f32[192]{0:T(256)S(1)}, u32[]{:S(2)}) copy-start(f32[192]{0:T(256)S(1)} %broadcast_multiply_fusion.21) | copy-start | bytes 2308
  17.9 151.8 %copy-start.112 = (f32[192]{0:T(256)}, f32[192]{0:T(256)S(1)}, u32[]{:S(2)}) copy-start(f32[192]{0:T(256)S(1)} %add_rsqrt_fusion.9) | copy-start | bytes 2308
  105.6 64.1 %copy-start.61 = (f32[1,1024]{1,0:T(1,128)}, f32[1,1024]{1,0:T(1,128)S(1)}, u32[]{:S(2)}) copy-start(f32[1,1024]{1,0:T(1,128)S(1)} %get-tuple-element.969) | copy-start | bytes 12292
  105.7 243.9 %copy-start.67 = (f32[1,1024]{1,0:T(1,128)}, f32[1,1024]{1,0:T(1,128)S(1)}, u32[]{:S(2)}) copy-start(f32[1,1024]{1,0:T(1,128)S(1)} %get-tuple-element.968) | copy-start | bytes 12292
  285.2 69.7 %copy-start.1 = (f32[192,1024]{1,0:T(8,128)}, f32[192,1024]{1,0:T(8,128)S(1)}, u32[]{:S(2)}) copy-start(f32[192,1024]{1,0:T(8,128)S(1)} %get-tuple-element.1005) | copy-start | bytes 2359300
  285.2 69.7 %copy-start.102 = (f32[192]{0:T(256)}, f32[192]{0:T(256)S(1)}, u32[]{:S(2)}) copy-start(f32[192]{0:T(256)S(1)} %broadcast_multiply_fusion.20) | copy-start | bytes 2308
  285.4 69.4 %copy-start.114 = (f32[192]{0:T(256)}, f32[192]{0:T(256)S(1)}, u32[]{:S(2)}) copy-start(f32[192]{0:T(256)S(1)} %add_rsqrt_fusion.8) | copy-start | bytes 2308
  358.8 20.5 all-to-all-start
  1342.5 951.3 %all-to-all-start.1 = ((bf16[4,2,24576]{2,1,0:T(2,128)(2,1)}), bf16[4,2,24576]{2,1,0:T(2,128)(2,1)}, u32[]{:S(2)}, u32[]{:S(2)}) async-start(bf16[4,2,24576]{2,1,0:T(2,128)(2,1)} %reshape.507), calls=%async_computation.1 | async-start | bytes 786432 | tf_op jit(solution)/shard_map/all_to_all | solution.py:240
  2293.8 13.8 all-to-all-start.2
  2311.3 15.5 collective-permute-start
  2313.7 13.1 collective-permute-start.1
  2315.7 104.0 %copy-start.6 = (f32[192,1024]{1,0:T(8,128)}, f32[192,1024]{1,0:T(8,128)S(1)}, u32[]{:S(2)}) copy-start(f32[192,1024]{1,0:T(8,128)S(1)} %get-tuple-element.1007) | copy-start | bytes 2359300
  2315.7 103.9 %copy-start.110 = (f32[192]{0:T(256)}, f32[192]{0:T(256)S(1)}, u32[]{:S(2)}) copy-start(f32[192]{0:T(256)S(1)} %broadcast_multiply_fusion.15) | copy-start | bytes 2308
  2320.3 111.0 %copy-start.4 = (bf16[192,1024]{1,0:T(8,128)(2,1)}, bf16[192,1024]{1,0:T(8,128)(2,1)S(1)}, u32[]{:S(2)}) copy-start(bf16[192,1024]{1,0:T(8,128)(2,1)S(1)} %multiply_convert_fusion.13) | copy-start | bytes 1179652
  2321.0 28.0 collective-permute-start.2
  2325.1 23.9 collective-permute-start.3
  2354.7 31.5 copy-start.16
  2354.7 31.5 copy-start.194
  2355.0 31.3 copy-start.199
  2355.9 27.2 copy-start.20
  2355.9 27.2 copy-start.104
  2356.2 26.9 copy-start.149
  2389.1 6.3 collective-permute-start.4
  2390.4 5.7 collective-permute-start.5
  2395.4 19.3 copy-start.12
  2395.4 19.6 copy-start.174
  2423.0 12.8 all-to-all-start.3
  4130.1 24.2 all-to-all-start.4
  4134.0 138.1 %reduce-scatter.27.cloned.1.call-start = ((), (), s32[]{:S(2)}) async-start(), calls=%async_computation.26 | async-start | bytes 540672
  4138.9 265.7 %reduce-scatter.25.cloned.1.call-start = ((), (), s32[]{:S(2)}) async-start(), calls=%async_computation.25 | async-start | bytes 540672
  4177.1 367.6 %reduce-scatter.19.cloned.1.call-start = ((), (), s32[]{:S(2)}) async-start(), calls=%async_computation.22 | async-start | bytes 4325376 | tf_op jit(solution)/shard_map/reduce_scatter | solution.py:509
  4180.0 504.8 %reduce-scatter.15.cloned.1.call-start = ((), (), s32[]{:S(2)}) async-start(), calls=%async_computation.20 | async-start | bytes 4325376 | tf_op jit(solution)/shard_map/reduce_scatter | solution.py:506
  4183.7 648.9 %reduce-scatter.17.cloned.1.call-start = ((), (), s32[]{:S(2)}) async-start(), calls=%async_computation.21 | async-start | bytes 8650752 | tf_op jit(solution)/shard_map/reduce_scatter | solution.py:507
  4189.7 801.1 %reduce-scatter.13.cloned.1.call-start = ((), (), s32[]{:S(2)}) async-start(), calls=%async_computation.19 | async-start | bytes 12976128 | tf_op jit(solution)/shard_map/reduce_scatter | solution.py:505
  4197.4 1149.5 %reduce-scatter.23.cloned.1.call-start = ((), (), s32[]{:S(2)}) async-start(), calls=%async_computation.24 | async-start | bytes 34603008 | tf_op jit(solution)/shard_map/reduce_scatter | solution.py:511
  4219.1 1488.3 %reduce-scatter.21.cloned.1.call-start = ((), (), s32[]{:S(2)}) async-start(), calls=%async_computation.23 | async-start | bytes 34603008 | tf_op jit(solution)/shard_map/reduce_scatter | solution.py:510
  4238.3 35.3 copy-start.53
  4238.3 73.2 %copy-start.39 = (f32[192,1024]{1,0:T(8,128)S(1)}, f32[192,1024]{1,0:T(8,128)}, u32[]{:S(2)}) copy-start(f32[192,1024]{1,0:T(8,128)} %copy-done.38) | copy-start | bytes 2359300
  4238.3 73.2 %copy-start.56 = (f32[192,1024]{1,0:T(8,128)S(1)}, f32[192,1024]{1,0:T(8,128)}, u32[]{:S(2)}) copy-start(f32[192,1024]{1,0:T(8,128)} %get-tuple-element.1022) | copy-start | bytes 2359300
  (198 other events, 1204.1 us)
Sparse Core Ops, SparseCore 0:
  10.9 151.8 all-gather.7
  165.7 113.0 all-gather.9
  281.8 67.7 all-gather.11
  352.3 54.9 all-gather.13
  410.0 60.8 all-gather.15
  473.6 54.9 all-gather.17
  4139.0 133.0 reduce-scatter.26
  4274.5 130.0 reduce-scatter.24
  4407.4 137.1 reduce-scatter.18
  4547.3 137.4 reduce-scatter.14
  4687.7 144.9 reduce-scatter.16
  4839.1 151.6 reduce-scatter.12
  4993.8 353.1 reduce-scatter.22
  5349.8 357.5 reduce-scatter.20
where the time goes:
time: 5740 us; the launch traced here: 5710 us
  other arithmetic  3530 us (61%)
  waiting for transfers between devices  1650 us (29%)
  matrix products  226 us (4%)
  blocking collectives  162 us (3%)
  local copies, waits for them, and re-layouts  70.3 us (1%)
    add x384, other arithmetic, add_one(): total + jnp.where((bucket == number)[None], column[:, None, None], 0.0)  1950 us
    eq x512, other arithmetic, add_one(): bucket == number  1090 us
    reduce_sum x128, other arithmetic, add_one(): jnp.sum(jnp.where((bucket == number)[None], score_grad, 0.0), axis=(1, 2))  412 us
    reduce_scatter x1, waiting for transfers between devices, on_device(): lax.psum_scatter(gradients[7], ('dp', 'head'), scatter_dimension=2, tiled...  360 us
    reduce_scatter x1, waiting for transfers between devices, on_device(): lax.psum_scatter(gradients[8], ('dp', 'head'), scatter_dimension=1, tiled...  356 us
    reduce_scatter x1, waiting for transfers between devices, on_device(): lax.psum_scatter(gradients[2], ('dp', 'head'), scatter_dimension=0, tiled...  158 us
    reduce_scatter x1, waiting for transfers between devices, on_device(): lax.psum_scatter(gradients[4], ('dp', 'head'), scatter_dimension=0, tiled...  148 us
    reduce_scatter x1, waiting for transfers between devices, on_device(): lax.psum_scatter(gradients[3], ('dp', 'head'), scatter_dimension=0, tiled...  140 us
  transfers between devices with their start and end apart: 25, of which 15 were waited for; matrix products, arithmetic and copies ran while one was open for 36% of the time, Pallas kernels for 0%

commit v1 on v0

v1 whole, which is shorter than its diff:
```python
import jax
import jax.numpy as jnp
from jax import lax
from jax.experimental import pallas as pl
from jax.experimental.pallas import tpu as pltpu
from jax.sharding import Mesh
from jax.sharding import PartitionSpec as P

HEADS = 16
HD = 64
NB = 64
ROWS = 128
VMEM = 50 * 1024 * 1024


def matmul_in(left, right, dims):
    return lax.dot_general(left, right, (dims, ((), ())), preferred_element_type=jnp.float32)


def spread_bias(info_ref, bias_ref, spread_ref):
    width = spread_ref.shape[1]
    row = jnp.broadcast_to(bias_ref[0], (ROWS, width))
    spread_ref[...] = pltpu.roll(row, 0, 1, stride=1, stride_axis=0)


def half_mask(rows):
    lane = lax.broadcasted_iota(jnp.int32, (rows, 2 * HD), 1)
    start = lax.rem(pl.program_id(0), 2) * HD
    return (lane >= start) & (lane < start + HD)


def segment_at(position, first_end, second_end):
    return (position >= first_end).astype(jnp.int32) + (position >= second_end).astype(jnp.int32)


def weights_of(info_ref, spread_ref, query, keys, number):
    group = keys.shape[0]
    first_end, second_end, start = info_ref[0], info_ref[1], info_ref[2]
    raw = matmul_in(query, keys, ((1,), (1,)))
    shift = pl.multiple_of(group - start - number * ROWS, ROWS)
    bias = spread_ref[:, pl.ds(shift, group)]
    row = start + number * ROWS + lax.broadcasted_iota(jnp.int32, (ROWS, 1), 0)
    column = lax.broadcasted_iota(jnp.int32, (1, group), 1)
    same = segment_at(row, first_end, second_end) == segment_at(column, first_end, second_end)
    scores = jnp.where(same, raw * 0.125 + bias, -1e30)
    raised = jnp.exp(scores - jnp.max(scores, axis=1, keepdims=True))
    return raised * (1.0 / jnp.sum(raised, axis=1, keepdims=True))


def attend_kernel(info_ref, bias_ref, query_ref, key_ref, value_ref, out_ref, spread_ref):
    spread_bias(info_ref, bias_ref, spread_ref)
    mask = half_mask(ROWS)
    first = lax.rem(pl.program_id(0), 2) == 0
    for number in range(query_ref.shape[0] // ROWS):
        rows = pl.ds(number * ROWS, ROWS)
        query = jnp.where(mask, query_ref[rows, :], jnp.bfloat16(0))
        weights = weights_of(info_ref, spread_ref, query, key_ref[...], number)
        out = matmul_in(weights.astype(jnp.bfloat16), value_ref[...], ((1,), (0,)))
        out = out.astype(jnp.bfloat16)
        kept = jnp.where(first, out, out_ref[rows, :])
        out_ref[rows, :] = jnp.where(mask, out, kept)


def attend_back_kernel(
    info_ref,
    bias_ref,
    query_ref,
    key_ref,
    value_ref,
    grad_ref,
    query_grad_ref,
    key_grad_ref,
    value_grad_ref,
    sums_ref,
    spread_ref,
    diag_ref,
    weight_ref,
    score_ref,
    query_mid_ref,
    grad_mid_ref,
):
    spread_bias(info_ref, bias_ref, spread_ref)
    mask = half_mask(ROWS)
    group, width = key_ref.shape[0], spread_ref.shape[1]
    first = lax.rem(pl.program_id(0), 2) == 0
    diag_ref[...] = jnp.zeros(diag_ref.shape, jnp.float32)
    for number in range(query_ref.shape[0] // ROWS):
        rows = pl.ds(number * ROWS, ROWS)
        query = jnp.where(mask, query_ref[rows, :], jnp.bfloat16(0))
        grad = jnp.where(mask, grad_ref[rows, :], jnp.bfloat16(0))
        query_mid_ref[rows, :] = query
        grad_mid_ref[rows, :] = grad
        weights = weights_of(info_ref, spread_ref, query, key_ref[...], number)
        weight_ref[rows, :] = weights.astype(jnp.bfloat16)
        weight_grad = matmul_in(grad, value_ref[...], ((1,), (1,)))
        inner = jnp.sum(weights * weight_grad, axis=1, keepdims=True)
        score_grad = weights * (weight_grad - inner)
        shift = pl.multiple_of(group - info_ref[2] - number * ROWS, ROWS)
        diag_ref[:, pl.ds(shift, group)] += score_grad
        raw_grad = (score_grad * 0.125).astype(jnp.bfloat16)
        score_ref[rows, :] = raw_grad
        out = matmul_in(raw_grad, key_ref[...], ((1,), (0,))).astype(jnp.bfloat16)
        kept = jnp.where(first, out, query_grad_ref[rows, :])
        query_grad_ref[rows, :] = jnp.where(mask, out, kept)
    key_grad = matmul_in(score_ref[...], query_mid_ref[...], ((0,), (0,)))
    value_grad = matmul_in(weight_ref[...], grad_mid_ref[...], ((0,), (0,)))

    @pl.when(first)
    def _():
        key_grad_ref[...] = key_grad
        value_grad_ref[...] = value_grad

    @pl.when(jnp.logical_not(first))
    def _():
        key_grad_ref[...] += key_grad
        value_grad_ref[...] += value_grad

    total = diag_ref[...]
    size = ROWS // 2
    while size >= 8:
        total = total[:size] + pltpu.roll(total[size:], width - size, 1)
        size //= 2
    for size in (4, 2, 1):
        total = total + pltpu.roll(pltpu.roll(total, 8 - size, 0), width - size, 1)
    sums_ref[0] = total[0:1]


def attend_specs(rows, group, width, pairs):
    return [
        pl.BlockSpec(memory_space=pltpu.SMEM),
        pl.BlockSpec((1, 1, width), lambda h: (h, 0, 0)),
        pl.BlockSpec((rows, 2 * HD), lambda h: (0, h // 2)),
        pl.BlockSpec((group, 2 * HD), lambda h: (0, h // 2)),
        pl.BlockSpec((group, 2 * HD), lambda h: (0, pairs + h // 2)),
    ]


def attend(info, bias, query, both):
    heads, _, width = bias.shape
    rows, group = query.shape[0], both.shape[0]
    pairs = heads // 2
    return pl.pallas_call(
        attend_kernel,
        grid=(heads,),
        in_specs=attend_specs(rows, group, width, pairs),
        out_specs=pl.BlockSpec((rows, 2 * HD), lambda h: (0, h // 2)),
        out_shape=jax.ShapeDtypeStruct((rows, heads * HD), jnp.bfloat16),
        scratch_shapes=[pltpu.VMEM((ROWS, width), jnp.float32)],
        compiler_params=pltpu.CompilerParams(vmem_limit_bytes=VMEM),
        name="attend",
    )(info, bias, query, both, both)


def attend_back(info, bias, query, both, grad):
    heads, _, width = bias.shape
    rows, group = query.shape[0], both.shape[0]
    pairs = heads // 2
    pair_block = pl.BlockSpec((rows, 2 * HD), lambda h: (0, h // 2))
    group_block = pl.BlockSpec((group, 2 * HD), lambda h: (0, h // 2))
    return pl.pallas_call(
        attend_back_kernel,
        grid=(heads,),
        in_specs=attend_specs(rows, group, width, pairs) + [pair_block],
        out_specs=[pair_block, group_block, group_block, pl.BlockSpec((1, 1, width), lambda h: (h, 0, 0))],
        out_shape=[
            jax.ShapeDtypeStruct((rows, heads * HD), jnp.bfloat16),
            jax.ShapeDtypeStruct((group, heads * HD), jnp.float32),
            jax.ShapeDtypeStruct((group, heads * HD), jnp.float32),
            jax.ShapeDtypeStruct((heads, 1, width), jnp.float32),
        ],
        scratch_shapes=[
            pltpu.VMEM((ROWS, width), jnp.float32),
            pltpu.VMEM((ROWS, width), jnp.float32),
            pltpu.VMEM((rows, group), jnp.bfloat16),
            pltpu.VMEM((rows, group), jnp.bfloat16),
            pltpu.VMEM((rows, 2 * HD), jnp.bfloat16),
            pltpu.VMEM((rows, 2 * HD), jnp.bfloat16),
        ],
        compiler_params=pltpu.CompilerParams(vmem_limit_bytes=VMEM),
        name="attend_back",
    )(info, bias, query, both, both, grad)


LANES = 128
EDGE = 16


def reach_of(info_ref, rows, group):
    position = info_ref[2] + lax.broadcasted_iota(jnp.int32, (rows, LANES), 0)
    first_end, second_end = info_ref[0], info_ref[1]
    low = jnp.where(position >= second_end, second_end, jnp.where(position >= first_end, first_end, 0))
    high = jnp.where(position < first_end, first_end, jnp.where(position < second_end, second_end, group))
    return (low - position, high - position)


def within(reach, shift):
    if shift < 0:
        return reach[0] <= shift
    return reach[1] > shift


def fill(pad_ref, low_ref, mid_ref, high_ref):
    rows = mid_ref.shape[0]
    pad_ref[0:EDGE, :] = low_ref[...].astype(jnp.float32)
    pad_ref[EDGE : EDGE + rows, :] = mid_ref[...].astype(jnp.float32)
    pad_ref[EDGE + rows :, :] = high_ref[...].astype(jnp.float32)


def taps_of(pad_ref, depth_ref, reach, base, rows, taps, mirror):
    margin = (taps - 1) // 2
    total = jnp.zeros((rows, LANES), jnp.float32)
    for tap in range(taps):
        shift = margin - tap if mirror else tap - margin
        piece = pad_ref[EDGE + base + shift : EDGE + base + shift + rows, :] * depth_ref[tap : tap + 1, :]
        if shift:
            piece = jnp.where(within(reach, shift), piece, 0.0)
        total = total + piece
    return total


def conv_kernel(group, taps, info_ref, low_ref, mid_ref, high_ref, depth_ref, out_ref, pad_ref):
    fill(pad_ref, low_ref, mid_ref, high_ref)
    low, high = reach_of(info_ref, mid_ref.shape[0], group)
    for base in range(0, mid_ref.shape[0], STEP):
        reach = (low[base : base + STEP], high[base : base + STEP])
        out_ref[base : base + STEP, :] = taps_of(pad_ref, depth_ref, reach, base, STEP, taps, False)


STEP = 64


def conv_back_kernel(
    group,
    taps,
    info_ref,
    low_ref,
    mid_ref,
    high_ref,
    grad_low_ref,
    grad_mid_ref,
    grad_high_ref,
    depth_ref,
    out_ref,
    depth_grad_ref,
    pad_ref,
    grad_pad_ref,
    sum_ref,
):
    fill(pad_ref, low_ref, mid_ref, high_ref)
    fill(grad_pad_ref, grad_low_ref, grad_mid_ref, grad_high_ref)
    low, high = reach_of(info_ref, mid_ref.shape[0], group)
    margin = (taps - 1) // 2
    sum_ref[...] = jnp.zeros(sum_ref.shape, jnp.float32)
    for base in range(0, mid_ref.shape[0], STEP):
        reach = (low[base : base + STEP], high[base : base + STEP])
        out_ref[base : base + STEP, :] = taps_of(grad_pad_ref, depth_ref, reach, base, STEP, taps, True)
        grad = grad_pad_ref[EDGE + base : EDGE + base + STEP, :]
        for tap in range(taps):
            shift = tap - margin
            piece = pad_ref[EDGE + base + shift : EDGE + base + shift + STEP, :] * grad
            if shift:
                piece = jnp.where(within(reach, shift), piece, 0.0)
            sum_ref[8 * tap : 8 * tap + 8, :] += jnp.sum(piece.reshape(STEP // 8, 8, LANES), axis=0)
    for tap in range(taps):
        depth_grad_ref[tap : tap + 1, :] = jnp.sum(sum_ref[8 * tap : 8 * tap + 8, :], axis=0, keepdims=True)


def lane_block(rows):
    return pl.BlockSpec((rows, LANES), lambda i: (0, i))


def conv(info, low, mid, high, depth, group):
    rows, width = mid.shape
    taps = depth.shape[0]
    return pl.pallas_call(
        lambda *refs: conv_kernel(group, taps, *refs),
        grid=(width // LANES,),
        in_specs=[pl.BlockSpec(memory_space=pltpu.SMEM)]
        + [lane_block(EDGE), lane_block(rows), lane_block(EDGE), lane_block(taps)],
        out_specs=lane_block(rows),
        out_shape=jax.ShapeDtypeStruct((rows, width), jnp.float32),
        scratch_shapes=[pltpu.VMEM((rows + 2 * EDGE, LANES), jnp.float32)],
        compiler_params=pltpu.CompilerParams(vmem_limit_bytes=VMEM),
        name="conv",
    )(info, low, mid, high, depth)


def conv_back(info, low, mid, high, grad_low, grad_mid, grad_high, depth, group):
    rows, width = mid.shape
    taps = depth.shape[0]
    return pl.pallas_call(
        lambda *refs: conv_back_kernel(group, taps, *refs),
        grid=(width // LANES,),
        in_specs=[pl.BlockSpec(memory_space=pltpu.SMEM)]
        + [lane_block(EDGE), lane_block(rows), lane_block(EDGE)] * 2
        + [lane_block(taps)],
        out_specs=[lane_block(rows), lane_block(taps)],
        out_shape=[
            jax.ShapeDtypeStruct((rows, width), jnp.float32),
            jax.ShapeDtypeStruct((taps, width), jnp.float32),
        ],
        scratch_shapes=[
            pltpu.VMEM((rows + 2 * EDGE, LANES), jnp.float32),
            pltpu.VMEM((rows + 2 * EDGE, LANES), jnp.float32),
            pltpu.VMEM((8 * taps, LANES), jnp.float32),
        ],
        compiler_params=pltpu.CompilerParams(vmem_limit_bytes=VMEM),
        name="conv_back",
    )(info, low, mid, high, grad_low, grad_mid, grad_high, depth)


EPS = 1e-05
CORES = [(0, 1), (1, 0)]


def low(values):
    return values.astype(jnp.bfloat16)


def product(left_in, right_in):
    return jnp.dot(left_in, right_in, preferred_element_type=jnp.float32)


def left_product(left_in, right_in):
    return jnp.einsum("nd,nf->df", left_in, right_in, preferred_element_type=jnp.float32)


def right_product(left_in, right_in):
    return jnp.einsum("nf,df->nd", left_in, right_in, preferred_element_type=jnp.float32)


def swap(values, axis="c"):
    return lax.ppermute(values, axis, CORES)


def ordered(mine, other, place, dim=0):
    first = place == 0
    return jnp.concatenate([jnp.where(first, mine, other), jnp.where(first, other, mine)], axis=dim)


def choose(values, place, dim):
    return lax.dynamic_index_in_dim(values, place, dim, keepdims=False)


def pair_rows(values):
    return ordered(values, swap(values), lax.axis_index("c"))


def pair_sum(partial):
    place = lax.axis_index("c")
    halves = partial.reshape(2, partial.shape[0] // 2, partial.shape[1])
    received = swap(low(choose(halves, 1 - place, 0)))
    return choose(halves, place, 0) + received.astype(jnp.float32)


def gather_axis(values, axis):
    if lax.axis_size(axis) == 2:
        return ordered(values, swap(values, axis), lax.axis_index(axis))
    return lax.all_gather(values, axis, axis=0, tiled=True)


def reduce_axis(values, axis, dim):
    if lax.axis_size(axis) == 2:
        place = lax.axis_index(axis)
        received = swap(choose(values, 1 - place, dim), axis)
        kept = choose(values, place, dim)
        return (kept.astype(jnp.float32) + received.astype(jnp.float32)).astype(values.dtype)
    return lax.psum_scatter(values, axis, scatter_dimension=dim, tiled=False)


def normalize(values):
    average = jnp.mean(values, axis=-1, keepdims=True)
    centred = values - average
    inverse = lax.rsqrt(jnp.mean(centred * centred, axis=-1, keepdims=True) + EPS)
    return (centred * inverse, inverse)


def norm_back(upstream, normed, inverse, gain):
    gain_grad = jnp.sum(upstream * normed, axis=0)
    scaled = upstream * gain
    back = inverse * (
        scaled
        - jnp.mean(scaled, axis=-1, keepdims=True)
        - normed * jnp.mean(scaled * normed, axis=-1, keepdims=True)
    )
    return (back, gain_grad)


def silu_slope(values):
    sigma = jax.nn.sigmoid(values)
    return sigma * (1.0 + values * (1.0 - sigma))


def split_normalize(values):
    width = values.shape[1]
    average = jnp.mean(values, axis=1)
    centred = values - average[:, None]
    spread = jnp.sum(centred * centred, axis=1)
    other = swap(jnp.stack([average, spread]))
    gap = average - other[0]
    whole = spread + other[1] + (0.5 * width) * gap * gap
    inverse = lax.rsqrt(whole / (2 * width) + EPS)
    middle = 0.5 * (average + other[0])
    return ((values - middle[:, None]) * inverse[:, None], inverse[:, None])


def split_norm_back(upstream, normed, inverse, gain):
    gain_grad = jnp.sum(upstream * normed, axis=0)
    scaled = upstream * gain
    sums = jnp.stack([jnp.sum(scaled, axis=1), jnp.sum(scaled * normed, axis=1)])
    means = (sums + swap(sums)) / (2 * scaled.shape[1])
    back = inverse * (scaled - means[0][:, None] - normed * means[1][:, None])
    return (back, gain_grad)


def feed_forward(hidden, gain, inner, outer):
    rows = hidden.shape[0]
    normed, inverse = normalize(hidden)
    entry = low(normed * gain)
    both = jnp.concatenate([entry, swap(entry)], axis=0)
    middle = right_product(both, inner)
    activated = low(jax.nn.silu(middle))
    partial = product(activated, outer)
    received = swap(low(partial[rows:]))
    result = hidden + 0.5 * (partial[:rows] + received.astype(jnp.float32))
    return (result, (normed, inverse, both, middle, activated))


def feed_back(upstream, gain, inner, outer, kept):
    normed, inverse, both, middle, activated = kept
    rows = upstream.shape[0]
    half = low(0.5 * upstream)
    half_both = jnp.concatenate([half, swap(half)], axis=0)
    outer_grad = low(left_product(activated, half_both))
    active_grad = right_product(half_both, outer)
    middle_grad = low(active_grad * silu_slope(middle))
    inner_grad = low(left_product(middle_grad, both))
    partial = product(middle_grad, inner)
    received = swap(low(partial[rows:]))
    entry_grad = partial[:rows] + received.astype(jnp.float32)
    back, gain_grad = norm_back(entry_grad, normed, inverse, gain)
    return (upstream + back, gain_grad, inner_grad, outer_grad)


def bucket_hits(group):
    offset = group - jnp.arange(2 * group, dtype=jnp.int32)
    distance = jnp.abs(offset)
    level = jnp.zeros_like(distance)
    for power in range(1, 14):
        level = level + (distance >= 2**power).astype(jnp.int32)
    plain = jnp.where(distance < 16, distance, jnp.minimum(12 + level, 31))
    bucket = plain + 32 * (offset < 0).astype(jnp.int32)
    return bucket[:, None] == jnp.arange(NB, dtype=jnp.int32)[None, :]


def halos(values):
    count = lax.axis_size("y")
    forward = [(i, i + 1) for i in range(count - 1)]
    backward = [(target, source) for source, target in forward]
    return (
        lax.ppermute(values[-EDGE:], "y", forward),
        lax.ppermute(values[:EDGE], "y", backward),
    )


CHIPS = ("p", "q", "y")


def on_device(
    frames,
    cotangent,
    lengths,
    norm_gains,
    position_bias,
    attend_weight,
    merge_weight,
    glu_weight,
    depth_weight,
    point_weight,
    inner_weight,
    outer_weight,
):
    core = lax.axis_index("c")
    grid = tuple(lax.axis_size(axis) for axis in CHIPS)
    chips = grid[0] * grid[1] * grid[2]
    rows, width = frames.shape
    pair = 2 * rows
    group = pair * grid[2]
    half = width // 2
    share = attend_weight.shape[0]
    units = inner_weight.shape[2]
    taps = depth_weight.shape[0]
    heads = HEADS // 2
    f32 = jnp.float32

    small = jnp.concatenate([norm_gains.reshape(-1), position_bias, depth_weight.reshape(-1)])
    count = small.shape[0]
    small_rows = -(-2 * count // (16 * width)) * 16
    small_both = ordered(small[None], swap(small[None]), core).reshape(-1)
    small_both = jnp.pad(small_both, (0, small_rows * width - 2 * count)).reshape(small_rows, width)

    def own_columns(weight, shape, dim):
        parts = weight.reshape((share,) + shape)
        mine = choose(parts, core, dim).reshape(share, -1)
        other = swap(choose(parts, 1 - core, dim).reshape(share, -1))
        return ordered(mine, other, core)

    attend_part = own_columns(attend_weight, (3, 2, half), 2)
    glu_part = own_columns(glu_weight, (2, chips, 2, share), 3)
    mixed_pack = jnp.concatenate(
        [attend_part.reshape(-1, width), glu_part, merge_weight, point_weight, small_both], axis=0
    )

    def feed_pack(number):
        return jnp.concatenate([inner_weight[number].T, outer_weight[number]], axis=0)

    def feed_gather(number):
        whole = lax.all_gather(feed_pack(number), CHIPS, axis=0)
        return (
            whole[:, :units].reshape(chips * units, width),
            whole[:, units:].reshape(chips * units, width),
        )

    inner_one, outer_one = feed_gather(0)
    mixed = lax.all_gather(mixed_pack, CHIPS, axis=0)
    inner_two, outer_two = feed_gather(1)

    marks = [0]
    for size in (3 * share, 2 * share, share, share, small_rows):
        marks.append(marks[-1] + size)
    attend_full = mixed[:, marks[0] : marks[1]].reshape(width, 3 * half)
    glu_full = mixed[:, marks[1] : marks[2]].reshape(width, width)
    merge_half = mixed[:, marks[2] : marks[3]]
    point_full = mixed[:, marks[3] : marks[4]].reshape(half, width)
    small_full = mixed[:, marks[4] :].reshape(chips, -1)[:, : 2 * count].reshape(chips, 2, count)
    sides = merge_half.reshape(2, chips // 2, share, width)
    merge_full = ordered(
        choose(sides, core, 0)[:, None], swap(choose(sides, 1 - core, 0))[:, None], core, 1
    ).reshape(half, width)

    gain_size = norm_gains.size
    gains = small_full[..., :gain_size].reshape(chips, 2, 6, -1).astype(f32)
    gain_table = gains.transpose(2, 0, 1, 3).reshape(6, width)
    gain_mid = choose(gains[:, :, 3], core, 1).reshape(half)
    bias_table = small_full[..., gain_size : gain_size + position_bias.size].reshape(NB, 2, heads)
    bias_table = choose(bias_table, core, 1)
    depth = choose(small_full[..., gain_size + position_bias.size :], core, 1)
    depth = depth.reshape(chips, taps, share).transpose(1, 0, 2).reshape(taps, half).astype(f32)

    start = lax.axis_index("y") * pair
    info = jnp.stack([lengths[0, 0], lengths[0, 0] + lengths[0, 1], start.astype(jnp.int32)])
    hits = bucket_hits(group)
    bias = jnp.einsum("bh,wb->hw", bias_table, hits.astype(jnp.bfloat16), preferred_element_type=f32)
    bias = bias[:, None, :]

    hidden = frames.astype(f32)
    first, first_kept = feed_forward(hidden, gain_table[0], inner_one, outer_one)
    normed_att, inverse_att = normalize(first)
    att_entry = pair_rows(low(normed_att * gain_table[1]))
    triple = low(product(att_entry, attend_full))
    query = triple[:, :half]
    both = gather_axis(triple[:, half:], "y")
    attended = attend(info, bias, query, both)
    second = first + pair_sum(product(attended, merge_full))
    normed_conv, inverse_conv = normalize(second)
    conv_entry = pair_rows(low(normed_conv * gain_table[2]))
    gate_up = product(conv_entry, glu_full)
    gate_sig = jax.nn.sigmoid(gate_up[:, half:])
    glu_rows = low(gate_up[:, :half] * gate_sig)
    glu_low, glu_high = halos(glu_rows)
    mixed_rows = conv(info, glu_low, glu_rows, glu_high, depth, group)
    normed_mid, inverse_mid = split_normalize(mixed_rows)
    activated = normed_mid * gain_mid
    swish = low(jax.nn.silu(activated))
    third = second + pair_sum(product(swish, point_full))
    fourth, fourth_kept = feed_forward(third, gain_table[4], inner_two, outer_two)
    normed_last, inverse_last = normalize(fourth)
    result = low(normed_last * gain_table[5])

    def by_chip(values):
        return values.reshape(grid + (values.shape[0] // chips, values.shape[1]))

    def lane(values, order):
        names = list(CHIPS)
        for axis in order:
            dim = names.index(axis)
            values = reduce_axis(values, axis, dim)
            names.pop(dim)
        return values

    def last_sum(parts):
        return lax.psum_scatter(jnp.concatenate(parts, axis=1), "p", scatter_dimension=0, tiled=False)

    grad_fourth, gain_five = norm_back(
        cotangent.astype(f32), normed_last, inverse_last, gain_table[5]
    )
    grad_third, gain_four, inner_grad, outer_grad = feed_back(
        grad_fourth, gain_table[4], inner_two, outer_two, fourth_kept
    )
    feed_two = last_sum([lane(by_chip(inner_grad), "yq"), lane(by_chip(outer_grad), "qy")])

    conv_out_grad = pair_rows(low(grad_third))
    point_grad = low(left_product(swish, conv_out_grad))
    swish_grad = right_product(conv_out_grad, point_full)
    act_grad = swish_grad * silu_slope(activated)
    mixed_grad, gain_three = split_norm_back(act_grad, normed_mid, inverse_mid, gain_mid)
    mixed_low = low(mixed_grad)
    grad_low, grad_high = halos(mixed_low)
    glu_back, depth_grad = conv_back(
        info, glu_low, glu_rows, glu_high, grad_low, mixed_low, grad_high, depth, group
    )
    value_part = gate_up[:, :half]
    gate_grad = low(
        jnp.concatenate(
            [glu_back * gate_sig, glu_back * value_part * gate_sig * (1.0 - gate_sig)], axis=1
        )
    )
    glu_grad = low(left_product(conv_entry, gate_grad))
    conv_entry_grad = pair_sum(right_product(gate_grad, glu_full))
    conv_sum = last_sum([lane(by_chip(glu_grad), "qy"), lane(by_chip(point_grad), "yq")])
    back_conv, gain_two = norm_back(conv_entry_grad, normed_conv, inverse_conv, gain_table[2])
    grad_second = grad_third + back_conv

    att_out_grad = pair_rows(low(grad_second))
    merge_grad = low(left_product(attended, att_out_grad)).reshape(chips // 2, 2, share, width)
    merge_grad = ordered(
        choose(merge_grad, core, 1)[None], swap(choose(merge_grad, 1 - core, 1))[None], core
    ).reshape(chips * share, width)
    attended_grad = low(right_product(att_out_grad, merge_full))
    query_grad, key_grad, value_grad, table_sums = attend_back(info, bias, query, both, attended_grad)
    both_grad = jnp.concatenate([key_grad, value_grad], axis=1).reshape(grid[2], pair, width)
    if grid[2] == 2:
        place = lax.axis_index("y")
        received = swap(low(choose(both_grad, 1 - place, 0)), "y")
        both_grad = low(choose(both_grad, place, 0) + received.astype(f32))
    else:
        both_grad = low(lax.psum_scatter(both_grad, "y", scatter_dimension=0, tiled=False))
    triple_grad = jnp.concatenate([query_grad, both_grad], axis=1)
    attend_grad = low(left_product(att_entry, triple_grad))
    att_entry_grad = pair_sum(right_product(triple_grad, attend_full))
    attend_sum = last_sum(
        [
            lane(by_chip(attend_grad).reshape(grid + (3 * share, width)), "yq"),
            lane(by_chip(merge_grad), "qy"),
        ]
    )
    back_att, gain_one = norm_back(att_entry_grad, normed_att, inverse_att, gain_table[1])
    grad_first = grad_second + back_att
    input_grad, gain_zero, inner_grad, outer_grad = feed_back(
        grad_first, gain_table[0], inner_one, outer_one, first_kept
    )

    table_grad = jnp.einsum(
        "hw,wb->bh", table_sums[:, 0], hits.astype(f32), precision=lax.Precision.HIGHEST
    )

    def of_core(values, dim):
        empty = jnp.zeros_like(values)
        return jnp.stack(
            [jnp.where(core == 0, values, empty), jnp.where(core == 1, values, empty)], axis=dim
        )

    gain_three = of_core(gain_three.reshape(chips, share), 1).reshape(width)
    gain_grads = jnp.stack([gain_zero, gain_one, gain_two, gain_three, gain_four, gain_five])
    small_grads = jnp.concatenate(
        [
            gain_grads.reshape(6, chips, 2, share).transpose(1, 2, 0, 3).reshape(chips, 2, -1),
            of_core(table_grad, 1).reshape(chips, 2, -1),
            of_core(depth_grad.reshape(taps, chips, share).transpose(1, 0, 2), 1).reshape(
                chips, 2, -1
            ),
        ],
        axis=2,
    )
    small_sum = choose(small_grads, core, 1) + swap(choose(small_grads, 1 - core, 1))
    small_sum = lane(small_sum.reshape(grid + (count,)), "yq")
    one_rows = -(-count // (16 * width)) * 16
    small_sum = jnp.pad(low(small_sum), ((0, 0), (0, one_rows * width - count)))
    small_sum = small_sum.reshape(grid[0], one_rows, width)

    feed_one = last_sum(
        [lane(by_chip(inner_grad), "yq"), lane(by_chip(outer_grad), "qy"), small_sum]
    )

    def whole_columns(values, shape, dim):
        parts = values.reshape(2, share, -1)
        mine = choose(parts, core, 0)
        other = swap(choose(parts, 1 - core, 0))
        joined = ordered(
            jnp.expand_dims(mine.reshape((share,) + shape), dim),
            jnp.expand_dims(other.reshape((share,) + shape), dim),
            core,
            dim,
        )
        return joined.reshape(share, -1).astype(f32)

    attend_out = whole_columns(attend_sum[: 3 * share].reshape(2 * share, -1), (3, half), 2)
    merge_out = attend_sum[3 * share :].astype(f32)
    glu_out = whole_columns(conv_sum[: 2 * share], (2, chips, share), 3)
    point_out = conv_sum[2 * share :].astype(f32)
    inner_out = jnp.stack([feed_one[:units].T, feed_two[:units].T]).astype(f32)
    outer_out = jnp.stack([feed_one[units : 2 * units], feed_two[units:]]).astype(f32)
    small_out = feed_one[2 * units :].reshape(-1)[:count].astype(f32)
    gains_out = small_out[:gain_size].reshape(norm_gains.shape)
    position_out = small_out[gain_size : gain_size + position_bias.size]
    depth_out = small_out[gain_size + position_bias.size :].reshape(taps, share)
    return (
        result,
        input_grad,
        gains_out,
        position_out,
        attend_out,
        merge_out,
        glu_out,
        depth_out,
        point_out,
        inner_out,
        outer_out,
    )


def solution(mesh):
    across, along = mesh.shape["dp"], mesh.shape["head"]
    fine = Mesh(mesh.devices.reshape(4, across // 4, along // 2, 2), ("p", "q", "y", "c"))
    every = ("p", "q", "y", "c")
    in_specs = (
        P(every, None),
        P(every, None),
        P(("p", "q"), None),
        P(None, every),
        P(every),
        P(every, None),
        P(every, None),
        P(every, None),
        P(None, every),
        P(every, None),
        P(None, None, every),
        P(None, every, None),
    )
    out_specs = (
        P(every, None),
        P(every, None),
        P(None, every),
        P(every),
        P(every, None),
        P(every, None),
        P(every, None),
        P(None, every),
        P(every, None),
        P(None, None, every),
        P(None, every, None),
    )
    return jax.shard_map(
        on_device, mesh=fine, in_specs=in_specs, out_specs=out_specs, check_vma=False
    )
```

time: 5740 us -> 812 us (0.14)
  other arithmetic: 3530 us -> 68.3 us
  waiting for transfers between devices: 1650 us -> 461 us
  matrix products: 226 us -> 56.2 us
  blocking collectives: 162 us -> 0 us
    add x389 -> x3, other arithmetic: 1950 us -> 0.06 us  [the longest x1 0.03 us: reduce_axis(): kept.astype(jnp.float32) + received.astype(jnp.float32)]
    reduce_scatter x6 -> x4, waiting for transfers between devices: 1300 us -> 30.3 us  [last_sum(): lax.psum_scatter(jnp.concatenate(parts, axis=1), 'p', scatter_dimension=0...]
    eq x518 -> x0, other arithmetic: 1090 us -> none  [the longest x512 1090 us: add_one(): bucket == number]
    reduce_sum x136 -> x2, other arithmetic: 424 us -> 0.39 us  [the longest x1 0.24 us: split_normalize(): spread = jnp.sum(centred * centred, axis=1)]
    ppermute x6 -> x50, waiting for transfers between devices: 0.78 us -> 200 us  [the longest x46 165 us: swap(): return lax.ppermute(values, axis, CORES)]
    unnamed x16 -> x7, waiting for transfers between devices: 129 us -> 0.11 us
    dot_general x18 -> x2, matrix products: 87.7 us -> 1.45 us  [the longest x1 0.98 us: on_device(): jnp.einsum('bh,wb->hw', bias_table, hits.astype(jnp.bfloat16), preferred_...]
    all_gather x2 -> x0, blocking collectives: 82.2 us -> none  [the longest x1 43.3 us: collect(): lax.all_gather(norm_gains, ('dp', 'head'), axis=1, tiled=True)]
  transfers between devices with their start and end apart: 25 -> 57, of which waited for: 15 -> 23; matrix products, arithmetic and copies ran while one was open for 36% -> 24% of each run, Pallas kernels for 0% -> 6%
where the time goes in v1:
time: 812 us; the launch traced here: 803 us
  waiting for transfers between devices  461 us (57%)
  local copies, waits for them, and re-layouts  113 us (14%)
  other arithmetic  68.3 us (8%)
  matrix products  56.2 us (7%)
  Pallas kernels  51.3 us (6%)
  starting transfers between devices  34.5 us (4%)
  between operations  18.4 us (2%)
    ppermute x46, waiting for transfers between devices, swap(): return lax.ppermute(values, axis, CORES)  165 us
    all_gather x2, waiting for transfers between devices, feed_gather(): whole = lax.all_gather(feed_pack(number), CHIPS, axis=0)  122 us
    all_gather x1, waiting for transfers between devices, on_device(): mixed = lax.all_gather(mixed_pack, CHIPS, axis=0)  108 us
    ppermute x2, waiting for transfers between devices, halos(): lax.ppermute(values[:EDGE], 'y', backward)  34.6 us
    reduce_scatter x4, waiting for transfers between devices, last_sum(): lax.psum_scatter(jnp.concatenate(parts, axis=1), 'p', scatter_dimension=0...  30.3 us
    pallas_call x1, Pallas kernels, attend_back(): pl.pallas_call(attend_back_kernel, grid=(heads,), in_specs=attend_specs(r...  25.6 us
    convert_element_type x16, other arithmetic, reduce_axis(): (kept.astype(jnp.float32) + received.astype(jnp.float32)).astype(values.d...  24.3 us
    dynamic_slice x23, local copies, waits for them, and re-layouts, choose(): return lax.dynamic_index_in_dim(values, place, dim, keepdims=False)  23.7 us
  transfers between devices with their start and end apart: 57, of which 23 were waited for; matrix products, arithmetic and copies ran while one was open for 24% of the time, Pallas kernels for 6%

profile of v1, /device:TPU:0, one launch (start us, length us, event | category | flops | bytes accessed | tf_op | source)
XLA Modules:
  0.0 803.2 jit_solution(5885694433372844344)
XLA Ops:
  13.9 3.5 dynamic-slice_reduce_fusion
  22.7 108.1 %all-gather.7.cloned.1.call-done = bf16[3840,1024]{1,0:T(8,128)(2,1)} async-done(((bf16[240,1024]{1,0:T(8,128)(2,1)}), bf16[3840,1024]{1,0:T(8,128)(2,1)}) %all-gather.7.cloned.1.call-update) | async-done | bytes 7864336 | tf_op jit(solution)/shard_map/all_gather | solution.py:525
  133.0 112.2 %all-gather.9.cloned.1.call-done = bf16[4096,1024]{1,0:T(8,128)(2,1)} async-done(((bf16[256,1024]{1,0:T(8,128)(2,1)}), bf16[4096,1024]{1,0:T(8,128)(2,1)}) %all-gather.9.cloned.1.call-update) | async-done | bytes 8388624 | tf_op jit(solution)/shard_map/all_gather | solution.py:518
  245.2 4.4 fusion.124
  257.1 3.9 slice.286
  263.3 2.8 fusion.125
  267.0 5.9 reshape.597
  273.2 3.6 convolution_convert_fusion.5
  282.7 19.2 %collective-permute-done.6 = bf16[384,1024]{1,0:T(8,128)(2,1)} collective-permute-done((bf16[384,1024]{1,0:T(8,128)(2,1)}, bf16[384,1024]{1,0:T(8,128)(2,1)}, u32[]{:S(2)}, u32[]{:S(2)}) %collective-permute-start.6) | collective-permute-done | bytes 786464 | tf_op jit(solution)/shard_map/ppermute | solution.py:333
  303.3 14.0 %attend.1 = bf16[384,512]{1,0:T(8,128)(2,1)S(1)} custom-call(s32[3]{0:T(128)S(1)} %pad_add_fusion.info_ref.refs_0_, f32[8,1,1536]{2,1,0:T(1,128)S(1)} %broadcast_in_dim.15.bias_ref, bf16[384,512]{1,0:T(8,128)(2,1)S(1)} %slice.287.query_ref, bf16[768,1024]{1,0:T(8,128)(2,1)S(1)} %pad_maximum_fusion.3.key_ref.value_ref, ...), custom_call_target="tpu_custom_call" | custom-call | tf_op jit(solution)/shard_map/attend/pallas_call | solution.py:142
  318.8 2.0 collective-permute-done.8
  328.4 4.7 collective-permute-start.10
  334.5 4.2 conv.1
  340.7 2.0 fusion.136
  348.8 10.2 %all-gather.11.cloned.1.call-done = bf16[4096,1024]{1,0:T(8,128)(2,1)} async-done(((bf16[256,1024]{1,0:T(8,128)(2,1)}), bf16[4096,1024]{1,0:T(8,128)(2,1)}) %all-gather.11.cloned.1.call-update) | async-done | bytes 8388624 | tf_op jit(solution)/shard_map/all_gather | solution.py:518
  359.1 4.0 fusion.123
  363.1 3.1 fusion.59
  370.3 2.0 collective-permute-done.15
  376.1 6.1 reshape.647
  382.3 5.7 multiply_convert_fusion.1
  390.4 3.6 convolution_convert_fusion
  394.0 3.5 convolution_convert_fusion.1
  416.1 4.5 collective-permute-start.20
  423.0 34.6 %collective-permute-done.21.refs_6_ = bf16[16,512]{1,0:T(8,128)(2,1)S(1)} collective-permute-done((bf16[16,512]{1,0:T(8,128)(2,1)S(1)}, bf16[16,512]{1,0:T(8,128)(2,1)S(1)}, u32[]{:S(2)}, u32[]{:S(2)}) %collective-permute-start.21) | collective-permute-done | bytes 16416 | tf_op jit(solution)/shard_map/ppermute | solution.py:462
  457.7 7.5 conv_back.1
  487.0 25.6 %attend_back.1 = (bf16[384,512]{1,0:T(8,128)(2,1)S(1)}, f32[768,512]{1,0:T(8,128)S(1)}, f32[768,512]{1,0:T(8,128)}, f32[8,1,1536]{2,1,0:T(1,128)S(1)}) custom-call(s32[3]{0:T(128)S(1)} %pad_add_fusion.info_ref.refs_0_, f32[8,1,1536]{2,1,0:T(1,128)S(1)} %broadcast_in_dim.15.bias_ref, bf16[384,512]{1,0:T(8,128)(2,1)S(1)} %slice.287.query_ref, ...), custom_call_target="tpu_custom_call" | custom-call | tf_op jit(solution)/shard_map/attend_back/pallas_call | solution.py:160
  520.9 4.0 fusion
  524.9 10.7 %collective-permute-done.24 = bf16[384,1024]{1,0:T(8,128)(2,1)S(1)} collective-permute-done((bf16[384,1024]{1,0:T(8,128)(2,1)S(1)}, bf16[384,1024]{1,0:T(8,128)(2,1)S(1)}, u32[]{:S(2)}, u32[]{:S(2)}) %collective-permute-start.24) | collective-permute-done | bytes 786464 | tf_op jit(solution)/shard_map/ppermute | solution.py:333
  536.8 3.5 convolution_convert_fusion.4
  540.4 5.9 reshape_reshape.9
  546.2 2.2 constant_dynamic-slice_fusion.11
  560.1 8.8 %collective-permute-done.38 = bf16[4,2,32,1024]{3,2,1,0:T(8,128)(2,1)} collective-permute-done((bf16[4,2,32,1024]{3,2,1,0:T(8,128)(2,1)}, bf16[4,2,32,1024]{3,2,1,0:T(8,128)(2,1)}, u32[]{:S(2)}, u32[]{:S(2)}) %collective-permute-start.38) | collective-permute-done | bytes 524320 | tf_op jit(solution)/shard_map/ppermute | solution.py:333
  571.5 16.0 %collective-permute-done.35 = bf16[4,2,96,1024]{3,2,0,1:T(8,128)(2,1)} collective-permute-done((bf16[4,2,96,1024]{3,2,0,1:T(8,128)(2,1)}, bf16[4,2,96,1024]{3,2,0,1:T(8,128)(2,1)}, u32[]{:S(2)}, u32[]{:S(2)}) %collective-permute-start.35) | collective-permute-done | bytes 1572896 | tf_op jit(solution)/shard_map/ppermute | solution.py:333
  587.4 2.2 fusion.4
  592.6 21.1 %collective-permute-done.39 = bf16[4,32,1024]{2,1,0:T(8,128)(2,1)S(1)} collective-permute-done((bf16[4,32,1024]{2,1,0:T(8,128)(2,1)S(1)}, bf16[4,32,1024]{2,1,0:T(8,128)(2,1)S(1)}, u32[]{:S(2)}, u32[]{:S(2)}) %collective-permute-start.39) | collective-permute-done | bytes 262176 | tf_op jit(solution)/shard_map/ppermute | solution.py:333
  616.1 2.6 fusion.1
  621.8 2.9 multiply_convert_fusion.4
  626.4 17.1 %collective-permute-done.47 = bf16[4,128,1024]{2,1,0:T(8,128)(2,1)} collective-permute-done((bf16[4,128,1024]{2,1,0:T(8,128)(2,1)}, bf16[4,128,1024]{2,1,0:T(8,128)(2,1)}, u32[]{:S(2)}, u32[]{:S(2)}) %collective-permute-start.47) | collective-permute-done | bytes 1048608 | tf_op jit(solution)/shard_map/ppermute | solution.py:333
  646.9 5.6 multiply_convert_fusion
  654.4 3.7 convolution_convert_fusion.2
  660.9 2.4 convolution_convert_fusion.3
  671.3 37.4 %collective-permute-done.30 = bf16[4,2,128,1024]{3,2,0,1:T(8,128)(2,1)} collective-permute-done((bf16[4,2,128,1024]{3,2,0,1:T(8,128)(2,1)}, bf16[4,2,128,1024]{3,2,0,1:T(8,128)(2,1)}, u32[]{:S(2)}, u32[]{:S(2)}) %collective-permute-start.30) | collective-permute-done | bytes 2097184 | tf_op jit(solution)/shard_map/ppermute | solution.py:333
  708.6 2.6 fusion.2
  712.0 3.4 collective-permute-done.28
  715.4 2.8 fusion.3
  720.5 21.9 %collective-permute-done.34 = f32[4,1216]{1,0:T(4,128)S(1)} collective-permute-done((f32[4,1216]{1,0:T(4,128)S(1)}, f32[4,1216]{1,0:T(4,128)S(1)}, u32[]{:S(2)}, u32[]{:S(2)}) %collective-permute-start.34) | collective-permute-done | bytes 19488 | tf_op jit(solution)/shard_map/ppermute | solution.py:333
  751.4 2.1 reshape.634
  759.4 30.3 %reduce-scatter.5.cloned.1.call-done = bf16[1,272,1024]{2,1,0:T(8,128)(2,1)} async-done(((bf16[4,272,1024]{2,1,0:T(8,128)(2,1)}), bf16[1,272,1024]{2,1,0:T(8,128)(2,1)}) %reduce-scatter.5.cloned.1.call-update) | async-done | bytes 557072 | tf_op jit(solution)/shard_map/reduce_scatter | solution.py:592
  (568 shorter events, 174.9 us)
Async XLA Ops:
  7.2 123.6 %all-gather.7.cloned.1.call-start = ((), (), s32[]{:S(2)}) async-start(), calls=%async_computation.8 | async-start | bytes 8355840 | tf_op jit(solution)/shard_map/all_gather | solution.py:525
  9.5 8.9 %collective-permute-start.2 = (bf16[1,1216]{1,0:T(2,128)(2,1)S(1)}, bf16[1,1216]{1,0:T(2,128)(2,1)S(1)}, u32[]{:S(2)}, u32[]{:S(2)}) collective-permute-start(bf16[1,1216]{1,0:T(2,128)(2,1)S(1)} %broadcast_in_dim.14), channel_id=1, source_target_pairs={{0,1},{1,0},{2,3},{3,2},{4,5},{5,4},{6,7},{7,6},{8,9},{9,8},{10,11... | collective-permute-start | bytes 7304 | tf_op jit(solution)/shard_map/ppermute | solution.py:333
  12.4 6.2 collective-permute-start
  20.0 225.2 %all-gather.9.cloned.1.call-start = ((), (), s32[]{:S(2)}) async-start(), calls=%async_computation.9 | async-start | bytes 8912896 | tf_op jit(solution)/shard_map/all_gather | solution.py:518
  21.2 337.9 %all-gather.11.cloned.1.call-start = ((), (), s32[]{:S(2)}) async-start(), calls=%async_computation.10 | async-start | bytes 8912896 | tf_op jit(solution)/shard_map/all_gather | solution.py:518
  22.2 725.2 %reduce-scatter.9.cloned.1.call-start = ((), (), s32[]{:S(2)}) async-start(), calls=%async_computation.6 | async-start | bytes 983040 | tf_op jit(solution)/shard_map/reduce_scatter | solution.py:592
  132.9 116.7 %collective-permute-start.3 = (bf16[192,1024]{1,0:T(8,128)(2,1)S(1)}, bf16[192,1024]{1,0:T(8,128)(2,1)S(1)}, u32[]{:S(2)}, u32[]{:S(2)}) collective-permute-start(bf16[192,1024]{1,0:T(8,128)(2,1)S(1)} %fusion.24), channel_id=1, source_target_pairs={{0,1},{1,0},{2,3},{3,2},{4,5},{5,4},{6,7},{7,6},{8,9},{9,8},{10,11... | collective-permute-start | bytes 1179656 | tf_op jit(solution)/shard_map/ppermute | solution.py:333
  255.1 6.0 collective-permute-start.4
  262.8 10.1 %collective-permute-start.5 = (bf16[192,1024]{1,0:T(8,128)(2,1)S(1)}, bf16[192,1024]{1,0:T(8,128)(2,1)S(1)}, u32[]{:S(2)}, u32[]{:S(2)}) collective-permute-start(bf16[192,1024]{1,0:T(8,128)(2,1)S(1)} %multiply_convert_fusion.14), channel_id=1, source_target_pairs={{0,1},{1,0},{2,3},{3,2},{4,5},{5,4},{6,7},{7,6},{8,9},{9,8},{10,11... | collective-permute-start | bytes 1179656 | tf_op jit(solution)/shard_map/ppermute | solution.py:333
  266.9 14.3 %collective-permute-start.7 = (bf16[8,32,1024]{2,1,0:T(8,128)(2,1)}, bf16[8,32,1024]{2,1,0:T(8,128)(2,1)}, u32[]{:S(2)}, u32[]{:S(2)}) collective-permute-start(bf16[8,32,1024]{2,1,0:T(8,128)(2,1)} %dynamic-slice_bitcast_fusion.8), channel_id=1, source_target_pairs={{0,1},{1,0},{2,3},{3,2},{4,5},{5,4},{6,7},{7,6},{8,9},{9,8},{10,11... | collective-permute-start | bytes 1572872 | tf_op jit(solution)/shard_map/ppermute | solution.py:333
  277.7 24.1 %collective-permute-start.6 = (bf16[384,1024]{1,0:T(8,128)(2,1)}, bf16[384,1024]{1,0:T(8,128)(2,1)}, u32[]{:S(2)}, u32[]{:S(2)}) collective-permute-start(bf16[384,1024]{1,0:T(8,128)(2,1)} %slice.288), channel_id=1, source_target_pairs={{0,2},{2,0},{1,3},{3,1},{4,6},{6,4},{5,7},{7,5},{8,10},{10,8},{9,1... | collective-permute-start | bytes 2359304 | tf_op jit(solution)/shard_map/ppermute | solution.py:333
  318.7 2.1 collective-permute-start.8
  327.0 6.8 collective-permute-start.11
  328.4 6.1 collective-permute-start.10
  348.6 14.4 %collective-permute-start.14 = (bf16[192,1024]{1,0:T(8,128)(2,1)S(1)}, bf16[192,1024]{1,0:T(8,128)(2,1)}, u32[]{:S(2)}, u32[]{:S(2)}) collective-permute-start(bf16[192,1024]{1,0:T(8,128)(2,1)S(1)} %multiply_convert_fusion.10), channel_id=1, source_target_pairs={{0,1},{1,0},{2,3},{3,2},{4,5},{5,4},{6,7},{7,6},{8,9},{9,8},{10,11... | collective-permute-start | bytes 1179656 | tf_op jit(solution)/shard_map/ppermute | solution.py:333
  376.0 6.3 collective-permute-start.16
  389.9 7.5 collective-permute-start.17
  400.3 9.5 %collective-permute-start.18 = (bf16[192,1024]{1,0:T(8,128)(2,1)}, bf16[192,1024]{1,0:T(8,128)(2,1)}, u32[]{:S(2)}, u32[]{:S(2)}) collective-permute-start(bf16[192,1024]{1,0:T(8,128)(2,1)} %get-tuple-element.97), channel_id=1, source_target_pairs={{0,1},{1,0},{2,3},{3,2},{4,5},{5,4},{6,7},{7,6},{8,9},{9,8},{10,11... | collective-permute-start | bytes 1179656 | tf_op jit(solution)/shard_map/ppermute | solution.py:333
  407.1 113.8 %collective-permute-start.48 = (bf16[4,2,128,1024]{3,2,0,1:T(8,128)(2,1)}, bf16[4,2,128,1024]{3,2,0,1:T(8,128)(2,1)}, u32[]{:S(2)}, u32[]{:S(2)}) collective-permute-start(bf16[4,2,128,1024]{3,2,0,1:T(8,128)(2,1)} %bitcast.319), channel_id=1, source_target_pairs={{0,4},{4,0},{1,5},{5,1},{2,6},{6,2},{3,7},{7,3},{8,12},{12,8},{9,1... | collective-permute-start | bytes 6291464 | tf_op jit(solution)/shard_map/ppermute | solution.py:333
  408.6 206.6 %collective-permute-start.46 = (bf16[4,2,128,1024]{3,2,0,1:T(8,128)(2,1)}, bf16[4,2,128,1024]{3,2,0,1:T(8,128)(2,1)}, u32[]{:S(2)}, u32[]{:S(2)}) collective-permute-start(bf16[4,2,128,1024]{3,2,0,1:T(8,128)(2,1)} %bitcast.320), channel_id=1, source_target_pairs={{0,2},{2,0},{1,3},{3,1},{4,6},{6,4},{5,7},{7,5},{8,10},{10,8},{9,1... | collective-permute-start | bytes 6291464 | tf_op jit(solution)/shard_map/ppermute | solution.py:333
  414.8 42.9 %collective-permute-start.21 = (bf16[16,512]{1,0:T(8,128)(2,1)S(1)}, bf16[16,512]{1,0:T(8,128)(2,1)S(1)}, u32[]{:S(2)}, u32[]{:S(2)}) collective-permute-start(bf16[16,512]{1,0:T(8,128)(2,1)S(1)} %get-tuple-element.156), channel_id=1, source_target_pairs={{2,0},{3,1},{6,4},{7,5},{10,8},{11,9},{14,12},{15,13},{18,16},{19,... | collective-permute-start | bytes 49160 | tf_op jit(solution)/shard_map/ppermute | solution.py:462
  416.1 41.6 %collective-permute-start.20 = (bf16[16,512]{1,0:T(8,128)(2,1)S(1)}, bf16[16,512]{1,0:T(8,128)(2,1)S(1)}, u32[]{:S(2)}, u32[]{:S(2)}) collective-permute-start(bf16[16,512]{1,0:T(8,128)(2,1)S(1)} %get-tuple-element.157), channel_id=1, source_target_pairs={{0,2},{1,3},{4,6},{5,7},{8,10},{9,11},{12,14},{13,15},{16,18},{17,... | collective-permute-start | bytes 49160 | tf_op jit(solution)/shard_map/ppermute | solution.py:461
  422.9 48.2 %collective-permute-start.43 = (bf16[4,2,32,1024]{3,2,0,1:T(8,128)(2,1)S(1)}, bf16[4,2,32,1024]{3,2,0,1:T(8,128)(2,1)S(1)}, u32[]{:S(2)}, u32[]{:S(2)}) collective-permute-start(bf16[4,2,32,1024]{3,2,0,1:T(8,128)(2,1)S(1)} %bitcast.378), channel_id=1, source_target_pairs={{0,2},{2,0},{1,3},{3,1},{4,6},{6,4},{5,7},{7,5},{8,10},{10,8},{9,1... | collective-permute-start | bytes 1572872 | tf_op jit(solution)/shard_map/ppermute | solution.py:333
  470.8 12.6 %collective-permute-start.23 = (bf16[192,1024]{1,0:T(8,128)(2,1)}, bf16[192,1024]{1,0:T(8,128)(2,1)}, u32[]{:S(2)}, u32[]{:S(2)}) collective-permute-start(bf16[192,1024]{1,0:T(8,128)(2,1)} %get-tuple-element.95), channel_id=1, source_target_pairs={{0,1},{1,0},{2,3},{3,2},{4,5},{5,4},{6,7},{7,6},{8,9},{9,8},{10,11... | collective-permute-start | bytes 1179656 | tf_op jit(solution)/shard_map/ppermute | solution.py:333
  472.0 10.3 %collective-permute-start.44 = (bf16[4,32,1024]{2,1,0:T(8,128)(2,1)}, bf16[4,32,1024]{2,1,0:T(8,128)(2,1)}, u32[]{:S(2)}, u32[]{:S(2)}) collective-permute-start(bf16[4,32,1024]{2,1,0:T(8,128)(2,1)} %dynamic-slice_bitcast_fusion.9), channel_id=1, source_target_pairs={{0,4},{4,0},{1,5},{5,1},{2,6},{6,2},{3,7},{7,3},{8,12},{12,8},{9,1... | collective-permute-start | bytes 786440 | tf_op jit(solution)/shard_map/ppermute | solution.py:333
  480.1 35.8 %collective-permute-start.41 = (bf16[4,2,64,1024]{3,2,0,1:T(8,128)(2,1)}, bf16[4,2,64,1024]{3,2,0,1:T(8,128)(2,1)}, u32[]{:S(2)}, u32[]{:S(2)}) collective-permute-start(bf16[4,2,64,1024]{3,2,0,1:T(8,128)(2,1)} %bitcast.324), channel_id=1, source_target_pairs={{0,4},{4,0},{1,5},{5,1},{2,6},{6,2},{3,7},{7,3},{8,12},{12,8},{9,1... | collective-permute-start | bytes 3145736 | tf_op jit(solution)/shard_map/ppermute | solution.py:333
  486.3 66.6 %collective-permute-start.37 = (bf16[8,32,1024]{2,1,0:T(8,128)(2,1)}, bf16[8,32,1024]{2,1,0:T(8,128)(2,1)}, u32[]{:S(2)}, u32[]{:S(2)}) collective-permute-start(bf16[8,32,1024]{2,1,0:T(8,128)(2,1)} %dynamic-slice_bitcast_fusion.7), channel_id=1, source_target_pairs={{0,1},{1,0},{2,3},{3,2},{4,5},{5,4},{6,7},{7,6},{8,9},{9,8},{10,11... | collective-permute-start | bytes 1572872 | tf_op jit(solution)/shard_map/ppermute | solution.py:333
  515.2 20.4 %collective-permute-start.24 = (bf16[384,1024]{1,0:T(8,128)(2,1)S(1)}, bf16[384,1024]{1,0:T(8,128)(2,1)S(1)}, u32[]{:S(2)}, u32[]{:S(2)}) collective-permute-start(bf16[384,1024]{1,0:T(8,128)(2,1)S(1)} %fusion.35), channel_id=1, source_target_pairs={{0,2},{2,0},{1,3},{3,1},{4,6},{6,4},{5,7},{7,5},{8,10},{10,8},{9,1... | collective-permute-start | bytes 2359304 | tf_op jit(solution)/shard_map/ppermute | solution.py:333
  519.9 36.8 %collective-permute-start.42 = (bf16[4,64,1024]{2,1,0:T(8,128)(2,1)}, bf16[4,64,1024]{2,1,0:T(8,128)(2,1)}, u32[]{:S(2)}, u32[]{:S(2)}) collective-permute-start(bf16[4,64,1024]{2,1,0:T(8,128)(2,1)} %dynamic-slice_bitcast_fusion.5), channel_id=1, source_target_pairs={{0,2},{2,0},{1,3},{3,1},{4,6},{6,4},{5,7},{7,5},{8,10},{10,8},{9,1... | collective-permute-start | bytes 1572872 | tf_op jit(solution)/shard_map/ppermute | solution.py:333
  549.8 37.6 %collective-permute-start.35 = (bf16[4,2,96,1024]{3,2,0,1:T(8,128)(2,1)}, bf16[4,2,96,1024]{3,2,0,1:T(8,128)(2,1)}, u32[]{:S(2)}, u32[]{:S(2)}) collective-permute-start(bf16[4,2,96,1024]{3,2,0,1:T(8,128)(2,1)} %bitcast.323), channel_id=1, source_target_pairs={{0,2},{2,0},{1,3},{3,1},{4,6},{6,4},{5,7},{7,5},{8,10},{10,8},{9,1... | collective-permute-start | bytes 4718600 | tf_op jit(solution)/shard_map/ppermute | solution.py:333
  551.7 73.0 %collective-permute-start.49 = (bf16[4,128,1024]{2,1,0:T(8,128)(2,1)}, bf16[4,128,1024]{2,1,0:T(8,128)(2,1)}, u32[]{:S(2)}, u32[]{:S(2)}) collective-permute-start(bf16[4,128,1024]{2,1,0:T(8,128)(2,1)} %dynamic-slice_bitcast_fusion), channel_id=1, source_target_pairs={{0,2},{2,0},{1,3},{3,1},{4,6},{6,4},{5,7},{7,5},{8,10},{10,8},{9,1... | collective-permute-start | bytes 3145736 | tf_op jit(solution)/shard_map/ppermute | solution.py:333
  555.9 12.9 %collective-permute-start.38 = (bf16[4,2,32,1024]{3,2,1,0:T(8,128)(2,1)}, bf16[4,2,32,1024]{3,2,1,0:T(8,128)(2,1)}, u32[]{:S(2)}, u32[]{:S(2)}) collective-permute-start(bf16[4,2,32,1024]{3,2,1,0:T(8,128)(2,1)} %dynamic-slice_bitcast_fusion.6), channel_id=1, source_target_pairs={{0,4},{4,0},{1,5},{5,1},{2,6},{6,2},{3,7},{7,3},{8,12},{12,8},{9,1... | collective-permute-start | bytes 1572872 | tf_op jit(solution)/shard_map/ppermute | solution.py:333
  560.1 193.4 %reduce-scatter.7.cloned.1.call-start = ((), (), s32[]{:S(2)}) async-start(), calls=%async_computation.5 | async-start | bytes 1310720 | tf_op jit(solution)/shard_map/reduce_scatter | solution.py:592
  570.3 43.4 %collective-permute-start.39 = (bf16[4,32,1024]{2,1,0:T(8,128)(2,1)S(1)}, bf16[4,32,1024]{2,1,0:T(8,128)(2,1)S(1)}, u32[]{:S(2)}, u32[]{:S(2)}) collective-permute-start(bf16[4,32,1024]{2,1,0:T(8,128)(2,1)S(1)} %dynamic-slice_bitcast_fusion.10), channel_id=1, source_target_pairs={{0,2},{2,0},{1,3},{3,1},{4,6},{6,4},{5,7},{7,5},{8,10},{10,8},{9,1... | collective-permute-start | bytes 786440 | tf_op jit(solution)/shard_map/ppermute | solution.py:333
  589.7 24.0 %collective-permute-start.36 = (bf16[4,96,1024]{2,1,0:T(8,128)(2,1)S(1)}, bf16[4,96,1024]{2,1,0:T(8,128)(2,1)S(1)}, u32[]{:S(2)}, u32[]{:S(2)}) collective-permute-start(bf16[4,96,1024]{2,1,0:T(8,128)(2,1)S(1)} %dynamic-slice_bitcast_fusion.4), channel_id=1, source_target_pairs={{0,4},{4,0},{1,5},{5,1},{2,6},{6,2},{3,7},{7,3},{8,12},{12,8},{9,1... | collective-permute-start | bytes 2359304 | tf_op jit(solution)/shard_map/ppermute | solution.py:333
  592.6 27.6 %collective-permute-start.25 = (bf16[192,1024]{1,0:T(8,128)(2,1)}, bf16[192,1024]{1,0:T(8,128)(2,1)S(1)}, u32[]{:S(2)}, u32[]{:S(2)}) collective-permute-start(bf16[192,1024]{1,0:T(8,128)(2,1)} %fusion.65), channel_id=1, source_target_pairs={{0,1},{1,0},{2,3},{3,2},{4,5},{5,4},{6,7},{7,6},{8,9},{9,8},{10,11... | collective-permute-start | bytes 1179656 | tf_op jit(solution)/shard_map/ppermute | solution.py:333
  615.2 143.1 %reduce-scatter.11.cloned.1.call-start = ((), (), s32[]{:S(2)}) async-start(), calls=%async_computation.7 | async-start | bytes 2621440 | tf_op jit(solution)/shard_map/reduce_scatter | solution.py:592
  619.7 23.8 %collective-permute-start.47 = (bf16[4,128,1024]{2,1,0:T(8,128)(2,1)}, bf16[4,128,1024]{2,1,0:T(8,128)(2,1)}, u32[]{:S(2)}, u32[]{:S(2)}) collective-permute-start(bf16[4,128,1024]{2,1,0:T(8,128)(2,1)} %dynamic-slice_bitcast_fusion.1), channel_id=1, source_target_pairs={{0,4},{4,0},{1,5},{5,1},{2,6},{6,2},{3,7},{7,3},{8,12},{12,8},{9,1... | collective-permute-start | bytes 3145736 | tf_op jit(solution)/shard_map/ppermute | solution.py:333
  624.6 22.3 %collective-permute-start.26 = (bf16[192,1024]{1,0:T(8,128)(2,1)}, bf16[192,1024]{1,0:T(8,128)(2,1)S(1)}, u32[]{:S(2)}, u32[]{:S(2)}) collective-permute-start(bf16[192,1024]{1,0:T(8,128)(2,1)} %get-tuple-element.93), channel_id=1, source_target_pairs={{0,1},{1,0},{2,3},{3,2},{4,5},{5,4},{6,7},{7,6},{8,9},{9,8},{10,11... | collective-permute-start | bytes 1179656 | tf_op jit(solution)/shard_map/ppermute | solution.py:333
  646.6 143.0 %reduce-scatter.5.cloned.1.call-start = ((), (), s32[]{:S(2)}) async-start(), calls=%async_computation.4 | async-start | bytes 2785280 | tf_op jit(solution)/shard_map/reduce_scatter | solution.py:592
  658.7 9.3 %collective-permute-start.27 = (bf16[192,1024]{1,0:T(8,128)(2,1)S(1)}, bf16[192,1024]{1,0:T(8,128)(2,1)S(1)}, u32[]{:S(2)}, u32[]{:S(2)}) collective-permute-start(bf16[192,1024]{1,0:T(8,128)(2,1)S(1)} %slice.395), channel_id=1, source_target_pairs={{0,1},{1,0},{2,3},{3,2},{4,5},{5,4},{6,7},{7,6},{8,9},{9,8},{10,11... | collective-permute-start | bytes 1179656 | tf_op jit(solution)/shard_map/ppermute | solution.py:333
  660.3 48.3 %collective-permute-start.30 = (bf16[4,2,128,1024]{3,2,0,1:T(8,128)(2,1)}, bf16[4,2,128,1024]{3,2,0,1:T(8,128)(2,1)}, u32[]{:S(2)}, u32[]{:S(2)}) collective-permute-start(bf16[4,2,128,1024]{3,2,0,1:T(8,128)(2,1)} %bitcast.321), channel_id=1, source_target_pairs={{0,4},{4,0},{1,5},{5,1},{2,6},{6,2},{3,7},{7,3},{8,12},{12,8},{9,1... | collective-permute-start | bytes 6291464 | tf_op jit(solution)/shard_map/ppermute | solution.py:333
  666.6 48.8 %collective-permute-start.28 = (bf16[4,2,128,1024]{3,2,0,1:T(8,128)(2,1)}, bf16[4,2,128,1024]{3,2,0,1:T(8,128)(2,1)}, u32[]{:S(2)}, u32[]{:S(2)}) collective-permute-start(bf16[4,2,128,1024]{3,2,0,1:T(8,128)(2,1)} %bitcast.322), channel_id=1, source_target_pairs={{0,2},{2,0},{1,3},{3,1},{4,6},{6,4},{5,7},{7,5},{8,10},{10,8},{9,1... | collective-permute-start | bytes 6291464 | tf_op jit(solution)/shard_map/ppermute | solution.py:333
  670.6 49.2 %collective-permute-start.33 = (f32[4,2,1216]{2,1,0:T(2,128)S(1)}, f32[4,2,1216]{2,1,0:T(2,128)S(1)}, u32[]{:S(2)}, u32[]{:S(2)}) collective-permute-start(f32[4,2,1216]{2,1,0:T(2,128)S(1)} %bitcast.387), channel_id=1, source_target_pairs={{0,2},{2,0},{1,3},{3,1},{4,6},{6,4},{5,7},{7,5},{8,10},{10,8},{9,1... | collective-permute-start | bytes 116744 | tf_op jit(solution)/shard_map/ppermute | solution.py:333
  711.3 31.3 %collective-permute-start.31 = (bf16[4,128,1024]{2,1,0:T(8,128)(2,1)S(1)}, bf16[4,128,1024]{2,1,0:T(8,128)(2,1)S(1)}, u32[]{:S(2)}, u32[]{:S(2)}) collective-permute-start(bf16[4,128,1024]{2,1,0:T(8,128)(2,1)S(1)} %dynamic-slice_bitcast_fusion.2), channel_id=1, source_target_pairs={{0,2},{2,0},{1,3},{3,1},{4,6},{6,4},{5,7},{7,5},{8,10},{10,8},{9,1... | collective-permute-start | bytes 3145736 | tf_op jit(solution)/shard_map/ppermute | solution.py:333
  718.3 24.8 %collective-permute-start.29 = (bf16[4,128,1024]{2,1,0:T(8,128)(2,1)S(1)}, bf16[4,128,1024]{2,1,0:T(8,128)(2,1)S(1)}, u32[]{:S(2)}, u32[]{:S(2)}) collective-permute-start(bf16[4,128,1024]{2,1,0:T(8,128)(2,1)S(1)} %dynamic-slice_bitcast_fusion.3), channel_id=1, source_target_pairs={{0,4},{4,0},{1,5},{5,1},{2,6},{6,2},{3,7},{7,3},{8,12},{12,8},{9,1... | collective-permute-start | bytes 3145736 | tf_op jit(solution)/shard_map/ppermute | solution.py:333
  719.9 22.6 %collective-permute-start.34 = (f32[4,1216]{1,0:T(4,128)S(1)}, f32[4,1216]{1,0:T(4,128)S(1)}, u32[]{:S(2)}, u32[]{:S(2)}) collective-permute-start(f32[4,1216]{1,0:T(4,128)S(1)} %bitcast.389), channel_id=1, source_target_pairs={{0,4},{4,0},{1,5},{5,1},{2,6},{6,2},{3,7},{7,3},{8,12},{12,8},{9,1... | collective-permute-start | bytes 58376 | tf_op jit(solution)/shard_map/ppermute | solution.py:333
  754.6 2.1 collective-permute-start.40
  (103 other events, 1194.2 us)
Sparse Core Ops, SparseCore 0:
  20.1 110.6 all-gather.6
  134.1 110.9 all-gather.8
  247.9 111.1 all-gather.10
  560.2 21.5 reduce-scatter.8
  615.3 25.2 reduce-scatter.6
  646.8 42.0 reduce-scatter.10
  745.1 44.4 reduce-scatter.4

commit v2 on v1

--- a/solution.py
+++ b/solution.py
@@ -359,13 +359,41 @@
     return lax.all_gather(values, axis, axis=0, tiled=True)
 
 
-def reduce_axis(values, axis, dim):
+def pick(values, axis, dim):
+    return choose(values, 1 - lax.axis_index(axis), dim)
+
+
+def send(values, axis, dim, *ties):
     if lax.axis_size(axis) == 2:
-        place = lax.axis_index(axis)
-        received = swap(choose(values, 1 - place, dim), axis)
-        kept = choose(values, place, dim)
-        return (kept.astype(jnp.float32) + received.astype(jnp.float32)).astype(values.dtype)
+        return swap(after(pick(values, axis, dim), *ties), axis)
     return lax.psum_scatter(values, axis, scatter_dimension=dim, tiled=False)
+
+
+def add(values, received, axis, dim):
+    if lax.axis_size(axis) != 2:
+        return received
+    kept = choose(values, lax.axis_index(axis), dim)
+    return (kept.astype(jnp.float32) + received.astype(jnp.float32)).astype(values.dtype)
+
+
+def after(values, *tokens):
+    if not tokens:
+        return values
+    return lax.optimization_barrier((values,) + tokens)[0]
+
+
+def together(*values):
+    return lax.optimization_barrier(values)
+
+
+def placed(parts):
+    own, across, both, along = parts
+    q, y = lax.axis_index("q"), lax.axis_index("y")
+    result = jnp.zeros((own.shape[0], 2, 2) + own.shape[1:], own.dtype)
+    for part, at_q, at_y in ((own, q, y), (across, 1 - q, y), (both, 1 - q, 1 - y), (along, q, 1 - y)):
+        at = (0, at_q, at_y) + (0,) * (own.ndim - 1)
+        result = lax.dynamic_update_slice(result, part[:, None, None], at)
+    return result
 
 
 def normalize(values):
@@ -431,14 +459,19 @@
     rows = upstream.shape[0]
     half = low(0.5 * upstream)
     half_both = jnp.concatenate([half, swap(half)], axis=0)
-    outer_grad = low(left_product(activated, half_both))
     active_grad = right_product(half_both, outer)
     middle_grad = low(active_grad * silu_slope(middle))
-    inner_grad = low(left_product(middle_grad, both))
     partial = product(middle_grad, inner)
     received = swap(low(partial[rows:]))
     entry_grad = partial[:rows] + received.astype(jnp.float32)
     back, gain_grad = norm_back(entry_grad, normed, inverse, gain)
+
+    def inner_grad(low_row, high_row):
+        return left_product(middle_grad[:, low_row:high_row], both)
+
+    def outer_grad(low_row, high_row):
+        return left_product(activated[:, low_row:high_row], half_both)
+
     return (upstream + back, gain_grad, inner_grad, outer_grad)
 
 
@@ -499,6 +532,13 @@
     small_both = ordered(small[None], swap(small[None]), core).reshape(-1)
     small_both = jnp.pad(small_both, (0, small_rows * width - 2 * count)).reshape(small_rows, width)
 
+    def feed_pack(number, *more):
+        return jnp.concatenate([inner_weight[number].T, outer_weight[number], *more], axis=0)
+
+    pack_one = feed_pack(0, small_both)
+    pack_two = feed_pack(1)
+    attend_weight, glu_weight = together(attend_weight, glu_weight, pack_one)[:2]
+
     def own_columns(weight, shape, dim):
         parts = weight.reshape((share,) + shape)
         mine = choose(parts, core, dim).reshape(share, -1)
@@ -508,36 +548,50 @@
     attend_part = own_columns(attend_weight, (3, 2, half), 2)
     glu_part = own_columns(glu_weight, (2, chips, 2, share), 3)
     mixed_pack = jnp.concatenate(
-        [attend_part.reshape(-1, width), glu_part, merge_weight, point_weight, small_both], axis=0
-    )
-
-    def feed_pack(number):
-        return jnp.concatenate([inner_weight[number].T, outer_weight[number]], axis=0)
-
-    def feed_gather(number):
-        whole = lax.all_gather(feed_pack(number), CHIPS, axis=0)
-        return (
-            whole[:, :units].reshape(chips * units, width),
-            whole[:, units:].reshape(chips * units, width),
+        [attend_part.reshape(-1, width), glu_part, merge_weight, point_weight], axis=0
+    )
+
+    square = grid[1] == 2 and grid[2] == 2
+    marks = [0]
+    for size in (3 * share, 2 * share, share, share):
+        marks.append(marks[-1] + size)
+
+    def gather_p(values):
+        return lax.all_gather(values, "p", axis=0)
+
+    if square:
+        whole_one = gather_p(pack_one)
+        two_x, two_y = together(swap(pack_two, "q"), swap(pack_two, "y"))
+        pack_two = jnp.stack([pack_two, two_x, swap(two_x, "y"), two_y])
+        mixed = gather_p(after(mixed_pack, pack_one))
+        inner = whole_one[:, :units].reshape(-1, width)
+        outer = whole_one[:, units : 2 * units].reshape(-1, width)
+        tiny = whole_one[:, 2 * units :]
+        inner, outer, tiny, pack_two = together(inner, outer, tiny, pack_two)
+        whole_two = gather_p(after(pack_two, mixed)).reshape(chips, 2 * units, width)
+        tiny_x = swap(tiny, "q")
+        inner_x, inner_y, outer_x, outer_y, tiny_x = together(
+            swap(inner, "q"), swap(inner, "y"), swap(outer, "q"), swap(outer, "y"), tiny_x
         )
-
-    inner_one, outer_one = feed_gather(0)
-    mixed = lax.all_gather(mixed_pack, CHIPS, axis=0)
-    inner_two, outer_two = feed_gather(1)
-
-    marks = [0]
-    for size in (3 * share, 2 * share, share, share, small_rows):
-        marks.append(marks[-1] + size)
-    attend_full = mixed[:, marks[0] : marks[1]].reshape(width, 3 * half)
-    glu_full = mixed[:, marks[1] : marks[2]].reshape(width, width)
-    merge_half = mixed[:, marks[2] : marks[3]]
-    point_full = mixed[:, marks[3] : marks[4]].reshape(half, width)
-    small_full = mixed[:, marks[4] :].reshape(chips, -1)[:, : 2 * count].reshape(chips, 2, count)
-    sides = merge_half.reshape(2, chips // 2, share, width)
-    merge_full = ordered(
-        choose(sides, core, 0)[:, None], swap(choose(sides, 1 - core, 0))[:, None], core, 1
-    ).reshape(half, width)
-
+        inner_xy, outer_xy = swap(inner_x, "y"), swap(outer_y, "q")
+        small_full = placed((tiny, tiny_x, swap(tiny_x, "y"), swap(tiny, "y")))
+        small_full = small_full.reshape(chips, -1)
+        inner_xy, outer_xy, mixed = together(inner_xy, outer_xy, mixed)
+        inner_one = jnp.concatenate([inner, inner_x, inner_xy, inner_y], axis=0)
+        outer_one = jnp.concatenate([outer, outer_x, outer_xy, outer_y], axis=0)
+        attend_part = mixed[:, : marks[1]].reshape(grid[0], 2 * share, 3 * half)
+        rest_part = mixed[:, marks[1] :]
+        attend_part, rest_part = together(attend_part, rest_part)
+        attend_x, attend_y = swap(attend_part, "q"), swap(attend_part, "y")
+    else:
+        whole_one = lax.all_gather(pack_one, CHIPS, axis=0)
+        mixed = lax.all_gather(mixed_pack, CHIPS, axis=0)
+        whole_two = lax.all_gather(pack_two, CHIPS, axis=0)
+        inner_one = whole_one[:, :units].reshape(chips * units, width)
+        outer_one = whole_one[:, units : 2 * units].reshape(chips * units, width)
+        small_full = whole_one[:, 2 * units :].reshape(chips, -1)
+
+    small_full = small_full[:, : 2 * count].reshape(chips, 2, count)
     gain_size = norm_gains.size
     gains = small_full[..., :gain_size].reshape(chips, 2, 6, -1).astype(f32)
     gain_table = gains.transpose(2, 0, 1, 3).reshape(6, width)
@@ -555,12 +609,39 @@
 
     hidden = frames.astype(f32)
     first, first_kept = feed_forward(hidden, gain_table[0], inner_one, outer_one)
+    if square:
+        first, attend_x, attend_y = together(first, attend_x, attend_y)
+        rest_y = swap(rest_part, "y")
+        attend_full = placed((attend_part, attend_x, swap(attend_y, "q"), attend_y))
+    else:
+        attend_full = mixed[:, : marks[1]]
+    attend_full = attend_full.reshape(width, 3 * half)
     normed_att, inverse_att = normalize(first)
     att_entry = pair_rows(low(normed_att * gain_table[1]))
     triple = low(product(att_entry, attend_full))
     query = triple[:, :half]
-    both = gather_axis(triple[:, half:], "y")
+    key_value = triple[:, half:]
+    if square:
+        key_value, rest_part = together(key_value, rest_part)
+        rest_x = swap(rest_part, "q")
+    both = gather_axis(key_value, "y")
+    if square:
+        query, both, rest_x, rest_y = together(query, both, rest_x, rest_y)
+        rest_xy = swap(rest_x, "y")
     attended = attend(info, bias, query, both)
+    if square:
+        attended, rest_xy = together(attended, rest_xy)
+        rest = placed((rest_part, rest_x, rest_xy, rest_y)).reshape(chips, -1, width)
+    else:
+        rest = mixed[:, marks[1] :]
+    marks = [mark - marks[1] for mark in marks]
+    glu_full = rest[:, : marks[2]].reshape(width, width)
+    merge_half = rest[:, marks[2] : marks[3]]
+    point_full = rest[:, marks[3] : marks[4]].reshape(half, width)
+    sides = merge_half.reshape(2, chips // 2, share, width)
+    merge_full = ordered(
+        choose(sides, core, 0)[:, None], swap(choose(sides, 1 - core, 0))[:, None], core, 1
+    ).reshape(half, width)
     second = first + pair_sum(product(attended, merge_full))
     normed_conv, inverse_conv = normalize(second)
     conv_entry = pair_rows(low(normed_conv * gain_table[2]))
@@ -573,6 +654,8 @@
     activated = normed_mid * gain_mid
     swish = low(jax.nn.silu(activated))
     third = second + pair_sum(product(swish, point_full))
+    inner_two = whole_two[:, :units].reshape(chips * units, width)
+    outer_two = whole_two[:, units:].reshape(chips * units, width)
     fourth, fourth_kept = feed_forward(third, gain_table[4], inner_two, outer_two)
     normed_last, inverse_last = normalize(fourth)
     result = low(normed_last * gain_table[5])
@@ -580,27 +663,28 @@
     def by_chip(values):
         return values.reshape(grid + (values.shape[0] // chips, values.shape[1]))
 
-    def lane(values, order):
-        names = list(CHIPS)
-        for axis in order:
-            dim = names.index(axis)
-            values = reduce_axis(values, axis, dim)
-            names.pop(dim)
-        return values
-
-    def last_sum(parts):
-        return lax.psum_scatter(jnp.concatenate(parts, axis=1), "p", scatter_dimension=0, tiled=False)
+    def last_sum(values):
+        return lax.psum_scatter(values, "p", scatter_dimension=0, tiled=False)
+
+    size = grid[0] * units
+
+    def early_sum(grad):
+        values = low(grad(0, chips * units))
+        if square:
+            return last_sum(values.reshape(grid[0], 4, units, width))
+        return last_sum(values.reshape(grid + (units, width)))
 
     grad_fourth, gain_five = norm_back(
         cotangent.astype(f32), normed_last, inverse_last, gain_table[5]
     )
-    grad_third, gain_four, inner_grad, outer_grad = feed_back(
+    grad_third, gain_four, inner_two_grad, outer_two_grad = feed_back(
         grad_fourth, gain_table[4], inner_two, outer_two, fourth_kept
     )
-    feed_two = last_sum([lane(by_chip(inner_grad), "yq"), lane(by_chip(outer_grad), "qy")])
+
+    outer_two_sum = early_sum(outer_two_grad)
+    inner_two_sum = early_sum(inner_two_grad)
 
     conv_out_grad = pair_rows(low(grad_third))
-    point_grad = low(left_product(swish, conv_out_grad))
     swish_grad = right_product(conv_out_grad, point_full)
     act_grad = swish_grad * silu_slope(activated)
     mixed_grad, gain_three = split_norm_back(act_grad, normed_mid, inverse_mid, gain_mid)
@@ -615,39 +699,90 @@
             [glu_back * gate_sig, glu_back * value_part * gate_sig * (1.0 - gate_sig)], axis=1
         )
     )
-    glu_grad = low(left_product(conv_entry, gate_grad))
     conv_entry_grad = pair_sum(right_product(gate_grad, glu_full))
-    conv_sum = last_sum([lane(by_chip(glu_grad), "qy"), lane(by_chip(point_grad), "yq")])
+    point_grad = by_chip(low(left_product(swish, conv_out_grad)))
+    glu_grad = by_chip(low(left_product(conv_entry, gate_grad)))
     back_conv, gain_two = norm_back(conv_entry_grad, normed_conv, inverse_conv, gain_table[2])
     grad_second = grad_third + back_conv
 
     att_out_grad = pair_rows(low(grad_second))
+    glu_a = send(glu_grad, "q", 1)
+    point_a = send(point_grad, "y", 2)
     merge_grad = low(left_product(attended, att_out_grad)).reshape(chips // 2, 2, share, width)
     merge_grad = ordered(
         choose(merge_grad, core, 1)[None], swap(choose(merge_grad, 1 - core, 1))[None], core
-    ).reshape(chips * share, width)
+    )
+    merge_grad = by_chip(merge_grad.reshape(chips * share, width))
     attended_grad = low(right_product(att_out_grad, merge_full))
     query_grad, key_grad, value_grad, table_sums = attend_back(info, bias, query, both, attended_grad)
+    query_grad, key_grad, value_grad, glu_a, point_a = together(
+        query_grad, key_grad, value_grad, glu_a, point_a
+    )
     both_grad = jnp.concatenate([key_grad, value_grad], axis=1).reshape(grid[2], pair, width)
     if grid[2] == 2:
         place = lax.axis_index("y")
-        received = swap(low(choose(both_grad, 1 - place, 0)), "y")
-        both_grad = low(choose(both_grad, place, 0) + received.astype(f32))
+        both_received = swap(low(choose(both_grad, 1 - place, 0)), "y")
+        both_grad = low(choose(both_grad, place, 0) + both_received.astype(f32))
     else:
-        both_grad = low(lax.psum_scatter(both_grad, "y", scatter_dimension=0, tiled=False))
+        both_received = low(lax.psum_scatter(both_grad, "y", scatter_dimension=0, tiled=False))
+        both_grad = both_received
     triple_grad = jnp.concatenate([query_grad, both_grad], axis=1)
     attend_grad = low(left_product(att_entry, triple_grad))
+    attend_grad = attend_grad.reshape(grid + (2 * share, 3 * half))
     att_entry_grad = pair_sum(right_product(triple_grad, attend_full))
-    attend_sum = last_sum(
-        [
-            lane(by_chip(attend_grad).reshape(grid + (3 * share, width)), "yq"),
-            lane(by_chip(merge_grad), "qy"),
-        ]
-    )
     back_att, gain_one = norm_back(att_entry_grad, normed_att, inverse_att, gain_table[1])
     grad_first = grad_second + back_att
-    input_grad, gain_zero, inner_grad, outer_grad = feed_back(
+    glu_half = add(glu_grad, glu_a, "q", 1)
+    point_half = add(point_grad, point_a, "y", 2)
+    glu_b = send(glu_half, "y", 1, both_received)
+    point_b = send(point_half, "q", 1, both_received)
+    merge_a = send(merge_grad, "y", 2, both_received)
+    attend_a = send(attend_grad, "q", 1)
+    if square:
+        grad_first, glu_b, point_b, merge_a = together(grad_first, glu_b, point_b, merge_a)
+    input_grad, gain_zero, inner_one_grad, outer_one_grad = feed_back(
         grad_first, gain_table[0], inner_one, outer_one, first_kept
+    )
+    conv_sum = jnp.concatenate([add(glu_half, glu_b, "y", 1), add(point_half, point_b, "q", 1)], axis=1)
+    merge_half = add(merge_grad, merge_a, "y", 2)
+    merge_b = send(merge_half, "q", 1)
+    if square:
+        outer_one_a = swap(low(outer_one_grad(2 * size, 4 * size)), "y")
+        inner_one_a = swap(low(inner_one_grad(size, 3 * size)), "q")
+        two_sum = jnp.concatenate([inner_two_sum, outer_two_sum], axis=1)
+        two_sum, input_grad = together(two_sum, input_grad)
+        two_a = swap(two_sum[2:], "y")
+        outer_one_a, inner_one_a, two_a, attend_a, merge_b = together(
+            outer_one_a, inner_one_a, two_a, attend_a, merge_b
+        )
+    attend_half = add(attend_grad, attend_a, "q", 1)
+    if square:
+        last = together(
+            low(outer_one_grad(size, 2 * size) + outer_one_a[:size].astype(f32)),
+            low(inner_one_grad(3 * size, 4 * size) + inner_one_a[size:].astype(f32)),
+            pick(attend_half, "y", 1),
+            low(two_sum[1].astype(f32) + two_a[0].astype(f32)),
+        )
+        outer_one_b, inner_one_b, attend_b, two_b = [
+            swap(part, axis) for part, axis in zip(last, "qyyq")
+        ]
+        two_sum = low(two_sum[0].astype(f32) + two_a[1].astype(f32) + two_b.astype(f32))
+        inner_sum_two, outer_sum_two = two_sum[:units], two_sum[units:]
+        outer_sum_one = outer_one_grad(0, size) + outer_one_a[size:].astype(f32)
+        inner_sum_one = inner_one_grad(0, size) + inner_one_a[:size].astype(f32)
+        outer_sum_one = low(outer_sum_one + outer_one_b.astype(f32)).reshape(grid[0], units, width)
+        inner_sum_one = low(inner_sum_one + inner_one_b.astype(f32)).reshape(grid[0], units, width)
+    else:
+        attend_b = send(attend_half, "y", 1)
+        inner_sum_one = by_chip(low(inner_one_grad(0, chips * units)))
+        outer_sum_one = by_chip(low(outer_one_grad(0, chips * units)))
+        inner_sum_one = send(send(inner_sum_one, "y", 2), "q", 1)
+        outer_sum_one = send(send(outer_sum_one, "y", 2), "q", 1)
+        inner_sum_two = send(send(inner_two_sum, "y", 1), "q", 0)
+        outer_sum_two = send(send(outer_two_sum, "y", 1), "q", 0)
+    attend_sum = add(attend_half, attend_b, "y", 1).reshape(grid[0], 3 * share, width)
+    mixed_sum = last_sum(
+        jnp.concatenate([attend_sum, conv_sum, add(merge_half, merge_b, "q", 1)], axis=1)
     )
 
     table_grad = jnp.einsum(
@@ -673,14 +808,14 @@
         axis=2,
     )
     small_sum = choose(small_grads, core, 1) + swap(choose(small_grads, 1 - core, 1))
-    small_sum = lane(small_sum.reshape(grid + (count,)), "yq")
+    small_sum = small_sum.reshape(grid + (count,))
+    small_sum = add(small_sum, send(small_sum, "y", 2), "y", 2)
+    small_sum = add(small_sum, send(small_sum, "q", 1), "q", 1)
     one_rows = -(-count // (16 * width)) * 16
     small_sum = jnp.pad(low(small_sum), ((0, 0), (0, one_rows * width - count)))
     small_sum = small_sum.reshape(grid[0], one_rows, width)
 
-    feed_one = last_sum(
-        [lane(by_chip(inner_grad), "yq"), lane(by_chip(outer_grad), "qy"), small_sum]
-    )
+    one_sum = last_sum(jnp.concatenate([inner_sum_one, outer_sum_one, small_sum], axis=1))
 
     def whole_columns(values, shape, dim):
         parts = values.reshape(2, share, -1)
@@ -694,13 +829,13 @@
         )
         return joined.reshape(share, -1).astype(f32)
 
-    attend_out = whole_columns(attend_sum[: 3 * share].reshape(2 * share, -1), (3, half), 2)
-    merge_out = attend_sum[3 * share :].astype(f32)
-    glu_out = whole_columns(conv_sum[: 2 * share], (2, chips, share), 3)
-    point_out = conv_sum[2 * share :].astype(f32)
-    inner_out = jnp.stack([feed_one[:units].T, feed_two[:units].T]).astype(f32)
-    outer_out = jnp.stack([feed_one[units : 2 * units], feed_two[units:]]).astype(f32)
-    small_out = feed_one[2 * units :].reshape(-1)[:count].astype(f32)
+    attend_out = whole_columns(mixed_sum[: 3 * share].reshape(2 * share, -1), (3, half), 2)
+    glu_out = whole_columns(mixed_sum[3 * share : 5 * share], (2, chips, share), 3)
+    point_out = mixed_sum[5 * share : 6 * share].astype(f32)
+    merge_out = mixed_sum[6 * share :].astype(f32)
+    inner_out = jnp.stack([one_sum[:units].T, inner_sum_two.T]).astype(f32)
+    outer_out = jnp.stack([one_sum[units : 2 * units], outer_sum_two]).astype(f32)
+    small_out = one_sum[2 * units :].reshape(-1)[:count].astype(f32)
     gains_out = small_out[:gain_size].reshape(norm_gains.shape)
     position_out = small_out[gain_size : gain_size + position_bias.size]
     depth_out = small_out[gain_size + position_bias.size :].reshape(taps, share)

time: 812 us -> 687 us (0.85)
  waiting for transfers between devices: 461 us -> 352 us
  local copies, waits for them, and re-layouts: 113 us -> 82 us
  starting transfers between devices: 34.5 us -> 56.8 us
  other arithmetic: 68.3 us -> 47.1 us
  matrix products: 56.2 us -> 70.7 us
    all_gather x3, waiting for transfers between devices: 231 us -> 46.1 us  [gather_p(): return lax.all_gather(values, 'p', axis=0)]
    ppermute x46 -> x62, waiting for transfers between devices: 165 us -> 275 us  [swap(): return lax.ppermute(values, axis, CORES)]
    ppermute x2, waiting for transfers between devices: 34.6 us -> 0.01 us  [halos(): lax.ppermute(values[:EDGE], 'y', backward)]
    ppermute x46 -> x62, starting transfers between devices: 22.1 us -> 43.9 us  [swap(): return lax.ppermute(values, axis, CORES)]
    convert_element_type x21 -> x12, other arithmetic: 28.4 us -> 9.79 us  [the longest x8 7.08 us: add(): (kept.astype(jnp.float32) + received.astype(jnp.float32)).astype(values.d...]
    dynamic_slice x23 -> x13, local copies, waits for them, and re-layouts: 23.7 us -> 5.45 us  [choose(): return lax.dynamic_index_in_dim(values, place, dim, keepdims=False)]
    dot_general x8 -> x12, matrix products: 19.4 us -> 33.5 us  [left_product(): jnp.einsum('nd,nf->df', left_in, right_in, preferred_element_type=jnp.flo...]
    reshape x4, local copies, waits for them, and re-layouts: 12.2 us -> 2.23 us  [the longest x1 1.57 us: on_device(): add(attend_half, attend_b, 'y', 1).reshape(grid[0], 3 * share, width)]
  transfers between devices with their start and end apart: 57 -> 73, of which waited for: 23 -> 39; matrix products, arithmetic and copies ran while one was open for 24% -> 22% of each run, Pallas kernels for 6% -> 8%
where the time goes in v2:
time: 687 us; the launch traced here: 679 us
  waiting for transfers between devices  352 us (51%)
  local copies, waits for them, and re-layouts  82 us (12%)
  matrix products  70.7 us (10%)
  starting transfers between devices  56.8 us (8%)
  Pallas kernels  51.7 us (8%)
  other arithmetic  47.1 us (7%)
  between operations  18.4 us (3%)
    ppermute x62, waiting for transfers between devices, swap(): return lax.ppermute(values, axis, CORES)  275 us
    all_gather x3, waiting for transfers between devices, gather_p(): return lax.all_gather(values, 'p', axis=0)  46.1 us
    ppermute x62, starting transfers between devices, swap(): return lax.ppermute(values, axis, CORES)  43.9 us
    dot_general x12, matrix products, left_product(): jnp.einsum('nd,nf->df', left_in, right_in, preferred_element_type=jnp.flo...  33.5 us
    reduce_scatter x4, waiting for transfers between devices, last_sum(): return lax.psum_scatter(values, 'p', scatter_dimension=0, tiled=False)  29.5 us
    pallas_call x1, Pallas kernels, attend_back(): pl.pallas_call(attend_back_kernel, grid=(heads,), in_specs=attend_specs(r...  25.5 us
    unnamed x210, local copies, waits for them, and re-layouts  24.3 us
    dot_general x8, matrix products, right_product(): jnp.einsum('nf,df->nd', left_in, right_in, preferred_element_type=jnp.flo...  21.4 us
  transfers between devices with their start and end apart: 73, of which 39 were waited for; matrix products, arithmetic and copies ran while one was open for 22% of the time, Pallas kernels for 8%

profile of v2, /device:TPU:0, one launch (start us, length us, event | category | flops | bytes accessed | tf_op | source)
XLA Modules:
  0.0 679.0 jit_solution(15731732400857787966)
XLA Ops:
  15.5 3.5 dynamic-slice_reduce_fusion
  22.1 2.9 collective-permute-start.1
  26.5 10.7 %collective-permute-done.1 = bf16[256,1024]{1,0:T(8,128)(2,1)S(1)} collective-permute-done((bf16[256,1024]{1,0:T(8,128)(2,1)S(1)}, bf16[256,1024]{1,0:T(8,128)(2,1)S(1)}, u32[]{:S(2)}, u32[]{:S(2)}) %collective-permute-start.1) | collective-permute-done | bytes 524320 | tf_op jit(solution)/shard_map/ppermute | solution.py:333
  40.2 11.4 %collective-permute-done.3 = bf16[256,1024]{1,0:T(8,128)(2,1)S(1)} collective-permute-done((bf16[256,1024]{1,0:T(8,128)(2,1)S(1)}, bf16[256,1024]{1,0:T(8,128)(2,1)S(1)}, u32[]{:S(2)}, u32[]{:S(2)}) %collective-permute-start.3) | collective-permute-done | bytes 524320 | tf_op jit(solution)/shard_map/ppermute | solution.py:333
  53.3 11.0 %all-gather.7.cloned.1.call-done = bf16[1088,1024]{1,0:T(8,128)(2,1)} async-done(((bf16[272,1024]{1,0:T(8,128)(2,1)}), bf16[1088,1024]{1,0:T(8,128)(2,1)}) %all-gather.7.cloned.1.call-update) | async-done | bytes 2228240 | tf_op jit(solution)/shard_map/all_gather | solution.py:560
  71.7 35.0 %all-gather.9.cloned.1.call-done = bf16[896,1024]{1,0:T(8,128)(2,1)} async-done(((bf16[224,1024]{1,0:T(8,128)(2,1)}), bf16[896,1024]{1,0:T(8,128)(2,1)}) %all-gather.9.cloned.1.call-update) | async-done | bytes 1835024 | tf_op jit(solution)/shard_map/all_gather | solution.py:560
  108.8 9.7 %collective-permute-done.8 = bf16[4,16,1024]{2,1,0:T(8,128)(2,1)S(1)} collective-permute-done((bf16[4,16,1024]{2,1,0:T(8,128)(2,1)S(1)}, bf16[4,16,1024]{2,1,0:T(8,128)(2,1)S(1)}, u32[]{:S(2)}, u32[]{:S(2)}) %collective-permute-start.8) | collective-permute-done | bytes 131104 | tf_op jit(solution)/shard_map/ppermute | solution.py:333
  130.9 17.1 %collective-permute-done.12 = bf16[512,1024]{1,0:T(8,128)(2,1)} collective-permute-done((bf16[512,1024]{1,0:T(8,128)(2,1)}, bf16[512,1024]{1,0:T(8,128)(2,1)}, u32[]{:S(2)}, u32[]{:S(2)}) %collective-permute-start.12) | collective-permute-done | bytes 1048608 | tf_op jit(solution)/shard_map/ppermute | solution.py:333
  151.7 2.3 constant_dynamic-update-slice_fusion.8
  154.0 2.3 constant_dynamic-update-slice_fusion.7
  156.3 2.3 constant_dynamic-update-slice_fusion.4
  158.6 2.3 constant_dynamic-update-slice_fusion.3
  160.9 6.3 multiply_convert_fusion.3
  174.6 17.1 %collective-permute-done.20 = bf16[4,64,1536]{2,1,0:T(8,128)(2,1)S(1)} collective-permute-done((bf16[4,64,1536]{2,1,0:T(8,128)(2,1)S(1)}, bf16[4,64,1536]{2,1,0:T(8,128)(2,1)S(1)}, u32[]{:S(2)}, u32[]{:S(2)}) %collective-permute-start.20) | collective-permute-done | bytes 786464 | tf_op jit(solution)/shard_map/ppermute | solution.py:333
  193.6 3.3 convolution_convert_fusion.3
  201.6 16.0 %collective-permute-done.21 = bf16[384,1024]{1,0:T(8,128)(2,1)} collective-permute-done((bf16[384,1024]{1,0:T(8,128)(2,1)S(1)}, bf16[384,1024]{1,0:T(8,128)(2,1)}, u32[]{:S(2)}, u32[]{:S(2)}) %collective-permute-start.21) | collective-permute-done | bytes 786464 | tf_op jit(solution)/shard_map/ppermute | solution.py:333
  219.0 19.9 %collective-permute-done.23 = bf16[4,128,1024]{2,1,0:T(8,128)(2,1)} collective-permute-done((bf16[4,128,1024]{2,1,0:T(8,128)(2,1)}, bf16[4,128,1024]{2,1,0:T(8,128)(2,1)}, u32[]{:S(2)}, u32[]{:S(2)}) %collective-permute-start.23) | collective-permute-done | bytes 1048608 | tf_op jit(solution)/shard_map/ppermute | solution.py:333
  244.6 14.0 %attend.1 = bf16[384,512]{1,0:T(8,128)(2,1)S(1)} custom-call(s32[3]{0:T(128)S(1)} %pad_add_fusion.info_ref.refs_0_, f32[8,1,1536]{2,1,0:T(1,128)S(1)} %broadcast_in_dim.50.bias_ref, bf16[384,512]{1,0:T(8,128)(2,1)S(1)} %slice.345.query_ref, bf16[768,1024]{1,0:T(8,128)(2,1)S(1)} %pad_maximum_fusion.5.key_ref.value_ref, ...), custom_call_target="tpu_custom_call" | custom-call | tf_op jit(solution)/shard_map/attend/pallas_call | solution.py:142
  259.9 3.3 collective-permute-done.24
  281.3 4.5 collective-permute-start.28
  287.3 4.7 conv.1
  302.3 4.0 fusion.118
  306.4 3.1 fusion.55
  320.2 4.5 convolution_convert_fusion
  324.9 5.7 multiply_convert_fusion.1
  342.3 4.5 collective-permute-start.38
  348.3 7.5 %conv_back.1 = (f32[384,512]{1,0:T(8,128)S(1)}, f32[31,512]{1,0:T(8,128)S(1)}) custom-call(s32[3]{0:T(128)S(1)} %pad_add_fusion.info_ref.refs_0_, bf16[16,512]{1,0:T(8,128)(2,1)S(1)} %collective-permute-done.28.refs_1_, bf16[384,512]{1,0:T(8,128)(2,1)S(1)} %multiply_convert_fusion.12.refs_2_, bf16[16,512]{1,0:T(8,128)(2,1)S(1)} %collective-permute-done.29.refs_3_, ...), custom_call_target="tpu_custom_call" | custom-call | tf_op jit(solution)/shard_map/conv_back/pallas_call | solution.py:291
  359.2 5.4 convolution_convert_fusion.1
  373.4 2.4 collective-permute-start.43
  377.7 25.5 %attend_back.1 = (bf16[384,512]{1,0:T(8,128)(2,1)S(1)}, f32[768,512]{1,0:T(8,128)S(1)}, f32[768,512]{1,0:T(8,128)}, f32[8,1,1536]{2,1,0:T(1,128)S(1)}) custom-call(s32[3]{0:T(128)S(1)} %pad_add_fusion.info_ref.refs_0_, f32[8,1,1536]{2,1,0:T(1,128)S(1)} %broadcast_in_dim.50.bias_ref, bf16[384,512]{1,0:T(8,128)(2,1)S(1)} %slice.345.query_ref, ...), custom_call_target="tpu_custom_call" | custom-call | tf_op jit(solution)/shard_map/attend_back/pallas_call | solution.py:160
  406.8 17.9 %collective-permute-done.44 = bf16[384,1024]{1,0:T(8,128)(2,1)S(1)} collective-permute-done((bf16[384,1024]{1,0:T(8,128)(2,1)S(1)}, bf16[384,1024]{1,0:T(8,128)(2,1)S(1)}, u32[]{:S(2)}, u32[]{:S(2)}) %collective-permute-start.44) | collective-permute-done | bytes 786464 | tf_op jit(solution)/shard_map/ppermute | solution.py:333
  432.3 4.4 collective-permute-done.47
  436.8 7.5 %collective-permute-done.46 = bf16[4,64,1024]{2,1,0:T(8,128)(2,1)S(1)} collective-permute-done((bf16[4,64,1024]{2,1,0:T(8,128)(2,1)S(1)}, bf16[4,64,1024]{2,1,0:T(8,128)(2,1)S(1)}, u32[]{:S(2)}, u32[]{:S(2)}) %collective-permute-start.46) | collective-permute-done | bytes 524320 | tf_op jit(solution)/shard_map/ppermute | solution.py:333
  444.3 10.5 %collective-permute-done.49 = bf16[4,2,32,1024]{3,2,1,0:T(8,128)(2,1)S(1)} collective-permute-done((bf16[4,2,32,1024]{3,2,1,0:T(8,128)(2,1)S(1)}, bf16[4,2,32,1024]{3,2,1,0:T(8,128)(2,1)S(1)}, u32[]{:S(2)}, u32[]{:S(2)}) %collective-permute-start.49) | collective-permute-done | bytes 524320 | tf_op jit(solution)/shard_map/ppermute | solution.py:333
  460.7 2.2 multiply_convert_fusion
  465.3 2.7 convolution_convert_fusion.5
  468.3 3.8 convolution_convert_fusion.4
  474.5 5.8 reduce-scatter.5.cloned.1.call-done
  489.4 56.3 %collective-permute-done.56 = bf16[4,32,1024]{2,1,0:T(8,128)(2,1)} collective-permute-done((bf16[4,32,1024]{2,1,0:T(8,128)(2,1)}, bf16[4,32,1024]{2,1,0:T(8,128)(2,1)}, u32[]{:S(2)}, u32[]{:S(2)}) %collective-permute-start.56) | collective-permute-done | bytes 262176 | tf_op jit(solution)/shard_map/ppermute | solution.py:333
  545.8 2.3 fusion
  550.2 3.4 add_convert_fusion.2
  553.6 3.2 add_convert_fusion.3
  560.5 15.5 %collective-permute-done.62 = bf16[4,64,1536]{2,1,0:T(8,128)(2,1)S(1)} collective-permute-done((bf16[4,64,1536]{2,1,0:T(8,128)(2,1)S(1)}, bf16[4,64,1536]{2,1,0:T(8,128)(2,1)S(1)}, u32[]{:S(2)}, u32[]{:S(2)}) %collective-permute-start.62) | collective-permute-done | bytes 786464 | tf_op jit(solution)/shard_map/ppermute | solution.py:333
  578.7 2.6 pad_maximum_fusion.4
  588.9 22.1 %collective-permute-done.61 = f32[4,1216]{1,0:T(4,128)S(1)} collective-permute-done((f32[4,1216]{1,0:T(4,128)S(1)}, f32[4,1216]{1,0:T(4,128)S(1)}, u32[]{:S(2)}, u32[]{:S(2)}) %collective-permute-start.61) | collective-permute-done | bytes 19488 | tf_op jit(solution)/shard_map/ppermute | solution.py:333
  611.2 2.5 add_convert_fusion.1
  619.2 12.0 %collective-permute-done.65 = bf16[256,1024]{1,0:T(8,128)(2,1)S(1)} collective-permute-done((bf16[256,1024]{1,0:T(8,128)(2,1)S(1)}, bf16[256,1024]{1,0:T(8,128)(2,1)S(1)}, u32[]{:S(2)}, u32[]{:S(2)}) %collective-permute-start.65) | collective-permute-done | bytes 524320 | tf_op jit(solution)/shard_map/ppermute | solution.py:333
  642.0 23.7 %reduce-scatter.9.cloned.1.call-done = bf16[1,272,1024]{2,1,0:T(8,128)(2,1)} async-done(((bf16[4,272,1024]{2,1,0:T(8,128)(2,1)}), bf16[1,272,1024]{2,1,0:T(8,128)(2,1)}) %reduce-scatter.9.cloned.1.call-update) | async-done | bytes 557072 | tf_op jit(solution)/shard_map/reduce_scatter | solution.py:667
  (609 shorter events, 199.8 us)
Async XLA Ops:
  7.2 57.1 %all-gather.7.cloned.1.call-start = ((), (), s32[]{:S(2)}) async-start(), calls=%async_computation.8 | async-start | bytes 2785280 | tf_op jit(solution)/shard_map/all_gather | solution.py:560
  13.4 93.3 %all-gather.9.cloned.1.call-start = ((), (), s32[]{:S(2)}) async-start(), calls=%async_computation.9 | async-start | bytes 2293760 | tf_op jit(solution)/shard_map/all_gather | solution.py:560
  21.8 280.5 %all-gather.11.cloned.1.call-start = ((), (), s32[]{:S(2)}) async-start(), calls=%async_computation.10 | async-start | bytes 10485760 | tf_op jit(solution)/shard_map/all_gather | solution.py:560
  22.1 15.2 %collective-permute-start.1 = (bf16[256,1024]{1,0:T(8,128)(2,1)S(1)}, bf16[256,1024]{1,0:T(8,128)(2,1)S(1)}, u32[]{:S(2)}, u32[]{:S(2)}) collective-permute-start(bf16[256,1024]{1,0:T(8,128)(2,1)S(1)} %get-tuple-element.269), channel_id=1, source_target_pairs={{0,4},{4,0},{1,5},{5,1},{2,6},{6,2},{3,7},{7,3},{8,12},{12,8},{9,1... | collective-permute-start | bytes 1572872 | tf_op jit(solution)/shard_map/ppermute | solution.py:333
  25.0 13.7 %collective-permute-start.2 = (bf16[256,1024]{1,0:T(8,128)(2,1)S(1)}, bf16[256,1024]{1,0:T(8,128)(2,1)S(1)}, u32[]{:S(2)}, u32[]{:S(2)}) collective-permute-start(bf16[256,1024]{1,0:T(8,128)(2,1)S(1)} %get-tuple-element.269), channel_id=1, source_target_pairs={{0,2},{2,0},{1,3},{3,1},{4,6},{6,4},{5,7},{7,5},{8,10},{10,8},{9,1... | collective-permute-start | bytes 1572872 | tf_op jit(solution)/shard_map/ppermute | solution.py:333
  38.7 12.9 %collective-permute-start.3 = (bf16[256,1024]{1,0:T(8,128)(2,1)S(1)}, bf16[256,1024]{1,0:T(8,128)(2,1)S(1)}, u32[]{:S(2)}, u32[]{:S(2)}) collective-permute-start(bf16[256,1024]{1,0:T(8,128)(2,1)S(1)} %collective-permute-done.1), channel_id=1, source_target_pairs={{0,2},{2,0},{1,3},{3,1},{4,6},{6,4},{5,7},{7,5},{8,10},{10,8},{9,1... | collective-permute-start | bytes 1572872 | tf_op jit(solution)/shard_map/ppermute | solution.py:333
  67.1 52.0 %collective-permute-start.5 = (bf16[512,1024]{1,0:T(8,128)(2,1)S(1)}, bf16[512,1024]{1,0:T(8,128)(2,1)}, u32[]{:S(2)}, u32[]{:S(2)}) collective-permute-start(bf16[512,1024]{1,0:T(8,128)(2,1)S(1)} %bitcast.355), channel_id=1, source_target_pairs={{0,2},{2,0},{1,3},{3,1},{4,6},{6,4},{5,7},{7,5},{8,10},{10,8},{9,1... | collective-permute-start | bytes 3145736 | tf_op jit(solution)/shard_map/ppermute | solution.py:333
  68.7 50.4 %collective-permute-start.4 = (bf16[512,1024]{1,0:T(8,128)(2,1)S(1)}, bf16[512,1024]{1,0:T(8,128)(2,1)}, u32[]{:S(2)}, u32[]{:S(2)}) collective-permute-start(bf16[512,1024]{1,0:T(8,128)(2,1)S(1)} %bitcast.356), channel_id=1, source_target_pairs={{0,4},{4,0},{1,5},{5,1},{2,6},{6,2},{3,7},{7,3},{8,12},{12,8},{9,1... | collective-permute-start | bytes 3145736 | tf_op jit(solution)/shard_map/ppermute | solution.py:333
  70.1 49.0 %collective-permute-start.7 = (bf16[512,1024]{1,0:T(8,128)(2,1)S(1)}, bf16[512,1024]{1,0:T(8,128)(2,1)}, u32[]{:S(2)}, u32[]{:S(2)}) collective-permute-start(bf16[512,1024]{1,0:T(8,128)(2,1)S(1)} %bitcast.352), channel_id=1, source_target_pairs={{0,2},{2,0},{1,3},{3,1},{4,6},{6,4},{5,7},{7,5},{8,10},{10,8},{9,1... | collective-permute-start | bytes 3145736 | tf_op jit(solution)/shard_map/ppermute | solution.py:333
  70.7 48.4 %collective-permute-start.6 = (bf16[512,1024]{1,0:T(8,128)(2,1)S(1)}, bf16[512,1024]{1,0:T(8,128)(2,1)}, u32[]{:S(2)}, u32[]{:S(2)}) collective-permute-start(bf16[512,1024]{1,0:T(8,128)(2,1)S(1)} %bitcast.353), channel_id=1, source_target_pairs={{0,4},{4,0},{1,5},{5,1},{2,6},{6,2},{3,7},{7,3},{8,12},{12,8},{9,1... | collective-permute-start | bytes 3145736 | tf_op jit(solution)/shard_map/ppermute | solution.py:333
  106.7 367.8 %reduce-scatter.7.cloned.1.call-start = ((), (), s32[]{:S(2)}) async-start(), calls=%async_computation.5 | async-start | bytes 5242880 | tf_op jit(solution)/shard_map/reduce_scatter | solution.py:667
  107.0 11.5 %collective-permute-start.8 = (bf16[4,16,1024]{2,1,0:T(8,128)(2,1)S(1)}, bf16[4,16,1024]{2,1,0:T(8,128)(2,1)S(1)}, u32[]{:S(2)}, u32[]{:S(2)}) collective-permute-start(bf16[4,16,1024]{2,1,0:T(8,128)(2,1)S(1)} %slice.337), channel_id=1, source_target_pairs={{0,4},{4,0},{1,5},{5,1},{2,6},{6,2},{3,7},{7,3},{8,12},{12,8},{9,1... | collective-permute-start | bytes 393224 | tf_op jit(solution)/shard_map/ppermute | solution.py:333
  118.5 9.3 %collective-permute-start.10 = (bf16[4,16,1024]{2,1,0:T(8,128)(2,1)S(1)}, bf16[4,16,1024]{2,1,0:T(8,128)(2,1)S(1)}, u32[]{:S(2)}, u32[]{:S(2)}) collective-permute-start(bf16[4,16,1024]{2,1,0:T(8,128)(2,1)S(1)} %slice.337), channel_id=1, source_target_pairs={{0,2},{2,0},{1,3},{3,1},{4,6},{6,4},{5,7},{7,5},{8,10},{10,8},{9,1... | collective-permute-start | bytes 393224 | tf_op jit(solution)/shard_map/ppermute | solution.py:333
  119.1 8.7 %collective-permute-start.9 = (bf16[4,16,1024]{2,1,0:T(8,128)(2,1)S(1)}, bf16[4,16,1024]{2,1,0:T(8,128)(2,1)S(1)}, u32[]{:S(2)}, u32[]{:S(2)}) collective-permute-start(bf16[4,16,1024]{2,1,0:T(8,128)(2,1)S(1)} %collective-permute-done.8), channel_id=1, source_target_pairs={{0,2},{2,0},{1,3},{3,1},{4,6},{6,4},{5,7},{7,5},{8,10},{10,8},{9,1... | collective-permute-start | bytes 393224 | tf_op jit(solution)/shard_map/ppermute | solution.py:333
  120.6 27.4 %collective-permute-start.12 = (bf16[512,1024]{1,0:T(8,128)(2,1)}, bf16[512,1024]{1,0:T(8,128)(2,1)}, u32[]{:S(2)}, u32[]{:S(2)}) collective-permute-start(bf16[512,1024]{1,0:T(8,128)(2,1)} %collective-permute-done.4), channel_id=1, source_target_pairs={{0,2},{2,0},{1,3},{3,1},{4,6},{6,4},{5,7},{7,5},{8,10},{10,8},{9,1... | collective-permute-start | bytes 3145736 | tf_op jit(solution)/shard_map/ppermute | solution.py:333
  121.2 26.8 %collective-permute-start.13 = (bf16[512,1024]{1,0:T(8,128)(2,1)}, bf16[512,1024]{1,0:T(8,128)(2,1)}, u32[]{:S(2)}, u32[]{:S(2)}) collective-permute-start(bf16[512,1024]{1,0:T(8,128)(2,1)} %collective-permute-done.7), channel_id=1, source_target_pairs={{0,4},{4,0},{1,5},{5,1},{2,6},{6,2},{3,7},{7,3},{8,12},{12,8},{9,1... | collective-permute-start | bytes 3145736 | tf_op jit(solution)/shard_map/ppermute | solution.py:333
  130.9 30.0 %collective-permute-start.11 = (bf16[192,1024]{1,0:T(8,128)(2,1)}, bf16[192,1024]{1,0:T(8,128)(2,1)}, u32[]{:S(2)}, u32[]{:S(2)}) collective-permute-start(bf16[192,1024]{1,0:T(8,128)(2,1)} %fusion.17), channel_id=1, source_target_pairs={{0,1},{1,0},{2,3},{3,2},{4,5},{5,4},{6,7},{7,6},{8,9},{9,8},{10,11... | collective-permute-start | bytes 1179656 | tf_op jit(solution)/shard_map/ppermute | solution.py:333
  149.6 21.7 %collective-permute-start.18 = (bf16[4,64,1536]{2,1,0:T(8,128)(2,1)S(1)}, bf16[4,64,1536]{2,1,0:T(8,128)(2,1)S(1)}, u32[]{:S(2)}, u32[]{:S(2)}) collective-permute-start(bf16[4,64,1536]{2,1,0:T(8,128)(2,1)S(1)} %reshape.599), channel_id=1, source_target_pairs={{0,2},{2,0},{1,3},{3,1},{4,6},{6,4},{5,7},{7,5},{8,10},{10,8},{9,1... | collective-permute-start | bytes 2359304 | tf_op jit(solution)/shard_map/ppermute | solution.py:333
  150.2 21.1 %collective-permute-start.17 = (bf16[4,64,1536]{2,1,0:T(8,128)(2,1)S(1)}, bf16[4,64,1536]{2,1,0:T(8,128)(2,1)S(1)}, u32[]{:S(2)}, u32[]{:S(2)}) collective-permute-start(bf16[4,64,1536]{2,1,0:T(8,128)(2,1)S(1)} %reshape.599), channel_id=1, source_target_pairs={{0,4},{4,0},{1,5},{5,1},{2,6},{6,2},{3,7},{7,3},{8,12},{12,8},{9,1... | collective-permute-start | bytes 2359304 | tf_op jit(solution)/shard_map/ppermute | solution.py:333
  171.6 20.0 %collective-permute-start.20 = (bf16[4,64,1536]{2,1,0:T(8,128)(2,1)S(1)}, bf16[4,64,1536]{2,1,0:T(8,128)(2,1)S(1)}, u32[]{:S(2)}, u32[]{:S(2)}) collective-permute-start(bf16[4,64,1536]{2,1,0:T(8,128)(2,1)S(1)} %collective-permute-done.18), channel_id=1, source_target_pairs={{0,4},{4,0},{1,5},{5,1},{2,6},{6,2},{3,7},{7,3},{8,12},{12,8},{9,1... | collective-permute-start | bytes 2359304 | tf_op jit(solution)/shard_map/ppermute | solution.py:333
  197.0 20.6 %collective-permute-start.21 = (bf16[384,1024]{1,0:T(8,128)(2,1)S(1)}, bf16[384,1024]{1,0:T(8,128)(2,1)}, u32[]{:S(2)}, u32[]{:S(2)}) collective-permute-start(bf16[384,1024]{1,0:T(8,128)(2,1)S(1)} %slice.346), channel_id=1, source_target_pairs={{0,2},{2,0},{1,3},{3,1},{4,6},{6,4},{5,7},{7,5},{8,10},{10,8},{9,1... | collective-permute-start | bytes 2359304 | tf_op jit(solution)/shard_map/ppermute | solution.py:333
  198.6 40.4 %collective-permute-start.23 = (bf16[4,128,1024]{2,1,0:T(8,128)(2,1)}, bf16[4,128,1024]{2,1,0:T(8,128)(2,1)}, u32[]{:S(2)}, u32[]{:S(2)}) collective-permute-start(bf16[4,128,1024]{2,1,0:T(8,128)(2,1)} %slice.271), channel_id=1, source_target_pairs={{0,2},{2,0},{1,3},{3,1},{4,6},{6,4},{5,7},{7,5},{8,10},{10,8},{9,1... | collective-permute-start | bytes 3145736 | tf_op jit(solution)/shard_map/ppermute | solution.py:333
  199.1 39.8 %collective-permute-start.22 = (bf16[4,128,1024]{2,1,0:T(8,128)(2,1)}, bf16[4,128,1024]{2,1,0:T(8,128)(2,1)}, u32[]{:S(2)}, u32[]{:S(2)}) collective-permute-start(bf16[4,128,1024]{2,1,0:T(8,128)(2,1)} %slice.271), channel_id=1, source_target_pairs={{0,4},{4,0},{1,5},{5,1},{2,6},{6,2},{3,7},{7,3},{8,12},{12,8},{9,1... | collective-permute-start | bytes 3145736 | tf_op jit(solution)/shard_map/ppermute | solution.py:333
  238.9 24.3 %collective-permute-start.24 = (bf16[4,128,1024]{2,1,0:T(8,128)(2,1)}, bf16[4,128,1024]{2,1,0:T(8,128)(2,1)}, u32[]{:S(2)}, u32[]{:S(2)}) collective-permute-start(bf16[4,128,1024]{2,1,0:T(8,128)(2,1)} %collective-permute-done.22), channel_id=1, source_target_pairs={{0,2},{2,0},{1,3},{3,1},{4,6},{6,4},{5,7},{7,5},{8,10},{10,8},{9,1... | collective-permute-start | bytes 3145736 | tf_op jit(solution)/shard_map/ppermute | solution.py:333
  280.0 6.6 collective-permute-start.29
  324.7 155.6 %reduce-scatter.5.cloned.1.call-start = ((), (), s32[]{:S(2)}) async-start(), calls=%async_computation.4 | async-start | bytes 5242880 | tf_op jit(solution)/shard_map/reduce_scatter | solution.py:667
  340.8 6.0 collective-permute-start.39
  359.2 8.0 %collective-permute-start.40 = (bf16[192,1024]{1,0:T(8,128)(2,1)}, bf16[192,1024]{1,0:T(8,128)(2,1)}, u32[]{:S(2)}, u32[]{:S(2)}) collective-permute-start(bf16[192,1024]{1,0:T(8,128)(2,1)} %fusion.59), channel_id=1, source_target_pairs={{0,1},{1,0},{2,3},{3,2},{4,5},{5,4},{6,7},{7,6},{8,9},{9,8},{10,11... | collective-permute-start | bytes 1179656 | tf_op jit(solution)/shard_map/ppermute | solution.py:333
  364.6 267.9 %reduce-scatter.11.cloned.1.call-start = ((), (), s32[]{:S(2)}) async-start(), calls=%async_computation.7 | async-start | bytes 2293760 | tf_op jit(solution)/shard_map/reduce_scatter | solution.py:667
  372.6 30.6 %collective-permute-start.42 = (bf16[4,2,64,1024]{3,2,0,1:T(8,128)(2,1)S(1)}, bf16[4,2,64,1024]{3,2,0,1:T(8,128)(2,1)S(1)}, u32[]{:S(2)}, u32[]{:S(2)}) collective-permute-start(bf16[4,2,64,1024]{3,2,0,1:T(8,128)(2,1)S(1)} %bitcast.380), channel_id=1, source_target_pairs={{0,4},{4,0},{1,5},{5,1},{2,6},{6,2},{3,7},{7,3},{8,12},{12,8},{9,1... | collective-permute-start | bytes 3145736 | tf_op jit(solution)/shard_map/ppermute | solution.py:333
  373.4 29.8 %collective-permute-start.43 = (bf16[4,2,32,1024]{3,2,0,1:T(8,128)(2,1)S(1)}, bf16[4,2,32,1024]{3,2,0,1:T(8,128)(2,1)S(1)}, u32[]{:S(2)}, u32[]{:S(2)}) collective-permute-start(bf16[4,2,32,1024]{3,2,0,1:T(8,128)(2,1)S(1)} %bitcast.391), channel_id=1, source_target_pairs={{0,2},{2,0},{1,3},{3,1},{4,6},{6,4},{5,7},{7,5},{8,10},{10,8},{9,1... | collective-permute-start | bytes 1572872 | tf_op jit(solution)/shard_map/ppermute | solution.py:333
  376.7 50.0 %collective-permute-start.48 = (bf16[8,32,1024]{2,1,0:T(8,128)(2,1)S(1)}, bf16[8,32,1024]{2,1,0:T(8,128)(2,1)}, u32[]{:S(2)}, u32[]{:S(2)}) collective-permute-start(bf16[8,32,1024]{2,1,0:T(8,128)(2,1)S(1)} %dynamic-slice_bitcast_fusion.3), channel_id=1, source_target_pairs={{0,1},{1,0},{2,3},{3,2},{4,5},{5,4},{6,7},{7,6},{8,9},{9,8},{10,11... | collective-permute-start | bytes 1572872 | tf_op jit(solution)/shard_map/ppermute | solution.py:333
  405.1 19.7 %collective-permute-start.44 = (bf16[384,1024]{1,0:T(8,128)(2,1)S(1)}, bf16[384,1024]{1,0:T(8,128)(2,1)S(1)}, u32[]{:S(2)}, u32[]{:S(2)}) collective-permute-start(bf16[384,1024]{1,0:T(8,128)(2,1)S(1)} %fusion.28), channel_id=1, source_target_pairs={{0,2},{2,0},{1,3},{3,1},{4,6},{6,4},{5,7},{7,5},{8,10},{10,8},{9,1... | collective-permute-start | bytes 2359304 | tf_op jit(solution)/shard_map/ppermute | solution.py:333
  428.0 8.8 %collective-permute-start.47 = (bf16[4,32,1024]{2,1,0:T(8,128)(2,1)S(1)}, bf16[4,32,1024]{2,1,0:T(8,128)(2,1)S(1)}, u32[]{:S(2)}, u32[]{:S(2)}) collective-permute-start(bf16[4,32,1024]{2,1,0:T(8,128)(2,1)S(1)} %dynamic-slice_bitcast_fusion.7), channel_id=1, source_target_pairs={{0,4},{4,0},{1,5},{5,1},{2,6},{6,2},{3,7},{7,3},{8,12},{12,8},{9,1... | collective-permute-start | bytes 786440 | tf_op jit(solution)/shard_map/ppermute | solution.py:333
  429.5 14.8 %collective-permute-start.46 = (bf16[4,64,1024]{2,1,0:T(8,128)(2,1)S(1)}, bf16[4,64,1024]{2,1,0:T(8,128)(2,1)S(1)}, u32[]{:S(2)}, u32[]{:S(2)}) collective-permute-start(bf16[4,64,1024]{2,1,0:T(8,128)(2,1)S(1)} %dynamic-slice_bitcast_fusion.4), channel_id=1, source_target_pairs={{0,2},{2,0},{1,3},{3,1},{4,6},{6,4},{5,7},{7,5},{8,10},{10,8},{9,1... | collective-permute-start | bytes 1572872 | tf_op jit(solution)/shard_map/ppermute | solution.py:333
  429.8 25.0 %collective-permute-start.49 = (bf16[4,2,32,1024]{3,2,1,0:T(8,128)(2,1)S(1)}, bf16[4,2,32,1024]{3,2,1,0:T(8,128)(2,1)S(1)}, u32[]{:S(2)}, u32[]{:S(2)}) collective-permute-start(bf16[4,2,32,1024]{3,2,1,0:T(8,128)(2,1)S(1)} %dynamic-slice_bitcast_fusion.2), channel_id=1, source_target_pairs={{0,2},{2,0},{1,3},{3,1},{4,6},{6,4},{5,7},{7,5},{8,10},{10,8},{9,1... | collective-permute-start | bytes 1572872 | tf_op jit(solution)/shard_map/ppermute | solution.py:333
  458.1 87.7 %collective-permute-start.55 = (bf16[4,2,64,1536]{3,2,1,0:T(8,128)(2,1)}, bf16[4,2,64,1536]{3,2,1,0:T(8,128)(2,1)}, u32[]{:S(2)}, u32[]{:S(2)}) collective-permute-start(bf16[4,2,64,1536]{3,2,1,0:T(8,128)(2,1)} %dynamic-slice_bitcast_fusion), channel_id=1, source_target_pairs={{0,4},{4,0},{1,5},{5,1},{2,6},{6,2},{3,7},{7,3},{8,12},{12,8},{9,1... | collective-permute-start | bytes 4718600 | tf_op jit(solution)/shard_map/ppermute | solution.py:333
  464.8 7.8 %collective-permute-start.51 = (bf16[192,1024]{1,0:T(8,128)(2,1)S(1)}, bf16[192,1024]{1,0:T(8,128)(2,1)S(1)}, u32[]{:S(2)}, u32[]{:S(2)}) collective-permute-start(bf16[192,1024]{1,0:T(8,128)(2,1)S(1)} %slice.478), channel_id=1, source_target_pairs={{0,1},{1,0},{2,3},{3,2},{4,5},{5,4},{6,7},{7,6},{8,9},{9,8},{10,11... | collective-permute-start | bytes 1179656 | tf_op jit(solution)/shard_map/ppermute | solution.py:333
  468.0 77.8 %collective-permute-start.52 = (bf16[1024,1024]{1,0:T(8,128)(2,1)}, bf16[1024,1024]{1,0:T(8,128)(2,1)}, u32[]{:S(2)}, u32[]{:S(2)}) collective-permute-start(bf16[1024,1024]{1,0:T(8,128)(2,1)} %convolution_convert_fusion.5), channel_id=1, source_target_pairs={{0,2},{2,0},{1,3},{3,1},{4,6},{6,4},{5,7},{7,5},{8,10},{10,8},{9,1... | collective-permute-start | bytes 6291464 | tf_op jit(solution)/shard_map/ppermute | solution.py:333
  472.1 73.7 %collective-permute-start.53 = (bf16[1024,1024]{1,0:T(8,128)(2,1)}, bf16[1024,1024]{1,0:T(8,128)(2,1)}, u32[]{:S(2)}, u32[]{:S(2)}) collective-permute-start(bf16[1024,1024]{1,0:T(8,128)(2,1)} %convolution_convert_fusion.4), channel_id=1, source_target_pairs={{0,4},{4,0},{1,5},{5,1},{2,6},{6,2},{3,7},{7,3},{8,12},{12,8},{9,1... | collective-permute-start | bytes 6291464 | tf_op jit(solution)/shard_map/ppermute | solution.py:333
  484.4 61.4 %collective-permute-start.54 = (bf16[2,256,1024]{2,1,0:T(8,128)(2,1)}, bf16[2,256,1024]{2,1,0:T(8,128)(2,1)}, u32[]{:S(2)}, u32[]{:S(2)}) collective-permute-start(bf16[2,256,1024]{2,1,0:T(8,128)(2,1)} %slice.307), channel_id=1, source_target_pairs={{0,2},{2,0},{1,3},{3,1},{4,6},{6,4},{5,7},{7,5},{8,10},{10,8},{9,1... | collective-permute-start | bytes 3145736 | tf_op jit(solution)/shard_map/ppermute | solution.py:333
  487.1 58.6 %collective-permute-start.56 = (bf16[4,32,1024]{2,1,0:T(8,128)(2,1)}, bf16[4,32,1024]{2,1,0:T(8,128)(2,1)}, u32[]{:S(2)}, u32[]{:S(2)}) collective-permute-start(bf16[4,32,1024]{2,1,0:T(8,128)(2,1)} %dynamic-slice_bitcast_fusion.6), channel_id=1, source_target_pairs={{0,4},{4,0},{1,5},{5,1},{2,6},{6,2},{3,7},{7,3},{8,12},{12,8},{9,1... | collective-permute-start | bytes 786440 | tf_op jit(solution)/shard_map/ppermute | solution.py:333
  556.8 19.1 %collective-permute-start.62 = (bf16[4,64,1536]{2,1,0:T(8,128)(2,1)S(1)}, bf16[4,64,1536]{2,1,0:T(8,128)(2,1)S(1)}, u32[]{:S(2)}, u32[]{:S(2)}) collective-permute-start(bf16[4,64,1536]{2,1,0:T(8,128)(2,1)S(1)} %dynamic-slice_bitcast_fusion.1), channel_id=1, source_target_pairs={{0,2},{2,0},{1,3},{3,1},{4,6},{6,4},{5,7},{7,5},{8,10},{10,8},{9,1... | collective-permute-start | bytes 2359304 | tf_op jit(solution)/shard_map/ppermute | solution.py:333
  581.3 84.4 %reduce-scatter.9.cloned.1.call-start = ((), (), s32[]{:S(2)}) async-start(), calls=%async_computation.6 | async-start | bytes 2785280 | tf_op jit(solution)/shard_map/reduce_scatter | solution.py:667
  584.0 27.2 %collective-permute-start.57 = (bf16[512,1024]{1,0:T(8,128)(2,1)}, bf16[512,1024]{1,0:T(8,128)(2,1)S(1)}, u32[]{:S(2)}, u32[]{:S(2)}) collective-permute-start(bf16[512,1024]{1,0:T(8,128)(2,1)} %add_convert_fusion.2), channel_id=1, source_target_pairs={{0,2},{2,0},{1,3},{3,1},{4,6},{6,4},{5,7},{7,5},{8,10},{10,8},{9,1... | collective-permute-start | bytes 3145736 | tf_op jit(solution)/shard_map/ppermute | solution.py:333
  585.8 27.9 %collective-permute-start.58 = (bf16[512,1024]{1,0:T(8,128)(2,1)}, bf16[512,1024]{1,0:T(8,128)(2,1)S(1)}, u32[]{:S(2)}, u32[]{:S(2)}) collective-permute-start(bf16[512,1024]{1,0:T(8,128)(2,1)} %add_convert_fusion.3), channel_id=1, source_target_pairs={{0,4},{4,0},{1,5},{5,1},{2,6},{6,2},{3,7},{7,3},{8,12},{12,8},{9,1... | collective-permute-start | bytes 3145736 | tf_op jit(solution)/shard_map/ppermute | solution.py:333
  588.2 22.8 %collective-permute-start.61 = (f32[4,1216]{1,0:T(4,128)S(1)}, f32[4,1216]{1,0:T(4,128)S(1)}, u32[]{:S(2)}, u32[]{:S(2)}) collective-permute-start(f32[4,1216]{1,0:T(4,128)S(1)} %bitcast.405), channel_id=1, source_target_pairs={{0,4},{4,0},{1,5},{5,1},{2,6},{6,2},{3,7},{7,3},{8,12},{12,8},{9,1... | collective-permute-start | bytes 58376 | tf_op jit(solution)/shard_map/ppermute | solution.py:333
  618.5 12.6 %collective-permute-start.65 = (bf16[256,1024]{1,0:T(8,128)(2,1)S(1)}, bf16[256,1024]{1,0:T(8,128)(2,1)S(1)}, u32[]{:S(2)}, u32[]{:S(2)}) collective-permute-start(bf16[256,1024]{1,0:T(8,128)(2,1)S(1)} %copy-done.39), channel_id=1, source_target_pairs={{0,4},{4,0},{1,5},{5,1},{2,6},{6,2},{3,7},{7,3},{8,12},{12,8},{9,1... | collective-permute-start | bytes 1572872 | tf_op jit(solution)/shard_map/ppermute | solution.py:333
  (119 other events, 710.0 us)
Sparse Core Ops, SparseCore 0:
  13.5 50.7 all-gather.6
  66.4 40.2 all-gather.8
  108.3 148.4 all-gather.10
  324.8 75.8 reduce-scatter.6
  402.9 77.3 reduce-scatter.4
  581.4 36.7 reduce-scatter.10
  620.5 45.1 reduce-scatter.8

commit v3 on v2

--- a/solution.py
+++ b/solution.py
@@ -135,6 +135,14 @@
     ]
 
 
+def cost_of(heads, rows, group, products):
+    return pl.CostEstimate(
+        flops=2 * products * heads * rows * group * HD,
+        bytes_accessed=4 * heads * HD * (rows + group),
+        transcendentals=heads * rows * group,
+    )
+
+
 def attend(info, bias, query, both):
     heads, _, width = bias.shape
     rows, group = query.shape[0], both.shape[0]
@@ -147,6 +155,7 @@
         out_shape=jax.ShapeDtypeStruct((rows, heads * HD), jnp.bfloat16),
         scratch_shapes=[pltpu.VMEM((ROWS, width), jnp.float32)],
         compiler_params=pltpu.CompilerParams(vmem_limit_bytes=VMEM),
+        cost_estimate=cost_of(heads, rows, group, 2),
         name="attend",
     )(info, bias, query, both, both)
 
@@ -177,6 +186,7 @@
             pltpu.VMEM((rows, 2 * HD), jnp.bfloat16),
         ],
         compiler_params=pltpu.CompilerParams(vmem_limit_bytes=VMEM),
+        cost_estimate=cost_of(heads, rows, group, 5),
         name="attend_back",
     )(info, bias, query, both, both, grad)
 
@@ -281,6 +291,9 @@
         out_shape=jax.ShapeDtypeStruct((rows, width), jnp.float32),
         scratch_shapes=[pltpu.VMEM((rows + 2 * EDGE, LANES), jnp.float32)],
         compiler_params=pltpu.CompilerParams(vmem_limit_bytes=VMEM),
+        cost_estimate=pl.CostEstimate(
+            flops=2 * taps * rows * width, bytes_accessed=6 * rows * width, transcendentals=0
+        ),
         name="conv",
     )(info, low, mid, high, depth)
 
@@ -305,6 +318,9 @@
             pltpu.VMEM((8 * taps, LANES), jnp.float32),
         ],
         compiler_params=pltpu.CompilerParams(vmem_limit_bytes=VMEM),
+        cost_estimate=pl.CostEstimate(
+            flops=4 * taps * rows * width, bytes_accessed=8 * rows * width, transcendentals=0
+        ),
         name="conv_back",
     )(info, low, mid, high, grad_low, grad_mid, grad_high, depth)
 
@@ -363,9 +379,9 @@
     return choose(values, 1 - lax.axis_index(axis), dim)
 
 
-def send(values, axis, dim, *ties):
+def send(values, axis, dim):
     if lax.axis_size(axis) == 2:
-        return swap(after(pick(values, axis, dim), *ties), axis)
+        return swap(pick(values, axis, dim), axis)
     return lax.psum_scatter(values, axis, scatter_dimension=dim, tiled=False)
 
 
@@ -374,12 +390,6 @@
         return received
     kept = choose(values, lax.axis_index(axis), dim)
     return (kept.astype(jnp.float32) + received.astype(jnp.float32)).astype(values.dtype)
-
-
-def after(values, *tokens):
-    if not tokens:
-        return values
-    return lax.optimization_barrier((values,) + tokens)[0]
 
 
 def together(*values):
@@ -466,11 +476,13 @@
     entry_grad = partial[:rows] + received.astype(jnp.float32)
     back, gain_grad = norm_back(entry_grad, normed, inverse, gain)
 
-    def inner_grad(low_row, high_row):
-        return left_product(middle_grad[:, low_row:high_row], both)
-
-    def outer_grad(low_row, high_row):
-        return left_product(activated[:, low_row:high_row], half_both)
+    eighth = middle.shape[1] // 8
+
+    def inner_grad(first, end):
+        return left_product(middle_grad[:, first * eighth : end * eighth], both)
+
+    def outer_grad(first, end):
+        return left_product(activated[:, first * eighth : end * eighth], half_both)
 
     return (upstream + back, gain_grad, inner_grad, outer_grad)
 
@@ -532,12 +544,10 @@
     small_both = ordered(small[None], swap(small[None]), core).reshape(-1)
     small_both = jnp.pad(small_both, (0, small_rows * width - 2 * count)).reshape(small_rows, width)
 
-    def feed_pack(number, *more):
-        return jnp.concatenate([inner_weight[number].T, outer_weight[number], *more], axis=0)
-
-    pack_one = feed_pack(0, small_both)
-    pack_two = feed_pack(1)
-    attend_weight, glu_weight = together(attend_weight, glu_weight, pack_one)[:2]
+    inner_pack = inner_weight[0].T
+    outer_pack = jnp.concatenate([outer_weight[0], small_both], axis=0)
+    pack_two = jnp.concatenate([inner_weight[1].T, outer_weight[1]], axis=0)
+    attend_weight, glu_weight = together(attend_weight, glu_weight, outer_pack)[:2]
 
     def own_columns(weight, shape, dim):
         parts = weight.reshape((share,) + shape)
@@ -559,37 +569,51 @@
     def gather_p(values):
         return lax.all_gather(values, "p", axis=0)
 
+    def in_halves(*parts):
+        parts = [part.reshape(grid[0], units, width) for part in parts]
+        near = [part[:, : units // 2].reshape(-1, width) for part in parts]
+        far = [part[:, units // 2 :].reshape(-1, width) for part in parts]
+        return jnp.concatenate(near + far, axis=0)
+
     if square:
-        whole_one = gather_p(pack_one)
+        inner = gather_p(inner_pack)
         two_x, two_y = together(swap(pack_two, "q"), swap(pack_two, "y"))
         pack_two = jnp.stack([pack_two, two_x, swap(two_x, "y"), two_y])
-        mixed = gather_p(after(mixed_pack, pack_one))
-        inner = whole_one[:, :units].reshape(-1, width)
-        outer = whole_one[:, units : 2 * units].reshape(-1, width)
-        tiny = whole_one[:, 2 * units :]
-        inner, outer, tiny, pack_two = together(inner, outer, tiny, pack_two)
-        whole_two = gather_p(after(pack_two, mixed)).reshape(chips, 2 * units, width)
-        tiny_x = swap(tiny, "q")
-        inner_x, inner_y, outer_x, outer_y, tiny_x = together(
-            swap(inner, "q"), swap(inner, "y"), swap(outer, "q"), swap(outer, "y"), tiny_x
+        whole_one = gather_p(outer_pack)
+        inner, pack_two = together(inner.reshape(-1, width), pack_two)
+        inner_x, inner_y = together(swap(inner, "q"), swap(inner, "y"))
+        mixed_pack, inner_x, inner_y = together(mixed_pack, inner_x, inner_y)
+        mixed = gather_p(mixed_pack)
+        inner_xy = swap(inner_y, "q")
+        outer = whole_one[:, :units].reshape(-1, width)
+        tiny = whole_one[:, units:]
+        outer, tiny = together(outer, tiny)
+        across = [(0, 3), (3, 0), (1, 2), (2, 1)]
+        tiny_xy = lax.ppermute(tiny, ("q", "y"), across)
+        outer_x, outer_y, tiny_x, tiny_y, tiny_xy = together(
+            swap(outer, "q"), swap(outer, "y"), swap(tiny, "q"), swap(tiny, "y"), tiny_xy
         )
-        inner_xy, outer_xy = swap(inner_x, "y"), swap(outer_y, "q")
-        small_full = placed((tiny, tiny_x, swap(tiny_x, "y"), swap(tiny, "y")))
-        small_full = small_full.reshape(chips, -1)
-        inner_xy, outer_xy, mixed = together(inner_xy, outer_xy, mixed)
-        inner_one = jnp.concatenate([inner, inner_x, inner_xy, inner_y], axis=0)
-        outer_one = jnp.concatenate([outer, outer_x, outer_xy, outer_y], axis=0)
+        small_full = placed((tiny, tiny_x, tiny_xy, tiny_y)).reshape(chips, -1)
+        outer_xy = swap(outer_x, "y")
+        mixed, pack_two = together(mixed, pack_two)
+        whole_two = gather_p(pack_two).reshape(chips, 2 * units, width)
         attend_part = mixed[:, : marks[1]].reshape(grid[0], 2 * share, 3 * half)
         rest_part = mixed[:, marks[1] :]
         attend_part, rest_part = together(attend_part, rest_part)
-        attend_x, attend_y = swap(attend_part, "q"), swap(attend_part, "y")
+        attend_x = swap(attend_part, "q")
+        inner_xy, outer_xy, attend_x, attend_part, rest_part = together(
+            inner_xy, outer_xy, attend_x, attend_part, rest_part
+        )
+        inner_one = in_halves(inner, inner_x, inner_xy, inner_y)
+        outer_one = in_halves(outer, outer_x, outer_xy, outer_y)
+        attend_y, rest_x = swap(attend_part, "y"), swap(rest_part, "q")
     else:
-        whole_one = lax.all_gather(pack_one, CHIPS, axis=0)
+        inner_one = lax.all_gather(inner_pack, CHIPS, axis=0, tiled=True)
+        whole_one = lax.all_gather(outer_pack, CHIPS, axis=0)
         mixed = lax.all_gather(mixed_pack, CHIPS, axis=0)
         whole_two = lax.all_gather(pack_two, CHIPS, axis=0)
-        inner_one = whole_one[:, :units].reshape(chips * units, width)
-        outer_one = whole_one[:, units : 2 * units].reshape(chips * units, width)
-        small_full = whole_one[:, 2 * units :].reshape(chips, -1)
+        outer_one = whole_one[:, :units].reshape(chips * units, width)
+        small_full = whole_one[:, units:].reshape(chips, -1)
 
     small_full = small_full[:, : 2 * count].reshape(chips, 2, count)
     gain_size = norm_gains.size
@@ -610,7 +634,7 @@
     hidden = frames.astype(f32)
     first, first_kept = feed_forward(hidden, gain_table[0], inner_one, outer_one)
     if square:
-        first, attend_x, attend_y = together(first, attend_x, attend_y)
+        first, attend_y, rest_part = together(first, attend_y, rest_part)
         rest_y = swap(rest_part, "y")
         attend_full = placed((attend_part, attend_x, swap(attend_y, "q"), attend_y))
     else:
@@ -622,12 +646,9 @@
     query = triple[:, :half]
     key_value = triple[:, half:]
     if square:
-        key_value, rest_part = together(key_value, rest_part)
-        rest_x = swap(rest_part, "q")
+        key_value, rest_x, rest_y = together(key_value, rest_x, rest_y)
+        rest_xy = swap(rest_y, "q")
     both = gather_axis(key_value, "y")
-    if square:
-        query, both, rest_x, rest_y = together(query, both, rest_x, rest_y)
-        rest_xy = swap(rest_x, "y")
     attended = attend(info, bias, query, both)
     if square:
         attended, rest_xy = together(attended, rest_xy)
@@ -666,13 +687,11 @@
     def last_sum(values):
         return lax.psum_scatter(values, "p", scatter_dimension=0, tiled=False)
 
-    size = grid[0] * units
+    size = grid[0] * units // 2
 
     def early_sum(grad):
-        values = low(grad(0, chips * units))
-        if square:
-            return last_sum(values.reshape(grid[0], 4, units, width))
-        return last_sum(values.reshape(grid + (units, width)))
+        shape = (grid[0], 4) if square else grid
+        return last_sum(low(grad).reshape(shape + (units, width)))
 
     grad_fourth, gain_five = norm_back(
         cotangent.astype(f32), normed_last, inverse_last, gain_table[5]
@@ -681,8 +700,7 @@
         grad_fourth, gain_table[4], inner_two, outer_two, fourth_kept
     )
 
-    outer_two_sum = early_sum(outer_two_grad)
-    inner_two_sum = early_sum(inner_two_grad)
+    outer_two_sum = early_sum(outer_two_grad(0, 8))
 
     conv_out_grad = pair_rows(low(grad_third))
     swish_grad = right_product(conv_out_grad, point_full)
@@ -690,6 +708,10 @@
     mixed_grad, gain_three = split_norm_back(act_grad, normed_mid, inverse_mid, gain_mid)
     mixed_low = low(mixed_grad)
     grad_low, grad_high = halos(mixed_low)
+    if square:
+        inner_two = low(inner_two_grad(0, 8)).reshape(grid[0], 4, units, width)
+        inner_two_a, mixed_low = together(inner_two[:, 1:3], mixed_low)
+        inner_two_a = swap(inner_two_a, "q")
     glu_back, depth_grad = conv_back(
         info, glu_low, glu_rows, glu_high, grad_low, mixed_low, grad_high, depth, group
     )
@@ -706,7 +728,7 @@
     grad_second = grad_third + back_conv
 
     att_out_grad = pair_rows(low(grad_second))
-    glu_a = send(glu_grad, "q", 1)
+    glu_sum = last_sum(glu_grad)
     point_a = send(point_grad, "y", 2)
     merge_grad = low(left_product(attended, att_out_grad)).reshape(chips // 2, 2, share, width)
     merge_grad = ordered(
@@ -714,10 +736,13 @@
     )
     merge_grad = by_chip(merge_grad.reshape(chips * share, width))
     attended_grad = low(right_product(att_out_grad, merge_full))
+    merge_a = send(merge_grad, "y", 2)
     query_grad, key_grad, value_grad, table_sums = attend_back(info, bias, query, both, attended_grad)
-    query_grad, key_grad, value_grad, glu_a, point_a = together(
-        query_grad, key_grad, value_grad, glu_a, point_a
-    )
+    query_grad, key_grad, value_grad, point_a, merge_a = together(
+        query_grad, key_grad, value_grad, point_a, merge_a
+    )
+    point_half = add(point_grad, point_a, "y", 2)
+    merge_half = add(merge_grad, merge_a, "y", 2)
     both_grad = jnp.concatenate([key_grad, value_grad], axis=1).reshape(grid[2], pair, width)
     if grid[2] == 2:
         place = lax.axis_index("y")
@@ -726,64 +751,103 @@
     else:
         both_received = low(lax.psum_scatter(both_grad, "y", scatter_dimension=0, tiled=False))
         both_grad = both_received
+    if square:
+        point_b, merge_b, outer_two_a, inner_two_a, both_grad = together(
+            pick(point_half, "q", 1),
+            pick(merge_half, "q", 1),
+            outer_two_sum[1:3],
+            inner_two_a,
+            both_grad,
+        )
+        inner_two_b = low(inner_two[:, 3].astype(f32) + inner_two_a[:, 1].astype(f32))
+        inner_two_b = swap(inner_two_b, "y")
+        point_b, merge_b, outer_two_a = [swap(part, "q") for part in (point_b, merge_b, outer_two_a)]
+    else:
+        point_b, merge_b = send(point_half, "q", 1), send(merge_half, "q", 1)
+        inner_two_sum = early_sum(inner_two_grad(0, 8))
     triple_grad = jnp.concatenate([query_grad, both_grad], axis=1)
     attend_grad = low(left_product(att_entry, triple_grad))
     attend_grad = attend_grad.reshape(grid + (2 * share, 3 * half))
     att_entry_grad = pair_sum(right_product(triple_grad, attend_full))
     back_att, gain_one = norm_back(att_entry_grad, normed_att, inverse_att, gain_table[1])
     grad_first = grad_second + back_att
-    glu_half = add(glu_grad, glu_a, "q", 1)
-    point_half = add(point_grad, point_a, "y", 2)
-    glu_b = send(glu_half, "y", 1, both_received)
-    point_b = send(point_half, "q", 1, both_received)
-    merge_a = send(merge_grad, "y", 2, both_received)
-    attend_a = send(attend_grad, "q", 1)
+    attend_grad, glu_sum = together(attend_grad, glu_sum)
+    attend_sum = last_sum(attend_grad)
     if square:
-        grad_first, glu_b, point_b, merge_a = together(grad_first, glu_b, point_b, merge_a)
+        inner_two_sum = inner_two[:, 0].astype(f32) + inner_two_a[:, 0].astype(f32)
     input_grad, gain_zero, inner_one_grad, outer_one_grad = feed_back(
         grad_first, gain_table[0], inner_one, outer_one, first_kept
     )
-    conv_sum = jnp.concatenate([add(glu_half, glu_b, "y", 1), add(point_half, point_b, "q", 1)], axis=1)
-    merge_half = add(merge_grad, merge_a, "y", 2)
-    merge_b = send(merge_half, "q", 1)
     if square:
-        outer_one_a = swap(low(outer_one_grad(2 * size, 4 * size)), "y")
-        inner_one_a = swap(low(inner_one_grad(size, 3 * size)), "q")
-        two_sum = jnp.concatenate([inner_two_sum, outer_two_sum], axis=1)
-        two_sum, input_grad = together(two_sum, input_grad)
-        two_a = swap(two_sum[2:], "y")
-        outer_one_a, inner_one_a, two_a, attend_a, merge_b = together(
-            outer_one_a, inner_one_a, two_a, attend_a, merge_b
+        near_o, near_i, point_b, merge_b, inner_two_b, glu_sum = together(
+            low(outer_one_grad(1, 3)),
+            low(inner_one_grad(2, 4)),
+            point_b,
+            merge_b,
+            inner_two_b,
+            glu_sum,
         )
-    attend_half = add(attend_grad, attend_a, "q", 1)
+        near_o, near_i = swap(near_o, "q"), swap(near_i, "y")
+        inner_two_sum = low(inner_two_sum + inner_two_b.astype(f32))
+    mixed_sum = jnp.concatenate(
+        [
+            add(point_half, point_b, "q", 1),
+            add(merge_half, merge_b, "q", 1),
+        ]
+        + ([inner_two_sum] if square else []),
+        axis=1,
+    )
     if square:
-        last = together(
-            low(outer_one_grad(size, 2 * size) + outer_one_a[:size].astype(f32)),
-            low(inner_one_grad(3 * size, 4 * size) + inner_one_a[size:].astype(f32)),
-            pick(attend_half, "y", 1),
-            low(two_sum[1].astype(f32) + two_a[0].astype(f32)),
+        near_o, near_i, far_o, far_i, mixed_sum, outer_two_a, attend_sum = together(
+            near_o,
+            near_i,
+            low(outer_one_grad(5, 7)),
+            low(inner_one_grad(6, 8)),
+            mixed_sum,
+            outer_two_a,
+            attend_sum,
         )
-        outer_one_b, inner_one_b, attend_b, two_b = [
-            swap(part, axis) for part, axis in zip(last, "qyyq")
-        ]
-        two_sum = low(two_sum[0].astype(f32) + two_a[1].astype(f32) + two_b.astype(f32))
-        inner_sum_two, outer_sum_two = two_sum[:units], two_sum[units:]
-        outer_sum_one = outer_one_grad(0, size) + outer_one_a[size:].astype(f32)
-        inner_sum_one = inner_one_grad(0, size) + inner_one_a[:size].astype(f32)
-        outer_sum_one = low(outer_sum_one + outer_one_b.astype(f32)).reshape(grid[0], units, width)
-        inner_sum_one = low(inner_sum_one + inner_one_b.astype(f32)).reshape(grid[0], units, width)
+        glu_a = swap(pick(glu_sum, "q", 0), "q")
+        far_o, far_i = swap(far_o, "q"), swap(far_i, "y")
+        mixed_sum = last_sum(mixed_sum)
+
+        def second(first, got_o, got_i):
+            return together(
+                low(outer_one_grad(first + 3, first + 4) + got_o[size:].astype(f32)),
+                low(inner_one_grad(first + 1, first + 2) + got_i[:size].astype(f32)),
+            )
+
+        def third(first, got_o, got_i, end_o, end_i):
+            sum_o = outer_one_grad(first, first + 1) + got_o[:size].astype(f32)
+            sum_i = inner_one_grad(first, first + 1) + got_i[size:].astype(f32)
+            sums = [low(sum_i + end_i.astype(f32)), low(sum_o + end_o.astype(f32))]
+            return [part.reshape(grid[0], units // 2, width) for part in sums]
+
+        near = second(0, near_o, near_i)
+        near = together(swap(near[0], "y"), swap(near[1], "q"))
+        near = jnp.concatenate(third(0, near_o, near_i, *near), axis=1)
+        far_o, far_i, near, mixed_sum = together(far_o, far_i, near, mixed_sum)
+        near_sum = last_sum(near)
+        far = second(4, far_o, far_i)
+        far = together(swap(far[0], "y"), swap(far[1], "q"))
+        far = third(4, far_o, far_i, *far)
+        outer_two_b = swap(low(outer_two_sum[3].astype(f32) + outer_two_a[1].astype(f32)), "y")
+        outer_sum_two = outer_two_sum[0].astype(f32) + outer_two_a[0].astype(f32)
+        outer_sum_two = low(outer_sum_two + outer_two_b.astype(f32))
+        inner_sum_two = mixed_sum[2 * share :]
+        glu_half = add(glu_sum, glu_a, "q", 0)
     else:
-        attend_b = send(attend_half, "y", 1)
-        inner_sum_one = by_chip(low(inner_one_grad(0, chips * units)))
-        outer_sum_one = by_chip(low(outer_one_grad(0, chips * units)))
+        mixed_sum = last_sum(mixed_sum)
+        glu_half = send(glu_sum, "q", 0)
+        inner_sum_one = by_chip(low(inner_one_grad(0, 8)))
+        outer_sum_one = by_chip(low(outer_one_grad(0, 8)))
         inner_sum_one = send(send(inner_sum_one, "y", 2), "q", 1)
         outer_sum_one = send(send(outer_sum_one, "y", 2), "q", 1)
         inner_sum_two = send(send(inner_two_sum, "y", 1), "q", 0)
         outer_sum_two = send(send(outer_two_sum, "y", 1), "q", 0)
-    attend_sum = add(attend_half, attend_b, "y", 1).reshape(grid[0], 3 * share, width)
-    mixed_sum = last_sum(
-        jnp.concatenate([attend_sum, conv_sum, add(merge_half, merge_b, "q", 1)], axis=1)
-    )
+    glu_sum = add(glu_half, send(glu_half, "y", 0), "y", 0)
+    attend_half = add(attend_sum, send(attend_sum, "q", 0), "q", 0)
+    attend_sum = add(attend_half, send(attend_half, "y", 0), "y", 0)
 
     table_grad = jnp.einsum(
         "hw,wb->bh", table_sums[:, 0], hits.astype(f32), precision=lax.Precision.HIGHEST
@@ -815,7 +879,17 @@
     small_sum = jnp.pad(low(small_sum), ((0, 0), (0, one_rows * width - count)))
     small_sum = small_sum.reshape(grid[0], one_rows, width)
 
-    one_sum = last_sum(jnp.concatenate([inner_sum_one, outer_sum_one, small_sum], axis=1))
+    if square:
+        far_sum, near_sum = together(jnp.concatenate(far + [small_sum], axis=1), near_sum)
+        far_sum = last_sum(far_sum)
+        half_units = units // 2
+        inner_sum_one = jnp.concatenate([near_sum[:half_units], far_sum[:half_units]])
+        outer_sum_one = jnp.concatenate([near_sum[half_units:], far_sum[half_units:units]])
+        small_sum = far_sum[units:]
+    else:
+        one_sum = last_sum(jnp.concatenate([inner_sum_one, outer_sum_one, small_sum], axis=1))
+        inner_sum_one, outer_sum_one = one_sum[:units], one_sum[units : 2 * units]
+        small_sum = one_sum[2 * units :]
 
     def whole_columns(values, shape, dim):
         parts = values.reshape(2, share, -1)
@@ -829,13 +903,13 @@
         )
         return joined.reshape(share, -1).astype(f32)
 
-    attend_out = whole_columns(mixed_sum[: 3 * share].reshape(2 * share, -1), (3, half), 2)
-    glu_out = whole_columns(mixed_sum[3 * share : 5 * share], (2, chips, share), 3)
-    point_out = mixed_sum[5 * share : 6 * share].astype(f32)
-    merge_out = mixed_sum[6 * share :].astype(f32)
-    inner_out = jnp.stack([one_sum[:units].T, inner_sum_two.T]).astype(f32)
-    outer_out = jnp.stack([one_sum[units : 2 * units], outer_sum_two]).astype(f32)
-    small_out = one_sum[2 * units :].reshape(-1)[:count].astype(f32)
+    attend_out = whole_columns(attend_sum, (3, half), 2)
+    glu_out = whole_columns(glu_sum, (2, chips, share), 3)
+    point_out = mixed_sum[:share].astype(f32)
+    merge_out = mixed_sum[share : 2 * share].astype(f32)
+    inner_out = jnp.stack([inner_sum_one.T, inner_sum_two.T]).astype(f32)
+    outer_out = jnp.stack([outer_sum_one, outer_sum_two]).astype(f32)
+    small_out = small_sum.reshape(-1)[:count].astype(f32)
     gains_out = small_out[:gain_size].reshape(norm_gains.shape)
     position_out = small_out[gain_size : gain_size + position_bias.size]
     depth_out = small_out[gain_size + position_bias.size :].reshape(taps, share)

time: 687 us -> 633 us (0.921)
  waiting for transfers between devices: 352 us -> 212 us
  local copies, waits for them, and re-layouts: 82 us -> 127 us
  matrix products: 70.7 us -> 85.3 us
  Pallas kernels: 51.7 us -> 61.7 us
  other arithmetic: 47.1 us -> 54.7 us
  starting transfers between devices: 56.8 us -> 64.1 us
    ppermute x62 -> x67, waiting for transfers between devices: 275 us -> 186 us  [swap(): return lax.ppermute(values, axis, CORES)]
    all_gather x3 -> x4, waiting for transfers between devices: 46.1 us -> 7.43 us  [gather_p(): return lax.all_gather(values, 'p', axis=0)]
    reduce_scatter x4 -> x6, waiting for transfers between devices: 29.5 us -> 17.2 us  [last_sum(): return lax.psum_scatter(values, 'p', scatter_dimension=0, tiled=False)]
    pallas_call x1, Pallas kernels: 14 us -> 24.3 us  [attend(): pl.pallas_call(attend_kernel, grid=(heads,), in_specs=attend_specs(rows,...]
    slice x8 -> x16, local copies, waits for them, and re-layouts: 7.96 us -> 17.4 us  [the longest x8 9.52 us: in_halves(): far = [part[:, units // 2:].reshape(-1, width) for part in parts]]
    unnamed x210 -> x275, local copies, waits for them, and re-layouts: 24.3 us -> 32.9 us
    dot_general x12 -> x18, matrix products: 33.5 us -> 41.9 us  [left_product(): jnp.einsum('nd,nf->df', left_in, right_in, preferred_element_type=jnp.flo...]
    ppermute x62 -> x67, starting transfers between devices: 43.9 us -> 48.1 us  [swap(): return lax.ppermute(values, axis, CORES)]
  transfers between devices with their start and end apart: 73 -> 82, of which waited for: 39 -> 40; matrix products, arithmetic and copies ran while one was open for 22% -> 36% of each run, Pallas kernels for 8% -> 10%
where the time goes in v3:
time: 633 us; the launch traced here: 624 us
  waiting for transfers between devices  212 us (33%)
  local copies, waits for them, and re-layouts  127 us (20%)
  matrix products  85.3 us (13%)
  starting transfers between devices  64.1 us (10%)
  Pallas kernels  61.7 us (10%)
  other arithmetic  54.7 us (9%)
  between operations  18.6 us (3%)
    ppermute x67, waiting for transfers between devices, swap(): return lax.ppermute(values, axis, CORES)  186 us
    ppermute x67, starting transfers between devices, swap(): return lax.ppermute(values, axis, CORES)  48.1 us
    dot_general x18, matrix products, left_product(): jnp.einsum('nd,nf->df', left_in, right_in, preferred_element_type=jnp.flo...  41.9 us
    unnamed x275, local copies, waits for them, and re-layouts  32.9 us
    dot_general x8, matrix products, right_product(): jnp.einsum('nf,df->nd', left_in, right_in, preferred_element_type=jnp.flo...  27.8 us
    pallas_call x1, Pallas kernels, attend_back(): pl.pallas_call(attend_back_kernel, grid=(heads,), in_specs=attend_specs(r...  25.6 us
    pallas_call x1, Pallas kernels, attend(): pl.pallas_call(attend_kernel, grid=(heads,), in_specs=attend_specs(rows,...  24.3 us
    reduce_scatter x6, waiting for transfers between devices, last_sum(): return lax.psum_scatter(values, 'p', scatter_dimension=0, tiled=False)  17.2 us
  transfers between devices with their start and end apart: 82, of which 40 were waited for; matrix products, arithmetic and copies ran while one was open for 36% of the time, Pallas kernels for 10%

profile of v3, /device:TPU:0, one launch (start us, length us, event | category | flops | bytes accessed | tf_op | source)
XLA Modules:
  0.0 623.7 jit_solution(15406638598986744528)
XLA Ops:
  10.4 3.0 collective-permute-start.7
  19.0 6.3 %collective-permute-done.7 = bf16[256,1024]{1,0:T(8,128)(2,1)S(1)} collective-permute-done((bf16[256,1024]{1,0:T(8,128)(2,1)S(1)}, bf16[256,1024]{1,0:T(8,128)(2,1)S(1)}, u32[]{:S(2)}, u32[]{:S(2)}) %collective-permute-start.7) | collective-permute-done | bytes 524320 | tf_op jit(solution)/shard_map/ppermute | solution.py:349
  34.3 3.5 dynamic-slice_reduce_fusion
  41.1 4.1 all-gather.11.cloned.1.call-done
  52.8 16.6 %collective-permute-done.13 = bf16[512,1024]{0,1:T(8,128)(2,1)} collective-permute-done((bf16[512,1024]{0,1:T(8,128)(2,1)}, bf16[512,1024]{0,1:T(8,128)(2,1)}, u32[]{:S(2)}, u32[]{:S(2)}) %collective-permute-start.13) | collective-permute-done | bytes 1048608 | tf_op jit(solution)/shard_map/ppermute | solution.py:349
  72.8 3.4 all-gather.9.cloned.1.call-done
  79.0 2.4 collective-permute-start.5
  95.1 15.1 %collective-permute-done.2 = bf16[512,1024]{1,0:T(8,128)(2,1)} collective-permute-done((bf16[512,1024]{1,0:T(8,128)(2,1)S(1)}, bf16[512,1024]{1,0:T(8,128)(2,1)}, u32[]{:S(2)}, u32[]{:S(2)}) %collective-permute-start.2) | collective-permute-done | bytes 1048608 | tf_op jit(solution)/shard_map/ppermute | solution.py:349
  134.4 7.8 %collective-permute-done.15 = bf16[512,1024]{1,0:T(8,128)(2,1)} collective-permute-done((bf16[512,1024]{1,0:T(8,128)(2,1)}, bf16[512,1024]{1,0:T(8,128)(2,1)}, u32[]{:S(2)}, u32[]{:S(2)}) %collective-permute-start.15) | collective-permute-done | bytes 1048608 | tf_op jit(solution)/shard_map/ppermute | solution.py:349
  142.2 7.5 %collective-permute-done.16 = bf16[4,64,1536]{2,1,0:T(8,128)(2,1)} collective-permute-done((bf16[4,64,1536]{2,1,0:T(8,128)(2,1)S(1)}, bf16[4,64,1536]{2,1,0:T(8,128)(2,1)}, u32[]{:S(2)}, u32[]{:S(2)}) %collective-permute-start.16) | collective-permute-done | bytes 786464 | tf_op jit(solution)/shard_map/ppermute | solution.py:349
  155.2 3.5 copy-done.97
  160.0 5.5 multiply_convert_fusion.3
  176.0 18.0 %collective-permute-done.20 = bf16[4,64,1536]{2,1,0:T(8,128)(2,1)S(1)} collective-permute-done((bf16[4,64,1536]{2,1,0:T(8,128)(2,1)}, bf16[4,64,1536]{2,1,0:T(8,128)(2,1)S(1)}, u32[]{:S(2)}, u32[]{:S(2)}) %collective-permute-start.20) | collective-permute-done | bytes 786464 | tf_op jit(solution)/shard_map/ppermute | solution.py:349
  197.0 3.3 convolution_convert_fusion.3
  209.3 11.8 %collective-permute-done.23 = bf16[384,1024]{1,0:T(8,128)(2,1)} collective-permute-done((bf16[384,1024]{1,0:T(8,128)(2,1)S(1)}, bf16[384,1024]{1,0:T(8,128)(2,1)}, u32[]{:S(2)}, u32[]{:S(2)}) %collective-permute-start.23) | collective-permute-done | bytes 786464 | tf_op jit(solution)/shard_map/ppermute | solution.py:349
  222.5 24.3 %attend.1 = bf16[384,512]{1,0:T(8,128)(2,1)S(1)} custom-call(s32[3]{0:T(128)S(1)} %pad_add_fusion.info_ref.refs_0_, f32[8,1,1536]{2,1,0:T(1,128)S(1)} %broadcast_in_dim.50.bias_ref, bf16[384,512]{1,0:T(8,128)(2,1)S(1)} %slice.481.query_ref, bf16[768,1024]{1,0:T(8,128)(2,1)S(1)} %pad_maximum_fusion.2.key_ref.value_ref, ...), custom_call_target="tpu_custom_call" | custom-call | flops 603979776 | bytes 2359296 | tf_op jit(solution)/shard_map/attend/pallas_call | solution.py:150
  262.9 4.5 collective-permute-start.28
  268.9 4.2 conv.1
  284.9 4.0 fusion.138
  288.9 3.5 fusion.66
  303.1 4.5 convolution_convert_fusion
  307.9 5.7 multiply_convert_fusion.1
  324.9 4.9 collective-permute-start.38
  329.9 3.5 convolution_convert_fusion.1
  336.9 7.5 %conv_back.1 = (f32[384,512]{1,0:T(8,128)S(1)}, f32[31,512]{1,0:T(8,128)S(1)}) custom-call(s32[3]{0:T(128)S(1)} %pad_add_fusion.info_ref.refs_0_, bf16[16,512]{1,0:T(8,128)(2,1)S(1)} %collective-permute-done.28.refs_1_, bf16[384,512]{1,0:T(8,128)(2,1)S(1)} %multiply_convert_fusion.12.refs_2_, bf16[16,512]{1,0:T(8,128)(2,1)S(1)} %collective-permute-done.29.refs_3_, ...), custom_call_target="tpu_custom_call" | custom-call | flops 24379392 | bytes 1572864 | tf_op jit(solution)/shard_map/conv_back/pallas_call | solution.py:304
  357.1 2.6 convolution_convert_fusion.4
  377.6 25.6 %attend_back.1 = (bf16[384,512]{1,0:T(8,128)(2,1)S(1)}, f32[768,512]{1,0:T(8,128)S(1)}, f32[768,512]{1,0:T(8,128)}, f32[8,1,1536]{2,1,0:T(1,128)S(1)}) custom-call(s32[3]{0:T(128)S(1)} %pad_add_fusion.info_ref.refs_0_, f32[8,1,1536]{2,1,0:T(1,128)S(1)} %copy-done.2, bf16[384,512]{1,0:T(8,128)(2,1)S(1)} %slice.481.query_ref, bf16[768,1024]{1,0:T(8,128)(2,1)} %copy-done, ...), custom_call_target="tpu_custom_call" | custom-call | flops 1509949440 | bytes 2359296 | tf_op jit(solution)/shard_map/attend_back/pallas_call | solution.py:169
  410.3 13.8 %collective-permute-done.46 = bf16[384,1024]{1,0:T(8,128)(2,1)S(1)} collective-permute-done((bf16[384,1024]{1,0:T(8,128)(2,1)S(1)}, bf16[384,1024]{1,0:T(8,128)(2,1)S(1)}, u32[]{:S(2)}, u32[]{:S(2)}) %collective-permute-start.46) | collective-permute-done | bytes 786464 | tf_op jit(solution)/shard_map/ppermute | solution.py:349
  427.2 3.8 fusion.160
  432.4 3.6 convolution_convert_fusion.2
  445.3 2.9 fusion.14
  449.2 5.5 multiply_convert_fusion
  457.4 2.9 convolution_convert_fusion.5
  460.3 3.0 convolution_convert_fusion.7
  466.8 6.0 collective-permute-done.52
  473.9 2.6 fusion
  491.0 15.4 %collective-permute-done.53 = bf16[512,1024]{1,0:T(8,128)(2,1)} collective-permute-done((bf16[512,1024]{1,0:T(8,128)(2,1)}, bf16[512,1024]{1,0:T(8,128)(2,1)}, u32[]{:S(2)}, u32[]{:S(2)}) %collective-permute-start.53) | collective-permute-done | bytes 1048608 | tf_op jit(solution)/shard_map/ppermute | solution.py:349
  511.3 3.7 collective-permute-done.69
  523.3 10.1 %collective-permute-done.58 = bf16[256,1024]{1,0:T(8,128)(2,1)S(1)} collective-permute-done((bf16[256,1024]{1,0:T(8,128)(2,1)S(1)}, bf16[256,1024]{1,0:T(8,128)(2,1)S(1)}, u32[]{:S(2)}, u32[]{:S(2)}) %collective-permute-start.58) | collective-permute-done | bytes 524320 | tf_op jit(solution)/shard_map/ppermute | solution.py:349
  538.5 14.5 %collective-permute-done.56 = bf16[512,1024]{1,0:T(8,128)(2,1)} collective-permute-done((bf16[512,1024]{1,0:T(8,128)(2,1)}, bf16[512,1024]{1,0:T(8,128)(2,1)}, u32[]{:S(2)}, u32[]{:S(2)}) %collective-permute-start.56) | collective-permute-done | bytes 1048608 | tf_op jit(solution)/shard_map/ppermute | solution.py:349
  554.1 2.6 fusion.13
  556.8 2.4 fusion.12
  565.4 3.3 collective-permute-done.60
  568.7 3.7 collective-permute-done.61
  577.3 2.8 reduce-scatter.15.cloned.1.call-done
  583.4 4.7 collective-permute-done.66
  588.2 4.1 collective-permute-done.71
  595.8 14.4 %reduce-scatter.17.cloned.1.call-done = bf16[1,144,1024]{2,1,0:T(8,128)(2,1)} async-done(((bf16[4,144,1024]{2,1,0:T(8,128)(2,1)}), bf16[1,144,1024]{2,1,0:T(8,128)(2,1)}) %reduce-scatter.17.cloned.1.call-update) | async-done | bytes 294928 | tf_op jit(solution)/shard_map/reduce_scatter | solution.py:688
  (713 shorter events, 272.6 us)
Async XLA Ops:
  7.2 38.0 %all-gather.11.cloned.1.call-start = ((), (), s32[]{:S(2)}) async-start(), calls=%async_computation.13 | async-start | bytes 1310720 | tf_op jit(solution)/shard_map/all_gather | solution.py:570
  10.4 14.9 %collective-permute-start.7 = (bf16[256,1024]{1,0:T(8,128)(2,1)S(1)}, bf16[256,1024]{1,0:T(8,128)(2,1)S(1)}, u32[]{:S(2)}, u32[]{:S(2)}) collective-permute-start(bf16[256,1024]{1,0:T(8,128)(2,1)S(1)} %get-tuple-element.323), channel_id=1, source_target_pairs={{0,4},{4,0},{1,5},{5,1},{2,6},{6,2},{3,7},{7,3},{8,12},{12,8},{9,1... | collective-permute-start | bytes 1572872 | tf_op jit(solution)/shard_map/ppermute | solution.py:349
  13.4 13.4 %collective-permute-start.8 = (bf16[256,1024]{1,0:T(8,128)(2,1)S(1)}, bf16[256,1024]{1,0:T(8,128)(2,1)S(1)}, u32[]{:S(2)}, u32[]{:S(2)}) collective-permute-start(bf16[256,1024]{1,0:T(8,128)(2,1)S(1)} %get-tuple-element.323), channel_id=1, source_target_pairs={{0,2},{2,0},{1,3},{3,1},{4,6},{6,4},{5,7},{7,5},{8,10},{10,8},{9,1... | collective-permute-start | bytes 1572872 | tf_op jit(solution)/shard_map/ppermute | solution.py:349
  15.3 60.8 %all-gather.9.cloned.1.call-start = ((), (), s32[]{:S(2)}) async-start(), calls=%async_computation.12 | async-start | bytes 1474560 | tf_op jit(solution)/shard_map/all_gather | solution.py:570
  29.3 91.5 %all-gather.13.cloned.1.call-start = ((), (), s32[]{:S(2)}) async-start(), calls=%async_computation.14 | async-start | bytes 2293760 | tf_op jit(solution)/shard_map/all_gather | solution.py:570
  33.0 14.1 %collective-permute-start.10 = (bf16[32,1536]{1,0:T(8,128)(2,1)}, bf16[32,1536]{1,0:T(8,128)(2,1)}, u32[]{:S(2)}, u32[]{:S(2)}) collective-permute-start(bf16[32,1536]{1,0:T(8,128)(2,1)} %bitcast.201), channel_id=1, source_target_pairs={{0,1},{1,0},{2,3},{3,2},{4,5},{5,4},{6,7},{7,6},{8,9},{9,8},{10,11... | collective-permute-start | bytes 294920 | tf_op jit(solution)/shard_map/ppermute | solution.py:349
  45.2 24.2 %collective-permute-start.13 = (bf16[512,1024]{0,1:T(8,128)(2,1)}, bf16[512,1024]{0,1:T(8,128)(2,1)}, u32[]{:S(2)}, u32[]{:S(2)}) collective-permute-start(bf16[512,1024]{0,1:T(8,128)(2,1)} %all-gather.11.cloned.1.call-done), channel_id=1, source_target_pairs={{0,2},{2,0},{1,3},{3,1},{4,6},{6,4},{5,7},{7,5},{8,10},{10,8},{9,1... | collective-permute-start | bytes 3145736 | tf_op jit(solution)/shard_map/ppermute | solution.py:349
  45.7 25.0 %collective-permute-start.12 = (bf16[512,1024]{0,1:T(8,128)(2,1)}, bf16[512,1024]{0,1:T(8,128)(2,1)S(1)}, u32[]{:S(2)}, u32[]{:S(2)}) collective-permute-start(bf16[512,1024]{0,1:T(8,128)(2,1)} %all-gather.11.cloned.1.call-done), channel_id=1, source_target_pairs={{0,4},{4,0},{1,5},{5,1},{2,6},{6,2},{3,7},{7,3},{8,12},{12,8},{9,1... | collective-permute-start | bytes 3145736 | tf_op jit(solution)/shard_map/ppermute | solution.py:349
  70.7 214.1 %all-gather.15.cloned.1.call-start = ((), (), s32[]{:S(2)}) async-start(), calls=%async_computation.15 | async-start | bytes 10485760 | tf_op jit(solution)/shard_map/all_gather | solution.py:570
  79.0 15.5 %collective-permute-start.5 = (bf16[4,16,1024]{2,1,0:T(8,128)(2,1)}, bf16[4,16,1024]{2,1,0:T(8,128)(2,1)}, u32[]{:S(2)}, u32[]{:S(2)}) collective-permute-start(bf16[4,16,1024]{2,1,0:T(8,128)(2,1)} %slice.457), channel_id=1, source_target_pairs={{0,6},{6,0},{2,4},{4,2},{1,7},{7,1},{3,5},{5,3},{8,14},{14,8},{10,... | collective-permute-start | bytes 393224 | tf_op jit(solution)/shard_map/ppermute | solution.py:592
  81.5 13.7 %collective-permute-start.4 = (bf16[4,16,1024]{2,1,0:T(8,128)(2,1)}, bf16[4,16,1024]{2,1,0:T(8,128)(2,1)}, u32[]{:S(2)}, u32[]{:S(2)}) collective-permute-start(bf16[4,16,1024]{2,1,0:T(8,128)(2,1)} %slice.457), channel_id=1, source_target_pairs={{0,2},{2,0},{1,3},{3,1},{4,6},{6,4},{5,7},{7,5},{8,10},{10,8},{9,1... | collective-permute-start | bytes 393224 | tf_op jit(solution)/shard_map/ppermute | solution.py:349
  82.0 13.1 %collective-permute-start.3 = (bf16[4,16,1024]{2,1,0:T(8,128)(2,1)}, bf16[4,16,1024]{2,1,0:T(8,128)(2,1)}, u32[]{:S(2)}, u32[]{:S(2)}) collective-permute-start(bf16[4,16,1024]{2,1,0:T(8,128)(2,1)} %slice.457), channel_id=1, source_target_pairs={{0,4},{4,0},{1,5},{5,1},{2,6},{6,2},{3,7},{7,3},{8,12},{12,8},{9,1... | collective-permute-start | bytes 393224 | tf_op jit(solution)/shard_map/ppermute | solution.py:349
  82.6 27.7 %collective-permute-start.2 = (bf16[512,1024]{1,0:T(8,128)(2,1)S(1)}, bf16[512,1024]{1,0:T(8,128)(2,1)}, u32[]{:S(2)}, u32[]{:S(2)}) collective-permute-start(bf16[512,1024]{1,0:T(8,128)(2,1)S(1)} %bitcast.396), channel_id=1, source_target_pairs={{0,2},{2,0},{1,3},{3,1},{4,6},{6,4},{5,7},{7,5},{8,10},{10,8},{9,1... | collective-permute-start | bytes 3145736 | tf_op jit(solution)/shard_map/ppermute | solution.py:349
  84.0 27.9 %collective-permute-start.1 = (bf16[512,1024]{1,0:T(8,128)(2,1)S(1)}, bf16[512,1024]{1,0:T(8,128)(2,1)}, u32[]{:S(2)}, u32[]{:S(2)}) collective-permute-start(bf16[512,1024]{1,0:T(8,128)(2,1)S(1)} %bitcast.397), channel_id=1, source_target_pairs={{0,4},{4,0},{1,5},{5,1},{2,6},{6,2},{3,7},{7,3},{8,12},{12,8},{9,1... | collective-permute-start | bytes 3145736 | tf_op jit(solution)/shard_map/ppermute | solution.py:349
  94.6 39.9 %collective-permute-start.14 = (bf16[512,1024]{0,1:T(8,128)(2,1)}, bf16[512,1024]{0,1:T(8,128)(2,1)}, u32[]{:S(2)}, u32[]{:S(2)}) collective-permute-start(bf16[512,1024]{0,1:T(8,128)(2,1)} %collective-permute-done.13), channel_id=1, source_target_pairs={{0,4},{4,0},{1,5},{5,1},{2,6},{6,2},{3,7},{7,3},{8,12},{12,8},{9,1... | collective-permute-start | bytes 3145736 | tf_op jit(solution)/shard_map/ppermute | solution.py:349
  119.1 23.1 %collective-permute-start.15 = (bf16[512,1024]{1,0:T(8,128)(2,1)}, bf16[512,1024]{1,0:T(8,128)(2,1)}, u32[]{:S(2)}, u32[]{:S(2)}) collective-permute-start(bf16[512,1024]{1,0:T(8,128)(2,1)} %collective-permute-done.1), channel_id=1, source_target_pairs={{0,2},{2,0},{1,3},{3,1},{4,6},{6,4},{5,7},{7,5},{8,10},{10,8},{9,1... | collective-permute-start | bytes 3145736 | tf_op jit(solution)/shard_map/ppermute | solution.py:349
  124.7 24.9 %collective-permute-start.16 = (bf16[4,64,1536]{2,1,0:T(8,128)(2,1)S(1)}, bf16[4,64,1536]{2,1,0:T(8,128)(2,1)}, u32[]{:S(2)}, u32[]{:S(2)}) collective-permute-start(bf16[4,64,1536]{2,1,0:T(8,128)(2,1)S(1)} %reshape.683), channel_id=1, source_target_pairs={{0,4},{4,0},{1,5},{5,1},{2,6},{6,2},{3,7},{7,3},{8,12},{12,8},{9,1... | collective-permute-start | bytes 2359304 | tf_op jit(solution)/shard_map/ppermute | solution.py:349
  127.1 32.9 %collective-permute-start.6 = (bf16[192,1024]{1,0:T(8,128)(2,1)}, bf16[192,1024]{1,0:T(8,128)(2,1)}, u32[]{:S(2)}, u32[]{:S(2)}) collective-permute-start(bf16[192,1024]{1,0:T(8,128)(2,1)} %fusion.26), channel_id=1, source_target_pairs={{0,1},{1,0},{2,3},{3,2},{4,5},{5,4},{6,7},{7,6},{8,9},{9,8},{10,11... | collective-permute-start | bytes 1179656 | tf_op jit(solution)/shard_map/ppermute | solution.py:349
  132.1 292.2 %reduce-scatter.7.cloned.1.call-start = ((), (), s32[]{:S(2)}) async-start(), calls=%async_computation.6 | async-start | bytes 5242880 | tf_op jit(solution)/shard_map/reduce_scatter | solution.py:688
  152.7 18.1 %collective-permute-start.18 = (bf16[4,64,1536]{2,1,0:T(8,128)(2,1)S(1)}, bf16[4,64,1536]{2,1,0:T(8,128)(2,1)}, u32[]{:S(2)}, u32[]{:S(2)}) collective-permute-start(bf16[4,64,1536]{2,1,0:T(8,128)(2,1)S(1)} %reshape.683), channel_id=1, source_target_pairs={{0,2},{2,0},{1,3},{3,1},{4,6},{6,4},{5,7},{7,5},{8,10},{10,8},{9,1... | collective-permute-start | bytes 2359304 | tf_op jit(solution)/shard_map/ppermute | solution.py:349
  153.6 46.8 %collective-permute-start.21 = (bf16[4,128,1024]{2,1,0:T(8,128)(2,1)}, bf16[4,128,1024]{2,1,0:T(8,128)(2,1)S(1)}, u32[]{:S(2)}, u32[]{:S(2)}) collective-permute-start(bf16[4,128,1024]{2,1,0:T(8,128)(2,1)} %slice.360), channel_id=1, source_target_pairs={{0,4},{4,0},{1,5},{5,1},{2,6},{6,2},{3,7},{7,3},{8,12},{12,8},{9,1... | collective-permute-start | bytes 3145736 | tf_op jit(solution)/shard_map/ppermute | solution.py:349
  170.9 23.0 %collective-permute-start.20 = (bf16[4,64,1536]{2,1,0:T(8,128)(2,1)}, bf16[4,64,1536]{2,1,0:T(8,128)(2,1)S(1)}, u32[]{:S(2)}, u32[]{:S(2)}) collective-permute-start(bf16[4,64,1536]{2,1,0:T(8,128)(2,1)} %collective-permute-done.18), channel_id=1, source_target_pairs={{0,4},{4,0},{1,5},{5,1},{2,6},{6,2},{3,7},{7,3},{8,12},{12,8},{9,1... | collective-permute-start | bytes 2359304 | tf_op jit(solution)/shard_map/ppermute | solution.py:349
  175.0 26.3 %collective-permute-start.22 = (bf16[4,128,1024]{2,1,0:T(8,128)(2,1)}, bf16[4,128,1024]{2,1,0:T(8,128)(2,1)S(1)}, u32[]{:S(2)}, u32[]{:S(2)}) collective-permute-start(bf16[4,128,1024]{2,1,0:T(8,128)(2,1)} %slice.360), channel_id=1, source_target_pairs={{0,2},{2,0},{1,3},{3,1},{4,6},{6,4},{5,7},{7,5},{8,10},{10,8},{9,1... | collective-permute-start | bytes 3145736 | tf_op jit(solution)/shard_map/ppermute | solution.py:349
  202.4 18.8 %collective-permute-start.23 = (bf16[384,1024]{1,0:T(8,128)(2,1)S(1)}, bf16[384,1024]{1,0:T(8,128)(2,1)}, u32[]{:S(2)}, u32[]{:S(2)}) collective-permute-start(bf16[384,1024]{1,0:T(8,128)(2,1)S(1)} %slice.482), channel_id=1, source_target_pairs={{0,2},{2,0},{1,3},{3,1},{4,6},{6,4},{5,7},{7,5},{8,10},{10,8},{9,1... | collective-permute-start | bytes 2359304 | tf_op jit(solution)/shard_map/ppermute | solution.py:349
  204.8 42.1 %collective-permute-start.24 = (bf16[4,128,1024]{2,1,0:T(8,128)(2,1)}, bf16[4,128,1024]{2,1,0:T(8,128)(2,1)S(1)}, u32[]{:S(2)}, u32[]{:S(2)}) collective-permute-start(bf16[4,128,1024]{2,1,0:T(8,128)(2,1)} %copy-done.51), channel_id=1, source_target_pairs={{0,4},{4,0},{1,5},{5,1},{2,6},{6,2},{3,7},{7,3},{8,12},{12,8},{9,1... | collective-permute-start | bytes 3145736 | tf_op jit(solution)/shard_map/ppermute | solution.py:349
  307.6 128.4 %reduce-scatter.9.cloned.1.call-start = ((), (), s32[]{:S(2)}) async-start(), calls=%async_computation.7 | async-start | bytes 2621440 | tf_op jit(solution)/shard_map/reduce_scatter | solution.py:688
  323.6 13.3 %collective-permute-start.39 = (bf16[16,512]{1,0:T(8,128)(2,1)S(1)}, bf16[16,512]{1,0:T(8,128)(2,1)S(1)}, u32[]{:S(2)}, u32[]{:S(2)}) collective-permute-start(bf16[16,512]{1,0:T(8,128)(2,1)S(1)} %get-tuple-element.328), channel_id=1, source_target_pairs={{2,0},{3,1},{6,4},{7,5},{10,8},{11,9},{14,12},{15,13},{18,16},{19,... | collective-permute-start | bytes 49160 | tf_op jit(solution)/shard_map/ppermute | solution.py:507
  359.8 146.7 %reduce-scatter.11.cloned.1.call-start = ((), (), s32[]{:S(2)}) async-start(), calls=%async_computation.8 | async-start | bytes 3932160 | tf_op jit(solution)/shard_map/reduce_scatter | solution.py:688
  362.3 40.9 %collective-permute-start.42 = (bf16[4,2,32,1024]{3,2,0,1:T(8,128)(2,1)}, bf16[4,2,32,1024]{3,2,0,1:T(8,128)(2,1)}, u32[]{:S(2)}, u32[]{:S(2)}) collective-permute-start(bf16[4,2,32,1024]{3,2,0,1:T(8,128)(2,1)} %bitcast.377), channel_id=1, source_target_pairs={{0,2},{2,0},{1,3},{3,1},{4,6},{6,4},{5,7},{7,5},{8,10},{10,8},{9,1... | collective-permute-start | bytes 1572872 | tf_op jit(solution)/shard_map/ppermute | solution.py:349
  362.3 63.9 %collective-permute-start.45 = (bf16[4,2,128,1024]{3,2,0,1:T(8,128)(2,1)}, bf16[4,2,128,1024]{3,2,0,1:T(8,128)(2,1)}, u32[]{:S(2)}, u32[]{:S(2)}) collective-permute-start(bf16[4,2,128,1024]{3,2,0,1:T(8,128)(2,1)} %copy.251), channel_id=1, source_target_pairs={{0,4},{4,0},{1,5},{5,1},{2,6},{6,2},{3,7},{7,3},{8,12},{12,8},{9,1... | collective-permute-start | bytes 6291464 | tf_op jit(solution)/shard_map/ppermute | solution.py:349
  365.1 38.1 %collective-permute-start.44 = (bf16[4,2,32,1024]{3,2,1,0:T(8,128)(2,1)}, bf16[4,2,32,1024]{3,2,1,0:T(8,128)(2,1)}, u32[]{:S(2)}, u32[]{:S(2)}) collective-permute-start(bf16[4,2,32,1024]{3,2,1,0:T(8,128)(2,1)} %dynamic-slice_bitcast_fusion), channel_id=1, source_target_pairs={{0,2},{2,0},{1,3},{3,1},{4,6},{6,4},{5,7},{7,5},{8,10},{10,8},{9,1... | collective-permute-start | bytes 1572872 | tf_op jit(solution)/shard_map/ppermute | solution.py:349
  405.2 18.8 %collective-permute-start.46 = (bf16[384,1024]{1,0:T(8,128)(2,1)S(1)}, bf16[384,1024]{1,0:T(8,128)(2,1)S(1)}, u32[]{:S(2)}, u32[]{:S(2)}) collective-permute-start(bf16[384,1024]{1,0:T(8,128)(2,1)S(1)} %fusion.37), channel_id=1, source_target_pairs={{0,2},{2,0},{1,3},{3,1},{4,6},{6,4},{5,7},{7,5},{8,10},{10,8},{9,1... | collective-permute-start | bytes 2359304 | tf_op jit(solution)/shard_map/ppermute | solution.py:349
  436.0 117.0 %reduce-scatter.13.cloned.1.call-start = ((), (), s32[]{:S(2)}) async-start(), calls=%async_computation.9 | async-start | bytes 1966080 | tf_op jit(solution)/shard_map/reduce_scatter | solution.py:688
  441.9 24.9 %collective-permute-start.50 = (bf16[4,32,1024]{2,1,0:T(8,128)(2,1)}, bf16[4,32,1024]{2,1,0:T(8,128)(2,1)}, u32[]{:S(2)}, u32[]{:S(2)}) collective-permute-start(bf16[4,32,1024]{2,1,0:T(8,128)(2,1)} %dynamic-slice_bitcast_fusion.6), channel_id=1, source_target_pairs={{0,4},{4,0},{1,5},{5,1},{2,6},{6,2},{3,7},{7,3},{8,12},{12,8},{9,1... | collective-permute-start | bytes 786440 | tf_op jit(solution)/shard_map/ppermute | solution.py:349
  443.3 23.5 %collective-permute-start.51 = (bf16[4,32,1024]{2,1,0:T(8,128)(2,1)}, bf16[4,32,1024]{2,1,0:T(8,128)(2,1)}, u32[]{:S(2)}, u32[]{:S(2)}) collective-permute-start(bf16[4,32,1024]{2,1,0:T(8,128)(2,1)} %dynamic-slice_bitcast_fusion.5), channel_id=1, source_target_pairs={{0,4},{4,0},{1,5},{5,1},{2,6},{6,2},{3,7},{7,3},{8,12},{12,8},{9,1... | collective-permute-start | bytes 786440 | tf_op jit(solution)/shard_map/ppermute | solution.py:349
  443.9 47.1 %collective-permute-start.55 = (bf16[2,128,1024]{2,1,0:T(8,128)(2,1)}, bf16[2,128,1024]{2,1,0:T(8,128)(2,1)}, u32[]{:S(2)}, u32[]{:S(2)}) collective-permute-start(bf16[2,128,1024]{2,1,0:T(8,128)(2,1)} %slice_bitcast_fusion.2), channel_id=1, source_target_pairs={{0,4},{4,0},{1,5},{5,1},{2,6},{6,2},{3,7},{7,3},{8,12},{12,8},{9,1... | collective-permute-start | bytes 1572872 | tf_op jit(solution)/shard_map/ppermute | solution.py:349
  448.2 24.6 %collective-permute-start.52 = (bf16[4,128,1024]{2,1,0:T(8,128)(2,1)}, bf16[4,128,1024]{2,1,0:T(8,128)(2,1)}, u32[]{:S(2)}, u32[]{:S(2)}) collective-permute-start(bf16[4,128,1024]{2,1,0:T(8,128)(2,1)} %fusion.14), channel_id=1, source_target_pairs={{0,2},{2,0},{1,3},{3,1},{4,6},{6,4},{5,7},{7,5},{8,10},{10,8},{9,1... | collective-permute-start | bytes 3145736 | tf_op jit(solution)/shard_map/ppermute | solution.py:349
  457.4 24.4 %collective-permute-start.49 = (bf16[192,1024]{1,0:T(8,128)(2,1)}, bf16[192,1024]{1,0:T(8,128)(2,1)S(1)}, u32[]{:S(2)}, u32[]{:S(2)}) collective-permute-start(bf16[192,1024]{1,0:T(8,128)(2,1)} %slice.646), channel_id=1, source_target_pairs={{0,1},{1,0},{2,3},{3,2},{4,5},{5,4},{6,7},{7,6},{8,9},{9,8},{10,11... | collective-permute-start | bytes 1179656 | tf_op jit(solution)/shard_map/ppermute | solution.py:349
  477.2 31.6 %collective-permute-start.68 = (bf16[2,64,1024]{2,1,0:T(8,128)(2,1)}, bf16[2,64,1024]{2,1,0:T(8,128)(2,1)}, u32[]{:S(2)}, u32[]{:S(2)}) collective-permute-start(bf16[2,64,1024]{2,1,0:T(8,128)(2,1)} %dynamic-slice_bitcast_fusion.4), channel_id=1, source_target_pairs={{0,4},{4,0},{1,5},{5,1},{2,6},{6,2},{3,7},{7,3},{8,12},{12,8},{9,1... | collective-permute-start | bytes 786440 | tf_op jit(solution)/shard_map/ppermute | solution.py:349
  477.9 28.6 %collective-permute-start.53 = (bf16[512,1024]{1,0:T(8,128)(2,1)}, bf16[512,1024]{1,0:T(8,128)(2,1)}, u32[]{:S(2)}, u32[]{:S(2)}) collective-permute-start(bf16[512,1024]{1,0:T(8,128)(2,1)} %convolution_convert_fusion.8), channel_id=1, source_target_pairs={{0,4},{4,0},{1,5},{5,1},{2,6},{6,2},{3,7},{7,3},{8,12},{12,8},{9,1... | collective-permute-start | bytes 3145736 | tf_op jit(solution)/shard_map/ppermute | solution.py:349
  479.2 27.3 %collective-permute-start.54 = (bf16[512,1024]{1,0:T(8,128)(2,1)}, bf16[512,1024]{1,0:T(8,128)(2,1)}, u32[]{:S(2)}, u32[]{:S(2)}) collective-permute-start(bf16[512,1024]{1,0:T(8,128)(2,1)} %convolution_convert_fusion.7), channel_id=1, source_target_pairs={{0,2},{2,0},{1,3},{3,1},{4,6},{6,4},{5,7},{7,5},{8,10},{10,8},{9,1... | collective-permute-start | bytes 3145736 | tf_op jit(solution)/shard_map/ppermute | solution.py:349
  489.2 19.5 %collective-permute-start.63 = (f32[4,2,1216]{2,1,0:T(2,128)S(1)}, f32[4,2,1216]{2,1,0:T(2,128)S(1)}, u32[]{:S(2)}, u32[]{:S(2)}) collective-permute-start(f32[4,2,1216]{2,1,0:T(2,128)S(1)} %bitcast.471), channel_id=1, source_target_pairs={{0,2},{2,0},{1,3},{3,1},{4,6},{6,4},{5,7},{7,5},{8,10},{10,8},{9,1... | collective-permute-start | bytes 116744 | tf_op jit(solution)/shard_map/ppermute | solution.py:349
  506.5 73.6 %reduce-scatter.15.cloned.1.call-start = ((), (), s32[]{:S(2)}) async-start(), calls=%async_computation.10 | async-start | bytes 1310720 | tf_op jit(solution)/shard_map/reduce_scatter | solution.py:688
  518.5 14.9 %collective-permute-start.58 = (bf16[256,1024]{1,0:T(8,128)(2,1)S(1)}, bf16[256,1024]{1,0:T(8,128)(2,1)S(1)}, u32[]{:S(2)}, u32[]{:S(2)}) collective-permute-start(bf16[256,1024]{1,0:T(8,128)(2,1)S(1)} %fusion.10), channel_id=1, source_target_pairs={{0,2},{2,0},{1,3},{3,1},{4,6},{6,4},{5,7},{7,5},{8,10},{10,8},{9,1... | collective-permute-start | bytes 1572872 | tf_op jit(solution)/shard_map/ppermute | solution.py:349
  518.9 14.9 %collective-permute-start.59 = (bf16[256,1024]{1,0:T(8,128)(2,1)S(1)}, bf16[256,1024]{1,0:T(8,128)(2,1)S(1)}, u32[]{:S(2)}, u32[]{:S(2)}) collective-permute-start(bf16[256,1024]{1,0:T(8,128)(2,1)S(1)} %fusion.11), channel_id=1, source_target_pairs={{0,4},{4,0},{1,5},{5,1},{2,6},{6,2},{3,7},{7,3},{8,12},{12,8},{9,1... | collective-permute-start | bytes 1572872 | tf_op jit(solution)/shard_map/ppermute | solution.py:349
  519.9 33.2 %collective-permute-start.56 = (bf16[512,1024]{1,0:T(8,128)(2,1)}, bf16[512,1024]{1,0:T(8,128)(2,1)}, u32[]{:S(2)}, u32[]{:S(2)}) collective-permute-start(bf16[512,1024]{1,0:T(8,128)(2,1)} %convolution_convert_fusion.6), channel_id=1, source_target_pairs={{0,4},{4,0},{1,5},{5,1},{2,6},{6,2},{3,7},{7,3},{8,12},{12,8},{9,1... | collective-permute-start | bytes 3145736 | tf_op jit(solution)/shard_map/ppermute | solution.py:349
  521.1 32.0 %collective-permute-start.57 = (bf16[512,1024]{1,0:T(8,128)(2,1)}, bf16[512,1024]{1,0:T(8,128)(2,1)}, u32[]{:S(2)}, u32[]{:S(2)}) collective-permute-start(bf16[512,1024]{1,0:T(8,128)(2,1)} %convolution_convert_fusion.5), channel_id=1, source_target_pairs={{0,2},{2,0},{1,3},{3,1},{4,6},{6,4},{5,7},{7,5},{8,10},{10,8},{9,1... | collective-permute-start | bytes 3145736 | tf_op jit(solution)/shard_map/ppermute | solution.py:349
  553.1 57.2 %reduce-scatter.17.cloned.1.call-start = ((), (), s32[]{:S(2)}) async-start(), calls=%async_computation.11 | async-start | bytes 1474560 | tf_op jit(solution)/shard_map/reduce_scatter | solution.py:688
  (156 other events, 1067.4 us)
Sparse Core Ops, SparseCore 0:
  15.5 29.6 all-gather.10
  47.3 28.7 all-gather.8
  77.7 40.5 all-gather.12
  132.2 148.0 all-gather.14
  307.8 77.2 reduce-scatter.6
  387.3 44.3 reduce-scatter.8
  436.2 59.9 reduce-scatter.10
  506.6 34.3 reduce-scatter.12
  553.2 26.8 reduce-scatter.14
  582.4 27.8 reduce-scatter.16

commit v4 on v3

--- a/solution.py
+++ b/solution.py
@@ -17,26 +17,23 @@
     return lax.dot_general(left, right, (dims, ((), ())), preferred_element_type=jnp.float32)
 
 
-def spread_bias(info_ref, bias_ref, spread_ref):
-    width = spread_ref.shape[1]
-    row = jnp.broadcast_to(bias_ref[0], (ROWS, width))
-    spread_ref[...] = pltpu.roll(row, 0, 1, stride=1, stride_axis=0)
-
-
-def half_mask(rows):
+def spread_of(bias):
+    row = jnp.broadcast_to(bias, (ROWS, bias.shape[1]))
+    return pltpu.roll(row, 0, 1, stride=1, stride_axis=0)
+
+
+def half_mask(rows, half):
     lane = lax.broadcasted_iota(jnp.int32, (rows, 2 * HD), 1)
-    start = lax.rem(pl.program_id(0), 2) * HD
-    return (lane >= start) & (lane < start + HD)
+    return lane < HD if half == 0 else lane >= HD
 
 
 def segment_at(position, first_end, second_end):
     return (position >= first_end).astype(jnp.int32) + (position >= second_end).astype(jnp.int32)
 
 
-def weights_of(info_ref, spread_ref, query, keys, number):
-    group = keys.shape[0]
+def weights_of(info_ref, spread_ref, raw, number):
+    group = raw.shape[1]
     first_end, second_end, start = info_ref[0], info_ref[1], info_ref[2]
-    raw = matmul_in(query, keys, ((1,), (1,)))
     shift = pl.multiple_of(group - start - number * ROWS, ROWS)
     bias = spread_ref[:, pl.ds(shift, group)]
     row = start + number * ROWS + lax.broadcasted_iota(jnp.int32, (ROWS, 1), 0)
@@ -47,18 +44,20 @@
     return raised * (1.0 / jnp.sum(raised, axis=1, keepdims=True))
 
 
-def attend_kernel(info_ref, bias_ref, query_ref, key_ref, value_ref, out_ref, spread_ref):
-    spread_bias(info_ref, bias_ref, spread_ref)
-    mask = half_mask(ROWS)
-    first = lax.rem(pl.program_id(0), 2) == 0
-    for number in range(query_ref.shape[0] // ROWS):
-        rows = pl.ds(number * ROWS, ROWS)
-        query = jnp.where(mask, query_ref[rows, :], jnp.bfloat16(0))
-        weights = weights_of(info_ref, spread_ref, query, key_ref[...], number)
-        out = matmul_in(weights.astype(jnp.bfloat16), value_ref[...], ((1,), (0,)))
-        out = out.astype(jnp.bfloat16)
-        kept = jnp.where(first, out, out_ref[rows, :])
-        out_ref[rows, :] = jnp.where(mask, out, kept)
+def attend_kernel(info_ref, bias_ref, query_ref, key_ref, value_ref, out_ref, spread_ref, raw_ref, weight_ref):
+    outs = []
+    for half in range(2):
+        mask = half_mask(query_ref.shape[0], half)
+        query = jnp.where(mask, query_ref[...], jnp.bfloat16(0))
+        raw_ref[half] = matmul_in(query, key_ref[...], ((1,), (1,)))
+        spread_ref[half] = spread_of(bias_ref[0, half : half + 1])
+    for half in range(2):
+        for number in range(query_ref.shape[0] // ROWS):
+            rows = pl.ds(number * ROWS, ROWS)
+            weights = weights_of(info_ref, spread_ref.at[half], raw_ref[half, rows, :], number)
+            weight_ref[half, rows, :] = weights.astype(jnp.bfloat16)
+        outs.append(matmul_in(weight_ref[half], value_ref[...], ((1,), (0,))).astype(jnp.bfloat16))
+    out_ref[...] = jnp.where(half_mask(query_ref.shape[0], 0), outs[0], outs[1])
 
 
 def attend_back_kernel(
@@ -76,62 +75,56 @@
     diag_ref,
     weight_ref,
     score_ref,
-    query_mid_ref,
-    grad_mid_ref,
+    raw_ref,
+    weight_grad_ref,
 ):
-    spread_bias(info_ref, bias_ref, spread_ref)
-    mask = half_mask(ROWS)
-    group, width = key_ref.shape[0], spread_ref.shape[1]
-    first = lax.rem(pl.program_id(0), 2) == 0
+    group, width = key_ref.shape[0], spread_ref.shape[2]
+    outs, key_grads, value_grads = [], [], []
+    for half in range(2):
+        mask = half_mask(query_ref.shape[0], half)
+        query = jnp.where(mask, query_ref[...], jnp.bfloat16(0))
+        grad = jnp.where(mask, grad_ref[...], jnp.bfloat16(0))
+        raw_ref[half] = matmul_in(query, key_ref[...], ((1,), (1,)))
+        weight_grad_ref[half] = matmul_in(grad, value_ref[...], ((1,), (1,)))
+        spread_ref[half] = spread_of(bias_ref[0, half : half + 1])
     diag_ref[...] = jnp.zeros(diag_ref.shape, jnp.float32)
-    for number in range(query_ref.shape[0] // ROWS):
-        rows = pl.ds(number * ROWS, ROWS)
-        query = jnp.where(mask, query_ref[rows, :], jnp.bfloat16(0))
-        grad = jnp.where(mask, grad_ref[rows, :], jnp.bfloat16(0))
-        query_mid_ref[rows, :] = query
-        grad_mid_ref[rows, :] = grad
-        weights = weights_of(info_ref, spread_ref, query, key_ref[...], number)
-        weight_ref[rows, :] = weights.astype(jnp.bfloat16)
-        weight_grad = matmul_in(grad, value_ref[...], ((1,), (1,)))
-        inner = jnp.sum(weights * weight_grad, axis=1, keepdims=True)
-        score_grad = weights * (weight_grad - inner)
-        shift = pl.multiple_of(group - info_ref[2] - number * ROWS, ROWS)
-        diag_ref[:, pl.ds(shift, group)] += score_grad
-        raw_grad = (score_grad * 0.125).astype(jnp.bfloat16)
-        score_ref[rows, :] = raw_grad
-        out = matmul_in(raw_grad, key_ref[...], ((1,), (0,))).astype(jnp.bfloat16)
-        kept = jnp.where(first, out, query_grad_ref[rows, :])
-        query_grad_ref[rows, :] = jnp.where(mask, out, kept)
-    key_grad = matmul_in(score_ref[...], query_mid_ref[...], ((0,), (0,)))
-    value_grad = matmul_in(weight_ref[...], grad_mid_ref[...], ((0,), (0,)))
-
-    @pl.when(first)
-    def _():
-        key_grad_ref[...] = key_grad
-        value_grad_ref[...] = value_grad
-
-    @pl.when(jnp.logical_not(first))
-    def _():
-        key_grad_ref[...] += key_grad
-        value_grad_ref[...] += value_grad
-
-    total = diag_ref[...]
-    size = ROWS // 2
-    while size >= 8:
-        total = total[:size] + pltpu.roll(total[size:], width - size, 1)
-        size //= 2
-    for size in (4, 2, 1):
-        total = total + pltpu.roll(pltpu.roll(total, 8 - size, 0), width - size, 1)
-    sums_ref[0] = total[0:1]
+    for half in range(2):
+        mask = half_mask(query_ref.shape[0], half)
+        query = jnp.where(mask, query_ref[...], jnp.bfloat16(0))
+        grad = jnp.where(mask, grad_ref[...], jnp.bfloat16(0))
+        for number in range(query_ref.shape[0] // ROWS):
+            rows = pl.ds(number * ROWS, ROWS)
+            weights = weights_of(info_ref, spread_ref.at[half], raw_ref[half, rows, :], number)
+            weight_ref[half, rows, :] = weights.astype(jnp.bfloat16)
+            weight_grad = weight_grad_ref[half, rows, :]
+            inner = jnp.sum(weights * weight_grad, axis=1, keepdims=True)
+            score_grad = weights * (weight_grad - inner)
+            shift = pl.multiple_of(group - info_ref[2] - number * ROWS, ROWS)
+            diag_ref[half, :, pl.ds(shift, group)] += score_grad
+            score_ref[half, rows, :] = (score_grad * 0.125).astype(jnp.bfloat16)
+        outs.append(matmul_in(score_ref[half], key_ref[...], ((1,), (0,))).astype(jnp.bfloat16))
+        key_grads.append(matmul_in(score_ref[half], query, ((0,), (0,))))
+        value_grads.append(matmul_in(weight_ref[half], grad, ((0,), (0,))))
+        total = diag_ref[half]
+        size = ROWS // 2
+        while size >= 8:
+            total = total[:size] + pltpu.roll(total[size:], width - size, 1)
+            size //= 2
+        for size in (4, 2, 1):
+            total = total + pltpu.roll(pltpu.roll(total, 8 - size, 0), width - size, 1)
+        sums_ref[0, half : half + 1] = total[0:1]
+    query_grad_ref[...] = jnp.where(half_mask(query_ref.shape[0], 0), outs[0], outs[1])
+    key_grad_ref[...] = key_grads[0] + key_grads[1]
+    value_grad_ref[...] = value_grads[0] + value_grads[1]
 
 
 def attend_specs(rows, group, width, pairs):
     return [
         pl.BlockSpec(memory_space=pltpu.SMEM),
-        pl.BlockSpec((1, 1, width), lambda h: (h, 0, 0)),
-        pl.BlockSpec((rows, 2 * HD), lambda h: (0, h // 2)),
-        pl.BlockSpec((group, 2 * HD), lambda h: (0, h // 2)),
-        pl.BlockSpec((group, 2 * HD), lambda h: (0, pairs + h // 2)),
+        pl.BlockSpec((1, 2, width), lambda h: (h, 0, 0)),
+        pl.BlockSpec((rows, 2 * HD), lambda h: (0, h)),
+        pl.BlockSpec((group, 2 * HD), lambda h: (0, h)),
+        pl.BlockSpec((group, 2 * HD), lambda h: (0, pairs + h)),
     ]
 
 
@@ -144,16 +137,20 @@
 
 
 def attend(info, bias, query, both):
-    heads, _, width = bias.shape
+    pairs, _, width = bias.shape
+    heads = 2 * pairs
     rows, group = query.shape[0], both.shape[0]
-    pairs = heads // 2
     return pl.pallas_call(
         attend_kernel,
-        grid=(heads,),
+        grid=(pairs,),
         in_specs=attend_specs(rows, group, width, pairs),
-        out_specs=pl.BlockSpec((rows, 2 * HD), lambda h: (0, h // 2)),
+        out_specs=pl.BlockSpec((rows, 2 * HD), lambda h: (0, h)),
         out_shape=jax.ShapeDtypeStruct((rows, heads * HD), jnp.bfloat16),
-        scratch_shapes=[pltpu.VMEM((ROWS, width), jnp.float32)],
+        scratch_shapes=[
+            pltpu.VMEM((2, ROWS, width), jnp.float32),
+            pltpu.VMEM((2, rows, group), jnp.float32),
+            pltpu.VMEM((2, rows, group), jnp.bfloat16),
+        ],
         compiler_params=pltpu.CompilerParams(vmem_limit_bytes=VMEM),
         cost_estimate=cost_of(heads, rows, group, 2),
         name="attend",
@@ -161,29 +158,29 @@
 
 
 def attend_back(info, bias, query, both, grad):
-    heads, _, width = bias.shape
+    pairs, _, width = bias.shape
+    heads = 2 * pairs
     rows, group = query.shape[0], both.shape[0]
-    pairs = heads // 2
-    pair_block = pl.BlockSpec((rows, 2 * HD), lambda h: (0, h // 2))
-    group_block = pl.BlockSpec((group, 2 * HD), lambda h: (0, h // 2))
+    pair_block = pl.BlockSpec((rows, 2 * HD), lambda h: (0, h))
+    group_block = pl.BlockSpec((group, 2 * HD), lambda h: (0, h))
     return pl.pallas_call(
         attend_back_kernel,
-        grid=(heads,),
+        grid=(pairs,),
         in_specs=attend_specs(rows, group, width, pairs) + [pair_block],
-        out_specs=[pair_block, group_block, group_block, pl.BlockSpec((1, 1, width), lambda h: (h, 0, 0))],
+        out_specs=[pair_block, group_block, group_block, pl.BlockSpec((1, 2, width), lambda h: (h, 0, 0))],
         out_shape=[
             jax.ShapeDtypeStruct((rows, heads * HD), jnp.bfloat16),
             jax.ShapeDtypeStruct((group, heads * HD), jnp.float32),
             jax.ShapeDtypeStruct((group, heads * HD), jnp.float32),
-            jax.ShapeDtypeStruct((heads, 1, width), jnp.float32),
+            jax.ShapeDtypeStruct((pairs, 2, width), jnp.float32),
         ],
         scratch_shapes=[
-            pltpu.VMEM((ROWS, width), jnp.float32),
-            pltpu.VMEM((ROWS, width), jnp.float32),
-            pltpu.VMEM((rows, group), jnp.bfloat16),
-            pltpu.VMEM((rows, group), jnp.bfloat16),
-            pltpu.VMEM((rows, 2 * HD), jnp.bfloat16),
-            pltpu.VMEM((rows, 2 * HD), jnp.bfloat16),
+            pltpu.VMEM((2, ROWS, width), jnp.float32),
+            pltpu.VMEM((2, ROWS, width), jnp.float32),
+            pltpu.VMEM((2, rows, group), jnp.bfloat16),
+            pltpu.VMEM((2, rows, group), jnp.bfloat16),
+            pltpu.VMEM((2, rows, group), jnp.float32),
+            pltpu.VMEM((2, rows, group), jnp.float32),
         ],
         compiler_params=pltpu.CompilerParams(vmem_limit_bytes=VMEM),
         cost_estimate=cost_of(heads, rows, group, 5),
@@ -595,7 +592,6 @@
         )
         small_full = placed((tiny, tiny_x, tiny_xy, tiny_y)).reshape(chips, -1)
         outer_xy = swap(outer_x, "y")
-        mixed, pack_two = together(mixed, pack_two)
         whole_two = gather_p(pack_two).reshape(chips, 2 * units, width)
         attend_part = mixed[:, : marks[1]].reshape(grid[0], 2 * share, 3 * half)
         rest_part = mixed[:, marks[1] :]
@@ -629,7 +625,7 @@
     info = jnp.stack([lengths[0, 0], lengths[0, 0] + lengths[0, 1], start.astype(jnp.int32)])
     hits = bucket_hits(group)
     bias = jnp.einsum("bh,wb->hw", bias_table, hits.astype(jnp.bfloat16), preferred_element_type=f32)
-    bias = bias[:, None, :]
+    bias = bias.reshape(heads // 2, 2, -1)
 
     hidden = frames.astype(f32)
     first, first_kept = feed_forward(hidden, gain_table[0], inner_one, outer_one)
@@ -728,21 +724,21 @@
     grad_second = grad_third + back_conv
 
     att_out_grad = pair_rows(low(grad_second))
-    glu_sum = last_sum(glu_grad)
+    glu_a = send(glu_grad, "y", 2)
     point_a = send(point_grad, "y", 2)
+    attended_grad = low(right_product(att_out_grad, merge_full))
+    query_grad, key_grad, value_grad, table_sums = attend_back(info, bias, query, both, attended_grad)
+    query_grad, key_grad, value_grad, glu_a, point_a = together(
+        query_grad, key_grad, value_grad, glu_a, point_a
+    )
+    att_out_grad, query_grad = together(att_out_grad, query_grad)
     merge_grad = low(left_product(attended, att_out_grad)).reshape(chips // 2, 2, share, width)
     merge_grad = ordered(
         choose(merge_grad, core, 1)[None], swap(choose(merge_grad, 1 - core, 1))[None], core
     )
     merge_grad = by_chip(merge_grad.reshape(chips * share, width))
-    attended_grad = low(right_product(att_out_grad, merge_full))
-    merge_a = send(merge_grad, "y", 2)
-    query_grad, key_grad, value_grad, table_sums = attend_back(info, bias, query, both, attended_grad)
-    query_grad, key_grad, value_grad, point_a, merge_a = together(
-        query_grad, key_grad, value_grad, point_a, merge_a
-    )
+    glu_half = add(glu_grad, glu_a, "y", 2)
     point_half = add(point_grad, point_a, "y", 2)
-    merge_half = add(merge_grad, merge_a, "y", 2)
     both_grad = jnp.concatenate([key_grad, value_grad], axis=1).reshape(grid[2], pair, width)
     if grid[2] == 2:
         place = lax.axis_index("y")
@@ -752,18 +748,21 @@
         both_received = low(lax.psum_scatter(both_grad, "y", scatter_dimension=0, tiled=False))
         both_grad = both_received
     if square:
-        point_b, merge_b, outer_two_a, inner_two_a, both_grad = together(
+        glu_b, point_b, merge_a, outer_two_a, inner_two_a, both_grad = together(
+            pick(glu_half, "q", 1),
             pick(point_half, "q", 1),
-            pick(merge_half, "q", 1),
+            pick(merge_grad, "q", 1),
             outer_two_sum[1:3],
             inner_two_a,
             both_grad,
         )
         inner_two_b = low(inner_two[:, 3].astype(f32) + inner_two_a[:, 1].astype(f32))
         inner_two_b = swap(inner_two_b, "y")
-        point_b, merge_b, outer_two_a = [swap(part, "q") for part in (point_b, merge_b, outer_two_a)]
+        glu_b, point_b, merge_a, outer_two_a = [
+            swap(part, "q") for part in (glu_b, point_b, merge_a, outer_two_a)
+        ]
     else:
-        point_b, merge_b = send(point_half, "q", 1), send(merge_half, "q", 1)
+        glu_b, point_b, merge_a = [send(part, "q", 1) for part in (glu_half, point_half, merge_grad)]
         inner_two_sum = early_sum(inner_two_grad(0, 8))
     triple_grad = jnp.concatenate([query_grad, both_grad], axis=1)
     attend_grad = low(left_product(att_entry, triple_grad))
@@ -771,7 +770,6 @@
     att_entry_grad = pair_sum(right_product(triple_grad, attend_full))
     back_att, gain_one = norm_back(att_entry_grad, normed_att, inverse_att, gain_table[1])
     grad_first = grad_second + back_att
-    attend_grad, glu_sum = together(attend_grad, glu_sum)
     attend_sum = last_sum(attend_grad)
     if square:
         inner_two_sum = inner_two[:, 0].astype(f32) + inner_two_a[:, 0].astype(f32)
@@ -779,20 +777,23 @@
         grad_first, gain_table[0], inner_one, outer_one, first_kept
     )
     if square:
-        near_o, near_i, point_b, merge_b, inner_two_b, glu_sum = together(
+        near_o, near_i, glu_b, point_b, merge_a, inner_two_b = together(
             low(outer_one_grad(1, 3)),
             low(inner_one_grad(2, 4)),
+            glu_b,
             point_b,
-            merge_b,
+            merge_a,
             inner_two_b,
-            glu_sum,
         )
         near_o, near_i = swap(near_o, "q"), swap(near_i, "y")
         inner_two_sum = low(inner_two_sum + inner_two_b.astype(f32))
+    merge_half = add(merge_grad, merge_a, "q", 1)
+    merge_b = send(merge_half, "y", 1)
     mixed_sum = jnp.concatenate(
         [
+            add(glu_half, glu_b, "q", 1),
             add(point_half, point_b, "q", 1),
-            add(merge_half, merge_b, "q", 1),
+            add(merge_half, merge_b, "y", 1),
         ]
         + ([inner_two_sum] if square else []),
         axis=1,
@@ -807,7 +808,6 @@
             outer_two_a,
             attend_sum,
         )
-        glu_a = swap(pick(glu_sum, "q", 0), "q")
         far_o, far_i = swap(far_o, "q"), swap(far_i, "y")
         mixed_sum = last_sum(mixed_sum)
 
@@ -824,33 +824,34 @@
             return [part.reshape(grid[0], units // 2, width) for part in sums]
 
         near = second(0, near_o, near_i)
-        near = together(swap(near[0], "y"), swap(near[1], "q"))
+        *near, far_o, far_i = together(swap(near[0], "y"), swap(near[1], "q"), far_o, far_i)
         near = jnp.concatenate(third(0, near_o, near_i, *near), axis=1)
-        far_o, far_i, near, mixed_sum = together(far_o, far_i, near, mixed_sum)
+        near, mixed_sum = together(near, mixed_sum)
         near_sum = last_sum(near)
+        far_o, attend_sum = together(far_o, attend_sum)
         far = second(4, far_o, far_i)
+        *far, table_sums, depth_grad, gain_one, gain_two, gain_three, gain_four, gain_five = together(
+            *far, table_sums, depth_grad, gain_one, gain_two, gain_three, gain_four, gain_five
+        )
         far = together(swap(far[0], "y"), swap(far[1], "q"))
         far = third(4, far_o, far_i, *far)
         outer_two_b = swap(low(outer_two_sum[3].astype(f32) + outer_two_a[1].astype(f32)), "y")
         outer_sum_two = outer_two_sum[0].astype(f32) + outer_two_a[0].astype(f32)
         outer_sum_two = low(outer_sum_two + outer_two_b.astype(f32))
-        inner_sum_two = mixed_sum[2 * share :]
-        glu_half = add(glu_sum, glu_a, "q", 0)
+        inner_sum_two = mixed_sum[4 * share :]
     else:
         mixed_sum = last_sum(mixed_sum)
-        glu_half = send(glu_sum, "q", 0)
         inner_sum_one = by_chip(low(inner_one_grad(0, 8)))
         outer_sum_one = by_chip(low(outer_one_grad(0, 8)))
         inner_sum_one = send(send(inner_sum_one, "y", 2), "q", 1)
         outer_sum_one = send(send(outer_sum_one, "y", 2), "q", 1)
         inner_sum_two = send(send(inner_two_sum, "y", 1), "q", 0)
         outer_sum_two = send(send(outer_two_sum, "y", 1), "q", 0)
-    glu_sum = add(glu_half, send(glu_half, "y", 0), "y", 0)
     attend_half = add(attend_sum, send(attend_sum, "q", 0), "q", 0)
     attend_sum = add(attend_half, send(attend_half, "y", 0), "y", 0)
 
     table_grad = jnp.einsum(
-        "hw,wb->bh", table_sums[:, 0], hits.astype(f32), precision=lax.Precision.HIGHEST
+        "hw,wb->bh", table_sums.reshape(heads, -1), hits.astype(f32), precision=lax.Precision.HIGHEST
     )
 
     def of_core(values, dim):
@@ -873,8 +874,19 @@
     )
     small_sum = choose(small_grads, core, 1) + swap(choose(small_grads, 1 - core, 1))
     small_sum = small_sum.reshape(grid + (count,))
-    small_sum = add(small_sum, send(small_sum, "y", 2), "y", 2)
-    small_sum = add(small_sum, send(small_sum, "q", 1), "q", 1)
+    if square:
+        at_q, at_y = lax.axis_index("q"), lax.axis_index("y")
+        here = [choose(small_sum, at_q, 1), choose(small_sum, 1 - at_q, 1)]
+        across = [(0, 3), (3, 0), (1, 2), (2, 1)]
+        small_sum = (
+            choose(here[0], at_y, 1)
+            + swap(choose(here[0], 1 - at_y, 1), "y")
+            + swap(choose(here[1], at_y, 1), "q")
+            + lax.ppermute(choose(here[1], 1 - at_y, 1), ("q", "y"), across)
+        )
+    else:
+        small_sum = add(small_sum, send(small_sum, "y", 2), "y", 2)
+        small_sum = add(small_sum, send(small_sum, "q", 1), "q", 1)
     one_rows = -(-count // (16 * width)) * 16
     small_sum = jnp.pad(low(small_sum), ((0, 0), (0, one_rows * width - count)))
     small_sum = small_sum.reshape(grid[0], one_rows, width)
@@ -904,9 +916,9 @@
         return joined.reshape(share, -1).astype(f32)
 
     attend_out = whole_columns(attend_sum, (3, half), 2)
-    glu_out = whole_columns(glu_sum, (2, chips, share), 3)
-    point_out = mixed_sum[:share].astype(f32)
-    merge_out = mixed_sum[share : 2 * share].astype(f32)
+    glu_out = whole_columns(mixed_sum[: 2 * share], (2, chips, share), 3)
+    point_out = mixed_sum[2 * share : 3 * share].astype(f32)
+    merge_out = mixed_sum[3 * share : 4 * share].astype(f32)
     inner_out = jnp.stack([inner_sum_one.T, inner_sum_two.T]).astype(f32)
     outer_out = jnp.stack([outer_sum_one, outer_sum_two]).astype(f32)
     small_out = small_sum.reshape(-1)[:count].astype(f32)

time: 633 us -> 608 us (0.961)
  waiting for transfers between devices: 212 us -> 240 us
  Pallas kernels: 61.7 us -> 40.8 us
  local copies, waits for them, and re-layouts: 127 us -> 110 us
  other arithmetic: 54.7 us -> 45.6 us
    ppermute x67, waiting for transfers between devices: 186 us -> 216 us  [swap(): return lax.ppermute(values, axis, CORES)]
    pallas_call x2, Pallas kernels: 50 us -> 28.7 us  [the longest x1 19.6 us: attend_back(): pl.pallas_call(attend_back_kernel, grid=(pairs,), in_specs=attend_specs(r...]
    unnamed x275 -> x262, local copies, waits for them, and re-layouts: 32.9 us -> 29.2 us
    reduce_scatter x6 -> x5, waiting for transfers between devices: 17.2 us -> 20.8 us  [last_sum(): return lax.psum_scatter(values, 'p', scatter_dimension=0, tiled=False)]
  transfers between devices with their start and end apart: 82 -> 82, of which waited for: 40 -> 36; matrix products, arithmetic and copies ran while one was open for 36% -> 31% of each run, Pallas kernels for 10% -> 7%
where the time goes in v4:
time: 608 us; the launch traced here: 599 us
  waiting for transfers between devices  240 us (39%)
  local copies, waits for them, and re-layouts  110 us (18%)
  matrix products  82.2 us (14%)
  starting transfers between devices  62.6 us (10%)
  other arithmetic  45.6 us (8%)
  Pallas kernels  40.8 us (7%)
  between operations  18.4 us (3%)
    ppermute x67, waiting for transfers between devices, swap(): return lax.ppermute(values, axis, CORES)  216 us
    ppermute x67, starting transfers between devices, swap(): return lax.ppermute(values, axis, CORES)  46.4 us
    dot_general x18, matrix products, left_product(): jnp.einsum('nd,nf->df', left_in, right_in, preferred_element_type=jnp.flo...  42.8 us
    unnamed x262, local copies, waits for them, and re-layouts  29.2 us
    dot_general x8, matrix products, right_product(): jnp.einsum('nf,df->nd', left_in, right_in, preferred_element_type=jnp.flo...  24.8 us
    reduce_scatter x5, waiting for transfers between devices, last_sum(): return lax.psum_scatter(values, 'p', scatter_dimension=0, tiled=False)  20.8 us
    pallas_call x1, Pallas kernels, attend_back(): pl.pallas_call(attend_back_kernel, grid=(pairs,), in_specs=attend_specs(r...  19.6 us
    dynamic_update_slice x12, local copies, waits for them, and re-layouts, placed(): result = lax.dynamic_update_slice(result, part[:, None, None], at)  15.5 us
  transfers between devices with their start and end apart: 82, of which 36 were waited for; matrix products, arithmetic and copies ran while one was open for 31% of the time, Pallas kernels for 7%

profile of v4, /device:TPU:0, one launch (start us, length us, event | category | flops | bytes accessed | tf_op | source)
XLA Modules:
  0.0 599.3 jit_solution(3739126321712570837)
XLA Ops:
  9.5 3.0 collective-permute-start.7
  14.4 10.0 %collective-permute-done.7 = bf16[256,1024]{1,0:T(8,128)(2,1)S(1)} collective-permute-done((bf16[256,1024]{1,0:T(8,128)(2,1)S(1)}, bf16[256,1024]{1,0:T(8,128)(2,1)S(1)}, u32[]{:S(2)}, u32[]{:S(2)}) %collective-permute-start.7) | collective-permute-done | bytes 524320 | tf_op jit(solution)/shard_map/ppermute | solution.py:346
  30.3 3.5 dynamic-slice_reduce_fusion
  35.6 3.0 collective-permute-done.9
  38.6 2.6 pad_maximum_fusion.1
  47.0 20.3 %collective-permute-done.13 = bf16[512,1024]{0,1:T(8,128)(2,1)} collective-permute-done((bf16[512,1024]{0,1:T(8,128)(2,1)}, bf16[512,1024]{0,1:T(8,128)(2,1)}, u32[]{:S(2)}, u32[]{:S(2)}) %collective-permute-start.13) | collective-permute-done | bytes 1048608 | tf_op jit(solution)/shard_map/ppermute | solution.py:346
  92.0 16.9 %collective-permute-done.2 = bf16[512,1024]{1,0:T(8,128)(2,1)} collective-permute-done((bf16[512,1024]{1,0:T(8,128)(2,1)S(1)}, bf16[512,1024]{1,0:T(8,128)(2,1)}, u32[]{:S(2)}, u32[]{:S(2)}) %collective-permute-start.2) | collective-permute-done | bytes 1048608 | tf_op jit(solution)/shard_map/ppermute | solution.py:346
  121.1 2.3 slice.468
  127.3 2.2 fusion.141
  132.6 8.6 %collective-permute-done.15 = bf16[512,1024]{1,0:T(8,128)(2,1)} collective-permute-done((bf16[512,1024]{1,0:T(8,128)(2,1)}, bf16[512,1024]{1,0:T(8,128)(2,1)}, u32[]{:S(2)}, u32[]{:S(2)}) %collective-permute-start.15) | collective-permute-done | bytes 1048608 | tf_op jit(solution)/shard_map/ppermute | solution.py:346
  141.2 6.6 %collective-permute-done.16 = bf16[4,64,1536]{2,1,0:T(8,128)(2,1)} collective-permute-done((bf16[4,64,1536]{2,1,0:T(8,128)(2,1)}, bf16[4,64,1536]{2,1,0:T(8,128)(2,1)}, u32[]{:S(2)}, u32[]{:S(2)}) %collective-permute-start.16) | collective-permute-done | bytes 786464 | tf_op jit(solution)/shard_map/ppermute | solution.py:346
  153.8 3.5 copy-done.86
  157.8 5.5 multiply_convert_fusion.3
  174.5 18.0 %collective-permute-done.20 = bf16[4,64,1536]{2,1,0:T(8,128)(2,1)S(1)} collective-permute-done((bf16[4,64,1536]{2,1,0:T(8,128)(2,1)}, bf16[4,64,1536]{2,1,0:T(8,128)(2,1)S(1)}, u32[]{:S(2)}, u32[]{:S(2)}) %collective-permute-start.20) | collective-permute-done | bytes 786464 | tf_op jit(solution)/shard_map/ppermute | solution.py:346
  195.5 3.3 convolution_convert_fusion.3
  207.2 11.8 %collective-permute-done.23 = bf16[384,1024]{1,0:T(8,128)(2,1)} collective-permute-done((bf16[384,1024]{1,0:T(8,128)(2,1)S(1)}, bf16[384,1024]{1,0:T(8,128)(2,1)}, u32[]{:S(2)}, u32[]{:S(2)}) %collective-permute-start.23) | collective-permute-done | bytes 786464 | tf_op jit(solution)/shard_map/ppermute | solution.py:346
  220.4 9.1 %attend.1 = bf16[384,512]{1,0:T(8,128)(2,1)S(1)} custom-call(s32[3]{0:T(128)S(1)} %pad_add_fusion.info_ref.refs_0_, f32[4,2,1536]{2,1,0:T(2,128)S(1)} %fusion.78.bias_ref, bf16[384,512]{1,0:T(8,128)(2,1)S(1)} %slice.487.query_ref, bf16[768,1024]{1,0:T(8,128)(2,1)S(1)} %pad_maximum_fusion.3.key_ref.value_ref, ...), custom_call_target="tpu_custom_call" | custom-call | flops 603979776 | bytes 2359296 | tf_op jit(solution)/shard_map/attend/pallas_call | solution.py:143
  245.7 4.5 collective-permute-start.28
  251.6 4.2 conv.1
  267.6 4.2 fusion.137
  271.8 3.6 fusion.65
  286.3 4.1 multiply_convert_fusion.1
  294.4 4.5 convolution_convert_fusion
  301.1 2.7 fusion.130
  310.0 4.5 collective-permute-start.38
  314.6 3.5 convolution_convert_fusion.1
  321.6 7.9 %conv_back.1 = (f32[384,512]{1,0:T(8,128)S(1)}, f32[31,512]{1,0:T(8,128)S(1)}) custom-call(s32[3]{0:T(128)S(1)} %pad_add_fusion.info_ref.refs_0_, bf16[16,512]{1,0:T(8,128)(2,1)S(1)} %collective-permute-done.28.refs_1_, bf16[384,512]{1,0:T(8,128)(2,1)S(1)} %multiply_convert_fusion.12.refs_2_, bf16[16,512]{1,0:T(8,128)(2,1)S(1)} %collective-permute-done.29.refs_3_, ...), custom_call_target="tpu_custom_call" | custom-call | flops 24379392 | bytes 1572864 | tf_op jit(solution)/shard_map/conv_back/pallas_call | solution.py:301
  340.6 19.6 %attend_back.1 = (bf16[384,512]{1,0:T(8,128)(2,1)S(1)}, f32[768,512]{1,0:T(8,128)S(1)}, f32[768,512]{1,0:T(8,128)}, f32[4,2,1536]{2,1,0:T(2,128)S(1)}) custom-call(s32[3]{0:T(128)S(1)} %pad_add_fusion.info_ref.refs_0_, f32[4,2,1536]{2,1,0:T(2,128)S(1)} %copy-done.2, bf16[384,512]{1,0:T(8,128)(2,1)S(1)} %slice.487.query_ref, bf16[768,1024]{1,0:T(8,128)(2,1)} %copy-done, ...), custom_call_target="tpu_custom_call" | custom-call | flops 1509949440 | bytes 2359296 | tf_op jit(solution)/shard_map/attend_back/pallas_call | solution.py:166
  360.3 10.5 %collective-permute-done.43 = bf16[4,2,32,1024]{3,2,0,1:T(8,128)(2,1)S(1)} collective-permute-done((bf16[4,2,32,1024]{3,2,0,1:T(8,128)(2,1)S(1)}, bf16[4,2,32,1024]{3,2,0,1:T(8,128)(2,1)S(1)}, u32[]{:S(2)}, u32[]{:S(2)}) %collective-permute-start.43) | collective-permute-done | bytes 524320 | tf_op jit(solution)/shard_map/ppermute | solution.py:346
  376.6 15.5 %collective-permute-done.46 = bf16[384,1024]{1,0:T(8,128)(2,1)S(1)} collective-permute-done((bf16[384,1024]{1,0:T(8,128)(2,1)S(1)}, bf16[384,1024]{1,0:T(8,128)(2,1)S(1)}, u32[]{:S(2)}, u32[]{:S(2)}) %collective-permute-start.46) | collective-permute-done | bytes 786464 | tf_op jit(solution)/shard_map/ppermute | solution.py:346
  395.3 3.8 fusion.157
  401.1 3.6 convolution_convert_fusion.2
  407.5 2.6 multiply_convert_fusion.4
  417.0 4.7 multiply_convert_fusion
  423.6 3.4 convolution_convert_fusion.5
  427.0 3.0 convolution_convert_fusion.7
  430.0 2.8 convolution_convert_fusion.8
  432.8 2.7 convolution_convert_fusion.6
  435.6 6.9 %collective-permute-done.52 = bf16[4,2,32,1024]{3,2,1,0:T(8,128)(2,1)S(1)} collective-permute-done((bf16[4,2,32,1024]{3,2,1,0:T(8,128)(2,1)}, bf16[4,2,32,1024]{3,2,1,0:T(8,128)(2,1)S(1)}, u32[]{:S(2)}, u32[]{:S(2)}) %collective-permute-start.52) | collective-permute-done | bytes 524320 | tf_op jit(solution)/shard_map/ppermute | solution.py:346
  449.3 3.1 collective-permute-done.56
  454.0 21.4 %collective-permute-done.54 = bf16[512,1024]{1,0:T(8,128)(2,1)} collective-permute-done((bf16[512,1024]{1,0:T(8,128)(2,1)}, bf16[512,1024]{1,0:T(8,128)(2,1)}, u32[]{:S(2)}, u32[]{:S(2)}) %collective-permute-start.54) | collective-permute-done | bytes 1048608 | tf_op jit(solution)/shard_map/ppermute | solution.py:346
  486.2 28.1 %collective-permute-done.58 = bf16[256,1024]{1,0:T(8,128)(2,1)S(1)} collective-permute-done((bf16[256,1024]{1,0:T(8,128)(2,1)S(1)}, bf16[256,1024]{1,0:T(8,128)(2,1)S(1)}, u32[]{:S(2)}, u32[]{:S(2)}) %collective-permute-start.58) | collective-permute-done | bytes 524320 | tf_op jit(solution)/shard_map/ppermute | solution.py:346
  514.3 2.9 fusion.13
  517.3 2.5 fusion.14
  533.7 9.3 %collective-permute-done.68 = bf16[2,64,1536]{2,1,0:T(8,128)(2,1)S(1)} collective-permute-done((bf16[2,64,1536]{2,1,0:T(8,128)(2,1)S(1)}, bf16[2,64,1536]{2,1,0:T(8,128)(2,1)S(1)}, u32[]{:S(2)}, u32[]{:S(2)}) %collective-permute-start.68) | collective-permute-done | bytes 393248 | tf_op jit(solution)/shard_map/ppermute | solution.py:346
  543.5 3.5 collective-permute-done.62
  546.9 6.1 %collective-permute-done.63 = bf16[256,1024]{1,0:T(8,128)(2,1)S(1)} collective-permute-done((bf16[256,1024]{1,0:T(8,128)(2,1)}, bf16[256,1024]{1,0:T(8,128)(2,1)S(1)}, u32[]{:S(2)}, u32[]{:S(2)}) %collective-permute-start.63) | collective-permute-done | bytes 524320 | tf_op jit(solution)/shard_map/ppermute | solution.py:346
  565.7 20.7 %reduce-scatter.14.cloned.1.call-done = bf16[1,144,1024]{2,1,0:T(8,128)(2,1)} async-done(((bf16[4,144,1024]{2,1,0:T(8,128)(2,1)}), bf16[1,144,1024]{2,1,0:T(8,128)(2,1)}) %reduce-scatter.14.cloned.1.call-update) | async-done | bytes 294928 | tf_op jit(solution)/shard_map/reduce_scatter | solution.py:684
  (700 shorter events, 230.1 us)
Async XLA Ops:
  7.2 35.9 %all-gather.11.cloned.1.call-start = ((), (), s32[]{:S(2)}) async-start(), calls=%async_computation.11 | async-start | bytes 1310720 | tf_op jit(solution)/shard_map/all_gather | solution.py:567
  9.1 66.0 %all-gather.9.cloned.1.call-start = ((), (), s32[]{:S(2)}) async-start(), calls=%async_computation.10 | async-start | bytes 1474560 | tf_op jit(solution)/shard_map/all_gather | solution.py:567
  9.5 14.9 %collective-permute-start.7 = (bf16[256,1024]{1,0:T(8,128)(2,1)S(1)}, bf16[256,1024]{1,0:T(8,128)(2,1)S(1)}, u32[]{:S(2)}, u32[]{:S(2)}) collective-permute-start(bf16[256,1024]{1,0:T(8,128)(2,1)S(1)} %get-tuple-element.347), channel_id=1, source_target_pairs={{0,4},{4,0},{1,5},{5,1},{2,6},{6,2},{3,7},{7,3},{8,12},{12,8},{9,1... | collective-permute-start | bytes 1572872 | tf_op jit(solution)/shard_map/ppermute | solution.py:346
  12.5 13.4 %collective-permute-start.8 = (bf16[256,1024]{1,0:T(8,128)(2,1)S(1)}, bf16[256,1024]{1,0:T(8,128)(2,1)S(1)}, u32[]{:S(2)}, u32[]{:S(2)}) collective-permute-start(bf16[256,1024]{1,0:T(8,128)(2,1)S(1)} %get-tuple-element.347), channel_id=1, source_target_pairs={{0,2},{2,0},{1,3},{3,1},{4,6},{6,4},{5,7},{7,5},{8,10},{10,8},{9,1... | collective-permute-start | bytes 1572872 | tf_op jit(solution)/shard_map/ppermute | solution.py:346
  14.3 13.1 %collective-permute-start = (bf16[1,1216]{1,0:T(2,128)(2,1)S(1)}, bf16[1,1216]{1,0:T(2,128)(2,1)S(1)}, u32[]{:S(2)}, u32[]{:S(2)}) collective-permute-start(bf16[1,1216]{1,0:T(2,128)(2,1)S(1)} %broadcast_in_dim.43), channel_id=1, source_target_pairs={{0,1},{1,0},{2,3},{3,2},{4,5},{5,4},{6,7},{7,6},{8,9},{9,8},{10,11... | collective-permute-start | bytes 7304 | tf_op jit(solution)/shard_map/ppermute | solution.py:346
  28.4 91.6 %all-gather.13.cloned.1.call-start = ((), (), s32[]{:S(2)}) async-start(), calls=%async_computation.12 | async-start | bytes 2293760 | tf_op jit(solution)/shard_map/all_gather | solution.py:567
  29.9 15.2 %collective-permute-start.10 = (bf16[32,1536]{1,0:T(8,128)(2,1)S(1)}, bf16[32,1536]{1,0:T(8,128)(2,1)S(1)}, u32[]{:S(2)}, u32[]{:S(2)}) collective-permute-start(bf16[32,1536]{1,0:T(8,128)(2,1)S(1)} %bitcast.480), channel_id=1, source_target_pairs={{0,1},{1,0},{2,3},{3,2},{4,5},{5,4},{6,7},{7,6},{8,9},{9,8},{10,11... | collective-permute-start | bytes 294920 | tf_op jit(solution)/shard_map/ppermute | solution.py:346
  43.1 24.2 %collective-permute-start.13 = (bf16[512,1024]{0,1:T(8,128)(2,1)}, bf16[512,1024]{0,1:T(8,128)(2,1)}, u32[]{:S(2)}, u32[]{:S(2)}) collective-permute-start(bf16[512,1024]{0,1:T(8,128)(2,1)} %all-gather.11.cloned.1.call-done), channel_id=1, source_target_pairs={{0,2},{2,0},{1,3},{3,1},{4,6},{6,4},{5,7},{7,5},{8,10},{10,8},{9,1... | collective-permute-start | bytes 3145736 | tf_op jit(solution)/shard_map/ppermute | solution.py:346
  43.6 25.0 %collective-permute-start.12 = (bf16[512,1024]{0,1:T(8,128)(2,1)}, bf16[512,1024]{0,1:T(8,128)(2,1)S(1)}, u32[]{:S(2)}, u32[]{:S(2)}) collective-permute-start(bf16[512,1024]{0,1:T(8,128)(2,1)} %all-gather.11.cloned.1.call-done), channel_id=1, source_target_pairs={{0,4},{4,0},{1,5},{5,1},{2,6},{6,2},{3,7},{7,3},{8,12},{12,8},{9,1... | collective-permute-start | bytes 3145736 | tf_op jit(solution)/shard_map/ppermute | solution.py:346
  68.7 199.0 %all-gather.15.cloned.1.call-start = ((), (), s32[]{:S(2)}) async-start(), calls=%async_computation.13 | async-start | bytes 10485760 | tf_op jit(solution)/shard_map/all_gather | solution.py:567
  74.8 317.6 %reduce-scatter.6.cloned.1.call-start = ((), (), s32[]{:S(2)}) async-start(), calls=%async_computation.5 | async-start | bytes 5242880 | tf_op jit(solution)/shard_map/reduce_scatter | solution.py:684
  78.0 13.6 %collective-permute-start.5 = (bf16[4,16,1024]{2,1,0:T(8,128)(2,1)}, bf16[4,16,1024]{2,1,0:T(8,128)(2,1)}, u32[]{:S(2)}, u32[]{:S(2)}) collective-permute-start(bf16[4,16,1024]{2,1,0:T(8,128)(2,1)} %slice.461), channel_id=1, source_target_pairs={{0,6},{6,0},{2,4},{4,2},{1,7},{7,1},{3,5},{5,3},{8,14},{14,8},{10,... | collective-permute-start | bytes 393224 | tf_op jit(solution)/shard_map/ppermute | solution.py:589
  81.5 27.4 %collective-permute-start.2 = (bf16[512,1024]{1,0:T(8,128)(2,1)S(1)}, bf16[512,1024]{1,0:T(8,128)(2,1)}, u32[]{:S(2)}, u32[]{:S(2)}) collective-permute-start(bf16[512,1024]{1,0:T(8,128)(2,1)S(1)} %bitcast.406), channel_id=1, source_target_pairs={{0,2},{2,0},{1,3},{3,1},{4,6},{6,4},{5,7},{7,5},{8,10},{10,8},{9,1... | collective-permute-start | bytes 3145736 | tf_op jit(solution)/shard_map/ppermute | solution.py:346
  82.0 28.2 %collective-permute-start.1 = (bf16[512,1024]{1,0:T(8,128)(2,1)S(1)}, bf16[512,1024]{1,0:T(8,128)(2,1)}, u32[]{:S(2)}, u32[]{:S(2)}) collective-permute-start(bf16[512,1024]{1,0:T(8,128)(2,1)S(1)} %bitcast.407), channel_id=1, source_target_pairs={{0,4},{4,0},{1,5},{5,1},{2,6},{6,2},{3,7},{7,3},{8,12},{12,8},{9,1... | collective-permute-start | bytes 3145736 | tf_op jit(solution)/shard_map/ppermute | solution.py:346
  91.5 41.1 %collective-permute-start.14 = (bf16[512,1024]{0,1:T(8,128)(2,1)}, bf16[512,1024]{0,1:T(8,128)(2,1)}, u32[]{:S(2)}, u32[]{:S(2)}) collective-permute-start(bf16[512,1024]{0,1:T(8,128)(2,1)} %collective-permute-done.13), channel_id=1, source_target_pairs={{0,4},{4,0},{1,5},{5,1},{2,6},{6,2},{3,7},{7,3},{8,12},{12,8},{9,1... | collective-permute-start | bytes 3145736 | tf_op jit(solution)/shard_map/ppermute | solution.py:346
  117.8 23.4 %collective-permute-start.15 = (bf16[512,1024]{1,0:T(8,128)(2,1)}, bf16[512,1024]{1,0:T(8,128)(2,1)}, u32[]{:S(2)}, u32[]{:S(2)}) collective-permute-start(bf16[512,1024]{1,0:T(8,128)(2,1)} %collective-permute-done.1), channel_id=1, source_target_pairs={{0,2},{2,0},{1,3},{3,1},{4,6},{6,4},{5,7},{7,5},{8,10},{10,8},{9,1... | collective-permute-start | bytes 3145736 | tf_op jit(solution)/shard_map/ppermute | solution.py:346
  124.7 23.1 %collective-permute-start.16 = (bf16[4,64,1536]{2,1,0:T(8,128)(2,1)}, bf16[4,64,1536]{2,1,0:T(8,128)(2,1)}, u32[]{:S(2)}, u32[]{:S(2)}) collective-permute-start(bf16[4,64,1536]{2,1,0:T(8,128)(2,1)} %reshape.696), channel_id=1, source_target_pairs={{0,4},{4,0},{1,5},{5,1},{2,6},{6,2},{3,7},{7,3},{8,12},{12,8},{9,1... | collective-permute-start | bytes 2359304 | tf_op jit(solution)/shard_map/ppermute | solution.py:346
  127.3 30.4 %collective-permute-start.6 = (bf16[192,1024]{1,0:T(8,128)(2,1)}, bf16[192,1024]{1,0:T(8,128)(2,1)}, u32[]{:S(2)}, u32[]{:S(2)}) collective-permute-start(bf16[192,1024]{1,0:T(8,128)(2,1)} %fusion.28), channel_id=1, source_target_pairs={{0,1},{1,0},{2,3},{3,2},{4,5},{5,4},{6,7},{7,6},{8,9},{9,8},{10,11... | collective-permute-start | bytes 1179656 | tf_op jit(solution)/shard_map/ppermute | solution.py:346
  150.9 18.2 %collective-permute-start.18 = (bf16[4,64,1536]{2,1,0:T(8,128)(2,1)}, bf16[4,64,1536]{2,1,0:T(8,128)(2,1)}, u32[]{:S(2)}, u32[]{:S(2)}) collective-permute-start(bf16[4,64,1536]{2,1,0:T(8,128)(2,1)} %reshape.696), channel_id=1, source_target_pairs={{0,2},{2,0},{1,3},{3,1},{4,6},{6,4},{5,7},{7,5},{8,10},{10,8},{9,1... | collective-permute-start | bytes 2359304 | tf_op jit(solution)/shard_map/ppermute | solution.py:346
  152.2 46.8 %collective-permute-start.21 = (bf16[4,128,1024]{2,1,0:T(8,128)(2,1)}, bf16[4,128,1024]{2,1,0:T(8,128)(2,1)}, u32[]{:S(2)}, u32[]{:S(2)}) collective-permute-start(bf16[4,128,1024]{2,1,0:T(8,128)(2,1)} %slice.468), channel_id=1, source_target_pairs={{0,4},{4,0},{1,5},{5,1},{2,6},{6,2},{3,7},{7,3},{8,12},{12,8},{9,1... | collective-permute-start | bytes 3145736 | tf_op jit(solution)/shard_map/ppermute | solution.py:346
  169.3 23.2 %collective-permute-start.20 = (bf16[4,64,1536]{2,1,0:T(8,128)(2,1)}, bf16[4,64,1536]{2,1,0:T(8,128)(2,1)S(1)}, u32[]{:S(2)}, u32[]{:S(2)}) collective-permute-start(bf16[4,64,1536]{2,1,0:T(8,128)(2,1)} %collective-permute-done.18), channel_id=1, source_target_pairs={{0,4},{4,0},{1,5},{5,1},{2,6},{6,2},{3,7},{7,3},{8,12},{12,8},{9,1... | collective-permute-start | bytes 2359304 | tf_op jit(solution)/shard_map/ppermute | solution.py:346
  172.9 27.0 %collective-permute-start.22 = (bf16[4,128,1024]{2,1,0:T(8,128)(2,1)}, bf16[4,128,1024]{2,1,0:T(8,128)(2,1)S(1)}, u32[]{:S(2)}, u32[]{:S(2)}) collective-permute-start(bf16[4,128,1024]{2,1,0:T(8,128)(2,1)} %slice.468), channel_id=1, source_target_pairs={{0,2},{2,0},{1,3},{3,1},{4,6},{6,4},{5,7},{7,5},{8,10},{10,8},{9,1... | collective-permute-start | bytes 3145736 | tf_op jit(solution)/shard_map/ppermute | solution.py:346
  200.9 18.1 %collective-permute-start.23 = (bf16[384,1024]{1,0:T(8,128)(2,1)S(1)}, bf16[384,1024]{1,0:T(8,128)(2,1)}, u32[]{:S(2)}, u32[]{:S(2)}) collective-permute-start(bf16[384,1024]{1,0:T(8,128)(2,1)S(1)} %slice.488), channel_id=1, source_target_pairs={{0,2},{2,0},{1,3},{3,1},{4,6},{6,4},{5,7},{7,5},{8,10},{10,8},{9,1... | collective-permute-start | bytes 2359304 | tf_op jit(solution)/shard_map/ppermute | solution.py:346
  201.9 27.6 %collective-permute-start.24 = (bf16[4,128,1024]{2,1,0:T(8,128)(2,1)}, bf16[4,128,1024]{2,1,0:T(8,128)(2,1)S(1)}, u32[]{:S(2)}, u32[]{:S(2)}) collective-permute-start(bf16[4,128,1024]{2,1,0:T(8,128)(2,1)} %copy-done.52), channel_id=1, source_target_pairs={{0,4},{4,0},{1,5},{5,1},{2,6},{6,2},{3,7},{7,3},{8,12},{12,8},{9,1... | collective-permute-start | bytes 3145736 | tf_op jit(solution)/shard_map/ppermute | solution.py:346
  298.9 176.5 %reduce-scatter.8.cloned.1.call-start = ((), (), s32[]{:S(2)}) async-start(), calls=%async_computation.6 | async-start | bytes 3932160 | tf_op jit(solution)/shard_map/reduce_scatter | solution.py:684
  308.7 12.9 %collective-permute-start.39 = (bf16[16,512]{1,0:T(8,128)(2,1)S(1)}, bf16[16,512]{1,0:T(8,128)(2,1)S(1)}, u32[]{:S(2)}, u32[]{:S(2)}) collective-permute-start(bf16[16,512]{1,0:T(8,128)(2,1)S(1)} %get-tuple-element.350), channel_id=1, source_target_pairs={{2,0},{3,1},{6,4},{7,5},{10,8},{11,9},{14,12},{15,13},{18,16},{19,... | collective-permute-start | bytes 49160 | tf_op jit(solution)/shard_map/ppermute | solution.py:504
  333.8 37.0 %collective-permute-start.42 = (bf16[4,2,64,1024]{3,2,0,1:T(8,128)(2,1)}, bf16[4,2,64,1024]{3,2,0,1:T(8,128)(2,1)S(1)}, u32[]{:S(2)}, u32[]{:S(2)}) collective-permute-start(bf16[4,2,64,1024]{3,2,0,1:T(8,128)(2,1)} %bitcast.385), channel_id=1, source_target_pairs={{0,2},{2,0},{1,3},{3,1},{4,6},{6,4},{5,7},{7,5},{8,10},{10,8},{9,1... | collective-permute-start | bytes 3145736 | tf_op jit(solution)/shard_map/ppermute | solution.py:346
  336.9 33.9 %collective-permute-start.43 = (bf16[4,2,32,1024]{3,2,0,1:T(8,128)(2,1)S(1)}, bf16[4,2,32,1024]{3,2,0,1:T(8,128)(2,1)S(1)}, u32[]{:S(2)}, u32[]{:S(2)}) collective-permute-start(bf16[4,2,32,1024]{3,2,0,1:T(8,128)(2,1)S(1)} %bitcast.464), channel_id=1, source_target_pairs={{0,2},{2,0},{1,3},{3,1},{4,6},{6,4},{5,7},{7,5},{8,10},{10,8},{9,1... | collective-permute-start | bytes 1572872 | tf_op jit(solution)/shard_map/ppermute | solution.py:346
  338.7 55.6 %collective-permute-start.45 = (bf16[4,2,128,1024]{3,2,0,1:T(8,128)(2,1)}, bf16[4,2,128,1024]{3,2,0,1:T(8,128)(2,1)}, u32[]{:S(2)}, u32[]{:S(2)}) collective-permute-start(bf16[4,2,128,1024]{3,2,0,1:T(8,128)(2,1)} %copy.281), channel_id=1, source_target_pairs={{0,4},{4,0},{1,5},{5,1},{2,6},{6,2},{3,7},{7,3},{8,12},{12,8},{9,1... | collective-permute-start | bytes 6291464 | tf_op jit(solution)/shard_map/ppermute | solution.py:346
  372.1 20.0 %collective-permute-start.46 = (bf16[384,1024]{1,0:T(8,128)(2,1)S(1)}, bf16[384,1024]{1,0:T(8,128)(2,1)S(1)}, u32[]{:S(2)}, u32[]{:S(2)}) collective-permute-start(bf16[384,1024]{1,0:T(8,128)(2,1)S(1)} %fusion.39), channel_id=1, source_target_pairs={{0,2},{2,0},{1,3},{3,1},{4,6},{6,4},{5,7},{7,5},{8,10},{10,8},{9,1... | collective-permute-start | bytes 2359304 | tf_op jit(solution)/shard_map/ppermute | solution.py:346
  404.7 122.4 %reduce-scatter.10.cloned.1.call-start = ((), (), s32[]{:S(2)}) async-start(), calls=%async_computation.7 | async-start | bytes 2621440 | tf_op jit(solution)/shard_map/reduce_scatter | solution.py:684
  410.6 24.9 %collective-permute-start.51 = (bf16[4,32,1024]{2,1,0:T(8,128)(2,1)}, bf16[4,32,1024]{2,1,0:T(8,128)(2,1)S(1)}, u32[]{:S(2)}, u32[]{:S(2)}) collective-permute-start(bf16[4,32,1024]{2,1,0:T(8,128)(2,1)} %dynamic-slice_bitcast_fusion.6), channel_id=1, source_target_pairs={{0,4},{4,0},{1,5},{5,1},{2,6},{6,2},{3,7},{7,3},{8,12},{12,8},{9,1... | collective-permute-start | bytes 786440 | tf_op jit(solution)/shard_map/ppermute | solution.py:346
  411.7 23.9 %collective-permute-start.50 = (bf16[4,64,1024]{2,1,0:T(8,128)(2,1)}, bf16[4,64,1024]{2,1,0:T(8,128)(2,1)S(1)}, u32[]{:S(2)}, u32[]{:S(2)}) collective-permute-start(bf16[4,64,1024]{2,1,0:T(8,128)(2,1)} %dynamic-slice_bitcast_fusion.2), channel_id=1, source_target_pairs={{0,4},{4,0},{1,5},{5,1},{2,6},{6,2},{3,7},{7,3},{8,12},{12,8},{9,1... | collective-permute-start | bytes 1572872 | tf_op jit(solution)/shard_map/ppermute | solution.py:346
  412.7 29.8 %collective-permute-start.52 = (bf16[4,2,32,1024]{3,2,1,0:T(8,128)(2,1)}, bf16[4,2,32,1024]{3,2,1,0:T(8,128)(2,1)S(1)}, u32[]{:S(2)}, u32[]{:S(2)}) collective-permute-start(bf16[4,2,32,1024]{3,2,1,0:T(8,128)(2,1)} %dynamic-slice_bitcast_fusion), channel_id=1, source_target_pairs={{0,4},{4,0},{1,5},{5,1},{2,6},{6,2},{3,7},{7,3},{8,12},{12,8},{9,1... | collective-permute-start | bytes 1572872 | tf_op jit(solution)/shard_map/ppermute | solution.py:346
  413.7 40.3 %collective-permute-start.57 = (bf16[2,128,1024]{2,1,0:T(8,128)(2,1)}, bf16[2,128,1024]{2,1,0:T(8,128)(2,1)}, u32[]{:S(2)}, u32[]{:S(2)}) collective-permute-start(bf16[2,128,1024]{2,1,0:T(8,128)(2,1)} %slice_bitcast_fusion.2), channel_id=1, source_target_pairs={{0,4},{4,0},{1,5},{5,1},{2,6},{6,2},{3,7},{7,3},{8,12},{12,8},{9,1... | collective-permute-start | bytes 1572872 | tf_op jit(solution)/shard_map/ppermute | solution.py:346
  416.7 25.8 %collective-permute-start.53 = (bf16[4,128,1024]{2,1,0:T(8,128)(2,1)S(1)}, bf16[4,128,1024]{2,1,0:T(8,128)(2,1)S(1)}, u32[]{:S(2)}, u32[]{:S(2)}) collective-permute-start(bf16[4,128,1024]{2,1,0:T(8,128)(2,1)S(1)} %fusion.15), channel_id=1, source_target_pairs={{0,2},{2,0},{1,3},{3,1},{4,6},{6,4},{5,7},{7,5},{8,10},{10,8},{9,1... | collective-permute-start | bytes 3145736 | tf_op jit(solution)/shard_map/ppermute | solution.py:346
  443.4 31.9 %collective-permute-start.54 = (bf16[512,1024]{1,0:T(8,128)(2,1)}, bf16[512,1024]{1,0:T(8,128)(2,1)}, u32[]{:S(2)}, u32[]{:S(2)}) collective-permute-start(bf16[512,1024]{1,0:T(8,128)(2,1)} %convolution_convert_fusion.8), channel_id=1, source_target_pairs={{0,4},{4,0},{1,5},{5,1},{2,6},{6,2},{3,7},{7,3},{8,12},{12,8},{9,1... | collective-permute-start | bytes 3145736 | tf_op jit(solution)/shard_map/ppermute | solution.py:346
  444.4 30.9 %collective-permute-start.55 = (bf16[512,1024]{1,0:T(8,128)(2,1)}, bf16[512,1024]{1,0:T(8,128)(2,1)}, u32[]{:S(2)}, u32[]{:S(2)}) collective-permute-start(bf16[512,1024]{1,0:T(8,128)(2,1)} %convolution_convert_fusion.7), channel_id=1, source_target_pairs={{0,2},{2,0},{1,3},{3,1},{4,6},{6,4},{5,7},{7,5},{8,10},{10,8},{9,1... | collective-permute-start | bytes 3145736 | tf_op jit(solution)/shard_map/ppermute | solution.py:346
  475.4 82.4 %reduce-scatter.12.cloned.1.call-start = ((), (), s32[]{:S(2)}) async-start(), calls=%async_computation.8 | async-start | bytes 1310720 | tf_op jit(solution)/shard_map/reduce_scatter | solution.py:684
  475.6 38.6 %collective-permute-start.60 = (bf16[512,1024]{1,0:T(8,128)(2,1)}, bf16[512,1024]{1,0:T(8,128)(2,1)S(1)}, u32[]{:S(2)}, u32[]{:S(2)}) collective-permute-start(bf16[512,1024]{1,0:T(8,128)(2,1)} %convolution_convert_fusion.6), channel_id=1, source_target_pairs={{0,4},{4,0},{1,5},{5,1},{2,6},{6,2},{3,7},{7,3},{8,12},{12,8},{9,1... | collective-permute-start | bytes 3145736 | tf_op jit(solution)/shard_map/ppermute | solution.py:346
  476.7 37.6 %collective-permute-start.61 = (bf16[512,1024]{1,0:T(8,128)(2,1)}, bf16[512,1024]{1,0:T(8,128)(2,1)S(1)}, u32[]{:S(2)}, u32[]{:S(2)}) collective-permute-start(bf16[512,1024]{1,0:T(8,128)(2,1)} %convolution_convert_fusion.5), channel_id=1, source_target_pairs={{0,2},{2,0},{1,3},{3,1},{4,6},{6,4},{5,7},{7,5},{8,10},{10,8},{9,1... | collective-permute-start | bytes 3145736 | tf_op jit(solution)/shard_map/ppermute | solution.py:346
  480.8 33.5 %collective-permute-start.58 = (bf16[256,1024]{1,0:T(8,128)(2,1)S(1)}, bf16[256,1024]{1,0:T(8,128)(2,1)S(1)}, u32[]{:S(2)}, u32[]{:S(2)}) collective-permute-start(bf16[256,1024]{1,0:T(8,128)(2,1)S(1)} %fusion.11), channel_id=1, source_target_pairs={{0,2},{2,0},{1,3},{3,1},{4,6},{6,4},{5,7},{7,5},{8,10},{10,8},{9,1... | collective-permute-start | bytes 1572872 | tf_op jit(solution)/shard_map/ppermute | solution.py:346
  482.6 31.7 %collective-permute-start.59 = (bf16[256,1024]{1,0:T(8,128)(2,1)S(1)}, bf16[256,1024]{1,0:T(8,128)(2,1)S(1)}, u32[]{:S(2)}, u32[]{:S(2)}) collective-permute-start(bf16[256,1024]{1,0:T(8,128)(2,1)S(1)} %fusion.12), channel_id=1, source_target_pairs={{0,4},{4,0},{1,5},{5,1},{2,6},{6,2},{3,7},{7,3},{8,12},{12,8},{9,1... | collective-permute-start | bytes 1572872 | tf_op jit(solution)/shard_map/ppermute | solution.py:346
  485.9 72.2 %collective-permute-start.72 = (bf16[128,1024]{1,0:T(8,128)(2,1)S(1)}, bf16[128,1024]{1,0:T(8,128)(2,1)S(1)}, u32[]{:S(2)}, u32[]{:S(2)}) collective-permute-start(bf16[128,1024]{1,0:T(8,128)(2,1)S(1)} %fusion.56), channel_id=1, source_target_pairs={{0,2},{2,0},{1,3},{3,1},{4,6},{6,4},{5,7},{7,5},{8,10},{10,8},{9,1... | collective-permute-start | bytes 786440 | tf_op jit(solution)/shard_map/ppermute | solution.py:346
  527.1 59.2 %reduce-scatter.14.cloned.1.call-start = ((), (), s32[]{:S(2)}) async-start(), calls=%async_computation.9 | async-start | bytes 1474560 | tf_op jit(solution)/shard_map/reduce_scatter | solution.py:684
  532.0 15.0 %collective-permute-start.62 = (bf16[256,1024]{1,0:T(8,128)(2,1)}, bf16[256,1024]{1,0:T(8,128)(2,1)S(1)}, u32[]{:S(2)}, u32[]{:S(2)}) collective-permute-start(bf16[256,1024]{1,0:T(8,128)(2,1)} %fusion.13), channel_id=1, source_target_pairs={{0,2},{2,0},{1,3},{3,1},{4,6},{6,4},{5,7},{7,5},{8,10},{10,8},{9,1... | collective-permute-start | bytes 1572872 | tf_op jit(solution)/shard_map/ppermute | solution.py:346
  532.3 20.8 %collective-permute-start.63 = (bf16[256,1024]{1,0:T(8,128)(2,1)}, bf16[256,1024]{1,0:T(8,128)(2,1)S(1)}, u32[]{:S(2)}, u32[]{:S(2)}) collective-permute-start(bf16[256,1024]{1,0:T(8,128)(2,1)} %fusion.14), channel_id=1, source_target_pairs={{0,4},{4,0},{1,5},{5,1},{2,6},{6,2},{3,7},{7,3},{8,12},{12,8},{9,1... | collective-permute-start | bytes 1572872 | tf_op jit(solution)/shard_map/ppermute | solution.py:346
  543.1 14.7 %collective-permute-start.69 = (bf16[64,1536]{1,0:T(8,128)(2,1)S(1)}, bf16[64,1536]{1,0:T(8,128)(2,1)S(1)}, u32[]{:S(2)}, u32[]{:S(2)}) collective-permute-start(bf16[64,1536]{1,0:T(8,128)(2,1)S(1)} %dynamic-slice_bitcast_fusion.7), channel_id=1, source_target_pairs={{0,2},{2,0},{1,3},{3,1},{4,6},{6,4},{5,7},{7,5},{8,10},{10,8},{9,1... | collective-permute-start | bytes 589832 | tf_op jit(solution)/shard_map/ppermute | solution.py:346
  (149 other events, 1046.7 us)
Sparse Core Ops, SparseCore 0:
  10.2 32.8 all-gather.10
  45.3 28.7 all-gather.8
  75.6 40.5 all-gather.12
  117.6 148.4 all-gather.14
  299.0 77.5 reduce-scatter.5
  404.8 59.3 reduce-scatter.7
  475.5 42.7 reduce-scatter.9
  527.3 26.6 reduce-scatter.11
  558.0 28.3 reduce-scatter.13

commit v5 on v4

--- a/solution.py
+++ b/solution.py
@@ -461,13 +461,15 @@
     return (result, (normed, inverse, both, middle, activated))
 
 
-def feed_back(upstream, gain, inner, outer, kept):
+def feed_back(upstream, gain, inner, outer, kept, *held):
     normed, inverse, both, middle, activated = kept
     rows = upstream.shape[0]
     half = low(0.5 * upstream)
     half_both = jnp.concatenate([half, swap(half)], axis=0)
     active_grad = right_product(half_both, outer)
     middle_grad = low(active_grad * silu_slope(middle))
+    if held:
+        middle_grad, *held = together(middle_grad, *held)
     partial = product(middle_grad, inner)
     received = swap(low(partial[rows:]))
     entry_grad = partial[:rows] + received.astype(jnp.float32)
@@ -481,7 +483,7 @@
     def outer_grad(first, end):
         return left_product(activated[:, first * eighth : end * eighth], half_both)
 
-    return (upstream + back, gain_grad, inner_grad, outer_grad)
+    return (upstream + back, gain_grad, inner_grad, outer_grad, *held)
 
 
 def bucket_hits(group):
@@ -689,6 +691,51 @@
         shape = (grid[0], 4) if square else grid
         return last_sum(low(grad).reshape(shape + (units, width)))
 
+    def small_of(table_sums, depth_grad, gain_zero, gain_one, gain_two, gain_three, gain_four, gain_five):
+        table_grad = jnp.einsum(
+            "hw,wb->bh", table_sums.reshape(heads, -1), hits.astype(f32), precision=lax.Precision.HIGHEST
+        )
+
+        def of_core(values, dim):
+            empty = jnp.zeros_like(values)
+            return jnp.stack(
+                [jnp.where(core == 0, values, empty), jnp.where(core == 1, values, empty)], axis=dim
+            )
+
+        gain_three = of_core(gain_three.reshape(chips, share), 1).reshape(width)
+        gain_grads = jnp.stack([gain_zero, gain_one, gain_two, gain_three, gain_four, gain_five])
+        small_grads = jnp.concatenate(
+            [
+                gain_grads.reshape(6, chips, 2, share).transpose(1, 2, 0, 3).reshape(chips, 2, -1),
+                of_core(table_grad, 1).reshape(chips, 2, -1),
+                of_core(depth_grad.reshape(taps, chips, share).transpose(1, 0, 2), 1).reshape(
+                    chips, 2, -1
+                ),
+            ],
+            axis=2,
+        )
+        small_sum = choose(small_grads, core, 1) + swap(choose(small_grads, 1 - core, 1))
+        small_sum = small_sum.reshape(grid + (count,))
+        if square:
+            at_q, at_y = lax.axis_index("q"), lax.axis_index("y")
+            here = [choose(small_sum, at_q, 1), choose(small_sum, 1 - at_q, 1)]
+            across = [(0, 3), (3, 0), (1, 2), (2, 1)]
+            own = choose(here[0], at_y, 1)
+            parts = together(
+                choose(here[0], 1 - at_y, 1), choose(here[1], at_y, 1), choose(here[1], 1 - at_y, 1)
+            )
+            parts = together(
+                swap(parts[0], "y"), swap(parts[1], "q"), lax.ppermute(parts[2], ("q", "y"), across)
+            )
+            small_sum = own + parts[0] + parts[1] + parts[2]
+        else:
+            small_sum = add(small_sum, send(small_sum, "y", 2), "y", 2)
+            small_sum = add(small_sum, send(small_sum, "q", 1), "q", 1)
+        one_rows = -(-count // (16 * width)) * 16
+        small_sum = jnp.pad(low(small_sum), ((0, 0), (0, one_rows * width - count)))
+        small_sum = small_sum.reshape(grid[0], one_rows, width)
+        return small_sum
+
     grad_fourth, gain_five = norm_back(
         cotangent.astype(f32), normed_last, inverse_last, gain_table[5]
     )
@@ -696,7 +743,12 @@
         grad_fourth, gain_table[4], inner_two, outer_two, fourth_kept
     )
 
-    outer_two_sum = early_sum(outer_two_grad(0, 8))
+    if square:
+        outer_two_rows = low(outer_two_grad(0, 8)).reshape(grid[0], 4, units, width)
+        outer_two_a, grad_third = together(outer_two_rows[:, 1:3], grad_third)
+        outer_two_a = swap(outer_two_a, "q")
+    else:
+        outer_two_sum = early_sum(outer_two_grad(0, 8))
 
     conv_out_grad = pair_rows(low(grad_third))
     swish_grad = right_product(conv_out_grad, point_full)
@@ -704,10 +756,13 @@
     mixed_grad, gain_three = split_norm_back(act_grad, normed_mid, inverse_mid, gain_mid)
     mixed_low = low(mixed_grad)
     grad_low, grad_high = halos(mixed_low)
-    if square:
-        inner_two = low(inner_two_grad(0, 8)).reshape(grid[0], 4, units, width)
-        inner_two_a, mixed_low = together(inner_two[:, 1:3], mixed_low)
-        inner_two_a = swap(inner_two_a, "q")
+    point_grad = by_chip(low(left_product(swish, conv_out_grad)))
+    point_a = send(point_grad, "q", 1)
+    if square:
+        mixed_low, point_a = together(mixed_low, point_a)
+    point_half = add(point_grad, point_a, "q", 1)
+    point_b = send(point_half, "y", 1)
+    inner_two_sum = early_sum(inner_two_grad(0, 8))
     glu_back, depth_grad = conv_back(
         info, glu_low, glu_rows, glu_high, grad_low, mixed_low, grad_high, depth, group
     )
@@ -718,19 +773,17 @@
         )
     )
     conv_entry_grad = pair_sum(right_product(gate_grad, glu_full))
-    point_grad = by_chip(low(left_product(swish, conv_out_grad)))
     glu_grad = by_chip(low(left_product(conv_entry, gate_grad)))
     back_conv, gain_two = norm_back(conv_entry_grad, normed_conv, inverse_conv, gain_table[2])
     grad_second = grad_third + back_conv
 
     att_out_grad = pair_rows(low(grad_second))
     glu_a = send(glu_grad, "y", 2)
-    point_a = send(point_grad, "y", 2)
     attended_grad = low(right_product(att_out_grad, merge_full))
     query_grad, key_grad, value_grad, table_sums = attend_back(info, bias, query, both, attended_grad)
-    query_grad, key_grad, value_grad, glu_a, point_a = together(
-        query_grad, key_grad, value_grad, glu_a, point_a
-    )
+    query_grad, key_grad, value_grad, glu_a = together(query_grad, key_grad, value_grad, glu_a)
+    if square:
+        query_grad, outer_two_a, point_b = together(query_grad, outer_two_a, point_b)
     att_out_grad, query_grad = together(att_out_grad, query_grad)
     merge_grad = low(left_product(attended, att_out_grad)).reshape(chips // 2, 2, share, width)
     merge_grad = ordered(
@@ -738,7 +791,6 @@
     )
     merge_grad = by_chip(merge_grad.reshape(chips * share, width))
     glu_half = add(glu_grad, glu_a, "y", 2)
-    point_half = add(point_grad, point_a, "y", 2)
     both_grad = jnp.concatenate([key_grad, value_grad], axis=1).reshape(grid[2], pair, width)
     if grid[2] == 2:
         place = lax.axis_index("y")
@@ -748,22 +800,17 @@
         both_received = low(lax.psum_scatter(both_grad, "y", scatter_dimension=0, tiled=False))
         both_grad = both_received
     if square:
-        glu_b, point_b, merge_a, outer_two_a, inner_two_a, both_grad = together(
+        outer_two_b = low(outer_two_rows[:, 3].astype(f32) + outer_two_a[:, 1].astype(f32))
+        glu_b, merge_a, outer_two_b, both_grad = together(
             pick(glu_half, "q", 1),
-            pick(point_half, "q", 1),
             pick(merge_grad, "q", 1),
-            outer_two_sum[1:3],
-            inner_two_a,
+            outer_two_b,
             both_grad,
         )
-        inner_two_b = low(inner_two[:, 3].astype(f32) + inner_two_a[:, 1].astype(f32))
-        inner_two_b = swap(inner_two_b, "y")
-        glu_b, point_b, merge_a, outer_two_a = [
-            swap(part, "q") for part in (glu_b, point_b, merge_a, outer_two_a)
-        ]
+        glu_b, merge_a = swap(glu_b, "q"), swap(merge_a, "q")
+        outer_two_b = swap(outer_two_b, "y")
     else:
-        glu_b, point_b, merge_a = [send(part, "q", 1) for part in (glu_half, point_half, merge_grad)]
-        inner_two_sum = early_sum(inner_two_grad(0, 8))
+        glu_b, merge_a = send(glu_half, "q", 1), send(merge_grad, "q", 1)
     triple_grad = jnp.concatenate([query_grad, both_grad], axis=1)
     attend_grad = low(left_product(att_entry, triple_grad))
     attend_grad = attend_grad.reshape(grid + (2 * share, 3 * half))
@@ -772,43 +819,36 @@
     grad_first = grad_second + back_att
     attend_sum = last_sum(attend_grad)
     if square:
-        inner_two_sum = inner_two[:, 0].astype(f32) + inner_two_a[:, 0].astype(f32)
-    input_grad, gain_zero, inner_one_grad, outer_one_grad = feed_back(
-        grad_first, gain_table[0], inner_one, outer_one, first_kept
-    )
-    if square:
-        near_o, near_i, glu_b, point_b, merge_a, inner_two_b = together(
-            low(outer_one_grad(1, 3)),
-            low(inner_one_grad(2, 4)),
-            glu_b,
-            point_b,
-            merge_a,
-            inner_two_b,
-        )
+        outer_two_sum = outer_two_rows[:, 0].astype(f32) + outer_two_a[:, 0].astype(f32)
+    input_grad, gain_zero, inner_one_grad, outer_one_grad, glu_b = feed_back(
+        grad_first, gain_table[0], inner_one, outer_one, first_kept, glu_b
+    )
+    if square:
+        near_o, near_i = together(low(outer_one_grad(1, 3)), low(inner_one_grad(2, 4)))
         near_o, near_i = swap(near_o, "q"), swap(near_i, "y")
-        inner_two_sum = low(inner_two_sum + inner_two_b.astype(f32))
-    merge_half = add(merge_grad, merge_a, "q", 1)
-    merge_b = send(merge_half, "y", 1)
-    mixed_sum = jnp.concatenate(
-        [
-            add(glu_half, glu_b, "q", 1),
-            add(point_half, point_b, "q", 1),
-            add(merge_half, merge_b, "y", 1),
-        ]
-        + ([inner_two_sum] if square else []),
-        axis=1,
-    )
-    if square:
-        near_o, near_i, far_o, far_i, mixed_sum, outer_two_a, attend_sum = together(
+    if square:
+        near_o, near_i, glu_b, outer_two_b, far_o, far_i, merge_a, attend_sum, inner_two_sum = together(
             near_o,
             near_i,
+            glu_b,
+            outer_two_b,
             low(outer_one_grad(5, 7)),
             low(inner_one_grad(6, 8)),
-            mixed_sum,
-            outer_two_a,
+            merge_a,
             attend_sum,
+            inner_two_sum,
         )
-        far_o, far_i = swap(far_o, "q"), swap(far_i, "y")
+    edge_half = add(merge_grad, merge_a, "q", 1)
+    edge_b = send(edge_half, "y", 1)
+    edge_b, table_sums, depth_grad, gain_one, gain_two, gain_three, gain_four, gain_five = together(
+        edge_b, table_sums, depth_grad, gain_one, gain_two, gain_three, gain_four, gain_five
+    )
+    mixed_sum = [add(glu_half, glu_b, "q", 1), add(point_half, point_b, "y", 1)]
+    if square:
+        outer_two_sum = low(outer_two_sum + outer_two_b.astype(f32))
+        mixed_sum += [outer_two_sum, add(edge_half, edge_b, "y", 1)]
+    mixed_sum = jnp.concatenate(mixed_sum, axis=1)
+    if square:
         mixed_sum = last_sum(mixed_sum)
 
         def second(first, got_o, got_i):
@@ -824,23 +864,27 @@
             return [part.reshape(grid[0], units // 2, width) for part in sums]
 
         near = second(0, near_o, near_i)
-        *near, far_o, far_i = together(swap(near[0], "y"), swap(near[1], "q"), far_o, far_i)
-        near = jnp.concatenate(third(0, near_o, near_i, *near), axis=1)
-        near, mixed_sum = together(near, mixed_sum)
-        near_sum = last_sum(near)
+        across_q = jnp.concatenate([far_o, near[1]], axis=0)
+        across_y = jnp.concatenate([far_i, near[0]], axis=0)
+        across_q, across_y = together(across_q, across_y)
+        across_q, across_y = swap(across_q, "q"), swap(across_y, "y")
+        small_sum = small_of(
+            table_sums, depth_grad, gain_zero, gain_one, gain_two, gain_three, gain_four, gain_five
+        )
+        across_q, across_y, small_sum = together(across_q, across_y, small_sum)
+        far_o, far_i = across_q[: 2 * size], across_y[: 2 * size]
+        near = [across_y[2 * size :], across_q[2 * size :]]
+        near = third(0, near_o, near_i, *near)
         far_o, attend_sum = together(far_o, attend_sum)
         far = second(4, far_o, far_i)
-        *far, table_sums, depth_grad, gain_one, gain_two, gain_three, gain_four, gain_five = together(
-            *far, table_sums, depth_grad, gain_one, gain_two, gain_three, gain_four, gain_five
-        )
         far = together(swap(far[0], "y"), swap(far[1], "q"))
         far = third(4, far_o, far_i, *far)
-        outer_two_b = swap(low(outer_two_sum[3].astype(f32) + outer_two_a[1].astype(f32)), "y")
-        outer_sum_two = outer_two_sum[0].astype(f32) + outer_two_a[0].astype(f32)
-        outer_sum_two = low(outer_sum_two + outer_two_b.astype(f32))
-        inner_sum_two = mixed_sum[4 * share :]
     else:
         mixed_sum = last_sum(mixed_sum)
+        edge_sum = last_sum(edge_b)
+        small_sum = small_of(
+            table_sums, depth_grad, gain_zero, gain_one, gain_two, gain_three, gain_four, gain_five
+        )
         inner_sum_one = by_chip(low(inner_one_grad(0, 8)))
         outer_sum_one = by_chip(low(outer_one_grad(0, 8)))
         inner_sum_one = send(send(inner_sum_one, "y", 2), "q", 1)
@@ -850,54 +894,20 @@
     attend_half = add(attend_sum, send(attend_sum, "q", 0), "q", 0)
     attend_sum = add(attend_half, send(attend_half, "y", 0), "y", 0)
 
-    table_grad = jnp.einsum(
-        "hw,wb->bh", table_sums.reshape(heads, -1), hits.astype(f32), precision=lax.Precision.HIGHEST
-    )
-
-    def of_core(values, dim):
-        empty = jnp.zeros_like(values)
-        return jnp.stack(
-            [jnp.where(core == 0, values, empty), jnp.where(core == 1, values, empty)], axis=dim
-        )
-
-    gain_three = of_core(gain_three.reshape(chips, share), 1).reshape(width)
-    gain_grads = jnp.stack([gain_zero, gain_one, gain_two, gain_three, gain_four, gain_five])
-    small_grads = jnp.concatenate(
-        [
-            gain_grads.reshape(6, chips, 2, share).transpose(1, 2, 0, 3).reshape(chips, 2, -1),
-            of_core(table_grad, 1).reshape(chips, 2, -1),
-            of_core(depth_grad.reshape(taps, chips, share).transpose(1, 0, 2), 1).reshape(
-                chips, 2, -1
-            ),
-        ],
-        axis=2,
-    )
-    small_sum = choose(small_grads, core, 1) + swap(choose(small_grads, 1 - core, 1))
-    small_sum = small_sum.reshape(grid + (count,))
-    if square:
-        at_q, at_y = lax.axis_index("q"), lax.axis_index("y")
-        here = [choose(small_sum, at_q, 1), choose(small_sum, 1 - at_q, 1)]
-        across = [(0, 3), (3, 0), (1, 2), (2, 1)]
-        small_sum = (
-            choose(here[0], at_y, 1)
-            + swap(choose(here[0], 1 - at_y, 1), "y")
-            + swap(choose(here[1], at_y, 1), "q")
-            + lax.ppermute(choose(here[1], 1 - at_y, 1), ("q", "y"), across)
-        )
-    else:
-        small_sum = add(small_sum, send(small_sum, "y", 2), "y", 2)
-        small_sum = add(small_sum, send(small_sum, "q", 1), "q", 1)
-    one_rows = -(-count // (16 * width)) * 16
-    small_sum = jnp.pad(low(small_sum), ((0, 0), (0, one_rows * width - count)))
-    small_sum = small_sum.reshape(grid[0], one_rows, width)
-
-    if square:
-        far_sum, near_sum = together(jnp.concatenate(far + [small_sum], axis=1), near_sum)
-        far_sum = last_sum(far_sum)
-        half_units = units // 2
-        inner_sum_one = jnp.concatenate([near_sum[:half_units], far_sum[:half_units]])
-        outer_sum_one = jnp.concatenate([near_sum[half_units:], far_sum[half_units:units]])
-        small_sum = far_sum[units:]
+    if square:
+        one_sum = jnp.concatenate(near + far + [small_sum], axis=1)
+        one_sum, mixed_sum, inner_two_sum = together(one_sum, mixed_sum, inner_two_sum)
+        one_sum = last_sum(one_sum)
+        inner_two_a = swap(inner_two_sum[2:], "y")
+        inner_two_b = swap(low(inner_two_sum[1].astype(f32) + inner_two_a[0].astype(f32)), "q")
+        inner_sum_two = inner_two_sum[0].astype(f32) + inner_two_a[1].astype(f32)
+        inner_sum_two = low(inner_sum_two + inner_two_b.astype(f32))
+        quarters = [one_sum[at * (units // 2) : (at + 1) * (units // 2)] for at in range(4)]
+        inner_sum_one = jnp.concatenate([quarters[0], quarters[2]])
+        outer_sum_one = jnp.concatenate([quarters[1], quarters[3]])
+        small_sum = one_sum[2 * units :]
+        outer_sum_two = mixed_sum[3 * share : 3 * share + units]
+        edge_sum = mixed_sum[3 * share + units :]
     else:
         one_sum = last_sum(jnp.concatenate([inner_sum_one, outer_sum_one, small_sum], axis=1))
         inner_sum_one, outer_sum_one = one_sum[:units], one_sum[units : 2 * units]
@@ -918,7 +928,7 @@
     attend_out = whole_columns(attend_sum, (3, half), 2)
     glu_out = whole_columns(mixed_sum[: 2 * share], (2, chips, share), 3)
     point_out = mixed_sum[2 * share : 3 * share].astype(f32)
-    merge_out = mixed_sum[3 * share : 4 * share].astype(f32)
+    merge_out = edge_sum.astype(f32)
     inner_out = jnp.stack([inner_sum_one.T, inner_sum_two.T]).astype(f32)
     outer_out = jnp.stack([outer_sum_one, outer_sum_two]).astype(f32)
     small_out = small_sum.reshape(-1)[:count].astype(f32)

time: 608 us -> 597 us (0.982)
  waiting for transfers between devices: 240 us -> 221 us
  starting transfers between devices: 62.6 us -> 71.5 us
    reduce_scatter x5 -> x4, waiting for transfers between devices: 20.8 us -> 5.15 us  [last_sum(): return lax.psum_scatter(values, 'p', scatter_dimension=0, tiled=False)]
    ppermute x67 -> x65, starting transfers between devices: 46.4 us -> 55.7 us  [swap(): return lax.ppermute(values, axis, CORES)]
    ppermute x67 -> x65, waiting for transfers between devices: 216 us -> 213 us  [swap(): return lax.ppermute(values, axis, CORES)]
    unnamed x262 -> x242, local copies, waits for them, and re-layouts: 29.2 us -> 28.5 us
  transfers between devices with their start and end apart: 82 -> 79, of which waited for: 36 -> 42; matrix products, arithmetic and copies ran while one was open for 31% -> 32% of each run, Pallas kernels for 7% -> 7%
where the time goes in v5:
time: 597 us; the launch traced here: 589 us
  waiting for transfers between devices  221 us (37%)
  local copies, waits for them, and re-layouts  106 us (18%)
  matrix products  82.5 us (14%)
  starting transfers between devices  71.5 us (12%)
  other arithmetic  48.3 us (8%)
  Pallas kernels  40.5 us (7%)
  between operations  18.5 us (3%)
    ppermute x65, waiting for transfers between devices, swap(): return lax.ppermute(values, axis, CORES)  213 us
    ppermute x65, starting transfers between devices, swap(): return lax.ppermute(values, axis, CORES)  55.7 us
    dot_general x18, matrix products, left_product(): jnp.einsum('nd,nf->df', left_in, right_in, preferred_element_type=jnp.flo...  41.4 us
    unnamed x242, local copies, waits for them, and re-layouts  28.5 us
    dot_general x8, matrix products, right_product(): jnp.einsum('nf,df->nd', left_in, right_in, preferred_element_type=jnp.flo...  26.5 us
    pallas_call x1, Pallas kernels, attend_back(): pl.pallas_call(attend_back_kernel, grid=(pairs,), in_specs=attend_specs(r...  19.9 us
    dynamic_update_slice x12, local copies, waits for them, and re-layouts, placed(): result = lax.dynamic_update_slice(result, part[:, None, None], at)  15.4 us
    dot_general x8, matrix products, product(): return jnp.dot(left_in, right_in, preferred_element_type=jnp.float32)  14.2 us
  transfers between devices with their start and end apart: 79, of which 42 were waited for; matrix products, arithmetic and copies ran while one was open for 32% of the time, Pallas kernels for 7%

profile of v5, /device:TPU:0, one launch (start us, length us, event | category | flops | bytes accessed | tf_op | source)
XLA Modules:
  0.0 588.5 jit_solution(12152777891613751931)
XLA Ops:
  9.5 3.0 collective-permute-start.7
  14.4 10.0 %collective-permute-done.7 = bf16[256,1024]{1,0:T(8,128)(2,1)S(1)} collective-permute-done((bf16[256,1024]{1,0:T(8,128)(2,1)S(1)}, bf16[256,1024]{1,0:T(8,128)(2,1)S(1)}, u32[]{:S(2)}, u32[]{:S(2)}) %collective-permute-start.7) | collective-permute-done | bytes 524320 | tf_op jit(solution)/shard_map/ppermute | solution.py:346
  30.3 3.5 dynamic-slice_reduce_fusion
  35.6 3.0 collective-permute-done.9
  38.6 2.7 pad_maximum_fusion.1
  47.0 20.3 %collective-permute-done.13 = bf16[512,1024]{0,1:T(8,128)(2,1)} collective-permute-done((bf16[512,1024]{0,1:T(8,128)(2,1)}, bf16[512,1024]{0,1:T(8,128)(2,1)}, u32[]{:S(2)}, u32[]{:S(2)}) %collective-permute-start.13) | collective-permute-done | bytes 1048608 | tf_op jit(solution)/shard_map/ppermute | solution.py:346
  92.8 16.9 %collective-permute-done.2 = bf16[512,1024]{1,0:T(8,128)(2,1)} collective-permute-done((bf16[512,1024]{1,0:T(8,128)(2,1)S(1)}, bf16[512,1024]{1,0:T(8,128)(2,1)}, u32[]{:S(2)}, u32[]{:S(2)}) %collective-permute-start.2) | collective-permute-done | bytes 1048608 | tf_op jit(solution)/shard_map/ppermute | solution.py:346
  122.0 2.4 slice.485
  133.5 8.6 %collective-permute-done.15 = bf16[512,1024]{1,0:T(8,128)(2,1)} collective-permute-done((bf16[512,1024]{1,0:T(8,128)(2,1)}, bf16[512,1024]{1,0:T(8,128)(2,1)}, u32[]{:S(2)}, u32[]{:S(2)}) %collective-permute-start.15) | collective-permute-done | bytes 1048608 | tf_op jit(solution)/shard_map/ppermute | solution.py:346
  142.1 6.5 %collective-permute-done.16 = bf16[4,64,1536]{2,1,0:T(8,128)(2,1)} collective-permute-done((bf16[4,64,1536]{2,1,0:T(8,128)(2,1)}, bf16[4,64,1536]{2,1,0:T(8,128)(2,1)}, u32[]{:S(2)}, u32[]{:S(2)}) %collective-permute-start.16) | collective-permute-done | bytes 786464 | tf_op jit(solution)/shard_map/ppermute | solution.py:346
  154.7 3.5 copy-done.83
  158.6 5.5 multiply_convert_fusion.3
  175.4 17.7 %collective-permute-done.20 = bf16[4,64,1536]{2,1,0:T(8,128)(2,1)S(1)} collective-permute-done((bf16[4,64,1536]{2,1,0:T(8,128)(2,1)}, bf16[4,64,1536]{2,1,0:T(8,128)(2,1)S(1)}, u32[]{:S(2)}, u32[]{:S(2)}) %collective-permute-start.20) | collective-permute-done | bytes 786464 | tf_op jit(solution)/shard_map/ppermute | solution.py:346
  196.2 3.3 convolution_convert_fusion.3
  208.0 11.8 %collective-permute-done.23 = bf16[384,1024]{1,0:T(8,128)(2,1)} collective-permute-done((bf16[384,1024]{1,0:T(8,128)(2,1)S(1)}, bf16[384,1024]{1,0:T(8,128)(2,1)}, u32[]{:S(2)}, u32[]{:S(2)}) %collective-permute-start.23) | collective-permute-done | bytes 786464 | tf_op jit(solution)/shard_map/ppermute | solution.py:346
  221.2 8.8 %attend.1 = bf16[384,512]{1,0:T(8,128)(2,1)S(1)} custom-call(s32[3]{0:T(128)S(1)} %pad_add_fusion.info_ref.refs_0_, f32[4,2,1536]{2,1,0:T(2,128)S(1)} %fusion.76.bias_ref, bf16[384,512]{1,0:T(8,128)(2,1)S(1)} %slice.504.query_ref, bf16[768,1024]{1,0:T(8,128)(2,1)S(1)} %pad_maximum_fusion.3.key_ref.value_ref, ...), custom_call_target="tpu_custom_call" | custom-call | flops 603979776 | bytes 2359296 | tf_op jit(solution)/shard_map/attend/pallas_call | solution.py:143
  246.2 4.5 collective-permute-start.28
  252.2 4.2 conv.1
  268.1 4.4 fusion.135
  272.5 3.6 fusion.63
  287.3 4.1 multiply_convert_fusion.1
  293.5 2.4 convolution_convert_fusion.1
  303.8 5.8 convolution_convert_fusion
  318.1 4.5 collective-permute-start.38
  322.7 6.8 %collective-permute-done.39 = bf16[4,2,32,1024]{3,2,0,1:T(8,128)(2,1)S(1)} collective-permute-done((bf16[4,2,32,1024]{3,2,0,1:T(8,128)(2,1)S(1)}, bf16[4,2,32,1024]{3,2,0,1:T(8,128)(2,1)S(1)}, u32[]{:S(2)}, u32[]{:S(2)}) %collective-permute-start.39) | collective-permute-done | bytes 524320 | tf_op jit(solution)/shard_map/ppermute | solution.py:346
  329.5 7.5 %conv_back.1 = (f32[384,512]{1,0:T(8,128)S(1)}, f32[31,512]{1,0:T(8,128)S(1)}) custom-call(s32[3]{0:T(128)S(1)} %pad_add_fusion.info_ref.refs_0_, bf16[16,512]{1,0:T(8,128)(2,1)S(1)} %collective-permute-done.28.refs_1_, bf16[384,512]{1,0:T(8,128)(2,1)S(1)} %multiply_convert_fusion.12.refs_2_, bf16[16,512]{1,0:T(8,128)(2,1)S(1)} %collective-permute-done.29.refs_3_, ...), custom_call_target="tpu_custom_call" | custom-call | flops 24379392 | bytes 1572864 | tf_op jit(solution)/shard_map/conv_back/pallas_call | solution.py:301
  344.1 2.4 collective-permute-start.43
  348.7 19.9 %attend_back.1 = (bf16[384,512]{1,0:T(8,128)(2,1)S(1)}, f32[768,512]{1,0:T(8,128)S(1)}, f32[768,512]{1,0:T(8,128)}, f32[4,2,1536]{2,1,0:T(2,128)S(1)}) custom-call(s32[3]{0:T(128)S(1)} %pad_add_fusion.info_ref.refs_0_, f32[4,2,1536]{2,1,0:T(2,128)S(1)} %copy-done.2, bf16[384,512]{1,0:T(8,128)(2,1)S(1)} %slice.504.query_ref, bf16[768,1024]{1,0:T(8,128)(2,1)} %copy-done, ...), custom_call_target="tpu_custom_call" | custom-call | flops 1509949440 | bytes 2359296 | tf_op jit(solution)/shard_map/attend_back/pallas_call | solution.py:166
  376.1 10.6 %collective-permute-done.44 = bf16[4,2,128,1024]{3,2,0,1:T(8,128)(2,1)S(1)} collective-permute-done((bf16[4,2,128,1024]{3,2,0,1:T(8,128)(2,1)S(1)}, bf16[4,2,128,1024]{3,2,0,1:T(8,128)(2,1)S(1)}, u32[]{:S(2)}, u32[]{:S(2)}) %collective-permute-start.44) | collective-permute-done | bytes 2097184 | tf_op jit(solution)/shard_map/ppermute | solution.py:346
  388.5 2.6 fusion.15
  393.2 3.5 convolution_convert_fusion.2
  396.8 3.7 fusion.154
  410.3 5.7 multiply_convert_fusion
  415.9 5.0 collective-permute-done.50
  420.9 3.0 convolution_convert_fusion.8
  423.9 2.9 convolution_convert_fusion.7
  427.7 2.3 collective-permute-start.53
  432.0 3.3 convolution_convert_fusion.5
  435.3 2.8 convolution_convert_fusion.6
  439.3 14.6 %collective-permute-done.52 = bf16[512,1024]{1,0:T(8,128)(2,1)} collective-permute-done((bf16[512,1024]{1,0:T(8,128)(2,1)}, bf16[512,1024]{1,0:T(8,128)(2,1)}, u32[]{:S(2)}, u32[]{:S(2)}) %collective-permute-start.52) | collective-permute-done | bytes 1048608 | tf_op jit(solution)/shard_map/ppermute | solution.py:346
  457.0 2.5 fusion.1
  480.6 26.4 %collective-permute-done.60 = f32[4,1216]{1,0:T(4,128)S(1)} collective-permute-done((f32[4,1216]{1,0:T(4,128)S(1)}, f32[4,1216]{1,0:T(4,128)S(1)}, u32[]{:S(2)}, u32[]{:S(2)}) %collective-permute-start.60) | collective-permute-done | bytes 19488 | tf_op jit(solution)/shard_map/ppermute | solution.py:346
  518.0 6.0 %collective-permute-done.63 = bf16[256,1024]{1,0:T(8,128)(2,1)S(1)} collective-permute-done((bf16[256,1024]{1,0:T(8,128)(2,1)S(1)}, bf16[256,1024]{1,0:T(8,128)(2,1)S(1)}, u32[]{:S(2)}, u32[]{:S(2)}) %collective-permute-start.63) | collective-permute-done | bytes 524320 | tf_op jit(solution)/shard_map/ppermute | solution.py:346
  530.8 6.7 %collective-permute-done.65 = bf16[2,64,1536]{2,1,0:T(8,128)(2,1)S(1)} collective-permute-done((bf16[2,64,1536]{2,1,0:T(8,128)(2,1)S(1)}, bf16[2,64,1536]{2,1,0:T(8,128)(2,1)S(1)}, u32[]{:S(2)}, u32[]{:S(2)}) %collective-permute-start.65) | collective-permute-done | bytes 393248 | tf_op jit(solution)/shard_map/ppermute | solution.py:346
  539.1 4.2 collective-permute-done.66
  550.2 11.5 %collective-permute-done.69 = bf16[2,128,1024]{2,1,0:T(8,128)(2,1)S(1)} collective-permute-done((bf16[2,128,1024]{2,1,0:T(8,128)(2,1)}, bf16[2,128,1024]{2,1,0:T(8,128)(2,1)S(1)}, u32[]{:S(2)}, u32[]{:S(2)}) %collective-permute-start.69) | collective-permute-done | bytes 524320 | tf_op jit(solution)/shard_map/ppermute | solution.py:346
  566.3 3.7 collective-permute-done.70
  571.1 4.1 reduce-scatter.11.cloned.1.call-done
  (675 shorter events, 247.1 us)
Async XLA Ops:
  7.2 35.9 %all-gather.11.cloned.1.call-start = ((), (), s32[]{:S(2)}) async-start(), calls=%async_computation.9 | async-start | bytes 1310720 | tf_op jit(solution)/shard_map/all_gather | solution.py:569
  9.1 66.8 %all-gather.9.cloned.1.call-start = ((), (), s32[]{:S(2)}) async-start(), calls=%async_computation.8 | async-start | bytes 1474560 | tf_op jit(solution)/shard_map/all_gather | solution.py:569
  9.5 14.9 %collective-permute-start.7 = (bf16[256,1024]{1,0:T(8,128)(2,1)S(1)}, bf16[256,1024]{1,0:T(8,128)(2,1)S(1)}, u32[]{:S(2)}, u32[]{:S(2)}) collective-permute-start(bf16[256,1024]{1,0:T(8,128)(2,1)S(1)} %get-tuple-element.366), channel_id=1, source_target_pairs={{0,4},{4,0},{1,5},{5,1},{2,6},{6,2},{3,7},{7,3},{8,12},{12,8},{9,1... | collective-permute-start | bytes 1572872 | tf_op jit(solution)/shard_map/ppermute | solution.py:346
  12.5 13.4 %collective-permute-start.8 = (bf16[256,1024]{1,0:T(8,128)(2,1)S(1)}, bf16[256,1024]{1,0:T(8,128)(2,1)S(1)}, u32[]{:S(2)}, u32[]{:S(2)}) collective-permute-start(bf16[256,1024]{1,0:T(8,128)(2,1)S(1)} %get-tuple-element.366), channel_id=1, source_target_pairs={{0,2},{2,0},{1,3},{3,1},{4,6},{6,4},{5,7},{7,5},{8,10},{10,8},{9,1... | collective-permute-start | bytes 1572872 | tf_op jit(solution)/shard_map/ppermute | solution.py:346
  14.3 13.1 %collective-permute-start = (bf16[1,1216]{1,0:T(2,128)(2,1)S(1)}, bf16[1,1216]{1,0:T(2,128)(2,1)S(1)}, u32[]{:S(2)}, u32[]{:S(2)}) collective-permute-start(bf16[1,1216]{1,0:T(2,128)(2,1)S(1)} %broadcast_in_dim.43), channel_id=1, source_target_pairs={{0,1},{1,0},{2,3},{3,2},{4,5},{5,4},{6,7},{7,6},{8,9},{9,8},{10,11... | collective-permute-start | bytes 7304 | tf_op jit(solution)/shard_map/ppermute | solution.py:346
  25.9 12.7 %collective-permute-start.9 = (bf16[256,1024]{1,0:T(8,128)(2,1)S(1)}, bf16[256,1024]{1,0:T(8,128)(2,1)}, u32[]{:S(2)}, u32[]{:S(2)}) collective-permute-start(bf16[256,1024]{1,0:T(8,128)(2,1)S(1)} %collective-permute-done.7), channel_id=1, source_target_pairs={{0,2},{2,0},{1,3},{3,1},{4,6},{6,4},{5,7},{7,5},{8,10},{10,8},{9,1... | collective-permute-start | bytes 1572872 | tf_op jit(solution)/shard_map/ppermute | solution.py:346
  28.4 92.4 %all-gather.13.cloned.1.call-start = ((), (), s32[]{:S(2)}) async-start(), calls=%async_computation.10 | async-start | bytes 2293760 | tf_op jit(solution)/shard_map/all_gather | solution.py:569
  29.9 15.2 %collective-permute-start.10 = (bf16[32,1536]{1,0:T(8,128)(2,1)S(1)}, bf16[32,1536]{1,0:T(8,128)(2,1)S(1)}, u32[]{:S(2)}, u32[]{:S(2)}) collective-permute-start(bf16[32,1536]{1,0:T(8,128)(2,1)S(1)} %bitcast.477), channel_id=1, source_target_pairs={{0,1},{1,0},{2,3},{3,2},{4,5},{5,4},{6,7},{7,6},{8,9},{9,8},{10,11... | collective-permute-start | bytes 294920 | tf_op jit(solution)/shard_map/ppermute | solution.py:346
  43.1 24.2 %collective-permute-start.13 = (bf16[512,1024]{0,1:T(8,128)(2,1)}, bf16[512,1024]{0,1:T(8,128)(2,1)}, u32[]{:S(2)}, u32[]{:S(2)}) collective-permute-start(bf16[512,1024]{0,1:T(8,128)(2,1)} %all-gather.11.cloned.1.call-done), channel_id=1, source_target_pairs={{0,2},{2,0},{1,3},{3,1},{4,6},{6,4},{5,7},{7,5},{8,10},{10,8},{9,1... | collective-permute-start | bytes 3145736 | tf_op jit(solution)/shard_map/ppermute | solution.py:346
  43.6 25.0 %collective-permute-start.12 = (bf16[512,1024]{0,1:T(8,128)(2,1)}, bf16[512,1024]{0,1:T(8,128)(2,1)S(1)}, u32[]{:S(2)}, u32[]{:S(2)}) collective-permute-start(bf16[512,1024]{0,1:T(8,128)(2,1)} %all-gather.11.cloned.1.call-done), channel_id=1, source_target_pairs={{0,4},{4,0},{1,5},{5,1},{2,6},{6,2},{3,7},{7,3},{8,12},{12,8},{9,1... | collective-permute-start | bytes 3145736 | tf_op jit(solution)/shard_map/ppermute | solution.py:346
  68.7 199.4 %all-gather.15.cloned.1.call-start = ((), (), s32[]{:S(2)}) async-start(), calls=%async_computation.11 | async-start | bytes 10485760 | tf_op jit(solution)/shard_map/all_gather | solution.py:569
  75.4 380.6 %reduce-scatter.7.cloned.1.call-start = ((), (), s32[]{:S(2)}) async-start(), calls=%async_computation.5 | async-start | bytes 5242880 | tf_op jit(solution)/shard_map/reduce_scatter | solution.py:686
  78.8 13.6 %collective-permute-start.5 = (bf16[4,16,1024]{2,1,0:T(8,128)(2,1)}, bf16[4,16,1024]{2,1,0:T(8,128)(2,1)}, u32[]{:S(2)}, u32[]{:S(2)}) collective-permute-start(bf16[4,16,1024]{2,1,0:T(8,128)(2,1)} %slice.478), channel_id=1, source_target_pairs={{0,6},{6,0},{2,4},{4,2},{1,7},{7,1},{3,5},{5,3},{8,14},{14,8},{10,... | collective-permute-start | bytes 393224 | tf_op jit(solution)/shard_map/ppermute | solution.py:591
  80.3 12.5 %collective-permute-start.4 = (bf16[4,16,1024]{2,1,0:T(8,128)(2,1)}, bf16[4,16,1024]{2,1,0:T(8,128)(2,1)}, u32[]{:S(2)}, u32[]{:S(2)}) collective-permute-start(bf16[4,16,1024]{2,1,0:T(8,128)(2,1)} %slice.478), channel_id=1, source_target_pairs={{0,2},{2,0},{1,3},{3,1},{4,6},{6,4},{5,7},{7,5},{8,10},{10,8},{9,1... | collective-permute-start | bytes 393224 | tf_op jit(solution)/shard_map/ppermute | solution.py:346
  82.4 27.4 %collective-permute-start.2 = (bf16[512,1024]{1,0:T(8,128)(2,1)S(1)}, bf16[512,1024]{1,0:T(8,128)(2,1)}, u32[]{:S(2)}, u32[]{:S(2)}) collective-permute-start(bf16[512,1024]{1,0:T(8,128)(2,1)S(1)} %bitcast.400), channel_id=1, source_target_pairs={{0,2},{2,0},{1,3},{3,1},{4,6},{6,4},{5,7},{7,5},{8,10},{10,8},{9,1... | collective-permute-start | bytes 3145736 | tf_op jit(solution)/shard_map/ppermute | solution.py:346
  82.8 28.3 %collective-permute-start.1 = (bf16[512,1024]{1,0:T(8,128)(2,1)S(1)}, bf16[512,1024]{1,0:T(8,128)(2,1)}, u32[]{:S(2)}, u32[]{:S(2)}) collective-permute-start(bf16[512,1024]{1,0:T(8,128)(2,1)S(1)} %bitcast.401), channel_id=1, source_target_pairs={{0,4},{4,0},{1,5},{5,1},{2,6},{6,2},{3,7},{7,3},{8,12},{12,8},{9,1... | collective-permute-start | bytes 3145736 | tf_op jit(solution)/shard_map/ppermute | solution.py:346
  92.4 41.1 %collective-permute-start.14 = (bf16[512,1024]{0,1:T(8,128)(2,1)}, bf16[512,1024]{0,1:T(8,128)(2,1)}, u32[]{:S(2)}, u32[]{:S(2)}) collective-permute-start(bf16[512,1024]{0,1:T(8,128)(2,1)} %collective-permute-done.13), channel_id=1, source_target_pairs={{0,4},{4,0},{1,5},{5,1},{2,6},{6,2},{3,7},{7,3},{8,12},{12,8},{9,1... | collective-permute-start | bytes 3145736 | tf_op jit(solution)/shard_map/ppermute | solution.py:346
  118.7 23.4 %collective-permute-start.15 = (bf16[512,1024]{1,0:T(8,128)(2,1)}, bf16[512,1024]{1,0:T(8,128)(2,1)}, u32[]{:S(2)}, u32[]{:S(2)}) collective-permute-start(bf16[512,1024]{1,0:T(8,128)(2,1)} %collective-permute-done.1), channel_id=1, source_target_pairs={{0,2},{2,0},{1,3},{3,1},{4,6},{6,4},{5,7},{7,5},{8,10},{10,8},{9,1... | collective-permute-start | bytes 3145736 | tf_op jit(solution)/shard_map/ppermute | solution.py:346
  125.7 22.9 %collective-permute-start.16 = (bf16[4,64,1536]{2,1,0:T(8,128)(2,1)}, bf16[4,64,1536]{2,1,0:T(8,128)(2,1)}, u32[]{:S(2)}, u32[]{:S(2)}) collective-permute-start(bf16[4,64,1536]{2,1,0:T(8,128)(2,1)} %reshape.692), channel_id=1, source_target_pairs={{0,4},{4,0},{1,5},{5,1},{2,6},{6,2},{3,7},{7,3},{8,12},{12,8},{9,1... | collective-permute-start | bytes 2359304 | tf_op jit(solution)/shard_map/ppermute | solution.py:346
  128.3 30.3 %collective-permute-start.6 = (bf16[192,1024]{1,0:T(8,128)(2,1)}, bf16[192,1024]{1,0:T(8,128)(2,1)}, u32[]{:S(2)}, u32[]{:S(2)}) collective-permute-start(bf16[192,1024]{1,0:T(8,128)(2,1)} %fusion.28), channel_id=1, source_target_pairs={{0,1},{1,0},{2,3},{3,2},{4,5},{5,4},{6,7},{7,6},{8,9},{9,8},{10,11... | collective-permute-start | bytes 1179656 | tf_op jit(solution)/shard_map/ppermute | solution.py:346
  151.7 18.2 %collective-permute-start.18 = (bf16[4,64,1536]{2,1,0:T(8,128)(2,1)}, bf16[4,64,1536]{2,1,0:T(8,128)(2,1)}, u32[]{:S(2)}, u32[]{:S(2)}) collective-permute-start(bf16[4,64,1536]{2,1,0:T(8,128)(2,1)} %reshape.692), channel_id=1, source_target_pairs={{0,2},{2,0},{1,3},{3,1},{4,6},{6,4},{5,7},{7,5},{8,10},{10,8},{9,1... | collective-permute-start | bytes 2359304 | tf_op jit(solution)/shard_map/ppermute | solution.py:346
  152.9 46.7 %collective-permute-start.21 = (bf16[4,128,1024]{2,1,0:T(8,128)(2,1)}, bf16[4,128,1024]{2,1,0:T(8,128)(2,1)}, u32[]{:S(2)}, u32[]{:S(2)}) collective-permute-start(bf16[4,128,1024]{2,1,0:T(8,128)(2,1)} %slice.485), channel_id=1, source_target_pairs={{0,4},{4,0},{1,5},{5,1},{2,6},{6,2},{3,7},{7,3},{8,12},{12,8},{9,1... | collective-permute-start | bytes 3145736 | tf_op jit(solution)/shard_map/ppermute | solution.py:346
  170.0 23.1 %collective-permute-start.20 = (bf16[4,64,1536]{2,1,0:T(8,128)(2,1)}, bf16[4,64,1536]{2,1,0:T(8,128)(2,1)S(1)}, u32[]{:S(2)}, u32[]{:S(2)}) collective-permute-start(bf16[4,64,1536]{2,1,0:T(8,128)(2,1)} %collective-permute-done.18), channel_id=1, source_target_pairs={{0,4},{4,0},{1,5},{5,1},{2,6},{6,2},{3,7},{7,3},{8,12},{12,8},{9,1... | collective-permute-start | bytes 2359304 | tf_op jit(solution)/shard_map/ppermute | solution.py:346
  173.7 26.8 %collective-permute-start.22 = (bf16[4,128,1024]{2,1,0:T(8,128)(2,1)}, bf16[4,128,1024]{2,1,0:T(8,128)(2,1)S(1)}, u32[]{:S(2)}, u32[]{:S(2)}) collective-permute-start(bf16[4,128,1024]{2,1,0:T(8,128)(2,1)} %slice.485), channel_id=1, source_target_pairs={{0,2},{2,0},{1,3},{3,1},{4,6},{6,4},{5,7},{7,5},{8,10},{10,8},{9,1... | collective-permute-start | bytes 3145736 | tf_op jit(solution)/shard_map/ppermute | solution.py:346
  201.5 18.3 %collective-permute-start.23 = (bf16[384,1024]{1,0:T(8,128)(2,1)S(1)}, bf16[384,1024]{1,0:T(8,128)(2,1)}, u32[]{:S(2)}, u32[]{:S(2)}) collective-permute-start(bf16[384,1024]{1,0:T(8,128)(2,1)S(1)} %slice.505), channel_id=1, source_target_pairs={{0,2},{2,0},{1,3},{3,1},{4,6},{6,4},{5,7},{7,5},{8,10},{10,8},{9,1... | collective-permute-start | bytes 2359304 | tf_op jit(solution)/shard_map/ppermute | solution.py:346
  202.6 27.4 %collective-permute-start.24 = (bf16[4,128,1024]{2,1,0:T(8,128)(2,1)}, bf16[4,128,1024]{2,1,0:T(8,128)(2,1)S(1)}, u32[]{:S(2)}, u32[]{:S(2)}) collective-permute-start(bf16[4,128,1024]{2,1,0:T(8,128)(2,1)} %copy-done.53), channel_id=1, source_target_pairs={{0,4},{4,0},{1,5},{5,1},{2,6},{6,2},{3,7},{7,3},{8,12},{12,8},{9,1... | collective-permute-start | bytes 3145736 | tf_op jit(solution)/shard_map/ppermute | solution.py:346
  309.6 147.3 %reduce-scatter.5.cloned.1.call-start = ((), (), s32[]{:S(2)}) async-start(), calls=%async_computation.4 | async-start | bytes 3932160 | tf_op jit(solution)/shard_map/reduce_scatter | solution.py:686
  315.2 14.3 %collective-permute-start.39 = (bf16[4,2,32,1024]{3,2,0,1:T(8,128)(2,1)S(1)}, bf16[4,2,32,1024]{3,2,0,1:T(8,128)(2,1)S(1)}, u32[]{:S(2)}, u32[]{:S(2)}) collective-permute-start(bf16[4,2,32,1024]{3,2,0,1:T(8,128)(2,1)S(1)} %bitcast.461), channel_id=1, source_target_pairs={{0,4},{4,0},{1,5},{5,1},{2,6},{6,2},{3,7},{7,3},{8,12},{12,8},{9,1... | collective-permute-start | bytes 1572872 | tf_op jit(solution)/shard_map/ppermute | solution.py:346
  316.7 12.8 %collective-permute-start.40 = (bf16[16,512]{1,0:T(8,128)(2,1)S(1)}, bf16[16,512]{1,0:T(8,128)(2,1)S(1)}, u32[]{:S(2)}, u32[]{:S(2)}) collective-permute-start(bf16[16,512]{1,0:T(8,128)(2,1)S(1)} %get-tuple-element.369), channel_id=1, source_target_pairs={{2,0},{3,1},{6,4},{7,5},{10,8},{11,9},{14,12},{15,13},{18,16},{19,... | collective-permute-start | bytes 49160 | tf_op jit(solution)/shard_map/ppermute | solution.py:506
  339.1 47.6 %collective-permute-start.44 = (bf16[4,2,128,1024]{3,2,0,1:T(8,128)(2,1)S(1)}, bf16[4,2,128,1024]{3,2,0,1:T(8,128)(2,1)S(1)}, u32[]{:S(2)}, u32[]{:S(2)}) collective-permute-start(bf16[4,2,128,1024]{3,2,0,1:T(8,128)(2,1)S(1)} %copy-done.35), channel_id=1, source_target_pairs={{0,4},{4,0},{1,5},{5,1},{2,6},{6,2},{3,7},{7,3},{8,12},{12,8},{9,1... | collective-permute-start | bytes 6291464 | tf_op jit(solution)/shard_map/ppermute | solution.py:346
  344.1 26.4 %collective-permute-start.43 = (bf16[4,2,64,1024]{3,2,0,1:T(8,128)(2,1)S(1)}, bf16[4,2,64,1024]{3,2,0,1:T(8,128)(2,1)S(1)}, u32[]{:S(2)}, u32[]{:S(2)}) collective-permute-start(bf16[4,2,64,1024]{3,2,0,1:T(8,128)(2,1)S(1)} %bitcast.449), channel_id=1, source_target_pairs={{0,2},{2,0},{1,3},{3,1},{4,6},{6,4},{5,7},{7,5},{8,10},{10,8},{9,1... | collective-permute-start | bytes 3145736 | tf_op jit(solution)/shard_map/ppermute | solution.py:346
  346.7 29.4 %collective-permute-start.45 = (bf16[4,32,1024]{2,1,0:T(8,128)(2,1)S(1)}, bf16[4,32,1024]{2,1,0:T(8,128)(2,1)S(1)}, u32[]{:S(2)}, u32[]{:S(2)}) collective-permute-start(bf16[4,32,1024]{2,1,0:T(8,128)(2,1)S(1)} %dynamic-slice_bitcast_fusion.6), channel_id=1, source_target_pairs={{0,2},{2,0},{1,3},{3,1},{4,6},{6,4},{5,7},{7,5},{8,10},{10,8},{9,1... | collective-permute-start | bytes 786440 | tf_op jit(solution)/shard_map/ppermute | solution.py:346
  372.3 20.4 %collective-permute-start.47 = (bf16[384,1024]{1,0:T(8,128)(2,1)S(1)}, bf16[384,1024]{1,0:T(8,128)(2,1)S(1)}, u32[]{:S(2)}, u32[]{:S(2)}) collective-permute-start(bf16[384,1024]{1,0:T(8,128)(2,1)S(1)} %fusion.39), channel_id=1, source_target_pairs={{0,2},{2,0},{1,3},{3,1},{4,6},{6,4},{5,7},{7,5},{8,10},{10,8},{9,1... | collective-permute-start | bytes 2359304 | tf_op jit(solution)/shard_map/ppermute | solution.py:346
  396.8 131.0 %reduce-scatter.9.cloned.1.call-start = ((), (), s32[]{:S(2)}) async-start(), calls=%async_computation.6 | async-start | bytes 2621440 | tf_op jit(solution)/shard_map/reduce_scatter | solution.py:686
  405.8 15.0 %collective-permute-start.50 = (bf16[4,64,1024]{2,1,0:T(8,128)(2,1)}, bf16[4,64,1024]{2,1,0:T(8,128)(2,1)S(1)}, u32[]{:S(2)}, u32[]{:S(2)}) collective-permute-start(bf16[4,64,1024]{2,1,0:T(8,128)(2,1)} %dynamic-slice_bitcast_fusion.2), channel_id=1, source_target_pairs={{0,4},{4,0},{1,5},{5,1},{2,6},{6,2},{3,7},{7,3},{8,12},{12,8},{9,1... | collective-permute-start | bytes 1572872 | tf_op jit(solution)/shard_map/ppermute | solution.py:346
  406.9 32.3 %collective-permute-start.55 = (bf16[4,2,32,1024]{3,2,1,0:T(8,128)(2,1)}, bf16[4,2,32,1024]{3,2,1,0:T(8,128)(2,1)}, u32[]{:S(2)}, u32[]{:S(2)}) collective-permute-start(bf16[4,2,32,1024]{3,2,1,0:T(8,128)(2,1)} %dynamic-slice_bitcast_fusion), channel_id=1, source_target_pairs={{0,4},{4,0},{1,5},{5,1},{2,6},{6,2},{3,7},{7,3},{8,12},{12,8},{9,1... | collective-permute-start | bytes 1572872 | tf_op jit(solution)/shard_map/ppermute | solution.py:346
  407.9 31.3 %collective-permute-start.54 = (bf16[4,128,1024]{2,1,0:T(8,128)(2,1)}, bf16[4,128,1024]{2,1,0:T(8,128)(2,1)}, u32[]{:S(2)}, u32[]{:S(2)}) collective-permute-start(bf16[4,128,1024]{2,1,0:T(8,128)(2,1)} %fusion.15), channel_id=1, source_target_pairs={{0,2},{2,0},{1,3},{3,1},{4,6},{6,4},{5,7},{7,5},{8,10},{10,8},{9,1... | collective-permute-start | bytes 3145736 | tf_op jit(solution)/shard_map/ppermute | solution.py:346
  426.7 27.2 %collective-permute-start.52 = (bf16[512,1024]{1,0:T(8,128)(2,1)}, bf16[512,1024]{1,0:T(8,128)(2,1)}, u32[]{:S(2)}, u32[]{:S(2)}) collective-permute-start(bf16[512,1024]{1,0:T(8,128)(2,1)} %convolution_convert_fusion.8), channel_id=1, source_target_pairs={{0,4},{4,0},{1,5},{5,1},{2,6},{6,2},{3,7},{7,3},{8,12},{12,8},{9,1... | collective-permute-start | bytes 3145736 | tf_op jit(solution)/shard_map/ppermute | solution.py:346
  427.7 28.2 %collective-permute-start.53 = (bf16[512,1024]{1,0:T(8,128)(2,1)}, bf16[512,1024]{1,0:T(8,128)(2,1)}, u32[]{:S(2)}, u32[]{:S(2)}) collective-permute-start(bf16[512,1024]{1,0:T(8,128)(2,1)} %convolution_convert_fusion.7), channel_id=1, source_target_pairs={{0,2},{2,0},{1,3},{3,1},{4,6},{6,4},{5,7},{7,5},{8,10},{10,8},{9,1... | collective-permute-start | bytes 3145736 | tf_op jit(solution)/shard_map/ppermute | solution.py:346
  469.0 38.1 %collective-permute-start.56 = (bf16[768,1024]{1,0:T(8,128)(2,1)}, bf16[768,1024]{1,0:T(8,128)(2,1)}, u32[]{:S(2)}, u32[]{:S(2)}) collective-permute-start(bf16[768,1024]{1,0:T(8,128)(2,1)} %pad_maximum_fusion.4), channel_id=1, source_target_pairs={{0,4},{4,0},{1,5},{5,1},{2,6},{6,2},{3,7},{7,3},{8,12},{12,8},{9,1... | collective-permute-start | bytes 4718600 | tf_op jit(solution)/shard_map/ppermute | solution.py:346
  470.5 36.6 %collective-permute-start.57 = (bf16[768,1024]{1,0:T(8,128)(2,1)}, bf16[768,1024]{1,0:T(8,128)(2,1)}, u32[]{:S(2)}, u32[]{:S(2)}) collective-permute-start(bf16[768,1024]{1,0:T(8,128)(2,1)} %pad_maximum_fusion.5), channel_id=1, source_target_pairs={{0,2},{2,0},{1,3},{3,1},{4,6},{6,4},{5,7},{7,5},{8,10},{10,8},{9,1... | collective-permute-start | bytes 4718600 | tf_op jit(solution)/shard_map/ppermute | solution.py:346
  472.9 102.3 %reduce-scatter.11.cloned.1.call-start = ((), (), s32[]{:S(2)}) async-start(), calls=%async_computation.7 | async-start | bytes 2785280 | tf_op jit(solution)/shard_map/reduce_scatter | solution.py:686
  477.0 30.0 %collective-permute-start.60 = (f32[4,1216]{1,0:T(4,128)S(1)}, f32[4,1216]{1,0:T(4,128)S(1)}, u32[]{:S(2)}, u32[]{:S(2)}) collective-permute-start(f32[4,1216]{1,0:T(4,128)S(1)} %bitcast.481), channel_id=1, source_target_pairs={{0,2},{2,0},{1,3},{3,1},{4,6},{6,4},{5,7},{7,5},{8,10},{10,8},{9,1... | collective-permute-start | bytes 58376 | tf_op jit(solution)/shard_map/ppermute | solution.py:346
  478.6 28.4 %collective-permute-start.61 = (f32[4,1216]{1,0:T(4,128)S(1)}, f32[4,1216]{1,0:T(4,128)S(1)}, u32[]{:S(2)}, u32[]{:S(2)}) collective-permute-start(f32[4,1216]{1,0:T(4,128)S(1)} %bitcast.480), channel_id=1, source_target_pairs={{0,4},{4,0},{1,5},{5,1},{2,6},{6,2},{3,7},{7,3},{8,12},{12,8},{9,1... | collective-permute-start | bytes 58376 | tf_op jit(solution)/shard_map/ppermute | solution.py:346
  479.1 27.9 %collective-permute-start.62 = (f32[4,1216]{1,0:T(4,128)S(1)}, f32[4,1216]{1,0:T(4,128)S(1)}, u32[]{:S(2)}, u32[]{:S(2)}) collective-permute-start(f32[4,1216]{1,0:T(4,128)S(1)} %bitcast.479), channel_id=1, source_target_pairs={{0,6},{6,0},{2,4},{4,2},{1,7},{7,1},{3,5},{5,3},{8,14},{14,8},{10,... | collective-permute-start | bytes 58376 | tf_op jit(solution)/shard_map/ppermute | solution.py:728
  512.0 12.0 %collective-permute-start.63 = (bf16[256,1024]{1,0:T(8,128)(2,1)S(1)}, bf16[256,1024]{1,0:T(8,128)(2,1)S(1)}, u32[]{:S(2)}, u32[]{:S(2)}) collective-permute-start(bf16[256,1024]{1,0:T(8,128)(2,1)S(1)} %fusion.13), channel_id=1, source_target_pairs={{0,2},{2,0},{1,3},{3,1},{4,6},{6,4},{5,7},{7,5},{8,10},{10,8},{9,1... | collective-permute-start | bytes 1572872 | tf_op jit(solution)/shard_map/ppermute | solution.py:346
  512.6 11.5 %collective-permute-start.64 = (bf16[256,1024]{1,0:T(8,128)(2,1)S(1)}, bf16[256,1024]{1,0:T(8,128)(2,1)S(1)}, u32[]{:S(2)}, u32[]{:S(2)}) collective-permute-start(bf16[256,1024]{1,0:T(8,128)(2,1)S(1)} %fusion.14), channel_id=1, source_target_pairs={{0,4},{4,0},{1,5},{5,1},{2,6},{6,2},{3,7},{7,3},{8,12},{12,8},{9,1... | collective-permute-start | bytes 1572872 | tf_op jit(solution)/shard_map/ppermute | solution.py:346
  547.2 14.5 %collective-permute-start.69 = (bf16[2,128,1024]{2,1,0:T(8,128)(2,1)}, bf16[2,128,1024]{2,1,0:T(8,128)(2,1)S(1)}, u32[]{:S(2)}, u32[]{:S(2)}) collective-permute-start(bf16[2,128,1024]{2,1,0:T(8,128)(2,1)} %slice.468), channel_id=1, source_target_pairs={{0,2},{2,0},{1,3},{3,1},{4,6},{6,4},{5,7},{7,5},{8,10},{10,8},{9,1... | collective-permute-start | bytes 1572872 | tf_op jit(solution)/shard_map/ppermute | solution.py:346
  (134 other events, 821.5 us)
Sparse Core Ops, SparseCore 0:
  10.2 32.8 all-gather.10
  45.3 28.7 all-gather.8
  75.6 40.5 all-gather.12
  117.6 148.5 all-gather.14
  309.8 76.3 reduce-scatter.6
  396.9 60.0 reduce-scatter.4
  473.0 42.9 reduce-scatter.8
  529.3 45.8 reduce-scatter.10

commit v6 on v5

--- a/solution.py
+++ b/solution.py
@@ -477,8 +477,12 @@
 
     eighth = middle.shape[1] // 8
 
-    def inner_grad(first, end):
-        return left_product(middle_grad[:, first * eighth : end * eighth], both)
+    def inner_grad(first, end, tie=None):
+        columns = middle_grad[:, first * eighth : end * eighth]
+        if tie is None:
+            return left_product(columns, both)
+        columns, tie = together(columns, tie)
+        return (left_product(columns, both), tie)
 
     def outer_grad(first, end):
         return left_product(activated[:, first * eighth : end * eighth], half_both)
@@ -756,13 +760,14 @@
     mixed_grad, gain_three = split_norm_back(act_grad, normed_mid, inverse_mid, gain_mid)
     mixed_low = low(mixed_grad)
     grad_low, grad_high = halos(mixed_low)
+    inner_two_rows, mixed_low = inner_two_grad(0, 8, mixed_low)
     point_grad = by_chip(low(left_product(swish, conv_out_grad)))
     point_a = send(point_grad, "q", 1)
     if square:
         mixed_low, point_a = together(mixed_low, point_a)
     point_half = add(point_grad, point_a, "q", 1)
     point_b = send(point_half, "y", 1)
-    inner_two_sum = early_sum(inner_two_grad(0, 8))
+    inner_two_sum = early_sum(inner_two_rows)
     glu_back, depth_grad = conv_back(
         info, glu_low, glu_rows, glu_high, grad_low, mixed_low, grad_high, depth, group
     )
@@ -824,10 +829,12 @@
         grad_first, gain_table[0], inner_one, outer_one, first_kept, glu_b
     )
     if square:
-        near_o, near_i = together(low(outer_one_grad(1, 3)), low(inner_one_grad(2, 4)))
+        near_o, near_i, inner_two_sum = together(
+            low(outer_one_grad(1, 3)), low(inner_one_grad(2, 4)), inner_two_sum
+        )
         near_o, near_i = swap(near_o, "q"), swap(near_i, "y")
     if square:
-        near_o, near_i, glu_b, outer_two_b, far_o, far_i, merge_a, attend_sum, inner_two_sum = together(
+        near_o, near_i, glu_b, outer_two_b, far_o, far_i, merge_a = together(
             near_o,
             near_i,
             glu_b,
@@ -835,8 +842,6 @@
             low(outer_one_grad(5, 7)),
             low(inner_one_grad(6, 8)),
             merge_a,
-            attend_sum,
-            inner_two_sum,
         )
     edge_half = add(merge_grad, merge_a, "q", 1)
     edge_b = send(edge_half, "y", 1)
@@ -871,7 +876,7 @@
         small_sum = small_of(
             table_sums, depth_grad, gain_zero, gain_one, gain_two, gain_three, gain_four, gain_five
         )
-        across_q, across_y, small_sum = together(across_q, across_y, small_sum)
+        across_q, across_y, small_sum, attend_sum = together(across_q, across_y, small_sum, attend_sum)
         far_o, far_i = across_q[: 2 * size], across_y[: 2 * size]
         near = [across_y[2 * size :], across_q[2 * size :]]
         near = third(0, near_o, near_i, *near)

time: 597 us -> 593 us (level)
    unnamed x242 -> x238, local copies, waits for them, and re-layouts: 28.5 us -> 31.7 us
where the time goes in v6:
time: 593 us; the launch traced here: 585 us
  waiting for transfers between devices  219 us (37%)
  local copies, waits for them, and re-layouts  106 us (18%)
  matrix products  82 us (14%)
  starting transfers between devices  69.2 us (12%)
  other arithmetic  49.8 us (8%)
  Pallas kernels  40.5 us (7%)
  between operations  18.4 us (3%)
    ppermute x65, waiting for transfers between devices, swap(): return lax.ppermute(values, axis, CORES)  213 us
    ppermute x65, starting transfers between devices, swap(): return lax.ppermute(values, axis, CORES)  53.9 us
    dot_general x18, matrix products, left_product(): jnp.einsum('nd,nf->df', left_in, right_in, preferred_element_type=jnp.flo...  41 us
    unnamed x238, local copies, waits for them, and re-layouts  31.7 us
    dot_general x8, matrix products, right_product(): jnp.einsum('nf,df->nd', left_in, right_in, preferred_element_type=jnp.flo...  23.6 us
    pallas_call x1, Pallas kernels, attend_back(): pl.pallas_call(attend_back_kernel, grid=(pairs,), in_specs=attend_specs(r...  19.9 us
    dot_general x8, matrix products, product(): return jnp.dot(left_in, right_in, preferred_element_type=jnp.float32)  16.9 us
    dynamic_update_slice x12, local copies, waits for them, and re-layouts, placed(): result = lax.dynamic_update_slice(result, part[:, None, None], at)  13.2 us
  transfers between devices with their start and end apart: 79, of which 42 were waited for; matrix products, arithmetic and copies ran while one was open for 32% of the time, Pallas kernels for 7%

profile of v6, /device:TPU:0, one launch (start us, length us, event | category | flops | bytes accessed | tf_op | source)
XLA Modules:
  0.0 584.5 jit_solution(6053655221168688707)
XLA Ops:
  9.5 3.0 collective-permute-start.7
  14.4 10.0 %collective-permute-done.7 = bf16[256,1024]{1,0:T(8,128)(2,1)S(1)} collective-permute-done((bf16[256,1024]{1,0:T(8,128)(2,1)S(1)}, bf16[256,1024]{1,0:T(8,128)(2,1)S(1)}, u32[]{:S(2)}, u32[]{:S(2)}) %collective-permute-start.7) | collective-permute-done | bytes 524320 | tf_op jit(solution)/shard_map/ppermute | solution.py:346
  30.9 3.5 dynamic-slice_reduce_fusion
  35.5 3.0 collective-permute-done.9
  40.1 3.0 all-gather.11.cloned.1.call-done
  47.1 20.3 %collective-permute-done.13 = bf16[512,1024]{0,1:T(8,128)(2,1)} collective-permute-done((bf16[512,1024]{0,1:T(8,128)(2,1)}, bf16[512,1024]{0,1:T(8,128)(2,1)}, u32[]{:S(2)}, u32[]{:S(2)}) %collective-permute-start.13) | collective-permute-done | bytes 1048608 | tf_op jit(solution)/shard_map/ppermute | solution.py:346
  93.3 15.9 %collective-permute-done.2 = bf16[512,1024]{1,0:T(8,128)(2,1)} collective-permute-done((bf16[512,1024]{1,0:T(8,128)(2,1)S(1)}, bf16[512,1024]{1,0:T(8,128)(2,1)}, u32[]{:S(2)}, u32[]{:S(2)}) %collective-permute-start.2) | collective-permute-done | bytes 1048608 | tf_op jit(solution)/shard_map/ppermute | solution.py:346
  127.2 2.4 fusion.137
  129.6 3.4 collective-permute-done.14
  133.0 7.4 %collective-permute-done.15 = bf16[512,1024]{1,0:T(8,128)(2,1)} collective-permute-done((bf16[512,1024]{1,0:T(8,128)(2,1)}, bf16[512,1024]{1,0:T(8,128)(2,1)}, u32[]{:S(2)}, u32[]{:S(2)}) %collective-permute-start.15) | collective-permute-done | bytes 1048608 | tf_op jit(solution)/shard_map/ppermute | solution.py:346
  140.4 7.7 %collective-permute-done.16 = bf16[4,64,1536]{2,1,0:T(8,128)(2,1)} collective-permute-done((bf16[4,64,1536]{2,1,0:T(8,128)(2,1)S(1)}, bf16[4,64,1536]{2,1,0:T(8,128)(2,1)}, u32[]{:S(2)}, u32[]{:S(2)}) %collective-permute-start.16) | collective-permute-done | bytes 786464 | tf_op jit(solution)/shard_map/ppermute | solution.py:346
  160.0 5.6 multiply_convert_fusion.3
  175.5 16.8 %collective-permute-done.20 = bf16[4,64,1536]{2,1,0:T(8,128)(2,1)S(1)} collective-permute-done((bf16[4,64,1536]{2,1,0:T(8,128)(2,1)}, bf16[4,64,1536]{2,1,0:T(8,128)(2,1)S(1)}, u32[]{:S(2)}, u32[]{:S(2)}) %collective-permute-start.20) | collective-permute-done | bytes 786464 | tf_op jit(solution)/shard_map/ppermute | solution.py:346
  195.3 3.3 convolution_convert_fusion.3
  206.2 13.8 %collective-permute-done.23 = bf16[384,1024]{1,0:T(8,128)(2,1)} collective-permute-done((bf16[384,1024]{1,0:T(8,128)(2,1)}, bf16[384,1024]{1,0:T(8,128)(2,1)}, u32[]{:S(2)}, u32[]{:S(2)}) %collective-permute-start.23) | collective-permute-done | bytes 786464 | tf_op jit(solution)/shard_map/ppermute | solution.py:346
  221.7 8.8 %attend.1 = bf16[384,512]{1,0:T(8,128)(2,1)S(1)} custom-call(s32[3]{0:T(128)S(1)} %pad_add_fusion.info_ref.refs_0_, f32[4,2,1536]{2,1,0:T(2,128)S(1)} %fusion.76.bias_ref, bf16[384,512]{1,0:T(8,128)(2,1)S(1)} %slice.504.query_ref, bf16[768,1024]{1,0:T(8,128)(2,1)S(1)} %pad_maximum_fusion.3.key_ref.value_ref, ...), custom_call_target="tpu_custom_call" | custom-call | flops 603979776 | bytes 2359296 | tf_op jit(solution)/shard_map/attend/pallas_call | solution.py:143
  247.4 4.5 collective-permute-start.28
  253.3 4.2 conv.1
  267.5 4.4 fusion.135
  271.9 3.6 fusion.63
  286.1 4.1 multiply_convert_fusion.1
  292.5 2.4 convolution_convert_fusion.1
  305.5 5.5 convolution_convert_fusion
  315.8 4.5 collective-permute-start.38
  320.3 6.8 %collective-permute-done.39 = bf16[4,2,32,1024]{3,2,0,1:T(8,128)(2,1)S(1)} collective-permute-done((bf16[4,2,32,1024]{3,2,0,1:T(8,128)(2,1)S(1)}, bf16[4,2,32,1024]{3,2,0,1:T(8,128)(2,1)S(1)}, u32[]{:S(2)}, u32[]{:S(2)}) %collective-permute-start.39) | collective-permute-done | bytes 524320 | tf_op jit(solution)/shard_map/ppermute | solution.py:346
  327.1 7.5 %conv_back.1 = (f32[384,512]{1,0:T(8,128)S(1)}, f32[31,512]{1,0:T(8,128)S(1)}) custom-call(s32[3]{0:T(128)S(1)} %pad_add_fusion.info_ref.refs_0_, bf16[16,512]{1,0:T(8,128)(2,1)S(1)} %collective-permute-done.28.refs_1_, bf16[384,512]{1,0:T(8,128)(2,1)S(1)} %multiply_convert_fusion.12.refs_2_, bf16[16,512]{1,0:T(8,128)(2,1)S(1)} %collective-permute-done.29.refs_3_, ...), custom_call_target="tpu_custom_call" | custom-call | flops 24379392 | bytes 1572864 | tf_op jit(solution)/shard_map/conv_back/pallas_call | solution.py:301
  341.9 2.3 collective-permute-start.43
  346.5 19.9 %attend_back.1 = (bf16[384,512]{1,0:T(8,128)(2,1)S(1)}, f32[768,512]{1,0:T(8,128)S(1)}, f32[768,512]{1,0:T(8,128)}, f32[4,2,1536]{2,1,0:T(2,128)S(1)}) custom-call(s32[3]{0:T(128)S(1)} %pad_add_fusion.info_ref.refs_0_, f32[4,2,1536]{2,1,0:T(2,128)S(1)} %copy-done.4, bf16[384,512]{1,0:T(8,128)(2,1)S(1)} %copy-done.2, bf16[768,1024]{1,0:T(8,128)(2,1)} %copy-done, ...), custom_call_target="tpu_custom_call" | custom-call | flops 1509949440 | bytes 2359296 | tf_op jit(solution)/shard_map/attend_back/pallas_call | solution.py:166
  373.8 10.8 %collective-permute-done.44 = bf16[4,2,128,1024]{3,2,0,1:T(8,128)(2,1)S(1)} collective-permute-done((bf16[4,2,128,1024]{3,2,0,1:T(8,128)(2,1)}, bf16[4,2,128,1024]{3,2,0,1:T(8,128)(2,1)S(1)}, u32[]{:S(2)}, u32[]{:S(2)}) %collective-permute-start.44) | collective-permute-done | bytes 2097184 | tf_op jit(solution)/shard_map/ppermute | solution.py:346
  386.3 2.6 fusion.15
  394.7 3.5 convolution_convert_fusion.2
  401.0 2.5 multiply_convert_fusion.4
  409.1 5.6 multiply_convert_fusion
  414.7 5.0 collective-permute-done.50
  419.7 3.0 convolution_convert_fusion.8
  422.8 2.8 convolution_convert_fusion.7
  426.9 2.4 collective-permute-start.53
  429.3 4.5 fusion.155
  434.0 3.5 convolution_convert_fusion.5
  437.5 2.9 convolution_convert_fusion.6
  441.5 11.7 %collective-permute-done.52 = bf16[512,1024]{1,0:T(8,128)(2,1)} collective-permute-done((bf16[512,1024]{1,0:T(8,128)(2,1)}, bf16[512,1024]{1,0:T(8,128)(2,1)}, u32[]{:S(2)}, u32[]{:S(2)}) %collective-permute-start.52) | collective-permute-done | bytes 1048608 | tf_op jit(solution)/shard_map/ppermute | solution.py:346
  472.8 2.6 pad_maximum_fusion.2
  482.2 22.6 %collective-permute-done.60 = f32[4,1216]{1,0:T(4,128)S(1)} collective-permute-done((f32[4,1216]{1,0:T(4,128)S(1)}, f32[4,1216]{1,0:T(4,128)S(1)}, u32[]{:S(2)}, u32[]{:S(2)}) %collective-permute-start.60) | collective-permute-done | bytes 19488 | tf_op jit(solution)/shard_map/ppermute | solution.py:346
  515.6 5.4 collective-permute-done.63
  528.7 6.9 %collective-permute-done.65 = bf16[2,64,1536]{2,1,0:T(8,128)(2,1)S(1)} collective-permute-done((bf16[2,64,1536]{2,1,0:T(8,128)(2,1)S(1)}, bf16[2,64,1536]{2,1,0:T(8,128)(2,1)S(1)}, u32[]{:S(2)}, u32[]{:S(2)}) %collective-permute-start.65) | collective-permute-done | bytes 393248 | tf_op jit(solution)/shard_map/ppermute | solution.py:346
  537.9 4.6 collective-permute-done.66
  549.0 11.9 %collective-permute-done.69 = bf16[2,128,1024]{2,1,0:T(8,128)(2,1)S(1)} collective-permute-done((bf16[2,128,1024]{2,1,0:T(8,128)(2,1)}, bf16[2,128,1024]{2,1,0:T(8,128)(2,1)S(1)}, u32[]{:S(2)}, u32[]{:S(2)}) %collective-permute-start.69) | collective-permute-done | bytes 524320 | tf_op jit(solution)/shard_map/ppermute | solution.py:346
  565.0 4.0 collective-permute-done.70
  (671 shorter events, 249.7 us)
Async XLA Ops:
  7.2 35.9 %all-gather.11.cloned.1.call-start = ((), (), s32[]{:S(2)}) async-start(), calls=%async_computation.9 | async-start | bytes 1310720 | tf_op jit(solution)/shard_map/all_gather | solution.py:573
  9.1 66.3 %all-gather.9.cloned.1.call-start = ((), (), s32[]{:S(2)}) async-start(), calls=%async_computation.8 | async-start | bytes 1474560 | tf_op jit(solution)/shard_map/all_gather | solution.py:573
  9.5 14.9 %collective-permute-start.7 = (bf16[256,1024]{1,0:T(8,128)(2,1)S(1)}, bf16[256,1024]{1,0:T(8,128)(2,1)S(1)}, u32[]{:S(2)}, u32[]{:S(2)}) collective-permute-start(bf16[256,1024]{1,0:T(8,128)(2,1)S(1)} %get-tuple-element.370), channel_id=1, source_target_pairs={{0,4},{4,0},{1,5},{5,1},{2,6},{6,2},{3,7},{7,3},{8,12},{12,8},{9,1... | collective-permute-start | bytes 1572872 | tf_op jit(solution)/shard_map/ppermute | solution.py:346
  12.5 13.4 %collective-permute-start.8 = (bf16[256,1024]{1,0:T(8,128)(2,1)S(1)}, bf16[256,1024]{1,0:T(8,128)(2,1)S(1)}, u32[]{:S(2)}, u32[]{:S(2)}) collective-permute-start(bf16[256,1024]{1,0:T(8,128)(2,1)S(1)} %get-tuple-element.370), channel_id=1, source_target_pairs={{0,2},{2,0},{1,3},{3,1},{4,6},{6,4},{5,7},{7,5},{8,10},{10,8},{9,1... | collective-permute-start | bytes 1572872 | tf_op jit(solution)/shard_map/ppermute | solution.py:346
  14.3 13.1 %collective-permute-start = (bf16[1,1216]{1,0:T(2,128)(2,1)S(1)}, bf16[1,1216]{1,0:T(2,128)(2,1)S(1)}, u32[]{:S(2)}, u32[]{:S(2)}) collective-permute-start(bf16[1,1216]{1,0:T(2,128)(2,1)S(1)} %broadcast_in_dim.43), channel_id=1, source_target_pairs={{0,1},{1,0},{2,3},{3,2},{4,5},{5,4},{6,7},{7,6},{8,9},{9,8},{10,11... | collective-permute-start | bytes 7304 | tf_op jit(solution)/shard_map/ppermute | solution.py:346
  25.9 12.6 %collective-permute-start.9 = (bf16[256,1024]{1,0:T(8,128)(2,1)S(1)}, bf16[256,1024]{1,0:T(8,128)(2,1)S(1)}, u32[]{:S(2)}, u32[]{:S(2)}) collective-permute-start(bf16[256,1024]{1,0:T(8,128)(2,1)S(1)} %collective-permute-done.7), channel_id=1, source_target_pairs={{0,2},{2,0},{1,3},{3,1},{4,6},{6,4},{5,7},{7,5},{8,10},{10,8},{9,1... | collective-permute-start | bytes 1572872 | tf_op jit(solution)/shard_map/ppermute | solution.py:346
  28.3 90.1 %all-gather.13.cloned.1.call-start = ((), (), s32[]{:S(2)}) async-start(), calls=%async_computation.10 | async-start | bytes 2293760 | tf_op jit(solution)/shard_map/all_gather | solution.py:573
  30.5 14.5 %collective-permute-start.10 = (bf16[32,1536]{1,0:T(8,128)(2,1)}, bf16[32,1536]{1,0:T(8,128)(2,1)}, u32[]{:S(2)}, u32[]{:S(2)}) collective-permute-start(bf16[32,1536]{1,0:T(8,128)(2,1)} %bitcast.199), channel_id=1, source_target_pairs={{0,1},{1,0},{2,3},{3,2},{4,5},{5,4},{6,7},{7,6},{8,9},{9,8},{10,11... | collective-permute-start | bytes 294920 | tf_op jit(solution)/shard_map/ppermute | solution.py:346
  43.1 24.2 %collective-permute-start.13 = (bf16[512,1024]{0,1:T(8,128)(2,1)}, bf16[512,1024]{0,1:T(8,128)(2,1)}, u32[]{:S(2)}, u32[]{:S(2)}) collective-permute-start(bf16[512,1024]{0,1:T(8,128)(2,1)} %all-gather.11.cloned.1.call-done), channel_id=1, source_target_pairs={{0,2},{2,0},{1,3},{3,1},{4,6},{6,4},{5,7},{7,5},{8,10},{10,8},{9,1... | collective-permute-start | bytes 3145736 | tf_op jit(solution)/shard_map/ppermute | solution.py:346
  43.6 25.0 %collective-permute-start.12 = (bf16[512,1024]{0,1:T(8,128)(2,1)}, bf16[512,1024]{0,1:T(8,128)(2,1)S(1)}, u32[]{:S(2)}, u32[]{:S(2)}) collective-permute-start(bf16[512,1024]{0,1:T(8,128)(2,1)} %all-gather.11.cloned.1.call-done), channel_id=1, source_target_pairs={{0,4},{4,0},{1,5},{5,1},{2,6},{6,2},{3,7},{7,3},{8,12},{12,8},{9,1... | collective-permute-start | bytes 3145736 | tf_op jit(solution)/shard_map/ppermute | solution.py:346
  68.7 198.8 %all-gather.15.cloned.1.call-start = ((), (), s32[]{:S(2)}) async-start(), calls=%async_computation.11 | async-start | bytes 10485760 | tf_op jit(solution)/shard_map/all_gather | solution.py:573
  74.8 350.8 %reduce-scatter.5.cloned.1.call-start = ((), (), s32[]{:S(2)}) async-start(), calls=%async_computation.4 | async-start | bytes 5242880 | tf_op jit(solution)/shard_map/reduce_scatter | solution.py:690
  78.3 14.6 %collective-permute-start.5 = (bf16[4,16,1024]{2,1,0:T(8,128)(2,1)}, bf16[4,16,1024]{2,1,0:T(8,128)(2,1)}, u32[]{:S(2)}, u32[]{:S(2)}) collective-permute-start(bf16[4,16,1024]{2,1,0:T(8,128)(2,1)} %slice.478), channel_id=1, source_target_pairs={{0,6},{6,0},{2,4},{4,2},{1,7},{7,1},{3,5},{5,3},{8,14},{14,8},{10,... | collective-permute-start | bytes 393224 | tf_op jit(solution)/shard_map/ppermute | solution.py:595
  79.8 13.5 %collective-permute-start.4 = (bf16[4,16,1024]{2,1,0:T(8,128)(2,1)}, bf16[4,16,1024]{2,1,0:T(8,128)(2,1)}, u32[]{:S(2)}, u32[]{:S(2)}) collective-permute-start(bf16[4,16,1024]{2,1,0:T(8,128)(2,1)} %slice.478), channel_id=1, source_target_pairs={{0,2},{2,0},{1,3},{3,1},{4,6},{6,4},{5,7},{7,5},{8,10},{10,8},{9,1... | collective-permute-start | bytes 393224 | tf_op jit(solution)/shard_map/ppermute | solution.py:346
  81.3 12.0 %collective-permute-start.3 = (bf16[4,16,1024]{2,1,0:T(8,128)(2,1)}, bf16[4,16,1024]{2,1,0:T(8,128)(2,1)}, u32[]{:S(2)}, u32[]{:S(2)}) collective-permute-start(bf16[4,16,1024]{2,1,0:T(8,128)(2,1)} %slice.478), channel_id=1, source_target_pairs={{0,4},{4,0},{1,5},{5,1},{2,6},{6,2},{3,7},{7,3},{8,12},{12,8},{9,1... | collective-permute-start | bytes 393224 | tf_op jit(solution)/shard_map/ppermute | solution.py:346
  81.8 27.4 %collective-permute-start.2 = (bf16[512,1024]{1,0:T(8,128)(2,1)S(1)}, bf16[512,1024]{1,0:T(8,128)(2,1)}, u32[]{:S(2)}, u32[]{:S(2)}) collective-permute-start(bf16[512,1024]{1,0:T(8,128)(2,1)S(1)} %bitcast.400), channel_id=1, source_target_pairs={{0,2},{2,0},{1,3},{3,1},{4,6},{6,4},{5,7},{7,5},{8,10},{10,8},{9,1... | collective-permute-start | bytes 3145736 | tf_op jit(solution)/shard_map/ppermute | solution.py:346
  82.2 28.3 %collective-permute-start.1 = (bf16[512,1024]{1,0:T(8,128)(2,1)S(1)}, bf16[512,1024]{1,0:T(8,128)(2,1)}, u32[]{:S(2)}, u32[]{:S(2)}) collective-permute-start(bf16[512,1024]{1,0:T(8,128)(2,1)S(1)} %bitcast.401), channel_id=1, source_target_pairs={{0,4},{4,0},{1,5},{5,1},{2,6},{6,2},{3,7},{7,3},{8,12},{12,8},{9,1... | collective-permute-start | bytes 3145736 | tf_op jit(solution)/shard_map/ppermute | solution.py:346
  92.9 40.1 %collective-permute-start.14 = (bf16[512,1024]{0,1:T(8,128)(2,1)}, bf16[512,1024]{0,1:T(8,128)(2,1)}, u32[]{:S(2)}, u32[]{:S(2)}) collective-permute-start(bf16[512,1024]{0,1:T(8,128)(2,1)} %collective-permute-done.13), channel_id=1, source_target_pairs={{0,4},{4,0},{1,5},{5,1},{2,6},{6,2},{3,7},{7,3},{8,12},{12,8},{9,1... | collective-permute-start | bytes 3145736 | tf_op jit(solution)/shard_map/ppermute | solution.py:346
  117.0 23.4 %collective-permute-start.15 = (bf16[512,1024]{1,0:T(8,128)(2,1)}, bf16[512,1024]{1,0:T(8,128)(2,1)}, u32[]{:S(2)}, u32[]{:S(2)}) collective-permute-start(bf16[512,1024]{1,0:T(8,128)(2,1)} %collective-permute-done.1), channel_id=1, source_target_pairs={{0,2},{2,0},{1,3},{3,1},{4,6},{6,4},{5,7},{7,5},{8,10},{10,8},{9,1... | collective-permute-start | bytes 3145736 | tf_op jit(solution)/shard_map/ppermute | solution.py:346
  121.5 26.6 %collective-permute-start.16 = (bf16[4,64,1536]{2,1,0:T(8,128)(2,1)S(1)}, bf16[4,64,1536]{2,1,0:T(8,128)(2,1)}, u32[]{:S(2)}, u32[]{:S(2)}) collective-permute-start(bf16[4,64,1536]{2,1,0:T(8,128)(2,1)S(1)} %reshape.692), channel_id=1, source_target_pairs={{0,4},{4,0},{1,5},{5,1},{2,6},{6,2},{3,7},{7,3},{8,12},{12,8},{9,1... | collective-permute-start | bytes 2359304 | tf_op jit(solution)/shard_map/ppermute | solution.py:346
  124.1 35.9 %collective-permute-start.6 = (bf16[192,1024]{1,0:T(8,128)(2,1)}, bf16[192,1024]{1,0:T(8,128)(2,1)}, u32[]{:S(2)}, u32[]{:S(2)}) collective-permute-start(bf16[192,1024]{1,0:T(8,128)(2,1)} %fusion.28), channel_id=1, source_target_pairs={{0,1},{1,0},{2,3},{3,2},{4,5},{5,4},{6,7},{7,6},{8,9},{9,8},{10,11... | collective-permute-start | bytes 1179656 | tf_op jit(solution)/shard_map/ppermute | solution.py:346
  151.1 19.7 %collective-permute-start.18 = (bf16[4,64,1536]{2,1,0:T(8,128)(2,1)S(1)}, bf16[4,64,1536]{2,1,0:T(8,128)(2,1)}, u32[]{:S(2)}, u32[]{:S(2)}) collective-permute-start(bf16[4,64,1536]{2,1,0:T(8,128)(2,1)S(1)} %copy-done.30), channel_id=1, source_target_pairs={{0,2},{2,0},{1,3},{3,1},{4,6},{6,4},{5,7},{7,5},{8,10},{10,8},{9,1... | collective-permute-start | bytes 2359304 | tf_op jit(solution)/shard_map/ppermute | solution.py:346
  152.3 47.4 %collective-permute-start.21 = (bf16[4,128,1024]{2,1,0:T(8,128)(2,1)S(1)}, bf16[4,128,1024]{2,1,0:T(8,128)(2,1)}, u32[]{:S(2)}, u32[]{:S(2)}) collective-permute-start(bf16[4,128,1024]{2,1,0:T(8,128)(2,1)S(1)} %slice.485), channel_id=1, source_target_pairs={{0,4},{4,0},{1,5},{5,1},{2,6},{6,2},{3,7},{7,3},{8,12},{12,8},{9,1... | collective-permute-start | bytes 3145736 | tf_op jit(solution)/shard_map/ppermute | solution.py:346
  170.9 21.4 %collective-permute-start.20 = (bf16[4,64,1536]{2,1,0:T(8,128)(2,1)}, bf16[4,64,1536]{2,1,0:T(8,128)(2,1)S(1)}, u32[]{:S(2)}, u32[]{:S(2)}) collective-permute-start(bf16[4,64,1536]{2,1,0:T(8,128)(2,1)} %collective-permute-done.18), channel_id=1, source_target_pairs={{0,4},{4,0},{1,5},{5,1},{2,6},{6,2},{3,7},{7,3},{8,12},{12,8},{9,1... | collective-permute-start | bytes 2359304 | tf_op jit(solution)/shard_map/ppermute | solution.py:346
  174.4 25.4 %collective-permute-start.22 = (bf16[4,128,1024]{2,1,0:T(8,128)(2,1)S(1)}, bf16[4,128,1024]{2,1,0:T(8,128)(2,1)S(1)}, u32[]{:S(2)}, u32[]{:S(2)}) collective-permute-start(bf16[4,128,1024]{2,1,0:T(8,128)(2,1)S(1)} %slice.485), channel_id=1, source_target_pairs={{0,2},{2,0},{1,3},{3,1},{4,6},{6,4},{5,7},{7,5},{8,10},{10,8},{9,1... | collective-permute-start | bytes 3145736 | tf_op jit(solution)/shard_map/ppermute | solution.py:346
  200.7 19.3 %collective-permute-start.23 = (bf16[384,1024]{1,0:T(8,128)(2,1)}, bf16[384,1024]{1,0:T(8,128)(2,1)}, u32[]{:S(2)}, u32[]{:S(2)}) collective-permute-start(bf16[384,1024]{1,0:T(8,128)(2,1)} %slice.505), channel_id=1, source_target_pairs={{0,2},{2,0},{1,3},{3,1},{4,6},{6,4},{5,7},{7,5},{8,10},{10,8},{9,1... | collective-permute-start | bytes 2359304 | tf_op jit(solution)/shard_map/ppermute | solution.py:346
  201.9 28.7 %collective-permute-start.24 = (bf16[4,128,1024]{2,1,0:T(8,128)(2,1)}, bf16[4,128,1024]{2,1,0:T(8,128)(2,1)S(1)}, u32[]{:S(2)}, u32[]{:S(2)}) collective-permute-start(bf16[4,128,1024]{2,1,0:T(8,128)(2,1)} %copy-done.60), channel_id=1, source_target_pairs={{0,4},{4,0},{1,5},{5,1},{2,6},{6,2},{3,7},{7,3},{8,12},{12,8},{9,1... | collective-permute-start | bytes 3145736 | tf_op jit(solution)/shard_map/ppermute | solution.py:346
  311.1 193.8 %reduce-scatter.7.cloned.1.call-start = ((), (), s32[]{:S(2)}) async-start(), calls=%async_computation.5 | async-start | bytes 3932160 | tf_op jit(solution)/shard_map/reduce_scatter | solution.py:690
  313.1 14.1 %collective-permute-start.39 = (bf16[4,2,32,1024]{3,2,0,1:T(8,128)(2,1)S(1)}, bf16[4,2,32,1024]{3,2,0,1:T(8,128)(2,1)S(1)}, u32[]{:S(2)}, u32[]{:S(2)}) collective-permute-start(bf16[4,2,32,1024]{3,2,0,1:T(8,128)(2,1)S(1)} %bitcast.461), channel_id=1, source_target_pairs={{0,4},{4,0},{1,5},{5,1},{2,6},{6,2},{3,7},{7,3},{8,12},{12,8},{9,1... | collective-permute-start | bytes 1572872 | tf_op jit(solution)/shard_map/ppermute | solution.py:346
  314.5 12.6 %collective-permute-start.40 = (bf16[16,512]{1,0:T(8,128)(2,1)S(1)}, bf16[16,512]{1,0:T(8,128)(2,1)S(1)}, u32[]{:S(2)}, u32[]{:S(2)}) collective-permute-start(bf16[16,512]{1,0:T(8,128)(2,1)S(1)} %get-tuple-element.373), channel_id=1, source_target_pairs={{2,0},{3,1},{6,4},{7,5},{10,8},{11,9},{14,12},{15,13},{18,16},{19,... | collective-permute-start | bytes 49160 | tf_op jit(solution)/shard_map/ppermute | solution.py:510
  336.3 48.3 %collective-permute-start.44 = (bf16[4,2,128,1024]{3,2,0,1:T(8,128)(2,1)}, bf16[4,2,128,1024]{3,2,0,1:T(8,128)(2,1)S(1)}, u32[]{:S(2)}, u32[]{:S(2)}) collective-permute-start(bf16[4,2,128,1024]{3,2,0,1:T(8,128)(2,1)} %copy.281), channel_id=1, source_target_pairs={{0,4},{4,0},{1,5},{5,1},{2,6},{6,2},{3,7},{7,3},{8,12},{12,8},{9,1... | collective-permute-start | bytes 6291464 | tf_op jit(solution)/shard_map/ppermute | solution.py:346
  341.9 26.3 %collective-permute-start.43 = (bf16[4,2,64,1024]{3,2,0,1:T(8,128)(2,1)S(1)}, bf16[4,2,64,1024]{3,2,0,1:T(8,128)(2,1)S(1)}, u32[]{:S(2)}, u32[]{:S(2)}) collective-permute-start(bf16[4,2,64,1024]{3,2,0,1:T(8,128)(2,1)S(1)} %bitcast.449), channel_id=1, source_target_pairs={{0,2},{2,0},{1,3},{3,1},{4,6},{6,4},{5,7},{7,5},{8,10},{10,8},{9,1... | collective-permute-start | bytes 3145736 | tf_op jit(solution)/shard_map/ppermute | solution.py:346
  344.5 29.3 %collective-permute-start.45 = (bf16[4,32,1024]{2,1,0:T(8,128)(2,1)S(1)}, bf16[4,32,1024]{2,1,0:T(8,128)(2,1)S(1)}, u32[]{:S(2)}, u32[]{:S(2)}) collective-permute-start(bf16[4,32,1024]{2,1,0:T(8,128)(2,1)S(1)} %dynamic-slice_bitcast_fusion.6), channel_id=1, source_target_pairs={{0,2},{2,0},{1,3},{3,1},{4,6},{6,4},{5,7},{7,5},{8,10},{10,8},{9,1... | collective-permute-start | bytes 786440 | tf_op jit(solution)/shard_map/ppermute | solution.py:346
  370.0 20.3 %collective-permute-start.47 = (bf16[384,1024]{1,0:T(8,128)(2,1)S(1)}, bf16[384,1024]{1,0:T(8,128)(2,1)S(1)}, u32[]{:S(2)}, u32[]{:S(2)}) collective-permute-start(bf16[384,1024]{1,0:T(8,128)(2,1)S(1)} %fusion.39), channel_id=1, source_target_pairs={{0,2},{2,0},{1,3},{3,1},{4,6},{6,4},{5,7},{7,5},{8,10},{10,8},{9,1... | collective-permute-start | bytes 2359304 | tf_op jit(solution)/shard_map/ppermute | solution.py:346
  398.3 127.0 %reduce-scatter.9.cloned.1.call-start = ((), (), s32[]{:S(2)}) async-start(), calls=%async_computation.6 | async-start | bytes 2621440 | tf_op jit(solution)/shard_map/reduce_scatter | solution.py:690
  404.7 15.0 %collective-permute-start.50 = (bf16[4,64,1024]{2,1,0:T(8,128)(2,1)}, bf16[4,64,1024]{2,1,0:T(8,128)(2,1)S(1)}, u32[]{:S(2)}, u32[]{:S(2)}) collective-permute-start(bf16[4,64,1024]{2,1,0:T(8,128)(2,1)} %dynamic-slice_bitcast_fusion.2), channel_id=1, source_target_pairs={{0,4},{4,0},{1,5},{5,1},{2,6},{6,2},{3,7},{7,3},{8,12},{12,8},{9,1... | collective-permute-start | bytes 1572872 | tf_op jit(solution)/shard_map/ppermute | solution.py:346
  406.1 35.3 %collective-permute-start.55 = (bf16[4,2,32,1024]{3,2,1,0:T(8,128)(2,1)}, bf16[4,2,32,1024]{3,2,1,0:T(8,128)(2,1)}, u32[]{:S(2)}, u32[]{:S(2)}) collective-permute-start(bf16[4,2,32,1024]{3,2,1,0:T(8,128)(2,1)} %dynamic-slice_bitcast_fusion), channel_id=1, source_target_pairs={{0,4},{4,0},{1,5},{5,1},{2,6},{6,2},{3,7},{7,3},{8,12},{12,8},{9,1... | collective-permute-start | bytes 1572872 | tf_op jit(solution)/shard_map/ppermute | solution.py:346
  406.8 34.6 %collective-permute-start.54 = (bf16[4,128,1024]{2,1,0:T(8,128)(2,1)}, bf16[4,128,1024]{2,1,0:T(8,128)(2,1)}, u32[]{:S(2)}, u32[]{:S(2)}) collective-permute-start(bf16[4,128,1024]{2,1,0:T(8,128)(2,1)} %fusion.15), channel_id=1, source_target_pairs={{0,2},{2,0},{1,3},{3,1},{4,6},{6,4},{5,7},{7,5},{8,10},{10,8},{9,1... | collective-permute-start | bytes 3145736 | tf_op jit(solution)/shard_map/ppermute | solution.py:346
  425.6 27.5 %collective-permute-start.52 = (bf16[512,1024]{1,0:T(8,128)(2,1)}, bf16[512,1024]{1,0:T(8,128)(2,1)}, u32[]{:S(2)}, u32[]{:S(2)}) collective-permute-start(bf16[512,1024]{1,0:T(8,128)(2,1)} %convolution_convert_fusion.8), channel_id=1, source_target_pairs={{0,4},{4,0},{1,5},{5,1},{2,6},{6,2},{3,7},{7,3},{8,12},{12,8},{9,1... | collective-permute-start | bytes 3145736 | tf_op jit(solution)/shard_map/ppermute | solution.py:346
  426.9 28.1 %collective-permute-start.53 = (bf16[512,1024]{1,0:T(8,128)(2,1)}, bf16[512,1024]{1,0:T(8,128)(2,1)}, u32[]{:S(2)}, u32[]{:S(2)}) collective-permute-start(bf16[512,1024]{1,0:T(8,128)(2,1)} %convolution_convert_fusion.7), channel_id=1, source_target_pairs={{0,2},{2,0},{1,3},{3,1},{4,6},{6,4},{5,7},{7,5},{8,10},{10,8},{9,1... | collective-permute-start | bytes 3145736 | tf_op jit(solution)/shard_map/ppermute | solution.py:346
  456.3 14.0 %collective-permute-start.58 = (bf16[4,32,1024]{2,1,0:T(8,128)(2,1)S(1)}, bf16[4,32,1024]{2,1,0:T(8,128)(2,1)S(1)}, u32[]{:S(2)}, u32[]{:S(2)}) collective-permute-start(bf16[4,32,1024]{2,1,0:T(8,128)(2,1)S(1)} %dynamic-slice_bitcast_fusion.5), channel_id=1, source_target_pairs={{0,2},{2,0},{1,3},{3,1},{4,6},{6,4},{5,7},{7,5},{8,10},{10,8},{9,1... | collective-permute-start | bytes 786440 | tf_op jit(solution)/shard_map/ppermute | solution.py:346
  467.6 37.3 %collective-permute-start.56 = (bf16[768,1024]{1,0:T(8,128)(2,1)}, bf16[768,1024]{1,0:T(8,128)(2,1)}, u32[]{:S(2)}, u32[]{:S(2)}) collective-permute-start(bf16[768,1024]{1,0:T(8,128)(2,1)} %pad_maximum_fusion.4), channel_id=1, source_target_pairs={{0,4},{4,0},{1,5},{5,1},{2,6},{6,2},{3,7},{7,3},{8,12},{12,8},{9,1... | collective-permute-start | bytes 4718600 | tf_op jit(solution)/shard_map/ppermute | solution.py:346
  469.0 35.9 %collective-permute-start.57 = (bf16[768,1024]{1,0:T(8,128)(2,1)}, bf16[768,1024]{1,0:T(8,128)(2,1)}, u32[]{:S(2)}, u32[]{:S(2)}) collective-permute-start(bf16[768,1024]{1,0:T(8,128)(2,1)} %pad_maximum_fusion.5), channel_id=1, source_target_pairs={{0,2},{2,0},{1,3},{3,1},{4,6},{6,4},{5,7},{7,5},{8,10},{10,8},{9,1... | collective-permute-start | bytes 4718600 | tf_op jit(solution)/shard_map/ppermute | solution.py:346
  475.4 95.8 %reduce-scatter.11.cloned.1.call-start = ((), (), s32[]{:S(2)}) async-start(), calls=%async_computation.7 | async-start | bytes 2785280 | tf_op jit(solution)/shard_map/reduce_scatter | solution.py:690
  478.6 26.1 %collective-permute-start.60 = (f32[4,1216]{1,0:T(4,128)S(1)}, f32[4,1216]{1,0:T(4,128)S(1)}, u32[]{:S(2)}, u32[]{:S(2)}) collective-permute-start(f32[4,1216]{1,0:T(4,128)S(1)} %bitcast.481), channel_id=1, source_target_pairs={{0,2},{2,0},{1,3},{3,1},{4,6},{6,4},{5,7},{7,5},{8,10},{10,8},{9,1... | collective-permute-start | bytes 58376 | tf_op jit(solution)/shard_map/ppermute | solution.py:346
  480.4 24.3 %collective-permute-start.61 = (f32[4,1216]{1,0:T(4,128)S(1)}, f32[4,1216]{1,0:T(4,128)S(1)}, u32[]{:S(2)}, u32[]{:S(2)}) collective-permute-start(f32[4,1216]{1,0:T(4,128)S(1)} %bitcast.480), channel_id=1, source_target_pairs={{0,4},{4,0},{1,5},{5,1},{2,6},{6,2},{3,7},{7,3},{8,12},{12,8},{9,1... | collective-permute-start | bytes 58376 | tf_op jit(solution)/shard_map/ppermute | solution.py:346
  481.0 23.7 %collective-permute-start.62 = (f32[4,1216]{1,0:T(4,128)S(1)}, f32[4,1216]{1,0:T(4,128)S(1)}, u32[]{:S(2)}, u32[]{:S(2)}) collective-permute-start(f32[4,1216]{1,0:T(4,128)S(1)} %bitcast.479), channel_id=1, source_target_pairs={{0,6},{6,0},{2,4},{4,2},{1,7},{7,1},{3,5},{5,3},{8,14},{14,8},{10,... | collective-permute-start | bytes 58376 | tf_op jit(solution)/shard_map/ppermute | solution.py:732
  546.4 14.5 %collective-permute-start.69 = (bf16[2,128,1024]{2,1,0:T(8,128)(2,1)}, bf16[2,128,1024]{2,1,0:T(8,128)(2,1)S(1)}, u32[]{:S(2)}, u32[]{:S(2)}) collective-permute-start(bf16[2,128,1024]{2,1,0:T(8,128)(2,1)} %slice.468), channel_id=1, source_target_pairs={{0,2},{2,0},{1,3},{3,1},{4,6},{6,4},{5,7},{7,5},{8,10},{10,8},{9,1... | collective-permute-start | bytes 1572872 | tf_op jit(solution)/shard_map/ppermute | solution.py:346
  (132 other events, 851.4 us)
Sparse Core Ops, SparseCore 0:
  10.2 32.8 all-gather.10
  45.3 28.7 all-gather.8
  75.6 40.5 all-gather.12
  117.6 148.4 all-gather.14
  311.2 76.3 reduce-scatter.4
  398.4 59.8 reduce-scatter.6
  475.5 42.6 reduce-scatter.8
  526.7 44.4 reduce-scatter.10

commit v7 on v6

--- a/solution.py
+++ b/solution.py
@@ -70,15 +70,14 @@
     query_grad_ref,
     key_grad_ref,
     value_grad_ref,
-    sums_ref,
+    diag_ref,
     spread_ref,
-    diag_ref,
     weight_ref,
     score_ref,
     raw_ref,
     weight_grad_ref,
 ):
-    group, width = key_ref.shape[0], spread_ref.shape[2]
+    group = key_ref.shape[0]
     outs, key_grads, value_grads = [], [], []
     for half in range(2):
         mask = half_mask(query_ref.shape[0], half)
@@ -100,19 +99,11 @@
             inner = jnp.sum(weights * weight_grad, axis=1, keepdims=True)
             score_grad = weights * (weight_grad - inner)
             shift = pl.multiple_of(group - info_ref[2] - number * ROWS, ROWS)
-            diag_ref[half, :, pl.ds(shift, group)] += score_grad
+            diag_ref[0, half, :, pl.ds(shift, group)] += score_grad
             score_ref[half, rows, :] = (score_grad * 0.125).astype(jnp.bfloat16)
         outs.append(matmul_in(score_ref[half], key_ref[...], ((1,), (0,))).astype(jnp.bfloat16))
         key_grads.append(matmul_in(score_ref[half], query, ((0,), (0,))))
         value_grads.append(matmul_in(weight_ref[half], grad, ((0,), (0,))))
-        total = diag_ref[half]
-        size = ROWS // 2
-        while size >= 8:
-            total = total[:size] + pltpu.roll(total[size:], width - size, 1)
-            size //= 2
-        for size in (4, 2, 1):
-            total = total + pltpu.roll(pltpu.roll(total, 8 - size, 0), width - size, 1)
-        sums_ref[0, half : half + 1] = total[0:1]
     query_grad_ref[...] = jnp.where(half_mask(query_ref.shape[0], 0), outs[0], outs[1])
     key_grad_ref[...] = key_grads[0] + key_grads[1]
     value_grad_ref[...] = value_grads[0] + value_grads[1]
@@ -167,15 +158,19 @@
         attend_back_kernel,
         grid=(pairs,),
         in_specs=attend_specs(rows, group, width, pairs) + [pair_block],
-        out_specs=[pair_block, group_block, group_block, pl.BlockSpec((1, 2, width), lambda h: (h, 0, 0))],
+        out_specs=[
+            pair_block,
+            group_block,
+            group_block,
+            pl.BlockSpec((1, 2, ROWS, width), lambda h: (h, 0, 0, 0)),
+        ],
         out_shape=[
             jax.ShapeDtypeStruct((rows, heads * HD), jnp.bfloat16),
             jax.ShapeDtypeStruct((group, heads * HD), jnp.float32),
             jax.ShapeDtypeStruct((group, heads * HD), jnp.float32),
-            jax.ShapeDtypeStruct((pairs, 2, width), jnp.float32),
+            jax.ShapeDtypeStruct((pairs, 2, ROWS, width), jnp.float32),
         ],
         scratch_shapes=[
-            pltpu.VMEM((2, ROWS, width), jnp.float32),
             pltpu.VMEM((2, ROWS, width), jnp.float32),
             pltpu.VMEM((2, rows, group), jnp.bfloat16),
             pltpu.VMEM((2, rows, group), jnp.bfloat16),
@@ -186,6 +181,32 @@
         cost_estimate=cost_of(heads, rows, group, 5),
         name="attend_back",
     )(info, bias, query, both, both, grad)
+
+
+def diagonal_kernel(diag_ref, sums_ref):
+    width = diag_ref.shape[3]
+    for half in range(2):
+        total = diag_ref[0, half]
+        size = ROWS // 2
+        while size >= 8:
+            total = total[:size] + pltpu.roll(total[size:], width - size, 1)
+            size //= 2
+        for size in (4, 2, 1):
+            total = total + pltpu.roll(pltpu.roll(total, 8 - size, 0), width - size, 1)
+        sums_ref[0, half : half + 1] = total[0:1]
+
+
+def diagonal_sums(diagonals):
+    pairs, _, rows, width = diagonals.shape
+    return pl.pallas_call(
+        diagonal_kernel,
+        grid=(pairs,),
+        in_specs=[pl.BlockSpec((1, 2, rows, width), lambda h: (h, 0, 0, 0))],
+        out_specs=pl.BlockSpec((1, 2, width), lambda h: (h, 0, 0)),
+        out_shape=jax.ShapeDtypeStruct((pairs, 2, width), jnp.float32),
+        compiler_params=pltpu.CompilerParams(vmem_limit_bytes=VMEM),
+        name="diagonal_sums",
+    )(diagonals)
 
 
 LANES = 128
@@ -697,7 +718,7 @@
 
     def small_of(table_sums, depth_grad, gain_zero, gain_one, gain_two, gain_three, gain_four, gain_five):
         table_grad = jnp.einsum(
-            "hw,wb->bh", table_sums.reshape(heads, -1), hits.astype(f32), precision=lax.Precision.HIGHEST
+            "hw,wb->bh", diagonal_sums(table_sums).reshape(heads, -1), hits.astype(f32), precision=lax.Precision.HIGHEST
         )
 
         def of_core(values, dim):

time: 593 us -> 593 us (level)
  transfers between devices with their start and end apart: 79 -> 79, of which waited for: 42 -> 43; matrix products, arithmetic and copies ran while one was open for 32% -> 32% of each run, Pallas kernels for 7% -> 7%
where the time goes in v7:
time: 593 us; the launch traced here: 585 us
  waiting for transfers between devices  218 us (37%)
  local copies, waits for them, and re-layouts  106 us (18%)
  matrix products  81.9 us (14%)
  starting transfers between devices  70.2 us (12%)
  other arithmetic  48.8 us (8%)
  Pallas kernels  42.1 us (7%)
  between operations  18.4 us (3%)
    ppermute x65, waiting for transfers between devices, swap(): return lax.ppermute(values, axis, CORES)  212 us
    ppermute x65, starting transfers between devices, swap(): return lax.ppermute(values, axis, CORES)  54.9 us
    dot_general x18, matrix products, left_product(): jnp.einsum('nd,nf->df', left_in, right_in, preferred_element_type=jnp.flo...  41.1 us
    unnamed x238, local copies, waits for them, and re-layouts  31.7 us
    dot_general x8, matrix products, right_product(): jnp.einsum('nf,df->nd', left_in, right_in, preferred_element_type=jnp.flo...  23.5 us
    dot_general x8, matrix products, product(): return jnp.dot(left_in, right_in, preferred_element_type=jnp.float32)  16.8 us
    pallas_call x1, Pallas kernels, attend_back(): pl.pallas_call(attend_back_kernel, grid=(pairs,), in_specs=attend_specs(r...  16 us
    dynamic_update_slice x12, local copies, waits for them, and re-layouts, placed(): result = lax.dynamic_update_slice(result, part[:, None, None], at)  13.3 us
  transfers between devices with their start and end apart: 79, of which 43 were waited for; matrix products, arithmetic and copies ran while one was open for 32% of the time, Pallas kernels for 7%

profile of v7, /device:TPU:0, one launch (start us, length us, event | category | flops | bytes accessed | tf_op | source)
XLA Modules:
  0.0 585.0 jit_solution(13409383696482494477)
XLA Ops:
  9.5 3.0 collective-permute-start.7
  14.4 10.0 %collective-permute-done.7 = bf16[256,1024]{1,0:T(8,128)(2,1)S(1)} collective-permute-done((bf16[256,1024]{1,0:T(8,128)(2,1)S(1)}, bf16[256,1024]{1,0:T(8,128)(2,1)S(1)}, u32[]{:S(2)}, u32[]{:S(2)}) %collective-permute-start.7) | collective-permute-done | bytes 524320 | tf_op jit(solution)/shard_map/ppermute | solution.py:367
  30.9 3.5 dynamic-slice_reduce_fusion
  35.5 3.0 collective-permute-done.9
  40.0 3.1 all-gather.11.cloned.1.call-done
  47.1 20.3 %collective-permute-done.13 = bf16[512,1024]{0,1:T(8,128)(2,1)} collective-permute-done((bf16[512,1024]{0,1:T(8,128)(2,1)}, bf16[512,1024]{0,1:T(8,128)(2,1)}, u32[]{:S(2)}, u32[]{:S(2)}) %collective-permute-start.13) | collective-permute-done | bytes 1048608 | tf_op jit(solution)/shard_map/ppermute | solution.py:367
  93.3 15.9 %collective-permute-done.2 = bf16[512,1024]{1,0:T(8,128)(2,1)} collective-permute-done((bf16[512,1024]{1,0:T(8,128)(2,1)S(1)}, bf16[512,1024]{1,0:T(8,128)(2,1)}, u32[]{:S(2)}, u32[]{:S(2)}) %collective-permute-start.2) | collective-permute-done | bytes 1048608 | tf_op jit(solution)/shard_map/ppermute | solution.py:367
  129.6 3.4 collective-permute-done.14
  132.9 7.4 %collective-permute-done.15 = bf16[512,1024]{1,0:T(8,128)(2,1)} collective-permute-done((bf16[512,1024]{1,0:T(8,128)(2,1)}, bf16[512,1024]{1,0:T(8,128)(2,1)}, u32[]{:S(2)}, u32[]{:S(2)}) %collective-permute-start.15) | collective-permute-done | bytes 1048608 | tf_op jit(solution)/shard_map/ppermute | solution.py:367
  140.4 7.7 %collective-permute-done.16 = bf16[4,64,1536]{2,1,0:T(8,128)(2,1)} collective-permute-done((bf16[4,64,1536]{2,1,0:T(8,128)(2,1)S(1)}, bf16[4,64,1536]{2,1,0:T(8,128)(2,1)}, u32[]{:S(2)}, u32[]{:S(2)}) %collective-permute-start.16) | collective-permute-done | bytes 786464 | tf_op jit(solution)/shard_map/ppermute | solution.py:367
  160.0 5.7 multiply_convert_fusion.3
  175.7 16.6 %collective-permute-done.20 = bf16[4,64,1536]{2,1,0:T(8,128)(2,1)S(1)} collective-permute-done((bf16[4,64,1536]{2,1,0:T(8,128)(2,1)}, bf16[4,64,1536]{2,1,0:T(8,128)(2,1)S(1)}, u32[]{:S(2)}, u32[]{:S(2)}) %collective-permute-start.20) | collective-permute-done | bytes 786464 | tf_op jit(solution)/shard_map/ppermute | solution.py:367
  195.3 3.3 convolution_convert_fusion.3
  206.4 13.8 %collective-permute-done.23 = bf16[384,1024]{1,0:T(8,128)(2,1)} collective-permute-done((bf16[384,1024]{1,0:T(8,128)(2,1)}, bf16[384,1024]{1,0:T(8,128)(2,1)}, u32[]{:S(2)}, u32[]{:S(2)}) %collective-permute-start.23) | collective-permute-done | bytes 786464 | tf_op jit(solution)/shard_map/ppermute | solution.py:367
  221.8 8.8 %attend.1 = bf16[384,512]{1,0:T(8,128)(2,1)S(1)} custom-call(s32[3]{0:T(128)S(1)} %pad_add_fusion.info_ref.refs_0_, f32[4,2,1536]{2,1,0:T(2,128)S(1)} %fusion.76.bias_ref, bf16[384,512]{1,0:T(8,128)(2,1)S(1)} %slice.504.query_ref, bf16[768,1024]{1,0:T(8,128)(2,1)S(1)} %pad_maximum_fusion.3.key_ref.value_ref, ...), custom_call_target="tpu_custom_call" | custom-call | flops 603979776 | bytes 2359296 | tf_op jit(solution)/shard_map/attend/pallas_call | solution.py:134
  247.4 4.5 collective-permute-start.28
  253.4 4.2 conv.1
  267.6 4.2 fusion.135
  271.8 3.6 fusion.63
  285.9 4.1 multiply_convert_fusion.1
  292.4 2.4 convolution_convert_fusion.1
  305.2 5.5 convolution_convert_fusion
  315.5 4.5 collective-permute-start.38
  320.0 6.8 %collective-permute-done.39 = bf16[4,2,32,1024]{3,2,0,1:T(8,128)(2,1)S(1)} collective-permute-done((bf16[4,2,32,1024]{3,2,0,1:T(8,128)(2,1)S(1)}, bf16[4,2,32,1024]{3,2,0,1:T(8,128)(2,1)S(1)}, u32[]{:S(2)}, u32[]{:S(2)}) %collective-permute-start.39) | collective-permute-done | bytes 524320 | tf_op jit(solution)/shard_map/ppermute | solution.py:367
  326.8 7.5 %conv_back.1 = (f32[384,512]{1,0:T(8,128)S(1)}, f32[31,512]{1,0:T(8,128)S(1)}) custom-call(s32[3]{0:T(128)S(1)} %pad_add_fusion.info_ref.refs_0_, bf16[16,512]{1,0:T(8,128)(2,1)S(1)} %collective-permute-done.28.refs_1_, bf16[384,512]{1,0:T(8,128)(2,1)S(1)} %multiply_convert_fusion.12.refs_2_, bf16[16,512]{1,0:T(8,128)(2,1)S(1)} %collective-permute-done.29.refs_3_, ...), custom_call_target="tpu_custom_call" | custom-call | flops 24379392 | bytes 1572864 | tf_op jit(solution)/shard_map/conv_back/pallas_call | solution.py:322
  341.5 2.4 collective-permute-start.43
  346.2 16.0 %attend_back.1 = (bf16[384,512]{1,0:T(8,128)(2,1)S(1)}, f32[768,512]{1,0:T(8,128)S(1)}, f32[768,512]{1,0:T(8,128)}, f32[4,2,128,1536]{3,2,1,0:T(8,128)}) custom-call(s32[3]{0:T(128)S(1)} %pad_add_fusion.info_ref.refs_0_, f32[4,2,1536]{2,1,0:T(2,128)S(1)} %copy-done.4, bf16[384,512]{1,0:T(8,128)(2,1)S(1)} %copy-done.2, bf16[768,1024]{1,0:T(8,128)(2,1)} %copy-done, ...), custom_call_target="tpu_custom_call" | custom-call | flops 1509949440 | bytes 2359296 | tf_op jit(solution)/shard_map/attend_back/pallas_call | solution.py:157
  362.2 5.6 collective-permute-done.43
  373.5 10.8 %collective-permute-done.44 = bf16[4,2,128,1024]{3,2,0,1:T(8,128)(2,1)S(1)} collective-permute-done((bf16[4,2,128,1024]{3,2,0,1:T(8,128)(2,1)}, bf16[4,2,128,1024]{3,2,0,1:T(8,128)(2,1)S(1)}, u32[]{:S(2)}, u32[]{:S(2)}) %collective-permute-start.44) | collective-permute-done | bytes 2097184 | tf_op jit(solution)/shard_map/ppermute | solution.py:367
  386.0 2.6 fusion.15
  394.4 3.5 convolution_convert_fusion.2
  400.7 2.5 multiply_convert_fusion.4
  409.4 5.6 multiply_convert_fusion
  415.1 5.0 collective-permute-done.50
  420.1 3.1 convolution_convert_fusion.8
  423.2 2.8 convolution_convert_fusion.7
  427.3 2.4 collective-permute-start.53
  429.7 4.5 fusion.155
  434.3 3.5 convolution_convert_fusion.5
  437.8 2.9 convolution_convert_fusion.6
  441.3 12.1 %collective-permute-done.52 = bf16[512,1024]{1,0:T(8,128)(2,1)} collective-permute-done((bf16[512,1024]{1,0:T(8,128)(2,1)}, bf16[512,1024]{1,0:T(8,128)(2,1)}, u32[]{:S(2)}, u32[]{:S(2)}) %collective-permute-start.52) | collective-permute-done | bytes 1048608 | tf_op jit(solution)/shard_map/ppermute | solution.py:367
  472.0 5.5 diagonal_sums.1
  487.0 18.0 %collective-permute-done.60 = f32[4,1216]{1,0:T(4,128)S(1)} collective-permute-done((f32[4,1216]{1,0:T(4,128)S(1)}, f32[4,1216]{1,0:T(4,128)S(1)}, u32[]{:S(2)}, u32[]{:S(2)}) %collective-permute-start.60) | collective-permute-done | bytes 19488 | tf_op jit(solution)/shard_map/ppermute | solution.py:367
  515.9 5.4 collective-permute-done.63
  529.4 6.4 %collective-permute-done.65 = bf16[2,64,1536]{2,1,0:T(8,128)(2,1)S(1)} collective-permute-done((bf16[2,64,1536]{2,1,0:T(8,128)(2,1)S(1)}, bf16[2,64,1536]{2,1,0:T(8,128)(2,1)S(1)}, u32[]{:S(2)}, u32[]{:S(2)}) %collective-permute-start.65) | collective-permute-done | bytes 393248 | tf_op jit(solution)/shard_map/ppermute | solution.py:367
  538.2 4.5 collective-permute-done.66
  549.3 11.8 %collective-permute-done.69 = bf16[2,128,1024]{2,1,0:T(8,128)(2,1)S(1)} collective-permute-done((bf16[2,128,1024]{2,1,0:T(8,128)(2,1)}, bf16[2,128,1024]{2,1,0:T(8,128)(2,1)S(1)}, u32[]{:S(2)}, u32[]{:S(2)}) %collective-permute-start.69) | collective-permute-done | bytes 524320 | tf_op jit(solution)/shard_map/ppermute | solution.py:367
  565.8 3.5 collective-permute-done.70
  (672 shorter events, 253.1 us)
Async XLA Ops:
  7.2 35.9 %all-gather.11.cloned.1.call-start = ((), (), s32[]{:S(2)}) async-start(), calls=%async_computation.9 | async-start | bytes 1310720 | tf_op jit(solution)/shard_map/all_gather | solution.py:594
  9.1 66.3 %all-gather.9.cloned.1.call-start = ((), (), s32[]{:S(2)}) async-start(), calls=%async_computation.8 | async-start | bytes 1474560 | tf_op jit(solution)/shard_map/all_gather | solution.py:594
  9.5 14.9 %collective-permute-start.7 = (bf16[256,1024]{1,0:T(8,128)(2,1)S(1)}, bf16[256,1024]{1,0:T(8,128)(2,1)S(1)}, u32[]{:S(2)}, u32[]{:S(2)}) collective-permute-start(bf16[256,1024]{1,0:T(8,128)(2,1)S(1)} %get-tuple-element.370), channel_id=1, source_target_pairs={{0,4},{4,0},{1,5},{5,1},{2,6},{6,2},{3,7},{7,3},{8,12},{12,8},{9,1... | collective-permute-start | bytes 1572872 | tf_op jit(solution)/shard_map/ppermute | solution.py:367
  12.5 13.4 %collective-permute-start.8 = (bf16[256,1024]{1,0:T(8,128)(2,1)S(1)}, bf16[256,1024]{1,0:T(8,128)(2,1)S(1)}, u32[]{:S(2)}, u32[]{:S(2)}) collective-permute-start(bf16[256,1024]{1,0:T(8,128)(2,1)S(1)} %get-tuple-element.370), channel_id=1, source_target_pairs={{0,2},{2,0},{1,3},{3,1},{4,6},{6,4},{5,7},{7,5},{8,10},{10,8},{9,1... | collective-permute-start | bytes 1572872 | tf_op jit(solution)/shard_map/ppermute | solution.py:367
  14.3 13.1 %collective-permute-start = (bf16[1,1216]{1,0:T(2,128)(2,1)S(1)}, bf16[1,1216]{1,0:T(2,128)(2,1)S(1)}, u32[]{:S(2)}, u32[]{:S(2)}) collective-permute-start(bf16[1,1216]{1,0:T(2,128)(2,1)S(1)} %broadcast_in_dim.43), channel_id=1, source_target_pairs={{0,1},{1,0},{2,3},{3,2},{4,5},{5,4},{6,7},{7,6},{8,9},{9,8},{10,11... | collective-permute-start | bytes 7304 | tf_op jit(solution)/shard_map/ppermute | solution.py:367
  25.9 12.6 %collective-permute-start.9 = (bf16[256,1024]{1,0:T(8,128)(2,1)S(1)}, bf16[256,1024]{1,0:T(8,128)(2,1)S(1)}, u32[]{:S(2)}, u32[]{:S(2)}) collective-permute-start(bf16[256,1024]{1,0:T(8,128)(2,1)S(1)} %collective-permute-done.7), channel_id=1, source_target_pairs={{0,2},{2,0},{1,3},{3,1},{4,6},{6,4},{5,7},{7,5},{8,10},{10,8},{9,1... | collective-permute-start | bytes 1572872 | tf_op jit(solution)/shard_map/ppermute | solution.py:367
  28.3 90.1 %all-gather.13.cloned.1.call-start = ((), (), s32[]{:S(2)}) async-start(), calls=%async_computation.10 | async-start | bytes 2293760 | tf_op jit(solution)/shard_map/all_gather | solution.py:594
  30.5 14.5 %collective-permute-start.10 = (bf16[32,1536]{1,0:T(8,128)(2,1)}, bf16[32,1536]{1,0:T(8,128)(2,1)}, u32[]{:S(2)}, u32[]{:S(2)}) collective-permute-start(bf16[32,1536]{1,0:T(8,128)(2,1)} %bitcast.199), channel_id=1, source_target_pairs={{0,1},{1,0},{2,3},{3,2},{4,5},{5,4},{6,7},{7,6},{8,9},{9,8},{10,11... | collective-permute-start | bytes 294920 | tf_op jit(solution)/shard_map/ppermute | solution.py:367
  43.1 24.2 %collective-permute-start.13 = (bf16[512,1024]{0,1:T(8,128)(2,1)}, bf16[512,1024]{0,1:T(8,128)(2,1)}, u32[]{:S(2)}, u32[]{:S(2)}) collective-permute-start(bf16[512,1024]{0,1:T(8,128)(2,1)} %all-gather.11.cloned.1.call-done), channel_id=1, source_target_pairs={{0,2},{2,0},{1,3},{3,1},{4,6},{6,4},{5,7},{7,5},{8,10},{10,8},{9,1... | collective-permute-start | bytes 3145736 | tf_op jit(solution)/shard_map/ppermute | solution.py:367
  43.6 25.0 %collective-permute-start.12 = (bf16[512,1024]{0,1:T(8,128)(2,1)}, bf16[512,1024]{0,1:T(8,128)(2,1)S(1)}, u32[]{:S(2)}, u32[]{:S(2)}) collective-permute-start(bf16[512,1024]{0,1:T(8,128)(2,1)} %all-gather.11.cloned.1.call-done), channel_id=1, source_target_pairs={{0,4},{4,0},{1,5},{5,1},{2,6},{6,2},{3,7},{7,3},{8,12},{12,8},{9,1... | collective-permute-start | bytes 3145736 | tf_op jit(solution)/shard_map/ppermute | solution.py:367
  68.7 198.9 %all-gather.15.cloned.1.call-start = ((), (), s32[]{:S(2)}) async-start(), calls=%async_computation.11 | async-start | bytes 10485760 | tf_op jit(solution)/shard_map/all_gather | solution.py:594
  74.8 351.2 %reduce-scatter.5.cloned.1.call-start = ((), (), s32[]{:S(2)}) async-start(), calls=%async_computation.4 | async-start | bytes 5242880 | tf_op jit(solution)/shard_map/reduce_scatter | solution.py:711
  78.2 14.7 %collective-permute-start.5 = (bf16[4,16,1024]{2,1,0:T(8,128)(2,1)}, bf16[4,16,1024]{2,1,0:T(8,128)(2,1)}, u32[]{:S(2)}, u32[]{:S(2)}) collective-permute-start(bf16[4,16,1024]{2,1,0:T(8,128)(2,1)} %slice.478), channel_id=1, source_target_pairs={{0,6},{6,0},{2,4},{4,2},{1,7},{7,1},{3,5},{5,3},{8,14},{14,8},{10,... | collective-permute-start | bytes 393224 | tf_op jit(solution)/shard_map/ppermute | solution.py:616
  79.8 13.5 %collective-permute-start.4 = (bf16[4,16,1024]{2,1,0:T(8,128)(2,1)}, bf16[4,16,1024]{2,1,0:T(8,128)(2,1)}, u32[]{:S(2)}, u32[]{:S(2)}) collective-permute-start(bf16[4,16,1024]{2,1,0:T(8,128)(2,1)} %slice.478), channel_id=1, source_target_pairs={{0,2},{2,0},{1,3},{3,1},{4,6},{6,4},{5,7},{7,5},{8,10},{10,8},{9,1... | collective-permute-start | bytes 393224 | tf_op jit(solution)/shard_map/ppermute | solution.py:367
  81.2 12.1 %collective-permute-start.3 = (bf16[4,16,1024]{2,1,0:T(8,128)(2,1)}, bf16[4,16,1024]{2,1,0:T(8,128)(2,1)}, u32[]{:S(2)}, u32[]{:S(2)}) collective-permute-start(bf16[4,16,1024]{2,1,0:T(8,128)(2,1)} %slice.478), channel_id=1, source_target_pairs={{0,4},{4,0},{1,5},{5,1},{2,6},{6,2},{3,7},{7,3},{8,12},{12,8},{9,1... | collective-permute-start | bytes 393224 | tf_op jit(solution)/shard_map/ppermute | solution.py:367
  81.8 27.4 %collective-permute-start.2 = (bf16[512,1024]{1,0:T(8,128)(2,1)S(1)}, bf16[512,1024]{1,0:T(8,128)(2,1)}, u32[]{:S(2)}, u32[]{:S(2)}) collective-permute-start(bf16[512,1024]{1,0:T(8,128)(2,1)S(1)} %bitcast.400), channel_id=1, source_target_pairs={{0,2},{2,0},{1,3},{3,1},{4,6},{6,4},{5,7},{7,5},{8,10},{10,8},{9,1... | collective-permute-start | bytes 3145736 | tf_op jit(solution)/shard_map/ppermute | solution.py:367
  82.2 28.3 %collective-permute-start.1 = (bf16[512,1024]{1,0:T(8,128)(2,1)S(1)}, bf16[512,1024]{1,0:T(8,128)(2,1)}, u32[]{:S(2)}, u32[]{:S(2)}) collective-permute-start(bf16[512,1024]{1,0:T(8,128)(2,1)S(1)} %bitcast.401), channel_id=1, source_target_pairs={{0,4},{4,0},{1,5},{5,1},{2,6},{6,2},{3,7},{7,3},{8,12},{12,8},{9,1... | collective-permute-start | bytes 3145736 | tf_op jit(solution)/shard_map/ppermute | solution.py:367
  92.9 40.0 %collective-permute-start.14 = (bf16[512,1024]{0,1:T(8,128)(2,1)}, bf16[512,1024]{0,1:T(8,128)(2,1)}, u32[]{:S(2)}, u32[]{:S(2)}) collective-permute-start(bf16[512,1024]{0,1:T(8,128)(2,1)} %collective-permute-done.13), channel_id=1, source_target_pairs={{0,4},{4,0},{1,5},{5,1},{2,6},{6,2},{3,7},{7,3},{8,12},{12,8},{9,1... | collective-permute-start | bytes 3145736 | tf_op jit(solution)/shard_map/ppermute | solution.py:367
  116.9 23.4 %collective-permute-start.15 = (bf16[512,1024]{1,0:T(8,128)(2,1)}, bf16[512,1024]{1,0:T(8,128)(2,1)}, u32[]{:S(2)}, u32[]{:S(2)}) collective-permute-start(bf16[512,1024]{1,0:T(8,128)(2,1)} %collective-permute-done.1), channel_id=1, source_target_pairs={{0,2},{2,0},{1,3},{3,1},{4,6},{6,4},{5,7},{7,5},{8,10},{10,8},{9,1... | collective-permute-start | bytes 3145736 | tf_op jit(solution)/shard_map/ppermute | solution.py:367
  121.4 26.6 %collective-permute-start.16 = (bf16[4,64,1536]{2,1,0:T(8,128)(2,1)S(1)}, bf16[4,64,1536]{2,1,0:T(8,128)(2,1)}, u32[]{:S(2)}, u32[]{:S(2)}) collective-permute-start(bf16[4,64,1536]{2,1,0:T(8,128)(2,1)S(1)} %reshape.692), channel_id=1, source_target_pairs={{0,4},{4,0},{1,5},{5,1},{2,6},{6,2},{3,7},{7,3},{8,12},{12,8},{9,1... | collective-permute-start | bytes 2359304 | tf_op jit(solution)/shard_map/ppermute | solution.py:367
  124.1 35.9 %collective-permute-start.6 = (bf16[192,1024]{1,0:T(8,128)(2,1)}, bf16[192,1024]{1,0:T(8,128)(2,1)}, u32[]{:S(2)}, u32[]{:S(2)}) collective-permute-start(bf16[192,1024]{1,0:T(8,128)(2,1)} %fusion.28), channel_id=1, source_target_pairs={{0,1},{1,0},{2,3},{3,2},{4,5},{5,4},{6,7},{7,6},{8,9},{9,8},{10,11... | collective-permute-start | bytes 1179656 | tf_op jit(solution)/shard_map/ppermute | solution.py:367
  151.1 19.8 %collective-permute-start.18 = (bf16[4,64,1536]{2,1,0:T(8,128)(2,1)S(1)}, bf16[4,64,1536]{2,1,0:T(8,128)(2,1)}, u32[]{:S(2)}, u32[]{:S(2)}) collective-permute-start(bf16[4,64,1536]{2,1,0:T(8,128)(2,1)S(1)} %copy-done.30), channel_id=1, source_target_pairs={{0,2},{2,0},{1,3},{3,1},{4,6},{6,4},{5,7},{7,5},{8,10},{10,8},{9,1... | collective-permute-start | bytes 2359304 | tf_op jit(solution)/shard_map/ppermute | solution.py:367
  152.3 47.4 %collective-permute-start.21 = (bf16[4,128,1024]{2,1,0:T(8,128)(2,1)S(1)}, bf16[4,128,1024]{2,1,0:T(8,128)(2,1)}, u32[]{:S(2)}, u32[]{:S(2)}) collective-permute-start(bf16[4,128,1024]{2,1,0:T(8,128)(2,1)S(1)} %slice.485), channel_id=1, source_target_pairs={{0,4},{4,0},{1,5},{5,1},{2,6},{6,2},{3,7},{7,3},{8,12},{12,8},{9,1... | collective-permute-start | bytes 3145736 | tf_op jit(solution)/shard_map/ppermute | solution.py:367
  171.0 21.3 %collective-permute-start.20 = (bf16[4,64,1536]{2,1,0:T(8,128)(2,1)}, bf16[4,64,1536]{2,1,0:T(8,128)(2,1)S(1)}, u32[]{:S(2)}, u32[]{:S(2)}) collective-permute-start(bf16[4,64,1536]{2,1,0:T(8,128)(2,1)} %collective-permute-done.18), channel_id=1, source_target_pairs={{0,4},{4,0},{1,5},{5,1},{2,6},{6,2},{3,7},{7,3},{8,12},{12,8},{9,1... | collective-permute-start | bytes 2359304 | tf_op jit(solution)/shard_map/ppermute | solution.py:367
  174.5 25.4 %collective-permute-start.22 = (bf16[4,128,1024]{2,1,0:T(8,128)(2,1)S(1)}, bf16[4,128,1024]{2,1,0:T(8,128)(2,1)S(1)}, u32[]{:S(2)}, u32[]{:S(2)}) collective-permute-start(bf16[4,128,1024]{2,1,0:T(8,128)(2,1)S(1)} %slice.485), channel_id=1, source_target_pairs={{0,2},{2,0},{1,3},{3,1},{4,6},{6,4},{5,7},{7,5},{8,10},{10,8},{9,1... | collective-permute-start | bytes 3145736 | tf_op jit(solution)/shard_map/ppermute | solution.py:367
  200.8 19.4 %collective-permute-start.23 = (bf16[384,1024]{1,0:T(8,128)(2,1)}, bf16[384,1024]{1,0:T(8,128)(2,1)}, u32[]{:S(2)}, u32[]{:S(2)}) collective-permute-start(bf16[384,1024]{1,0:T(8,128)(2,1)} %slice.505), channel_id=1, source_target_pairs={{0,2},{2,0},{1,3},{3,1},{4,6},{6,4},{5,7},{7,5},{8,10},{10,8},{9,1... | collective-permute-start | bytes 2359304 | tf_op jit(solution)/shard_map/ppermute | solution.py:367
  202.0 28.7 %collective-permute-start.24 = (bf16[4,128,1024]{2,1,0:T(8,128)(2,1)}, bf16[4,128,1024]{2,1,0:T(8,128)(2,1)S(1)}, u32[]{:S(2)}, u32[]{:S(2)}) collective-permute-start(bf16[4,128,1024]{2,1,0:T(8,128)(2,1)} %copy-done.62), channel_id=1, source_target_pairs={{0,4},{4,0},{1,5},{5,1},{2,6},{6,2},{3,7},{7,3},{8,12},{12,8},{9,1... | collective-permute-start | bytes 3145736 | tf_op jit(solution)/shard_map/ppermute | solution.py:367
  310.8 194.4 %reduce-scatter.7.cloned.1.call-start = ((), (), s32[]{:S(2)}) async-start(), calls=%async_computation.5 | async-start | bytes 3932160 | tf_op jit(solution)/shard_map/reduce_scatter | solution.py:711
  312.8 14.1 %collective-permute-start.39 = (bf16[4,2,32,1024]{3,2,0,1:T(8,128)(2,1)S(1)}, bf16[4,2,32,1024]{3,2,0,1:T(8,128)(2,1)S(1)}, u32[]{:S(2)}, u32[]{:S(2)}) collective-permute-start(bf16[4,2,32,1024]{3,2,0,1:T(8,128)(2,1)S(1)} %bitcast.461), channel_id=1, source_target_pairs={{0,4},{4,0},{1,5},{5,1},{2,6},{6,2},{3,7},{7,3},{8,12},{12,8},{9,1... | collective-permute-start | bytes 1572872 | tf_op jit(solution)/shard_map/ppermute | solution.py:367
  314.2 12.7 %collective-permute-start.40 = (bf16[16,512]{1,0:T(8,128)(2,1)S(1)}, bf16[16,512]{1,0:T(8,128)(2,1)S(1)}, u32[]{:S(2)}, u32[]{:S(2)}) collective-permute-start(bf16[16,512]{1,0:T(8,128)(2,1)S(1)} %get-tuple-element.373), channel_id=1, source_target_pairs={{2,0},{3,1},{6,4},{7,5},{10,8},{11,9},{14,12},{15,13},{18,16},{19,... | collective-permute-start | bytes 49160 | tf_op jit(solution)/shard_map/ppermute | solution.py:531
  336.0 48.3 %collective-permute-start.44 = (bf16[4,2,128,1024]{3,2,0,1:T(8,128)(2,1)}, bf16[4,2,128,1024]{3,2,0,1:T(8,128)(2,1)S(1)}, u32[]{:S(2)}, u32[]{:S(2)}) collective-permute-start(bf16[4,2,128,1024]{3,2,0,1:T(8,128)(2,1)} %copy.281), channel_id=1, source_target_pairs={{0,4},{4,0},{1,5},{5,1},{2,6},{6,2},{3,7},{7,3},{8,12},{12,8},{9,1... | collective-permute-start | bytes 6291464 | tf_op jit(solution)/shard_map/ppermute | solution.py:367
  341.5 26.3 %collective-permute-start.43 = (bf16[4,2,64,1024]{3,2,0,1:T(8,128)(2,1)S(1)}, bf16[4,2,64,1024]{3,2,0,1:T(8,128)(2,1)S(1)}, u32[]{:S(2)}, u32[]{:S(2)}) collective-permute-start(bf16[4,2,64,1024]{3,2,0,1:T(8,128)(2,1)S(1)} %bitcast.449), channel_id=1, source_target_pairs={{0,2},{2,0},{1,3},{3,1},{4,6},{6,4},{5,7},{7,5},{8,10},{10,8},{9,1... | collective-permute-start | bytes 3145736 | tf_op jit(solution)/shard_map/ppermute | solution.py:367
  344.2 29.3 %collective-permute-start.45 = (bf16[4,32,1024]{2,1,0:T(8,128)(2,1)S(1)}, bf16[4,32,1024]{2,1,0:T(8,128)(2,1)S(1)}, u32[]{:S(2)}, u32[]{:S(2)}) collective-permute-start(bf16[4,32,1024]{2,1,0:T(8,128)(2,1)S(1)} %dynamic-slice_bitcast_fusion.6), channel_id=1, source_target_pairs={{0,2},{2,0},{1,3},{3,1},{4,6},{6,4},{5,7},{7,5},{8,10},{10,8},{9,1... | collective-permute-start | bytes 786440 | tf_op jit(solution)/shard_map/ppermute | solution.py:367
  369.7 20.3 %collective-permute-start.47 = (bf16[384,1024]{1,0:T(8,128)(2,1)S(1)}, bf16[384,1024]{1,0:T(8,128)(2,1)S(1)}, u32[]{:S(2)}, u32[]{:S(2)}) collective-permute-start(bf16[384,1024]{1,0:T(8,128)(2,1)S(1)} %fusion.39), channel_id=1, source_target_pairs={{0,2},{2,0},{1,3},{3,1},{4,6},{6,4},{5,7},{7,5},{8,10},{10,8},{9,1... | collective-permute-start | bytes 2359304 | tf_op jit(solution)/shard_map/ppermute | solution.py:367
  398.0 127.5 %reduce-scatter.9.cloned.1.call-start = ((), (), s32[]{:S(2)}) async-start(), calls=%async_computation.6 | async-start | bytes 2621440 | tf_op jit(solution)/shard_map/reduce_scatter | solution.py:711
  405.1 14.9 %collective-permute-start.50 = (bf16[4,64,1024]{2,1,0:T(8,128)(2,1)}, bf16[4,64,1024]{2,1,0:T(8,128)(2,1)S(1)}, u32[]{:S(2)}, u32[]{:S(2)}) collective-permute-start(bf16[4,64,1024]{2,1,0:T(8,128)(2,1)} %dynamic-slice_bitcast_fusion.2), channel_id=1, source_target_pairs={{0,4},{4,0},{1,5},{5,1},{2,6},{6,2},{3,7},{7,3},{8,12},{12,8},{9,1... | collective-permute-start | bytes 1572872 | tf_op jit(solution)/shard_map/ppermute | solution.py:367
  406.4 34.9 %collective-permute-start.55 = (bf16[4,2,32,1024]{3,2,1,0:T(8,128)(2,1)}, bf16[4,2,32,1024]{3,2,1,0:T(8,128)(2,1)}, u32[]{:S(2)}, u32[]{:S(2)}) collective-permute-start(bf16[4,2,32,1024]{3,2,1,0:T(8,128)(2,1)} %dynamic-slice_bitcast_fusion), channel_id=1, source_target_pairs={{0,4},{4,0},{1,5},{5,1},{2,6},{6,2},{3,7},{7,3},{8,12},{12,8},{9,1... | collective-permute-start | bytes 1572872 | tf_op jit(solution)/shard_map/ppermute | solution.py:367
  407.2 34.2 %collective-permute-start.54 = (bf16[4,128,1024]{2,1,0:T(8,128)(2,1)}, bf16[4,128,1024]{2,1,0:T(8,128)(2,1)}, u32[]{:S(2)}, u32[]{:S(2)}) collective-permute-start(bf16[4,128,1024]{2,1,0:T(8,128)(2,1)} %fusion.15), channel_id=1, source_target_pairs={{0,2},{2,0},{1,3},{3,1},{4,6},{6,4},{5,7},{7,5},{8,10},{10,8},{9,1... | collective-permute-start | bytes 3145736 | tf_op jit(solution)/shard_map/ppermute | solution.py:367
  426.0 27.4 %collective-permute-start.52 = (bf16[512,1024]{1,0:T(8,128)(2,1)}, bf16[512,1024]{1,0:T(8,128)(2,1)}, u32[]{:S(2)}, u32[]{:S(2)}) collective-permute-start(bf16[512,1024]{1,0:T(8,128)(2,1)} %convolution_convert_fusion.8), channel_id=1, source_target_pairs={{0,4},{4,0},{1,5},{5,1},{2,6},{6,2},{3,7},{7,3},{8,12},{12,8},{9,1... | collective-permute-start | bytes 3145736 | tf_op jit(solution)/shard_map/ppermute | solution.py:367
  427.3 28.0 %collective-permute-start.53 = (bf16[512,1024]{1,0:T(8,128)(2,1)}, bf16[512,1024]{1,0:T(8,128)(2,1)}, u32[]{:S(2)}, u32[]{:S(2)}) collective-permute-start(bf16[512,1024]{1,0:T(8,128)(2,1)} %convolution_convert_fusion.7), channel_id=1, source_target_pairs={{0,2},{2,0},{1,3},{3,1},{4,6},{6,4},{5,7},{7,5},{8,10},{10,8},{9,1... | collective-permute-start | bytes 3145736 | tf_op jit(solution)/shard_map/ppermute | solution.py:367
  456.6 14.0 %collective-permute-start.58 = (bf16[4,32,1024]{2,1,0:T(8,128)(2,1)S(1)}, bf16[4,32,1024]{2,1,0:T(8,128)(2,1)S(1)}, u32[]{:S(2)}, u32[]{:S(2)}) collective-permute-start(bf16[4,32,1024]{2,1,0:T(8,128)(2,1)S(1)} %dynamic-slice_bitcast_fusion.5), channel_id=1, source_target_pairs={{0,2},{2,0},{1,3},{3,1},{4,6},{6,4},{5,7},{7,5},{8,10},{10,8},{9,1... | collective-permute-start | bytes 786440 | tf_op jit(solution)/shard_map/ppermute | solution.py:367
  467.8 37.3 %collective-permute-start.56 = (bf16[768,1024]{1,0:T(8,128)(2,1)}, bf16[768,1024]{1,0:T(8,128)(2,1)}, u32[]{:S(2)}, u32[]{:S(2)}) collective-permute-start(bf16[768,1024]{1,0:T(8,128)(2,1)} %pad_maximum_fusion.4), channel_id=1, source_target_pairs={{0,4},{4,0},{1,5},{5,1},{2,6},{6,2},{3,7},{7,3},{8,12},{12,8},{9,1... | collective-permute-start | bytes 4718600 | tf_op jit(solution)/shard_map/ppermute | solution.py:367
  469.2 36.0 %collective-permute-start.57 = (bf16[768,1024]{1,0:T(8,128)(2,1)}, bf16[768,1024]{1,0:T(8,128)(2,1)}, u32[]{:S(2)}, u32[]{:S(2)}) collective-permute-start(bf16[768,1024]{1,0:T(8,128)(2,1)} %pad_maximum_fusion.5), channel_id=1, source_target_pairs={{0,2},{2,0},{1,3},{3,1},{4,6},{6,4},{5,7},{7,5},{8,10},{10,8},{9,1... | collective-permute-start | bytes 4718600 | tf_op jit(solution)/shard_map/ppermute | solution.py:367
  480.2 91.4 %reduce-scatter.11.cloned.1.call-start = ((), (), s32[]{:S(2)}) async-start(), calls=%async_computation.7 | async-start | bytes 2785280 | tf_op jit(solution)/shard_map/reduce_scatter | solution.py:711
  483.4 21.6 %collective-permute-start.60 = (f32[4,1216]{1,0:T(4,128)S(1)}, f32[4,1216]{1,0:T(4,128)S(1)}, u32[]{:S(2)}, u32[]{:S(2)}) collective-permute-start(f32[4,1216]{1,0:T(4,128)S(1)} %bitcast.481), channel_id=1, source_target_pairs={{0,2},{2,0},{1,3},{3,1},{4,6},{6,4},{5,7},{7,5},{8,10},{10,8},{9,1... | collective-permute-start | bytes 58376 | tf_op jit(solution)/shard_map/ppermute | solution.py:367
  485.2 19.8 %collective-permute-start.61 = (f32[4,1216]{1,0:T(4,128)S(1)}, f32[4,1216]{1,0:T(4,128)S(1)}, u32[]{:S(2)}, u32[]{:S(2)}) collective-permute-start(f32[4,1216]{1,0:T(4,128)S(1)} %bitcast.480), channel_id=1, source_target_pairs={{0,4},{4,0},{1,5},{5,1},{2,6},{6,2},{3,7},{7,3},{8,12},{12,8},{9,1... | collective-permute-start | bytes 58376 | tf_op jit(solution)/shard_map/ppermute | solution.py:367
  485.8 19.2 %collective-permute-start.62 = (f32[4,1216]{1,0:T(4,128)S(1)}, f32[4,1216]{1,0:T(4,128)S(1)}, u32[]{:S(2)}, u32[]{:S(2)}) collective-permute-start(f32[4,1216]{1,0:T(4,128)S(1)} %bitcast.479), channel_id=1, source_target_pairs={{0,6},{6,0},{2,4},{4,2},{1,7},{7,1},{3,5},{5,3},{8,14},{14,8},{10,... | collective-permute-start | bytes 58376 | tf_op jit(solution)/shard_map/ppermute | solution.py:753
  546.6 14.5 %collective-permute-start.69 = (bf16[2,128,1024]{2,1,0:T(8,128)(2,1)}, bf16[2,128,1024]{2,1,0:T(8,128)(2,1)S(1)}, u32[]{:S(2)}, u32[]{:S(2)}) collective-permute-start(bf16[2,128,1024]{2,1,0:T(8,128)(2,1)} %slice.468), channel_id=1, source_target_pairs={{0,2},{2,0},{1,3},{3,1},{4,6},{6,4},{5,7},{7,5},{8,10},{10,8},{9,1... | collective-permute-start | bytes 1572872 | tf_op jit(solution)/shard_map/ppermute | solution.py:367
  (132 other events, 857.0 us)
Sparse Core Ops, SparseCore 0:
  10.2 32.8 all-gather.10
  45.3 28.7 all-gather.8
  75.6 40.5 all-gather.12
  117.6 148.4 all-gather.14
  310.9 76.3 reduce-scatter.4
  398.1 59.7 reduce-scatter.6
  480.3 42.6 reduce-scatter.8
  526.9 44.6 reduce-scatter.10
